TPU v7x, 32 devices: a whole 2x2x4 slice. The times are simulated.
32 devices in a mesh: rows: 16 (over z, y, x), task: 2 (over core).
Axes of the slice: x: 2, y: 2, z: 4, core: 2. Of those that a mesh axis runs over, the one named last changes fastest.
Arguments:
- emb: bfloat16 [98304, 416], P('rows'), may hold values from -6 to 6
- dense: bfloat16 [98304, 13], P('rows'), may hold values from -6 to 6
- group_sizes: int32 [48, 512], P('rows'), may hold values from 1 to 16, 2048 in all within a row
- labels: int32 [2, 98304], P('task', 'rows'), may hold values 0 or 1
- w_emb: bfloat16 [416, 512], P(None, 'rows'), may hold values from -0.3125 to 0.3125
- w_dense: bfloat16 [13, 512], P(None, 'rows'), may hold values from -0.3125 to 0.3125
- b_in: bfloat16 [512], P('rows'), may hold values from -4 to 4
- expert_w1: bfloat16 [8, 512, 256], P('task', 'rows'), may hold values from -0.25 to 0.25
- expert_b1: bfloat16 [8, 256], P('task', 'rows'), may hold values from -4 to 4
- expert_w2: bfloat16 [8, 256, 128], P('task', 'rows'), may hold values from -0.375 to 0.375
- expert_b2: bfloat16 [8, 128], P('task', 'rows'), may hold values from -4 to 4
- gate_w: bfloat16 [2, 512, 8], P('task', 'rows'), may hold values from -0.125 to 0.125
- gate_b: bfloat16 [2, 8], P('task'), may hold values from -4 to 4
- tower_w1: bfloat16 [2, 128, 64], P('task', 'rows'), may hold values from -1 to 1
- tower_b1: bfloat16 [2, 64], P('task'), may hold values from -4 to 4
- tower_w2: bfloat16 [2, 64], P('task'), may hold values from -1.5 to 1.5
- tower_b2: bfloat16 [2], P('task'), may hold values from -6 to 6
Outputs:
- emb_grad: float32 [98304, 416], P('rows')
- dense_grad: float32 [98304, 13], P('rows')
- w_emb_grad: float32 [416, 512], P(None, 'rows')
- w_dense_grad: float32 [13, 512], P(None, 'rows')
- b_in_grad: float32 [512], P('rows')
- expert_w1_grad: float32 [8, 512, 256], P('task', 'rows')
- expert_b1_grad: float32 [8, 256], P('task', 'rows')
- expert_w2_grad: float32 [8, 256, 128], P('task', 'rows')
- expert_b2_grad: float32 [8, 128], P('task', 'rows')
- gate_w_grad: float32 [2, 512, 8], P('task', 'rows')
- gate_b_grad: float32 [2, 8], P('task')
- tower_w1_grad: float32 [2, 128, 64], P('task', 'rows')
- tower_b1_grad: float32 [2, 64], P('task')
- tower_w2_grad: float32 [2, 64], P('task')
- tower_b2_grad: float32 [2], P('task')
Inputs may be any that keep to these rules, and one draw needn't show every extreme that they name: Each row of group_sizes sums to 2048; its largest entry is exactly 16.
All inputs are finite; a program needn't handle non-finite values. No bound on the sum of `labels` on one device may be relied on, other than what follows from the above.
Results may differ from a plain program's by a relative error of at most 0.02.
Values may be sent and summed in bfloat16 or wider, within the bound.
No kernel may reach another device: no remote copies, remote signals or barrier semaphores. Data moves between devices by JAX's collectives and lax.ppermute only.
A program may use at most 192 MiB of HBM per device.

v0:
```python
import jax
import jax.numpy as jnp
from jax import lax
from jax.sharding import PartitionSpec as P


def silu_slope(values):
    logistic = jax.nn.sigmoid(values)
    return logistic * (1.0 + values * (1.0 - logistic))


def body(
    emb,
    dense,
    group_sizes,
    labels,
    w_emb,
    w_dense,
    b_in,
    expert_w1,
    expert_b1,
    expert_w2,
    expert_b2,
    gate_w,
    gate_b,
    tower_w1,
    tower_b1,
    tower_w2,
    tower_b2,
):
    batches = group_sizes.shape[0]
    batch_rows = emb.shape[0] // batches
    user_count = group_sizes.shape[1] * batches * lax.axis_size("rows")
    highest = lax.Precision.HIGHEST
    wide = jnp.float32
    narrow = jnp.bfloat16
    emb_parts = []
    dense_parts = []
    shards = None
    totals = None
    for batch_id in range(batches):
        fetch_pulled = (
            lax.all_gather(w_emb, "rows", axis=1, tiled=True),
            lax.all_gather(w_dense, "rows", axis=1, tiled=True),
            lax.all_gather(b_in, "rows", axis=0, tiled=True),
            lax.all_gather(expert_w1, "rows", axis=1, tiled=True),
            lax.all_gather(expert_b1, "rows", axis=1, tiled=True),
            lax.all_gather(expert_w2, "rows", axis=1, tiled=True),
            lax.all_gather(expert_b2, "rows", axis=1, tiled=True),
            lax.all_gather(gate_w, "rows", axis=1, tiled=True),
            lax.all_gather(tower_w1, "rows", axis=1, tiled=True),
        )
        paired = None
        pulled, paired = (fetch_pulled, paired)
        row_start = batch_id * batch_rows
        features = emb[row_start : row_start + batch_rows]
        dense_in = dense[row_start : row_start + batch_rows]
        group_rows = group_sizes[batch_id]
        target = labels[0, row_start : row_start + batch_rows].astype(wide)
        emb_w, dense_w, in_bias, own_w1, own_b1, own_w2, own_b2, gate_full, tower_full = pulled
        hidden = (
            jnp.dot(features, emb_w, preferred_element_type=wide)
            + jnp.dot(dense_in, dense_w, preferred_element_type=wide)
            + in_bias.astype(wide)[None, :]
        )
        shared = hidden.astype(narrow)
        first_pre = (
            jnp.einsum("rd,kdf->rkf", shared, own_w1, preferred_element_type=wide)
            + own_b1.astype(wide)[None]
        )
        middle = jax.nn.silu(first_pre).astype(narrow)
        second_pre = (
            jnp.einsum("rkf,kfo->rko", middle, own_w2, preferred_element_type=wide)
            + own_b2.astype(wide)[None]
        )
        own_out = jax.nn.silu(second_pre).astype(narrow)
        experts_all = lax.all_gather(own_out, "task", axis=1, tiled=True)
        logits = (
            jnp.dot(shared, gate_full[0], preferred_element_type=wide)
            + gate_b[0].astype(wide)[None, :]
        )
        gate_probs = jax.nn.softmax(logits, axis=-1)
        experts_wide = experts_all.astype(wide)
        mixture = jnp.einsum("rk,rko->ro", gate_probs, experts_wide, precision=highest)
        tower_in = mixture.astype(narrow)
        tower_pre = (
            jnp.dot(tower_in, tower_full[0], preferred_element_type=wide)
            + tower_b1[0].astype(wide)[None, :]
        )
        tower_act = jax.nn.silu(tower_pre)
        head_w = tower_w2[0].astype(wide)
        task_logit = jnp.sum(tower_act * head_w[None, :], axis=1) + tower_b2[0].astype(wide)
        group_ends = jnp.cumsum(group_rows)
        group_starts = group_ends - group_rows
        places = jnp.arange(batch_rows, dtype=jnp.int32)[:, None]
        inside = (places >= group_starts[None, :]) & (places < group_ends[None, :])
        inverse = 1.0 / group_rows.astype(wide)
        weights_row = jnp.sum(
            jnp.where(inside, inverse[None, :], jnp.zeros_like(inverse)[None, :]), axis=1
        )
        logit_slope = weights_row * (jax.nn.sigmoid(task_logit) - target)
        grad_head_bias = jnp.sum(logit_slope)
        grad_head_w = jnp.sum(logit_slope[:, None] * tower_act, axis=0)
        tower_grad = (logit_slope[:, None] * head_w[None, :] * silu_slope(tower_pre)).astype(narrow)
        grad_tower_w = jnp.einsum("ro,rh->oh", tower_in, tower_grad, preferred_element_type=wide)
        grad_tower_b = jnp.sum(tower_grad.astype(wide), axis=0)
        mix_grad = (
            jnp.einsum("rh,oh->ro", tower_grad, tower_full[0], preferred_element_type=wide)
            .astype(narrow)
            .astype(wide)
        )
        probs_grad = jnp.einsum("rko,ro->rk", experts_wide, mix_grad, precision=highest)
        logit_grad = gate_probs * (
            probs_grad - jnp.sum(gate_probs * probs_grad, axis=1, keepdims=True)
        )
        grad_gate_b = jnp.sum(logit_grad, axis=0)
        grad_gate_w = jnp.einsum("rd,rk->dk", shared.astype(wide), logit_grad, precision=highest)
        expert_part = gate_probs[:, :, None] * mix_grad[:, None, :]
        expert_grad = lax.psum_scatter(
            expert_part.astype(jnp.bfloat16), "task", scatter_dimension=1, tiled=True
        ).astype(jnp.float32)
        second_grad = (expert_grad * silu_slope(second_pre)).astype(narrow)
        grad_b2 = jnp.sum(second_grad.astype(wide), axis=0)
        grad_w2 = jnp.einsum("rkf,rko->kfo", middle, second_grad, preferred_element_type=wide)
        middle_grad = jnp.einsum("rko,kfo->rkf", second_grad, own_w2, preferred_element_type=wide)
        first_grad = (middle_grad * silu_slope(first_pre)).astype(narrow)
        grad_b1 = jnp.sum(first_grad.astype(wide), axis=0)
        grad_w1 = jnp.einsum("rd,rkf->kdf", shared, first_grad, preferred_element_type=wide)
        input_part = jnp.einsum(
            "rkf,kdf->rd", first_grad, own_w1, preferred_element_type=wide
        ) + jnp.einsum("rk,dk->rd", logit_grad, gate_full[0].astype(wide), precision=highest)
        hidden_grad = (
            lax.psum(input_part.astype(jnp.bfloat16), "task").astype(jnp.float32).astype(narrow)
        )
        grad_emb_w = jnp.einsum("re,rd->ed", features, hidden_grad, preferred_element_type=wide)
        grad_dense_w = jnp.einsum("re,rd->ed", dense_in, hidden_grad, preferred_element_type=wide)
        grad_in_bias = jnp.sum(hidden_grad.astype(wide), axis=0)
        emb_piece = jnp.einsum("rd,ed->re", hidden_grad, emb_w, preferred_element_type=wide)
        dense_piece = jnp.einsum("rd,ed->re", hidden_grad, dense_w, preferred_element_type=wide)
        micro_large_grads = (
            grad_emb_w,
            grad_dense_w,
            grad_in_bias,
            grad_w1,
            grad_b1,
            grad_w2,
            grad_b2,
            grad_gate_w[None],
            grad_tower_w[None],
        )
        micro_tiny_terms = (grad_gate_b, grad_tower_b, grad_head_w, grad_head_bias[None])
        large_grads, tiny_terms, emb_piece, dense_piece = (
            micro_large_grads,
            micro_tiny_terms,
            emb_piece,
            dense_piece,
        )
        reduce_shards = (
            lax.psum_scatter(large_grads[0], "rows", scatter_dimension=1, tiled=True),
            lax.psum_scatter(large_grads[1], "rows", scatter_dimension=1, tiled=True),
            lax.psum_scatter(large_grads[2], "rows", scatter_dimension=0, tiled=True),
            lax.psum_scatter(large_grads[3], "rows", scatter_dimension=1, tiled=True),
            lax.psum_scatter(large_grads[4], "rows", scatter_dimension=1, tiled=True),
            lax.psum_scatter(large_grads[5], "rows", scatter_dimension=1, tiled=True),
            lax.psum_scatter(large_grads[6], "rows", scatter_dimension=1, tiled=True),
            lax.psum_scatter(large_grads[7], "rows", scatter_dimension=1, tiled=True),
            lax.psum_scatter(large_grads[8], "rows", scatter_dimension=1, tiled=True),
        )
        reduce_totals = lax.psum(
            (tiny_terms[0], tiny_terms[1], tiny_terms[2], tiny_terms[3]), "rows"
        )
        emb_parts.append(emb_piece)
        dense_parts.append(dense_piece)
        if batch_id == 0:
            shards, totals = (reduce_shards, reduce_totals)
        else:
            shards = jax.tree.map(jnp.add, shards, reduce_shards)
            totals = jax.tree.map(jnp.add, totals, reduce_totals)
    emb_grad = jnp.concatenate(emb_parts, axis=0)
    dense_grad = jnp.concatenate(dense_parts, axis=0)
    scaled = [part / user_count for part in shards]
    small_scaled = [part / user_count for part in totals]
    return (
        emb_grad,
        dense_grad,
        scaled[0],
        scaled[1],
        scaled[2],
        scaled[3],
        scaled[4],
        scaled[5],
        scaled[6],
        scaled[7],
        small_scaled[0][None],
        scaled[8],
        small_scaled[1][None],
        small_scaled[2][None],
        small_scaled[3],
    )


def solution(mesh):
    in_specs = (
        P("rows", None),
        P("rows", None),
        P("rows", None),
        P("task", "rows"),
        P(None, "rows"),
        P(None, "rows"),
        P("rows"),
        P("task", "rows", None),
        P("task", "rows"),
        P("task", "rows", None),
        P("task", "rows"),
        P("task", "rows", None),
        P("task", None),
        P("task", "rows", None),
        P("task", None),
        P("task", None),
        P("task"),
    )
    out_specs = (
        P("rows", None),
        P("rows", None),
        P(None, "rows"),
        P(None, "rows"),
        P("rows"),
        P("task", "rows", None),
        P("task", "rows"),
        P("task", "rows", None),
        P("task", "rows"),
        P("task", "rows", None),
        P("task", None),
        P("task", "rows", None),
        P("task", None),
        P("task", None),
        P("task"),
    )
    return jax.shard_map(body, mesh=mesh, in_specs=in_specs, out_specs=out_specs, check_vma=False)
```

profile of v0, /device:TPU:0, one launch (start us, length us, event | category | flops | bytes accessed | tf_op | source)
XLA Modules:
  0.0 1138.4 jit_solution(17640242086680916027)
XLA Ops:
  8.0 42.7 %all-gather.1 = bf16[16,16,4]{1,2,0:T(4,128)(2,1)S(1)} all-gather(bf16[1,16,4]{1,2,0:T(4,128)(2,1)} %bitcast.398), channel_id=1, replica_groups=mesh['rows'=16,'task'=2] {'rows'}, dimensions={0}, use_global_device_ids=true | all-gather | bytes 2176 | tf_op jit(solution)/shard_map/all_gather | solution.py:47
  50.7 39.8 %all_gather.24 = bf16[416,512]{0,1:T(8,128)(2,1)S(1)} all-gather(bf16[416,32]{0,1:T(8,128)(2,1)} %param.21), channel_id=1, replica_groups=mesh['rows'=16,'task'=2] {'rows'}, dimensions={1}, use_global_device_ids=true | all-gather | bytes 452608 | tf_op jit(solution)/shard_map/all_gather | solution.py:43
  90.5 5.0 fusion.61
  95.6 39.0 %all_gather.60 = bf16[4,256,128]{2,1,0:T(8,128)(2,1)S(1)} all-gather(bf16[4,16,128]{2,1,0:T(8,128)(2,1)S(1)} %copy-done.39), channel_id=1, replica_groups=mesh['rows'=16,'task'=2] {'rows'}, dimensions={1}, use_global_device_ids=true | all-gather | bytes 278528 | tf_op jit(solution)/shard_map/all_gather | solution.py:48
  136.1 36.6 %all-reduce = bf16[512]{0:T(512)(128)(2,1)S(1)} all-reduce(bf16[512]{0:T(512)(128)(2,1)S(1)} %dynamic-update-slice), channel_id=1, replica_groups=mesh['rows'=16,'task'=2] {'rows'}, use_global_device_ids=true, to_apply=%add | all-reduce | flops 512 | bytes 2048
  172.8 37.5 %all-gather.2 = bf16[16,8,4]{1,2,0:T(4,128)(2,1)S(1)} all-gather(bf16[1,8,4]{1,2,0:T(4,128)(2,1)S(1)} %bitcast.399), channel_id=1, replica_groups=mesh['rows'=16,'task'=2] {'rows'}, dimensions={0}, use_global_device_ids=true | all-gather | bytes 1088 | tf_op jit(solution)/shard_map/all_gather | solution.py:49
  210.6 35.8 %all-gather = bf16[16,32,13]{1,2,0:T(8,128)(2,1)S(1)} all-gather(bf16[1,32,13]{1,2,0:T(8,128)(2,1)S(1)} %bitcast.386), channel_id=1, replica_groups=mesh['rows'=16,'task'=2] {'rows'}, dimensions={0}, use_global_device_ids=true | all-gather | bytes 14144 | tf_op jit(solution)/shard_map/all_gather | solution.py:44
  246.5 4.4 add_convert_fusion
  251.0 2.9 fusion.65
  258.0 7.6 fusion.55
  265.6 5.7 fusion.47
  271.3 15.4 %multiply_convert_fusion.3 = (bf16[2048,4,256]{2,0,1:T(8,128)(2,1)}, bf16[2048,4,256]{2,0,1:T(8,128)(2,1)S(1)}, bf16[2048,4,256]{2,0,1:T(8,128)(2,1)S(1)}, f32[2048,4,256]{2,0,1:T(8,128)}) fusion(f32[4,256]{1,0:T(4,128)S(1)} %bitcast.387, f32[2048,4,256]{2,0,1:T(8,128)} %fusion.47, f32[2048,4,256]{2,0,1:T(8,128)} %fusion.55, ...), kind=kOutput, calls=%fused_computation.14 | convolution fusion | flops 2185232384 | bytes 40898560 | tf_op jit(solution)/shard_map/rd,kdf->rkf/dot_general | solution.py:68
  291.3 3.0 copy-done.15
  294.3 4.9 fusion.16
  301.3 38.8 %all_gather.27 = bf16[1,512,8]{2,0,1:T(2,128)(2,1)S(1)} all-gather(bf16[1,32,8]{2,0,1:T(2,128)(2,1)S(1)} %copy.101), channel_id=1, replica_groups=mesh['rows'=16,'task'=2] {'rows'}, dimensions={1}, use_global_device_ids=true | all-gather | bytes 8704 | tf_op jit(solution)/shard_map/all_gather | solution.py:50
  351.4 35.9 %all_gather.63 = bf16[1,128,64]{2,1,0:T(8,128)(2,1)S(1)} all-gather(bf16[1,8,64]{2,1,0:T(8,128)(2,1)S(1)} %copy-done.48), channel_id=1, replica_groups=mesh['rows'=16,'task'=2] {'rows'}, dimensions={1}, use_global_device_ids=true | all-gather | bytes 17408 | tf_op jit(solution)/shard_map/all_gather | solution.py:51
  390.9 11.8 %fusion.35 = f32[2048,1,128]{2,1,0:T(1,128)S(1)} fusion(f32[2048,8,1]{1,2,0:T(1,128)} %copy.127, bf16[2048,8,128]{2,0,1:T(8,128)(2,1)} %all-gather.14.cloned.1.call-done), kind=kOutput, calls=%fused_computation.81 | convolution fusion | flops 25165824 | bytes 5308416 | tf_op jit(solution)/shard_map/rk,rko->ro/dot_general | solution.py:84
  404.1 11.7 %fusion.39 = f32[2048,1,128]{2,1,0:T(1,128)S(1)} fusion(f32[2048,8,1]{1,2,0:T(1,128)} %copy.122, bf16[2048,8,128]{2,0,1:T(8,128)(2,1)} %all-gather.12.cloned.1.call-done), kind=kOutput, calls=%fused_computation.85 | convolution fusion | flops 25165824 | bytes 5308416 | tf_op jit(solution)/shard_map/rk,rko->ro/dot_general | solution.py:84
  418.0 11.4 fusion.43
  435.3 4.3 multiply_convert_fusion.2
  440.9 4.2 multiply_convert_fusion.4
  446.4 4.2 multiply_convert_fusion
  450.9 6.4 fusion.33
  459.6 7.1 fusion.41
  468.9 6.4 fusion.37
  489.6 9.2 convert_reduce_fusion.5
  498.9 8.0 convert_reduce_fusion.2
  508.5 3.8 convert_reduce_fusion
  512.3 5.2 convert_reduce_fusion.1
  519.7 3.7 fusion.45
  524.3 5.0 convolution_add_fusion.6
  529.5 4.7 fusion.49
  538.7 5.1 fusion.153
  543.7 3.4 fusion.3
  549.5 3.4 fusion.21
  555.3 3.4 fusion.12
  566.1 71.6 %reduce-scatter.30.cloned.1.call-done = f32[16,4]{1,0:T(8,128)} async-done(((f32[256,4]{1,0:T(8,128)}), f32[16,4]{1,0:T(8,128)}) %reduce-scatter.30.cloned.1.call-update) | async-done | bytes 272
  639.1 73.8 %reduce-scatter.24.cloned.1.call-done = f32[4,16,128]{2,1,0:T(8,128)} async-done(((f32[4,256,128]{2,1,0:T(8,128)}), f32[4,16,128]{2,1,0:T(8,128)}) %reduce-scatter.24.cloned.1.call-update) | async-done | bytes 32784 | tf_op jit(solution)/shard_map/reduce_scatter | solution.py:164
  714.2 126.5 %all-reduce.10.cloned.1.call-done = f32[4,512,256]{2,0,1:T(4,128)} async-done(((f32[4,512,256]{2,0,1:T(4,128)}), f32[4,512,256]{2,0,1:T(4,128)}) %all-reduce.10.cloned.1.call-update) | async-done | bytes 2097168
  842.3 33.4 %all-reduce.12.cloned.1.call-done = (bf16[2048,512]{1,0:T(8,128)(2,1)}, bf16[2048,512]{1,0:T(8,128)(2,1)}, bf16[2048,512]{1,0:T(8,128)(2,1)}) async-done(((bf16[2048,512]{1,0:T(8,128)(2,1)}, bf16[2048,512]{1,0:T(8,128)(2,1)}, bf16[2048,512]{1,0:T(8,128)(2,1)}), (bf16[2048,512]{1,0:T(8,128)(2,1)}, bf16[2048,512]{1,0:T(8,128)(2,1)}, bf16[2048,512]{1,0:T(8,128)(2,1)})) %all-reduce.12.cloned.1.call-update) | async-done | bytes 6291472 | tf_op jit(solution)/shard_map/psum | solution.py:133
  882.6 3.5 fusion.63
  888.9 2.9 fusion.149
  891.8 2.9 fusion.151
  894.6 79.5 %all-reduce.5 = (f32[512]{0:T(512)S(1)}, f32[4,128]{1,0:T(4,128)S(1)}, f32[8]{0:T(128)S(1)}, f32[1,128,64]{2,0,1:T(1,128)S(1)}, f32[64]{0:T(128)S(1)}, /*index=5*/f32[64]{0:T(128)S(1)}, f32[1]{0:T(128)}) all-reduce(f32[512]{0:T(512)S(1)} %add_add_fusion.2, ...), channel_id=25, replica_groups=mesh['rows'=16,'task'=2] {'rows'}, use_global_device_ids=true, to_apply=%region_34.35.clone | all-reduce | flops 9353 | bytes 74824
  980.2 3.4 fusion.71
  989.4 9.2 pad_maximum_fusion
  998.7 53.7 %reduce-scatter.28.cloned.1.call-done = f32[32,13]{1,0:T(8,128)} async-done(((f32[512,13]{1,0:T(8,128)}), f32[32,13]{1,0:T(8,128)}) %reduce-scatter.28.cloned.1.call-update) | async-done | bytes 1680
  1053.7 74.8 %reduce-scatter.26.cloned.1.call-done = f32[32,416]{1,0:T(8,128)} async-done(((f32[512,416]{1,0:T(8,128)}), f32[32,416]{1,0:T(8,128)}) %reduce-scatter.26.cloned.1.call-update) | async-done | bytes 53264
  (314 shorter events, 104.0 us)
Async XLA Ops:
  7.2 250.8 %all-gather.8.cloned.1.call-start = ((), (), s32[]{:S(2)}) async-start(), calls=%async_computation.8 | async-start | bytes 1114112 | tf_op jit(solution)/shard_map/all_gather | solution.py:46
  7.9 383.0 %all-gather.14.cloned.1.call-start = ((), (), s32[]{:S(2)}) async-start(), calls=%async_computation.13 | async-start | bytes 6291456 | tf_op jit(solution)/shard_map/all_gather | solution.py:77
  90.5 164.1 %copy-start.11 = (bf16[416,512]{0,1:T(8,128)(2,1)}, bf16[416,512]{0,1:T(8,128)(2,1)S(1)}, u32[]{:S(2)}) copy-start(bf16[416,512]{0,1:T(8,128)(2,1)S(1)} %all_gather.24) | copy-start | bytes 1277956
  90.5 44.1 %copy-start.49 = (u32[32]{0:T(128)S(1)}, u32[32]{0:T(128)}, u32[]{:S(2)}) copy-start(u32[32]{0:T(128)} %constant.68) | copy-start | bytes 388
  90.5 45.4 %copy-start.60 = (bf16[32]{0:T(256)(128)(2,1)S(1)}, bf16[32]{0:T(256)(128)(2,1)}, u32[]{:S(2)}) copy-start(bf16[32]{0:T(256)(128)(2,1)} %param.23) | copy-start | bytes 196
  90.5 82.3 %copy-start.56 = (bf16[4,8]{1,0:T(4,128)(2,1)S(1)}, bf16[4,8]{1,0:T(4,128)(2,1)}, u32[]{:S(2)}) copy-start(bf16[4,8]{1,0:T(4,128)(2,1)} %param.27) | copy-start | bytes 196
  90.5 120.1 %copy-start.42 = (bf16[13,32]{1,0:T(8,128)(2,1)S(1)}, bf16[13,32]{1,0:T(8,128)(2,1)}, u32[]{:S(2)}) copy-start(bf16[13,32]{1,0:T(8,128)(2,1)} %param.22) | copy-start | bytes 2500
  90.5 156.0 %copy-start.29 = (bf16[6144,13]{0,1:T(8,128)(2,1)S(1)}, bf16[6144,13]{0,1:T(8,128)(2,1)}, u32[]{:S(2)}) copy-start(bf16[6144,13]{0,1:T(8,128)(2,1)} %param.18) | copy-start | bytes 479236
  172.8 98.6 %copy-start.43 = (f32[256,4]{0,1:T(4,128)}, f32[256,4]{0,1:T(4,128)S(1)}, u32[]{:S(2)}) copy-start(f32[256,4]{0,1:T(4,128)S(1)} %reshape.248) | copy-start | bytes 12292
  210.5 80.7 %copy-start.40 = (f32[128,4]{0,1:T(4,128)}, f32[128,4]{0,1:T(4,128)S(1)}, u32[]{:S(2)}) copy-start(f32[128,4]{0,1:T(4,128)S(1)} %reshape.249) | copy-start | bytes 6148
  246.5 9.4 copy-start.27
  246.5 8.1 slice-start
  258.0 7.6 copy-start.58
  291.3 8.0 copy-start.10
  299.2 41.1 %copy-start.61 = (bf16[1,8]{1,0:T(2,128)(2,1)S(1)}, bf16[1,8]{1,0:T(2,128)(2,1)}, u32[]{:S(2)}) copy-start(bf16[1,8]{1,0:T(2,128)(2,1)} %param.29) | copy-start | bytes 52
  299.2 104.8 %all-gather.12.cloned.1.call-start = ((), (), s32[]{:S(2)}) async-start(), calls=%async_computation.11 | async-start | bytes 6291456 | tf_op jit(solution)/shard_map/all_gather | solution.py:77
  340.3 77.7 %all-gather.10.cloned.1.call-start = ((), (), s32[]{:S(2)}) async-start(), calls=%async_computation.9 | async-start | bytes 6291456 | tf_op jit(solution)/shard_map/all_gather | solution.py:77
  342.6 102.5 %copy-start.32 = (f32[2048]{0:T(1024)}, f32[2048]{0:T(1024)S(1)}, u32[]{:S(2)}) copy-start(f32[2048]{0:T(1024)S(1)} %get-tuple-element.176) | copy-start | bytes 24580
  342.6 8.7 copy-start.48
  342.7 102.5 %copy-start.35 = (f32[2048]{0:T(1024)}, f32[2048]{0:T(1024)S(1)}, u32[]{:S(2)}) copy-start(f32[2048]{0:T(1024)S(1)} %fusion.107) | copy-start | bytes 24580
  342.7 44.9 %copy-start.62 = (bf16[1,64]{1,0:T(2,128)(2,1)S(1)}, bf16[1,64]{1,0:T(2,128)(2,1)}, u32[]{:S(2)}) copy-start(bf16[1,64]{1,0:T(2,128)(2,1)} %param.31) | copy-start | bytes 388
  344.6 43.6 %copy-start.63 = (bf16[1,64]{1,0:T(2,128)(2,1)S(1)}, bf16[1,64]{1,0:T(2,128)(2,1)}, u32[]{:S(2)}) copy-start(bf16[1,64]{1,0:T(2,128)(2,1)} %param.32) | copy-start | bytes 388
  344.6 46.2 %copy-start.38 = (s32[1,6144]{1,0:T(1,128)S(1)}, s32[1,6144]{1,0:T(1,128)}, u32[]{:S(2)}) copy-start(s32[1,6144]{1,0:T(1,128)} %param.20) | copy-start | bytes 73732
  345.3 57.4 %copy-start.34 = (f32[2048]{0:T(1024)}, f32[2048]{0:T(1024)S(1)}, u32[]{:S(2)}) copy-start(f32[2048]{0:T(1024)S(1)} %fusion.105) | copy-start | bytes 24580
  349.4 90.3 %copy-start.33 = (f32[2048]{0:T(1024)}, f32[2048]{0:T(1024)S(1)}, u32[]{:S(2)}) copy-start(f32[2048]{0:T(1024)S(1)} %get-tuple-element.179) | copy-start | bytes 24580
  349.5 90.2 %copy-start.36 = (f32[2048]{0:T(1024)}, f32[2048]{0:T(1024)S(1)}, u32[]{:S(2)}) copy-start(f32[2048]{0:T(1024)S(1)} %fusion.103) | copy-start | bytes 24580
  387.9 101.5 %reduce-scatter.20.cloned.1.call-start = ((), (), s32[]{:S(2)}) async-start(), calls=%async_computation.12 | async-start | bytes 6291456 | tf_op jit(solution)/shard_map/reduce_scatter | solution.py:119
  388.2 41.2 %copy-start.57 = (f32[64]{0:T(128)}, f32[64]{0:T(128)S(1)}, u32[]{:S(2)}) copy-start(f32[64]{0:T(128)S(1)} %bitcast_convert_fusion) | copy-start | bytes 772
  404.1 25.4 %copy-start.23 = (f32[2048,64]{0,1:T(8,128)}, f32[2048,64]{0,1:T(8,128)S(1)}, u32[]{:S(2)}) copy-start(f32[2048,64]{0,1:T(8,128)S(1)} %convolution_add_fusion) | copy-start | bytes 1572868
  418.0 11.4 %copy-start.24 = (f32[2048,64]{0,1:T(8,128)S(1)}, f32[2048,64]{0,1:T(8,128)}, u32[]{:S(2)}) copy-start(f32[2048,64]{0,1:T(8,128)} %convolution_add_fusion.1) | copy-start | bytes 1572868
  439.6 49.9 %reduce-scatter.18.cloned.1.call-start = ((), (), s32[]{:S(2)}) async-start(), calls=%async_computation.10 | async-start | bytes 6291456 | tf_op jit(solution)/shard_map/reduce_scatter | solution.py:119
  445.1 44.4 %reduce-scatter.22.cloned.1.call-start = ((), (), s32[]{:S(2)}) async-start(), calls=%async_computation.14 | async-start | bytes 6291456 | tf_op jit(solution)/shard_map/reduce_scatter | solution.py:119
  450.6 114.1 %reduce-scatter.32.cloned.1.call-start = ((), (), s32[]{:S(2)}) async-start(), calls=%async_computation.19 | async-start | bytes 278528
  459.6 18.0 %copy-start.31 = (f32[2048,1,8]{0,2,1:T(8,128)}, f32[2048,1,8]{0,2,1:T(8,128)S(1)}, u32[]{:S(2)}) copy-start(f32[2048,1,8]{0,2,1:T(8,128)S(1)} %copy.131) | copy-start | bytes 196612
  477.6 9.6 copy-start.4
  489.0 148.7 %reduce-scatter.30.cloned.1.call-start = ((), (), s32[]{:S(2)}) async-start(), calls=%async_computation.18 | async-start | bytes 139264
  489.5 9.3 copy-start.44
  489.6 18.9 %slice-start.2 = ((s8[8388608]{0:T(1024)(128)(4,1)}), s8[4194304]{0:T(1024)(128)(4,1)S(1)}, s32[]{:S(2)}) async-start(s8[8388608]{0:T(1024)(128)(4,1)} %bitcast.400), calls=%async_computation.24 | async-start | bytes 8388608
  498.8 9.7 copy-start.14
  498.8 8.0 copy-start.8
  498.8 9.6 slice-start.3
  524.3 188.6 %reduce-scatter.24.cloned.1.call-start = ((), (), s32[]{:S(2)}) async-start(), calls=%async_computation.15 | async-start | bytes 557056 | tf_op jit(solution)/shard_map/reduce_scatter | solution.py:164
  529.4 311.3 %all-reduce.10.cloned.1.call-start = ((), (), s32[]{:S(2)}) async-start(), calls=%async_computation.20 | async-start | bytes 4194304
  538.4 337.3 %all-reduce.12.cloned.1.call-start = ((), (), s32[]{:S(2)}) async-start(), calls=%async_computation.21 | async-start | bytes 12582912 | tf_op jit(solution)/shard_map/psum | solution.py:133
  558.8 319.0 %copy-start.30 = (bf16[6144,13]{0,1:T(8,128)(2,1)S(1)}, bf16[6144,13]{0,1:T(8,128)(2,1)}, u32[]{:S(2)}) copy-start(bf16[6144,13]{0,1:T(8,128)(2,1)} %param.18) | copy-start | bytes 479236
  558.8 493.6 %reduce-scatter.28.cloned.1.call-start = ((), (), s32[]{:S(2)}) async-start(), calls=%async_computation.17 | async-start | bytes 278528
  562.5 317.8 %copy-start.28 = (bf16[512,13]{0,1:T(8,128)(2,1)S(1)}, bf16[512,13]{0,1:T(8,128)(2,1)}, u32[]{:S(2)}) copy-start(bf16[512,13]{0,1:T(8,128)(2,1)} %copy-done.27) | copy-start | bytes 39940
  980.2 148.3 %reduce-scatter.26.cloned.1.call-start = ((), (), s32[]{:S(2)}) async-start(), calls=%async_computation.16 | async-start | bytes 1114112
  (38 other events, 170.3 us)
Sparse Core Ops, SparseCore 0:
  10.8 58.3 all-gather.7
  299.4 11.4 all-gather.13
  340.4 9.5 all-gather.11
  388.1 11.1 all-gather.9
  439.7 9.5 reduce-scatter.19
  451.5 13.3 reduce-scatter.17
  467.2 13.3 reduce-scatter.21
  489.1 73.5 reduce-scatter.31
  565.5 72.1 reduce-scatter.29
  639.9 72.9 reduce-scatter.23
  718.3 122.3 all-reduce.9
  844.1 31.5 all-reduce.11
  980.3 72.0 reduce-scatter.27
  1054.6 73.9 reduce-scatter.25
where the time goes:
time: 1150 us; the launch traced here: 1140 us
  waiting for transfers between devices  435 us (38%)
  blocking collectives  386 us (34%)
  matrix products  205 us (18%)
  other arithmetic  56.6 us (5%)
  local copies, waits for them, and re-layouts  32.3 us (3%)
  between operations  22.1 us (2%)
    unnamed x19, waiting for transfers between devices  327 us
    unnamed x2, blocking collectives  116 us
    reduce_scatter x1, waiting for transfers between devices, body(): lax.psum_scatter(large_grads[5], 'rows', scatter_dimension=1, tiled=True)  73.8 us
    all_gather x1, blocking collectives, body(): lax.all_gather(expert_b1, 'rows', axis=1, tiled=True)  42.7 us
    all_gather x1, blocking collectives, body(): lax.all_gather(w_emb, 'rows', axis=1, tiled=True)  39.8 us
    all_gather x1, blocking collectives, body(): lax.all_gather(expert_w2, 'rows', axis=1, tiled=True)  39 us
    all_gather x1, blocking collectives, body(): lax.all_gather(gate_w, 'rows', axis=1, tiled=True)  38.8 us
    all_gather x1, blocking collectives, body(): lax.all_gather(expert_b2, 'rows', axis=1, tiled=True)  37.5 us
  transfers between devices with their start and end apart: 14, of which 6 were waited for; matrix products, arithmetic and copies ran while one was open for 18% of the time, Pallas kernels for 0%

commit v1 on v0

v1 whole, which is shorter than its diff:
```python
import functools

import jax
import jax.numpy as jnp
from jax import lax
from jax.experimental import pallas as pl
from jax.experimental.pallas import tpu as pltpu
from jax.sharding import PartitionSpec as P

F32 = jnp.float32
BF = jnp.bfloat16
NT = (((1,), (1,)), ((), ()))
D, FH, EO, TW, NE = 512, 256, 128, 64, 8
HALF = NE // 2
EMB, DENSE = 416, 13
XR = 448
PC = 512 + HALF * FH
QC = HALF * EO + 256
FG = NE * FH + 128
TILE = 512
BOTH = (((0, 1), (1, 0)))


def mm(a, b):
    return jnp.dot(a, b, preferred_element_type=F32)


def mm_nt(a, b):
    return lax.dot_general(a, b, NT, preferred_element_type=F32)


def act_pair(half):
    t = jnp.tanh(half)
    q = 1.0 + t
    m = half * q
    return m, q + m * (1.0 - t)


def swap_halves(a, flag):
    return jnp.where(flag, jnp.concatenate([a[HALF:NE], a[0:HALF]], axis=0), a)


def lane_fold(a):
    total = a[:, 0:128]
    for c in range(1, a.shape[1] // 128):
        total = total + a[:, 128 * c : 128 * c + 128]
    return total


def main_kernel(pieces, chunks, tab_ref, *refs):
    emb_ref, dense_ref, row_ref, vec_ref = refs[:4]
    p_refs = (refs[4 : 4 + pieces], refs[4 + pieces : 4 + 2 * pieces])
    q_refs = (refs[4 + 2 * pieces : 4 + 3 * pieces], refs[4 + 3 * pieces : 4 + 4 * pieces])
    refs = refs[4 + 4 * pieces :]
    eg_ref, dg_ref, hg_ref, wa_ref, dpo_ref, dpx_ref, dqo_ref, dqx_ref = refs[:8]
    (
        x_s, hid_s, mid_s, sl1_s, out_s, sl2_s, sg_s, fg_s, mix_s,
        wat_s, wa_s, w1t_s, gt_s, w1_s, w2t_s, w2_s, b1_s, b2_s, gb_s, tt_s, tw_s, tcol_s, q_s,
        dwa_s, dw1_s, dw2_s, dtw_s, dcol_s, dlog_s, db1_s, ob_s,
    ) = refs[8:]
    n = emb_ref.shape[1]
    fs, osz = FH // chunks, EO // chunks
    step = pl.program_id(0)
    second_core = tab_ref[0] == 1

    @pl.when(step == 0)
    def _():
        rows = lax.broadcasted_iota(jnp.int32, (32, n), 0)
        x_s[EMB:XR, :] = jnp.where(rows == DENSE, 1.0, 0.0).astype(BF)
        ones = jnp.where(lax.broadcasted_iota(jnp.int32, (16, n), 0) == 0, 1.0, 0.0).astype(BF)
        hid_s[D : D + 16, :] = ones
        for k in range(NE):
            mid_s[k, FH : FH + 16, :] = ones
        mix_s[2 * EO : 2 * EO + 16, :] = ones
        fg_s[NE * FH + 16 : FG, :] = jnp.zeros((FG - NE * FH - 16, n), BF)
        for ref in (dwa_s, dw1_s, dw2_s, dtw_s, dcol_s, dlog_s):
            ref[...] = jnp.zeros_like(ref)
        gates = []
        for side in range(2):
            base = HALF * FH * side
            start = 0
            for ref in p_refs[side]:
                size = ref.shape[0] * ref.shape[1]
                flat = ref[...].reshape(size, PC)
                if side == 0:
                    wat_s[start : start + size, :] = flat[:, 0:XR]
                w1_s[start : start + size, base : base + HALF * FH] = flat[:, 512:PC]
                gt_s[start : start + size, :] = flat[:, 384:512].astype(F32)
                start += size
            gates.append(swap_halves(gt_s[...].T[48 : 48 + NE], second_core))
            for k in range(HALF):
                block = w1_s[:, base + FH * k : base + FH * k + FH]
                w1t_s[base + FH * k : base + FH * k + FH, :] = (block.astype(F32).T * 0.5).astype(BF)
            at = 0
            for ref in q_refs[side]:
                for c in range(ref.shape[0]):
                    q_s[tab_ref[1 + at]] = ref[c].astype(F32)
                    at += 1
            cols = HALF * EO
            w2 = q_s[:, :, 0:cols].reshape(FH, cols) * 0.5
            w2_s[:, cols * side : cols * side + cols] = w2.astype(BF)
            w2t_s[cols * side : cols * side + cols, :] = w2.T.astype(BF)
            b1_s[side] = q_s[:, :, cols : cols + 128].reshape(FH, 128) * 0.5
            last = q_s[:, 0:osz, cols + 128 : QC].reshape(EO, 128)
            b2_s[side] = last * 0.5
            tower = last[:, 0:TW]
            rest = jnp.zeros_like(tower)
            both = jnp.concatenate([tower, rest] if side == 0 else [rest, tower], axis=1)
            tw_s[EO * side : EO * side + EO, :] = both.astype(BF)
            tt_s[:, EO * side : EO * side + EO] = (both.T * 0.5).astype(BF)
        wa_s[...] = wat_s[...].astype(F32).T.astype(BF)
        wa_ref[...] = wa_s[...]
        gates = jnp.concatenate(gates, axis=0)
        gt_s[0:16, 0:128] = gates[:, 0:128]
        w1t_s[NE * FH : NE * FH + 16, :] = gates.astype(BF)
        pad = jnp.concatenate([gates, jnp.zeros((112, D), F32)], axis=0)
        w1_s[:, NE * FH : FG] = pad.T.astype(BF)
        vec = vec_ref[...].T
        gb_s[...] = jnp.concatenate([swap_halves(vec[0:NE, 1 + s : 2 + s], second_core) for s in range(2)], axis=0)
        b1 = jnp.concatenate([vec[NE : NE + TW, 1 + s : 2 + s] for s in range(2)], axis=0)
        head = jnp.concatenate([vec[NE + TW : NE + 2 * TW, 1 + s : 2 + s] for s in range(2)], axis=0)
        last = jnp.concatenate([vec[NE + 2 * TW : NE + 2 * TW + 1, 1 + s : 2 + s] for s in range(2)] * 64, axis=0)
        tcol_s[...] = jnp.concatenate([b1 * 0.5, head, head * 0.5, last], axis=1)

    x_s[0:EMB, :] = emb_ref[...]
    x_s[EMB : EMB + DENSE, :] = dense_ref[...]
    x = x_s[...]
    hid = mm(wat_s[...], x).astype(BF)
    hid_s[0:D, :] = hid
    logits = mm(w1t_s[NE * FH : NE * FH + 16, :], hid) + gb_s[...]
    probs = []
    for t in range(2):
        lt = logits[NE * t : NE * t + NE]
        e = jnp.exp(lt - jnp.max(lt, axis=0, keepdims=True))
        probs.append(e / jnp.sum(e, axis=0, keepdims=True))
    mix = [None, None]
    pend = None
    nxt = mm(w1t_s[0:FH, :], hid)
    for k in range(NE + 1):
        h = nxt
        if k < NE - 1:
            nxt = mm(w1t_s[FH * (k + 1) : FH * (k + 2), :], hid)
        if k < NE:
            m, s = act_pair(h + b1_s[k // HALF, :, k % HALF : k % HALF + 1])
            mb = m.astype(BF)
            mid_s[k, 0:FH, :] = mb
            sl1_s[FH * k : FH * k + FH, :] = s.astype(BF)
            h2 = mm(w2t_s[EO * k : EO * k + EO, :], mb)
        if pend is not None:
            j = k - 1
            o, s = act_pair(pend + b2_s[j // HALF, :, TW + j % HALF : TW + j % HALF + 1])
            out_s[EO * j : EO * j + EO, :] = o.astype(out_s.dtype)
            sl2_s[EO * j : EO * j + EO, :] = s.astype(sl2_s.dtype)
            for t in range(2):
                term = probs[t][j : j + 1, :] * o
                mix[t] = term if j == 0 else mix[t] + term
        pend = h2
    mix_s[0:EO, :] = mix[0].astype(BF)
    mix_s[EO : 2 * EO, :] = mix[1].astype(BF)
    act, slope = act_pair(mm(tt_s[...], mix_s[0 : 2 * EO, :]) + tcol_s[:, 0:1])
    weighted = act * tcol_s[:, 1:2]
    lgos = []
    for t in range(2):
        logit = jnp.sum(weighted[TW * t : TW * t + TW], axis=0, keepdims=True) + tcol_s[t : t + 1, 3:4]
        lgos.append(row_ref[0:1, :] * (0.5 * jnp.tanh(0.5 * logit) + 0.5 - row_ref[1 + t : 2 + t, :]))
    lgo = jnp.concatenate([jnp.broadcast_to(lgos[t], (TW, n)) for t in range(2)], axis=0)
    dcol_s[...] += lane_fold(lgo * act)
    dlog_s[...] += lane_fold(jnp.concatenate([jnp.broadcast_to(lgos[t], (8, n)) for t in range(2)], axis=0))
    tg = (lgo * (tcol_s[:, 2:3] * slope)).astype(BF)
    dtw_s[...] += mm_nt(mix_s[...], tg)
    mgh = mm(tw_s[...], tg) * 0.5
    pgs = [[], []]
    mgs = [None] * NE
    for k in range(NE + 2):
        if k < NE:
            o = out_s[EO * k : EO * k + EO, :].astype(F32)
            og = None
            for t in range(2):
                mg = mgh[EO * t : EO * t + EO]
                pgs[t].append(jnp.sum(o * mg, axis=0, keepdims=True))
                term = probs[t][k : k + 1, :] * mg
                og = term if og is None else og + term
            sg = (og * sl2_s[EO * k : EO * k + EO, :].astype(F32)).astype(BF)
            sg_s[EO * k : EO * k + EO, :] = sg
            mgs[k] = mm(w2_s[:, EO * k : EO * k + EO], sg)
        if 1 <= k < NE + 1:
            j = k - 1
            dw2_s[:, EO * j : EO * j + EO] += mm_nt(mid_s[j], sg_s[EO * j : EO * j + EO, :])
            fg = (mgs[j] * sl1_s[FH * j : FH * j + FH, :].astype(F32)).astype(BF)
            fg_s[FH * j : FH * j + FH, :] = fg
        if k >= 2:
            j = k - 2
            dw1_s[:, FH * j : FH * j + FH] += mm_nt(hid_s[...], fg_s[FH * j : FH * j + FH, :])
    lgs = []
    for t in range(2):
        pg = jnp.concatenate(pgs[t], axis=0)
        lgs.append(2.0 * probs[t] * (pg - jnp.sum(probs[t] * pg, axis=0, keepdims=True)))
    fg_s[NE * FH : NE * FH + 16, :] = jnp.concatenate(lgs, axis=0).astype(BF)
    dw1_s[:, NE * FH : FG] += mm_nt(hid_s[...], fg_s[NE * FH : FG, :])
    hg = mm(w1_s[...], fg_s[...]).astype(BF)
    hg_ref[...] = hg
    dwa_s[...] += mm_nt(hg, x)
    eg = mm(wa_s[...], hg)
    eg_ref[...] = eg[0:EMB]
    dg_ref[...] = eg[EMB : EMB + DENSE]

    @pl.when(step == pl.num_programs(0) - 1)
    def _():
        gate = dw1_s[0 : D + 16, NE * FH : FG].T
        dlog = jnp.sum(dlog_s[...], axis=1, keepdims=True)
        dcol = jnp.sum(dcol_s[...].T, axis=0, keepdims=True)
        for side, (dp_ref, dq_ref) in enumerate(((dpo_ref, dqo_ref), (dpx_ref, dqx_ref))):
            own_gate = swap_halves(gate[NE * side : NE * side + NE], second_core)
            col = jnp.concatenate([own_gate[:, 0:D], jnp.zeros((120, D), F32)], axis=0).T
            dp_ref[:, 0:384] = dwa_s[:, 0:384].astype(BF)
            dp_ref[:, 384:512] = jnp.concatenate([dwa_s[:, 384:432], col[:, 0:80]], axis=1).astype(BF)
            dp_ref[:, 512:PC] = dw1_s[0:D, HALF * FH * side : HALF * FH * side + HALF * FH].astype(BF)
            b1 = [dw1_s[D : D + 1, FH * k : FH * k + FH] for k in range(HALF * side, HALF * side + HALF)]
            db1_s[...] = jnp.concatenate(b1 + [jnp.zeros((124, FH), F32)], axis=0).T
            b2 = [dw2_s[FH : FH + 1, EO * k : EO * k + EO] for k in range(HALF * side, HALF * side + HALF)]
            b2 = jnp.concatenate(b2 + [jnp.zeros((60, EO), F32)], axis=0).T
            tower = dtw_s[EO * side : EO * side + EO, TW * side : TW * side + TW]
            ob_s[...] = jnp.concatenate([tower, b2], axis=1)
            lanes = slice(TW * side, TW * side + TW)
            line = jnp.concatenate([dtw_s[2 * EO : 2 * EO + 1, lanes], dcol[:, lanes]], axis=1)
            gate_b = jnp.sum(jnp.where(lax.broadcasted_iota(jnp.int32, (NE, D + 16), 1) == D, own_gate, 0.0), axis=1, keepdims=True)
            small = jnp.concatenate([gate_b, dlog[8 * side : 8 * side + 8]], axis=0)
            small = jnp.concatenate([jnp.broadcast_to(small, (16, 128)), jnp.zeros((112, 128), F32)], axis=0).T[0:1]
            tail = jnp.concatenate([line, small, jnp.zeros((fs - osz - 2, 128), F32)], axis=0)
            for c in range(chunks):
                at = tab_ref[1 + c]
                body_rows = dw2_s[pl.ds(pl.multiple_of(at * fs, fs), fs), HALF * EO * side : HALF * EO * side + HALF * EO]
                dq_ref[fs * c : fs * c + fs, 0 : HALF * EO] = body_rows.astype(BF)
                dq_ref[fs * c : fs * c + fs, HALF * EO : HALF * EO + 128] = db1_s[pl.ds(pl.multiple_of(at * fs, fs), fs), :].astype(BF)
                o_rows = ob_s[pl.ds(pl.multiple_of(at * osz, osz), osz), :]
                dq_ref[fs * c : fs * c + fs, HALF * EO + 128 : QC] = jnp.concatenate([o_rows, tail], axis=0).astype(BF)


def main_call(table, embt, denset, rowdata, p_own, p_other, q_own, q_other):
    rows = embt.shape[1]
    half = rows // 2
    steps = half // TILE
    pieces = len(p_own)
    chunks = sum(a.shape[0] for a in q_own)

    def own(i, c):
        return (0, c[0] * steps + i)

    def const2(i, c):
        return (0, 0)

    def const3(i, c):
        return (0, 0, 0)

    weights = [*p_own, *p_other, *q_own, *q_other]
    vec_at = rows // 256
    spec = pltpu.PrefetchScalarGridSpec(
        num_scalar_prefetch=1,
        grid=(steps,),
        in_specs=[
            pl.BlockSpec((EMB, TILE), own),
            pl.BlockSpec((DENSE, TILE), own),
            pl.BlockSpec((8, TILE), own),
            pl.BlockSpec((8, 256), lambda i, c: (0, vec_at), pipeline_mode=pl.Buffered(1)),
        ]
        + [pl.BlockSpec(a.shape, const3, pipeline_mode=pl.Buffered(1)) for a in weights],
        out_specs=[
            pl.BlockSpec((EMB, TILE), own),
            pl.BlockSpec((DENSE, TILE), own),
            pl.BlockSpec((D, TILE), lambda i, c: (0, i)),
            pl.BlockSpec((XR, D), const2),
            pl.BlockSpec((D, PC), const2),
            pl.BlockSpec((D, PC), const2),
            pl.BlockSpec((FH, QC), const2),
            pl.BlockSpec((FH, QC), const2),
        ],
        scratch_shapes=[
            pltpu.VMEM((XR, TILE), BF),
            pltpu.VMEM((D + 16, TILE), BF),
            pltpu.VMEM((NE, FH + 16, TILE), BF),
            pltpu.VMEM((NE * FH, TILE), BF),
            pltpu.VMEM((NE * EO, TILE), F32),
            pltpu.VMEM((NE * EO, TILE), F32),
            pltpu.VMEM((NE * EO, TILE), BF),
            pltpu.VMEM((FG, TILE), BF),
            pltpu.VMEM((2 * EO + 16, TILE), BF),
            pltpu.VMEM((D, XR), BF),
            pltpu.VMEM((XR, D), BF),
            pltpu.VMEM((NE * FH + 16, D), BF),
            pltpu.VMEM((D, 128), F32),
            pltpu.VMEM((D, FG), BF),
            pltpu.VMEM((NE * EO, FH), BF),
            pltpu.VMEM((FH, NE * EO), BF),
            pltpu.VMEM((2, FH, 128), F32),
            pltpu.VMEM((2, EO, 128), F32),
            pltpu.VMEM((16, 1), F32),
            pltpu.VMEM((2 * TW, 2 * EO), BF),
            pltpu.VMEM((2 * EO, 2 * TW), BF),
            pltpu.VMEM((2 * TW, 4), F32),
            pltpu.VMEM((chunks, FH // chunks, QC), F32),
            pltpu.VMEM((D, XR), F32),
            pltpu.VMEM((D + 16, FG), F32),
            pltpu.VMEM((FH + 16, NE * EO), F32),
            pltpu.VMEM((2 * EO + 16, 2 * TW), F32),
            pltpu.VMEM((2 * TW, 128), F32),
            pltpu.VMEM((16, 128), F32),
            pltpu.VMEM((FH, 128), F32),
            pltpu.VMEM((EO, 128), F32),
        ],
    )
    return pl.pallas_call(
        functools.partial(main_kernel, pieces, chunks),
        grid_spec=spec,
        out_shape=[
            jax.ShapeDtypeStruct((EMB, rows), F32),
            jax.ShapeDtypeStruct((DENSE, rows), F32),
            jax.ShapeDtypeStruct((D, half), BF),
            jax.ShapeDtypeStruct((XR, D), BF),
            jax.ShapeDtypeStruct((D, PC), BF),
            jax.ShapeDtypeStruct((D, PC), BF),
            jax.ShapeDtypeStruct((FH, QC), BF),
            jax.ShapeDtypeStruct((FH, QC), BF),
        ],
        compiler_params=pltpu.CompilerParams(vmem_limit_bytes=60 * 1024 * 1024),
        cost_estimate=pl.CostEstimate(flops=30_000_000_000, bytes_accessed=24_000_000, transcendentals=0),
    )(table, embt, denset, rowdata, rowdata, *weights)


def other_kernel(tab_ref, hg_ref, wa_ref, eg_in, dg_in, eg_ref, dg_ref):
    eg = mm(wa_ref[...], hg_ref[...])
    eg_ref[...] = eg[0:EMB]
    dg_ref[...] = eg[EMB : EMB + DENSE]


def other_call(table, hg, wa, eg, dg):
    steps = hg.shape[1] // TILE

    def far(i, c):
        return (0, (1 - c[0]) * steps + i)

    spec = pltpu.PrefetchScalarGridSpec(
        num_scalar_prefetch=1,
        grid=(steps,),
        in_specs=[
            pl.BlockSpec((D, TILE), lambda i, c: (0, i)),
            pl.BlockSpec((XR, D), lambda i, c: (0, 0)),
            pl.BlockSpec(memory_space=pl.ANY),
            pl.BlockSpec(memory_space=pl.ANY),
        ],
        out_specs=[pl.BlockSpec((EMB, TILE), far), pl.BlockSpec((DENSE, TILE), far)],
    )
    return pl.pallas_call(
        other_kernel,
        grid_spec=spec,
        out_shape=[jax.ShapeDtypeStruct(eg.shape, F32), jax.ShapeDtypeStruct(dg.shape, F32)],
        input_output_aliases={3: 0, 4: 1},
        compiler_params=pltpu.CompilerParams(vmem_limit_bytes=32 * 1024 * 1024),
        cost_estimate=pl.CostEstimate(flops=1_500_000_000, bytes_accessed=9_000_000, transcendentals=0),
    )(table, hg, wa, eg, dg)


def hop(a, mask, size):
    return lax.ppermute(a, "rows", [(i, i ^ mask) for i in range(size)])


def partner(a):
    return lax.ppermute(a, "task", [(0, 1), (1, 0)])


def pad_to(a, rows, cols):
    return jnp.pad(a, ((0, rows - a.shape[0]), (0, cols - a.shape[1])))


def body(
    emb, dense, group_sizes, labels, w_emb, w_dense, b_in, expert_w1, expert_b1, expert_w2, expert_b2,
    gate_w, gate_b, tower_w1, tower_b1, tower_w2, tower_b2,
):
    size = lax.axis_size("rows")
    core = lax.axis_index("task")
    place = lax.axis_index("rows")
    batches = group_sizes.shape[0]
    batch_rows = emb.shape[0] // batches
    user_count = group_sizes.shape[1] * batches * size
    ds, fs, osz = D // size, FH // size, EO // size
    fast = size == 16

    first = jnp.concatenate([w_emb.T, w_dense.T, b_in[:, None], jnp.zeros((ds, 2), BF), gate_w[0], jnp.zeros((ds, 72), BF)], axis=1)
    p_shard = jnp.concatenate([first, jnp.transpose(expert_w1, (1, 0, 2)).reshape(ds, HALF * FH)], axis=1)
    q_shard = jnp.concatenate([jnp.transpose(expert_w2, (1, 0, 2)).reshape(fs, HALF * EO), pad_to(expert_b1.T, fs, 128)], axis=1)
    o_shard = pad_to(jnp.concatenate([tower_w1[0], expert_b2.T], axis=1), osz, 128)
    vec = jnp.concatenate([gate_b, tower_b1, tower_w2, tower_b2[:, None], jnp.zeros((1, 119), BF)], axis=1)
    line = jnp.concatenate([labels.astype(BF), vec], axis=1)
    far_line = partner(line)

    ends = jnp.cumsum(group_sizes, axis=1)
    starts = ends - group_sizes
    places = jnp.arange(batch_rows, dtype=jnp.int32)[None, :, None]
    inside = (places >= starts[:, None, :]) & (places < ends[:, None, :])
    inverse = 1.0 / group_sizes.astype(F32)
    weights_row = jnp.sum(jnp.where(inside, inverse[:, None, :], 0.0), axis=2).reshape(1, -1)
    weights_row = jnp.pad(weights_row, ((0, 0), (0, 256)))
    rowdata = jnp.concatenate([weights_row, line.astype(F32), far_line.astype(F32), jnp.zeros((5, line.shape[1]), F32)], axis=0)

    if fast:
        q_shard = jnp.concatenate([q_shard, pad_to(o_shard, fs, 128)], axis=1)
        zp = jnp.stack([p_shard] + [hop(p_shard, 4 * a, size) for a in range(1, 4)])
        zq = jnp.stack([q_shard] + [hop(q_shard, b, size) for b in range(1, 4)])
        p_own = [zp] + [hop(zp, b, size) for b in range(1, 4)]
        q_own = [zq] + [hop(zq, 4 * a, size) for a in range(1, 4)]
        order = place ^ jnp.arange(16, dtype=jnp.int32)
    else:
        q_all = lax.all_gather(q_shard, "rows", axis=0, tiled=True)
        o_all = lax.all_gather(o_shard, "rows", axis=0, tiled=True)
        p_own = [lax.all_gather(p_shard, "rows", axis=0, tiled=True)[None]]
        q_own = [jnp.concatenate([q_all, pad_to(o_all, FH, 128)], axis=1)[None]]
        order = jnp.zeros((1,), jnp.int32)
    p_other = [partner(a) for a in p_own]
    q_other = [partner(a) for a in q_own]
    table = jnp.concatenate([core[None].astype(jnp.int32), order])

    eg, dg, hg, wa, dp_own, dp_other, dq_own, dq_other = main_call(
        table, emb.T, dense.T, rowdata, p_own, p_other, q_own, q_other
    )
    dp = (dp_own.astype(F32) + partner(dp_other).astype(F32)).astype(BF)
    dq = (dq_own.astype(F32) + partner(dq_other).astype(F32)).astype(BF)
    far_hg = partner(hg)
    eg, dg = other_call(table, far_hg, wa, eg, dg)

    if fast:
        dp = dp.reshape(4, 4, ds, PC)
        dq = dq.reshape(4, 4, fs, QC)
        sp = dp[0].astype(F32) + sum(hop(dp[b], b, size).astype(F32) for b in range(1, 4))
        sq = dq[0].astype(F32) + sum(hop(dq[a], 4 * a, size).astype(F32) for a in range(1, 4))
        sp, sq = sp.astype(BF), sq.astype(BF)
        tp = sp[0].astype(F32) + sum(hop(sp[a], 4 * a, size).astype(F32) for a in range(1, 4))
        tq = sq[0].astype(F32) + sum(hop(sq[b], b, size).astype(F32) for b in range(1, 4))
        to = tq[0:osz, QC - 128 : QC]
        ts = tq[osz : osz + 2, QC - 128 : QC]
    else:
        tp = lax.psum_scatter(dp.astype(F32), "rows", scatter_dimension=0, tiled=True)
        tq = lax.psum_scatter(dq[:, 0 : QC - 128].astype(F32), "rows", scatter_dimension=0, tiled=True)
        to = lax.psum_scatter(dq[0:EO, QC - 128 : QC].astype(F32), "rows", scatter_dimension=0, tiled=True)
        ts = lax.psum(dq[EO : EO + 2, QC - 128 : QC].astype(F32), "rows")
    scale = 1.0 / user_count
    tp, tq, to, ts = tp * scale, tq * scale, to * scale, ts * scale
    return (
        eg.T,
        dg.T,
        tp[:, 0:EMB].T,
        tp[:, EMB : EMB + DENSE].T,
        tp[:, EMB + DENSE],
        jnp.transpose(tp[:, 512:PC].reshape(ds, HALF, FH), (1, 0, 2)),
        tq[:, HALF * EO : HALF * EO + HALF].T,
        jnp.transpose(tq[:, 0 : HALF * EO].reshape(fs, HALF, EO), (1, 0, 2)),
        to[:, TW : TW + HALF].T,
        tp[:, 432:440][None],
        ts[1:2, 0:NE],
        to[:, 0:TW][None],
        ts[0:1, 0:TW],
        ts[0:1, TW : 2 * TW],
        ts[1, NE : NE + 1],
    )


def solution(mesh):
    in_specs = (
        P("rows", None),
        P("rows", None),
        P("rows", None),
        P("task", "rows"),
        P(None, "rows"),
        P(None, "rows"),
        P("rows"),
        P("task", "rows", None),
        P("task", "rows"),
        P("task", "rows", None),
        P("task", "rows"),
        P("task", "rows", None),
        P("task", None),
        P("task", "rows", None),
        P("task", None),
        P("task", None),
        P("task"),
    )
    out_specs = (
        P("rows", None),
        P("rows", None),
        P(None, "rows"),
        P(None, "rows"),
        P("rows"),
        P("task", "rows", None),
        P("task", "rows"),
        P("task", "rows", None),
        P("task", "rows"),
        P("task", "rows", None),
        P("task", None),
        P("task", "rows", None),
        P("task", None),
        P("task", None),
        P("task"),
    )
    return jax.shard_map(body, mesh=mesh, in_specs=in_specs, out_specs=out_specs, check_vma=False)
```

time: 1150 us -> 172 us (0.15)
  waiting for transfers between devices: 435 us -> 40.4 us
  blocking collectives: 386 us -> 0 us
  matrix products: 205 us -> 0 us
  Pallas kernels: 0 us -> 62.4 us
  other arithmetic: 56.6 us -> 11.1 us
  starting transfers between devices: 1.87 us -> 37.6 us
  between operations: 22.1 us -> 1.69 us
  local copies, waits for them, and re-layouts: 32.3 us -> 18.4 us
    unnamed x19 -> x0, waiting for transfers between devices: 327 us -> none
    all_gather x7 -> x0, blocking collectives: 270 us -> none  [the longest x1 42.7 us: body(): lax.all_gather(expert_b1, 'rows', axis=1, tiled=True)]
    dot_general x60 -> x0, matrix products: 205 us -> none  [the longest x3 34.9 us: body(): jnp.einsum('rk,rko->ro', gate_probs, experts_wide, precision=highest)]
    unnamed x2 -> x0, blocking collectives: 116 us -> none
    reduce_scatter x4 -> x0, waiting for transfers between devices: 73.8 us -> none  [the longest x1 73.8 us: body(): lax.psum_scatter(large_grads[5], 'rows', scatter_dimension=1, tiled=True)]
    pallas_call x0 -> x2, Pallas kernels: none -> 62.4 us  [the longest x1 57.4 us: main_call(): pl.pallas_call(functools.partial(main_kernel, pieces, chunks), grid_spec=...]
    ppermute x0 -> x36, waiting for transfers between devices: none -> 40.4 us  [the longest x24 37.6 us: hop(): return lax.ppermute(a, 'rows', [(i, i ^ mask) for i in range(size)])]
    ppermute x0 -> x36, starting transfers between devices: none -> 37.6 us  [the longest x24 35.3 us: hop(): return lax.ppermute(a, 'rows', [(i, i ^ mask) for i in range(size)])]
  transfers between devices with their start and end apart: 14 -> 36, of which waited for: 6 -> 19; matrix products, arithmetic and copies ran while one was open for 18% -> 14% of each run, Pallas kernels for 0% -> 0%
where the time goes in v1:
time: 172 us
  Pallas kernels  62.4 us (36%)
  waiting for transfers between devices  40.4 us (23%)
  starting transfers between devices  37.6 us (22%)
  local copies, waits for them, and re-layouts  18.4 us (11%)
  other arithmetic  11.1 us (6%)
    pallas_call x1, Pallas kernels, main_call(): pl.pallas_call(functools.partial(main_kernel, pieces, chunks), grid_spec=...  57.4 us
    ppermute x24, waiting for transfers between devices, hop(): return lax.ppermute(a, 'rows', [(i, i ^ mask) for i in range(size)])  37.6 us
    ppermute x24, starting transfers between devices, hop(): return lax.ppermute(a, 'rows', [(i, i ^ mask) for i in range(size)])  35.3 us
    unnamed x52, local copies, waits for them, and re-layouts  8.21 us
    pallas_call x1, Pallas kernels, other_call(): pl.pallas_call(other_kernel, grid_spec=spec, out_shape=[jax.ShapeDtypeStr...  5.04 us
  transfers between devices with their start and end apart: 36, of which 19 were waited for; matrix products, arithmetic and copies ran while one was open for 14% of the time, Pallas kernels for 0%

profile of v1, /device:TPU:0, one launch (start us, length us, event | category | flops | bytes accessed | tf_op | source)
XLA Modules:
  0.0 171.5 jit_solution(5274162183945682155)
XLA Ops:
  0.7 0.8 copy.98
  1.4 0.8 copy.97
  2.2 0.8 fusion.13
  3.0 3.0 %collective-permute-start.12 = (bf16[16,768]{1,0:T(8,128)(2,1)S(1)}, bf16[16,768]{1,0:T(8,128)(2,1)S(1)}, u32[]{:S(2)}, u32[]{:S(2)}) collective-permute-start(bf16[16,768]{1,0:T(8,128)(2,1)S(1)} %fusion.10), channel_id=1, source_target_pairs={{0,4},{2,6},{4,0},{6,2},{8,12},{10,14},{12,8},{14,10},{16,20},{18,... | collective-permute-start | bytes 73736 | tf_op jit(solution)/shard_map/ppermute | solution.py:363
  6.0 1.5 collective-permute-start.11
  7.5 0.8 copy.92
  8.3 0.8 copy.95
  9.1 0.8 copy.93
  9.8 0.8 copy.107
  10.7 0.8 concatenate.32
  11.5 4.1 %collective-permute-start.3 = (bf16[32,1536]{1,0:T(8,128)(2,1)S(1)}, bf16[32,1536]{1,0:T(8,128)(2,1)S(1)}, u32[]{:S(2)}, u32[]{:S(2)}) collective-permute-start(bf16[32,1536]{1,0:T(8,128)(2,1)S(1)} %concatenate.32), channel_id=1, source_target_pairs={{0,24},{2,26},{4,28},{6,30},{8,16},{10,18},{12,20},{14,22},{16,8},... | collective-permute-start | bytes 294920 | tf_op jit(solution)/shard_map/ppermute | solution.py:363
  15.6 0.7 reshape.171
  17.0 0.9 reduce-window.6
  18.4 0.7 fusion.14
  19.8 0.8 convert_element_type.113
  20.6 0.8 concatenate.30
  22.7 3.7 %collective-permute-start.16 = (bf16[4,16,768]{2,1,0:T(8,128)(2,1)S(1)}, bf16[4,16,768]{2,1,0:T(8,128)(2,1)S(1)}, u32[]{:S(2)}, u32[]{:S(2)}) collective-permute-start(bf16[4,16,768]{2,1,0:T(8,128)(2,1)S(1)} %pad_maximum_fusion.1.refs_12_), channel_id=1, source_target_pairs={{0,24},{2,26},{4,28},{6,30},{8,16},{10,18},{12,20},{14,22},{16,8},... | collective-permute-start | bytes 294920 | tf_op jit(solution)/shard_map/ppermute | solution.py:363
  26.5 2.5 %collective-permute-start.6 = (bf16[4,32,1536]{2,1,0:T(8,128)(2,1)S(1)}, bf16[4,32,1536]{2,1,0:T(8,128)(2,1)S(1)}, u32[]{:S(2)}, u32[]{:S(2)}) collective-permute-start(bf16[4,32,1536]{2,1,0:T(8,128)(2,1)S(1)} %pad_maximum_fusion.refs_4_), channel_id=1, source_target_pairs={{0,6},{2,4},{4,2},{6,0},{8,14},{10,12},{12,10},{14,8},{16,22},{18,... | collective-permute-start | bytes 1179656 | tf_op jit(solution)/shard_map/ppermute | solution.py:363
  30.1 2.7 %select_reduce_fusion = f32[3,2048]{1,0:T(4,128)S(1)} fusion(f32[3,512]{1,0:T(4,128)S(1)} %convert_divide_fusion, s32[3,512]{1,0:T(4,128)S(1)} %bitcast.131, s32[3,512]{1,0:T(4,128)S(1)} %fusion.14), kind=kLoop, calls=%fused_computation | loop fusion | flops 15722496 | bytes 43008 | tf_op jit(solution)/shard_map/reduce_sum | solution.py:400
  32.9 3.6 %collective-permute-start.15 = (bf16[4,16,768]{2,1,0:T(8,128)(2,1)S(1)}, bf16[4,16,768]{2,1,0:T(8,128)(2,1)S(1)}, u32[]{:S(2)}, u32[]{:S(2)}) collective-permute-start(bf16[4,16,768]{2,1,0:T(8,128)(2,1)S(1)} %pad_maximum_fusion.1.refs_12_), channel_id=1, source_target_pairs={{0,16},{2,18},{4,20},{6,22},{8,24},{10,26},{12,28},{14,30},{16,0},... | collective-permute-start | bytes 294920 | tf_op jit(solution)/shard_map/ppermute | solution.py:363
  36.5 3.1 %collective-permute-done.15.refs_14_ = bf16[4,16,768]{2,1,0:T(8,128)(2,1)S(1)} collective-permute-done((bf16[4,16,768]{2,1,0:T(8,128)(2,1)S(1)}, bf16[4,16,768]{2,1,0:T(8,128)(2,1)S(1)}, u32[]{:S(2)}, u32[]{:S(2)}) %collective-permute-start.15) | collective-permute-done | bytes 98336 | tf_op jit(solution)/shard_map/ppermute | solution.py:363
  39.6 1.5 collective-permute-done.14.refs_13_
  43.0 3.8 %collective-permute-done.5.refs_6_ = bf16[4,32,1536]{2,1,0:T(8,128)(2,1)S(1)} collective-permute-done((bf16[4,32,1536]{2,1,0:T(8,128)(2,1)S(1)}, bf16[4,32,1536]{2,1,0:T(8,128)(2,1)S(1)}, u32[]{:S(2)}, u32[]{:S(2)}) %collective-permute-start.5) | collective-permute-done | bytes 393248 | tf_op jit(solution)/shard_map/ppermute | solution.py:363
  47.2 0.8 fusion.3.refs_2_.refs_3_
  49.8 57.4 %shard_map.280 = (f32[416,6144]{1,0:T(8,128)}, f32[13,6144]{1,0:T(8,128)}, bf16[512,3072]{1,0:T(8,128)(2,1)}, bf16[448,512]{1,0:T(8,128)(2,1)}, bf16[512,1536]{1...) custom-call(s32[17]{0:T(128)} %pad_add_fusion.tab_ref, ...), custom_call_target="tpu_custom_call" | custom-call | flops 30000001024 | bytes 24000000 | tf_op jit(solution)/shard_map/pallas_call | solution.py:311
  107.3 1.8 %collective-permute-done.29 = bf16[256,768]{1,0:T(8,128)(2,1)S(1)} collective-permute-done((bf16[256,768]{1,0:T(8,128)(2,1)}, bf16[256,768]{1,0:T(8,128)(2,1)S(1)}, u32[]{:S(2)}, u32[]{:S(2)}) %collective-permute-start.29) | collective-permute-done | bytes 393248 | tf_op jit(solution)/shard_map/ppermute | solution.py:367
  109.1 1.1 add_convert_fusion.1
  110.9 3.8 %collective-permute-start.31 = (bf16[4,16,768]{2,1,0:T(8,128)(2,1)S(1)}, bf16[4,16,768]{2,1,0:T(8,128)(2,1)S(1)}, u32[]{:S(2)}, u32[]{:S(2)}) collective-permute-start(bf16[4,16,768]{2,1,0:T(8,128)(2,1)S(1)} %bitcast.117), channel_id=1, source_target_pairs={{0,16},{2,18},{4,20},{6,22},{8,24},{10,26},{12,28},{14,30},{16,0},... | collective-permute-start | bytes 294920 | tf_op jit(solution)/shard_map/ppermute | solution.py:363
  114.7 3.1 %collective-permute-done.32 = bf16[4,16,768]{2,1,0:T(8,128)(2,1)S(1)} collective-permute-done((bf16[4,16,768]{2,1,0:T(8,128)(2,1)S(1)}, bf16[4,16,768]{2,1,0:T(8,128)(2,1)S(1)}, u32[]{:S(2)}, u32[]{:S(2)}) %collective-permute-start.32) | collective-permute-done | bytes 98336 | tf_op jit(solution)/shard_map/ppermute | solution.py:363
  117.8 1.1 collective-permute-done.30
  119.0 1.0 collective-permute-done.31
  120.0 1.6 collective-permute-start.33
  121.5 1.5 collective-permute-start.35
  123.9 2.4 %collective-permute-done.35 = bf16[16,768]{1,0:T(8,128)(2,1)S(1)} collective-permute-done((bf16[16,768]{1,0:T(8,128)(2,1)S(1)}, bf16[16,768]{1,0:T(8,128)(2,1)S(1)}, u32[]{:S(2)}, u32[]{:S(2)}) %collective-permute-start.35) | collective-permute-done | bytes 24608 | tf_op jit(solution)/shard_map/ppermute | solution.py:363
  128.1 1.5 collective-permute-start.25
  130.1 1.5 collective-permute-start.24
  132.3 8.8 %collective-permute-done.25 = bf16[4,32,1536]{2,1,0:T(8,128)(2,1)S(1)} collective-permute-done((bf16[4,32,1536]{2,1,0:T(8,128)(2,1)S(1)}, bf16[4,32,1536]{2,1,0:T(8,128)(2,1)S(1)}, u32[]{:S(2)}, u32[]{:S(2)}) %collective-permute-start.25) | collective-permute-done | bytes 393248 | tf_op jit(solution)/shard_map/ppermute | solution.py:363
  141.1 5.0 %collective-permute-done.23 = bf16[4,32,1536]{2,1,0:T(8,128)(2,1)S(1)} collective-permute-done((bf16[4,32,1536]{2,1,0:T(8,128)(2,1)S(1)}, bf16[4,32,1536]{2,1,0:T(8,128)(2,1)S(1)}, u32[]{:S(2)}, u32[]{:S(2)}) %collective-permute-start.23) | collective-permute-done | bytes 393248 | tf_op jit(solution)/shard_map/ppermute | solution.py:363
  146.1 0.7 collective-permute-done.24
  147.0 0.7 copy-done.4
  148.4 1.1 collective-permute-start.26
  149.5 1.0 collective-permute-start.28
  150.5 1.4 collective-permute-start.27
  154.9 2.2 %collective-permute-done.28 = bf16[32,1536]{1,0:T(8,128)(2,1)} collective-permute-done((bf16[32,1536]{1,0:T(8,128)(2,1)S(1)}, bf16[32,1536]{1,0:T(8,128)(2,1)}, u32[]{:S(2)}, u32[]{:S(2)}) %collective-permute-start.28) | collective-permute-done | bytes 98336 | tf_op jit(solution)/shard_map/ppermute | solution.py:363
  157.1 3.8 %collective-permute-done.27 = bf16[32,1536]{1,0:T(8,128)(2,1)} collective-permute-done((bf16[32,1536]{1,0:T(8,128)(2,1)S(1)}, bf16[32,1536]{1,0:T(8,128)(2,1)}, u32[]{:S(2)}, u32[]{:S(2)}) %collective-permute-start.27) | collective-permute-done | bytes 98336 | tf_op jit(solution)/shard_map/ppermute | solution.py:363
  160.9 1.0 fusion.5
  165.5 1.0 copy-done.1
  166.5 5.0 %shard_map.281 = (f32[416,6144]{1,0:T(8,128)}, f32[13,6144]{1,0:T(8,128)}) custom-call(s32[17]{0:T(128)S(1)} %copy-done.2, bf16[512,3072]{1,0:T(8,128)(2,1)S(1)} %collective-permute-done.21.hg_ref, bf16[448,512]{1,0:T(8,128)(2,1)S(1)} %copy-done.1, f32[416,6144]{1,0:T(8,128)} %get-tuple-element.27.eg_in, ...), custom_call_target="tpu_custom_call", output_to_operand_aliasing={{0}: (3, {}), {1}: (4, {})} | custom-call | flops 1500000000 | bytes 9000000 | tf_op jit(solution)/shard_map/pallas_call | solution.py:352
  (132 shorter events, 19.8 us)
Async XLA Ops:
  3.0 18.4 %collective-permute-start.12 = (bf16[16,768]{1,0:T(8,128)(2,1)S(1)}, bf16[16,768]{1,0:T(8,128)(2,1)S(1)}, u32[]{:S(2)}, u32[]{:S(2)}) collective-permute-start(bf16[16,768]{1,0:T(8,128)(2,1)S(1)} %fusion.10), channel_id=1, source_target_pairs={{0,4},{2,6},{4,0},{6,2},{8,12},{10,14},{12,8},{14,10},{16,20},{18,... | collective-permute-start | bytes 73736 | tf_op jit(solution)/shard_map/ppermute | solution.py:363
  6.0 16.1 %collective-permute-start.11 = (bf16[16,768]{1,0:T(8,128)(2,1)S(1)}, bf16[16,768]{1,0:T(8,128)(2,1)S(1)}, u32[]{:S(2)}, u32[]{:S(2)}) collective-permute-start(bf16[16,768]{1,0:T(8,128)(2,1)S(1)} %fusion.10), channel_id=1, source_target_pairs={{0,2},{2,0},{4,6},{6,4},{8,10},{10,8},{12,14},{14,12},{16,18},{18,... | collective-permute-start | bytes 73736 | tf_op jit(solution)/shard_map/ppermute | solution.py:363
  7.5 14.6 %collective-permute-start.13 = (bf16[16,768]{1,0:T(8,128)(2,1)S(1)}, bf16[16,768]{1,0:T(8,128)(2,1)S(1)}, u32[]{:S(2)}, u32[]{:S(2)}) collective-permute-start(bf16[16,768]{1,0:T(8,128)(2,1)S(1)} %fusion.10), channel_id=1, source_target_pairs={{0,6},{2,4},{4,2},{6,0},{8,14},{10,12},{12,10},{14,8},{16,22},{18,... | collective-permute-start | bytes 73736 | tf_op jit(solution)/shard_map/ppermute | solution.py:363
  11.5 11.2 %collective-permute-start.3 = (bf16[32,1536]{1,0:T(8,128)(2,1)S(1)}, bf16[32,1536]{1,0:T(8,128)(2,1)S(1)}, u32[]{:S(2)}, u32[]{:S(2)}) collective-permute-start(bf16[32,1536]{1,0:T(8,128)(2,1)S(1)} %concatenate.32), channel_id=1, source_target_pairs={{0,24},{2,26},{4,28},{6,30},{8,16},{10,18},{12,20},{14,22},{16,8},... | collective-permute-start | bytes 294920 | tf_op jit(solution)/shard_map/ppermute | solution.py:363
  15.6 10.8 %collective-permute-start.2 = (bf16[32,1536]{1,0:T(8,128)(2,1)S(1)}, bf16[32,1536]{1,0:T(8,128)(2,1)S(1)}, u32[]{:S(2)}, u32[]{:S(2)}) collective-permute-start(bf16[32,1536]{1,0:T(8,128)(2,1)S(1)} %concatenate.32), channel_id=1, source_target_pairs={{0,16},{2,18},{4,20},{6,22},{8,24},{10,26},{12,28},{14,30},{16,0},... | collective-permute-start | bytes 294920 | tf_op jit(solution)/shard_map/ppermute | solution.py:363
  21.4 5.1 %collective-permute-start.1 = (bf16[32,1536]{1,0:T(8,128)(2,1)S(1)}, bf16[32,1536]{1,0:T(8,128)(2,1)S(1)}, u32[]{:S(2)}, u32[]{:S(2)}) collective-permute-start(bf16[32,1536]{1,0:T(8,128)(2,1)S(1)} %concatenate.32), channel_id=1, source_target_pairs={{0,8},{2,10},{4,12},{6,14},{8,0},{10,2},{12,4},{14,6},{16,24},{18,... | collective-permute-start | bytes 294920 | tf_op jit(solution)/shard_map/ppermute | solution.py:363
  22.1 7.5 %collective-permute-start = (bf16[1,6400]{1,0:T(2,128)(2,1)S(1)}, bf16[1,6400]{1,0:T(2,128)(2,1)S(1)}, u32[]{:S(2)}, u32[]{:S(2)}) collective-permute-start(bf16[1,6400]{1,0:T(2,128)(2,1)S(1)} %concatenate.30), channel_id=1, source_target_pairs={{0,1},{1,0},{2,3},{3,2},{4,5},{5,4},{6,7},{7,6},{8,9},{9,8},{10,11... | collective-permute-start | bytes 38408 | tf_op jit(solution)/shard_map/ppermute | solution.py:367
  22.1 26.9 %copy-start.6 = (bf16[4,16,768]{2,1,0:T(8,128)(2,1)}, bf16[4,16,768]{2,1,0:T(8,128)(2,1)S(1)}, u32[]{:S(2)}) copy-start(bf16[4,16,768]{2,1,0:T(8,128)(2,1)S(1)} %pad_maximum_fusion.1.refs_12_) | copy-start | bytes 294916
  22.1 10.8 %collective-permute-start.17 = (bf16[4,16,768]{2,1,0:T(8,128)(2,1)S(1)}, bf16[4,16,768]{2,1,0:T(8,128)(2,1)S(1)}, u32[]{:S(2)}, u32[]{:S(2)}) collective-permute-start(bf16[4,16,768]{2,1,0:T(8,128)(2,1)S(1)} %pad_maximum_fusion.1.refs_12_), channel_id=1, source_target_pairs={{0,1},{1,0},{2,3},{3,2},{4,5},{5,4},{6,7},{7,6},{8,9},{9,8},{10,11... | collective-permute-start | bytes 294920 | tf_op jit(solution)/shard_map/ppermute | solution.py:367
  22.7 13.8 %collective-permute-start.16 = (bf16[4,16,768]{2,1,0:T(8,128)(2,1)S(1)}, bf16[4,16,768]{2,1,0:T(8,128)(2,1)S(1)}, u32[]{:S(2)}, u32[]{:S(2)}) collective-permute-start(bf16[4,16,768]{2,1,0:T(8,128)(2,1)S(1)} %pad_maximum_fusion.1.refs_12_), channel_id=1, source_target_pairs={{0,24},{2,26},{4,28},{6,30},{8,16},{10,18},{12,20},{14,22},{16,8},... | collective-permute-start | bytes 294920 | tf_op jit(solution)/shard_map/ppermute | solution.py:363
  26.5 22.5 %copy-start.5 = (bf16[4,32,1536]{2,1,0:T(8,128)(2,1)}, bf16[4,32,1536]{2,1,0:T(8,128)(2,1)S(1)}, u32[]{:S(2)}) copy-start(bf16[4,32,1536]{2,1,0:T(8,128)(2,1)S(1)} %pad_maximum_fusion.refs_4_) | copy-start | bytes 1179652
  26.5 16.1 %collective-permute-start.6 = (bf16[4,32,1536]{2,1,0:T(8,128)(2,1)S(1)}, bf16[4,32,1536]{2,1,0:T(8,128)(2,1)S(1)}, u32[]{:S(2)}, u32[]{:S(2)}) collective-permute-start(bf16[4,32,1536]{2,1,0:T(8,128)(2,1)S(1)} %pad_maximum_fusion.refs_4_), channel_id=1, source_target_pairs={{0,6},{2,4},{4,2},{6,0},{8,14},{10,12},{12,10},{14,8},{16,22},{18,... | collective-permute-start | bytes 1179656 | tf_op jit(solution)/shard_map/ppermute | solution.py:363
  29.0 17.7 %collective-permute-start.5 = (bf16[4,32,1536]{2,1,0:T(8,128)(2,1)S(1)}, bf16[4,32,1536]{2,1,0:T(8,128)(2,1)S(1)}, u32[]{:S(2)}, u32[]{:S(2)}) collective-permute-start(bf16[4,32,1536]{2,1,0:T(8,128)(2,1)S(1)} %pad_maximum_fusion.refs_4_), channel_id=1, source_target_pairs={{0,4},{2,6},{4,0},{6,2},{8,12},{10,14},{12,8},{14,10},{16,20},{18,... | collective-permute-start | bytes 1179656 | tf_op jit(solution)/shard_map/ppermute | solution.py:363
  29.5 17.3 %collective-permute-start.4 = (bf16[4,32,1536]{2,1,0:T(8,128)(2,1)S(1)}, bf16[4,32,1536]{2,1,0:T(8,128)(2,1)S(1)}, u32[]{:S(2)}, u32[]{:S(2)}) collective-permute-start(bf16[4,32,1536]{2,1,0:T(8,128)(2,1)S(1)} %pad_maximum_fusion.refs_4_), channel_id=1, source_target_pairs={{0,2},{2,0},{4,6},{6,4},{8,10},{10,8},{12,14},{14,12},{16,18},{18,... | collective-permute-start | bytes 1179656 | tf_op jit(solution)/shard_map/ppermute | solution.py:363
  32.9 16.1 %copy-start.14 = (bf16[4,16,768]{2,1,0:T(8,128)(2,1)}, bf16[4,16,768]{2,1,0:T(8,128)(2,1)S(1)}, u32[]{:S(2)}) copy-start(bf16[4,16,768]{2,1,0:T(8,128)(2,1)S(1)} %collective-permute-done.17.refs_16_) | copy-start | bytes 294916
  32.9 6.7 %collective-permute-start.15 = (bf16[4,16,768]{2,1,0:T(8,128)(2,1)S(1)}, bf16[4,16,768]{2,1,0:T(8,128)(2,1)S(1)}, u32[]{:S(2)}, u32[]{:S(2)}) collective-permute-start(bf16[4,16,768]{2,1,0:T(8,128)(2,1)S(1)} %pad_maximum_fusion.1.refs_12_), channel_id=1, source_target_pairs={{0,16},{2,18},{4,20},{6,22},{8,24},{10,26},{12,28},{14,30},{16,0},... | collective-permute-start | bytes 294920 | tf_op jit(solution)/shard_map/ppermute | solution.py:363
  36.5 12.5 %copy-start.15 = (bf16[4,16,768]{2,1,0:T(8,128)(2,1)}, bf16[4,16,768]{2,1,0:T(8,128)(2,1)S(1)}, u32[]{:S(2)}) copy-start(bf16[4,16,768]{2,1,0:T(8,128)(2,1)S(1)} %collective-permute-done.16.refs_15_) | copy-start | bytes 294916
  36.5 4.6 %collective-permute-start.14 = (bf16[4,16,768]{2,1,0:T(8,128)(2,1)S(1)}, bf16[4,16,768]{2,1,0:T(8,128)(2,1)S(1)}, u32[]{:S(2)}, u32[]{:S(2)}) collective-permute-start(bf16[4,16,768]{2,1,0:T(8,128)(2,1)S(1)} %pad_maximum_fusion.1.refs_12_), channel_id=1, source_target_pairs={{0,8},{2,10},{4,12},{6,14},{8,0},{10,2},{12,4},{14,6},{16,24},{18,... | collective-permute-start | bytes 294920 | tf_op jit(solution)/shard_map/ppermute | solution.py:363
  39.6 9.4 %copy-start.16 = (bf16[4,16,768]{2,1,0:T(8,128)(2,1)}, bf16[4,16,768]{2,1,0:T(8,128)(2,1)S(1)}, u32[]{:S(2)}) copy-start(bf16[4,16,768]{2,1,0:T(8,128)(2,1)S(1)} %collective-permute-done.15.refs_14_) | copy-start | bytes 294916
  39.6 2.1 %collective-permute-start.20 = (bf16[4,16,768]{2,1,0:T(8,128)(2,1)S(1)}, bf16[4,16,768]{2,1,0:T(8,128)(2,1)S(1)}, u32[]{:S(2)}, u32[]{:S(2)}) collective-permute-start(bf16[4,16,768]{2,1,0:T(8,128)(2,1)S(1)} %collective-permute-done.16.refs_15_), channel_id=1, source_target_pairs={{0,1},{1,0},{2,3},{3,2},{4,5},{5,4},{6,7},{7,6},{8,9},{9,8},{10,11... | collective-permute-start | bytes 294920 | tf_op jit(solution)/shard_map/ppermute | solution.py:367
  41.1 7.9 %copy-start.17 = (bf16[4,16,768]{2,1,0:T(8,128)(2,1)}, bf16[4,16,768]{2,1,0:T(8,128)(2,1)S(1)}, u32[]{:S(2)}) copy-start(bf16[4,16,768]{2,1,0:T(8,128)(2,1)S(1)} %collective-permute-done.14.refs_13_) | copy-start | bytes 294916
  41.1 1.3 collective-permute-start.19
  41.8 7.3 %copy-start.18 = (bf16[4,16,768]{2,1,0:T(8,128)(2,1)}, bf16[4,16,768]{2,1,0:T(8,128)(2,1)S(1)}, u32[]{:S(2)}) copy-start(bf16[4,16,768]{2,1,0:T(8,128)(2,1)S(1)} %collective-permute-done.20.refs_19_) | copy-start | bytes 294916
  41.8 6.2 %collective-permute-start.7 = (bf16[4,32,1536]{2,1,0:T(8,128)(2,1)S(1)}, bf16[4,32,1536]{2,1,0:T(8,128)(2,1)S(1)}, u32[]{:S(2)}, u32[]{:S(2)}) collective-permute-start(bf16[4,32,1536]{2,1,0:T(8,128)(2,1)S(1)} %pad_maximum_fusion.refs_4_), channel_id=1, source_target_pairs={{0,1},{1,0},{2,3},{3,2},{4,5},{5,4},{6,7},{7,6},{8,9},{9,8},{10,11... | collective-permute-start | bytes 1179656 | tf_op jit(solution)/shard_map/ppermute | solution.py:367
  42.4 6.6 %copy-start.19 = (bf16[4,16,768]{2,1,0:T(8,128)(2,1)}, bf16[4,16,768]{2,1,0:T(8,128)(2,1)S(1)}, u32[]{:S(2)}) copy-start(bf16[4,16,768]{2,1,0:T(8,128)(2,1)S(1)} %collective-permute-done.19.refs_18_) | copy-start | bytes 294916
  42.4 5.6 %collective-permute-start.18 = (bf16[4,16,768]{2,1,0:T(8,128)(2,1)S(1)}, bf16[4,16,768]{2,1,0:T(8,128)(2,1)S(1)}, u32[]{:S(2)}, u32[]{:S(2)}) collective-permute-start(bf16[4,16,768]{2,1,0:T(8,128)(2,1)S(1)} %collective-permute-done.14.refs_13_), channel_id=1, source_target_pairs={{0,1},{1,0},{2,3},{3,2},{4,5},{5,4},{6,7},{7,6},{8,9},{9,8},{10,11... | collective-permute-start | bytes 294920 | tf_op jit(solution)/shard_map/ppermute | solution.py:367
  42.6 6.5 %copy-start.7 = (bf16[4,32,1536]{2,1,0:T(8,128)(2,1)}, bf16[4,32,1536]{2,1,0:T(8,128)(2,1)S(1)}, u32[]{:S(2)}) copy-start(bf16[4,32,1536]{2,1,0:T(8,128)(2,1)S(1)} %collective-permute-done.6.refs_7_) | copy-start | bytes 1179652
  42.6 5.4 %collective-permute-start.10 = (bf16[4,32,1536]{2,1,0:T(8,128)(2,1)S(1)}, bf16[4,32,1536]{2,1,0:T(8,128)(2,1)S(1)}, u32[]{:S(2)}, u32[]{:S(2)}) collective-permute-start(bf16[4,32,1536]{2,1,0:T(8,128)(2,1)S(1)} %collective-permute-done.6.refs_7_), channel_id=1, source_target_pairs={{0,1},{1,0},{2,3},{3,2},{4,5},{5,4},{6,7},{7,6},{8,9},{9,8},{10,11... | collective-permute-start | bytes 1179656 | tf_op jit(solution)/shard_map/ppermute | solution.py:367
  46.7 2.4 %copy-start.8 = (bf16[4,32,1536]{2,1,0:T(8,128)(2,1)}, bf16[4,32,1536]{2,1,0:T(8,128)(2,1)S(1)}, u32[]{:S(2)}) copy-start(bf16[4,32,1536]{2,1,0:T(8,128)(2,1)S(1)} %collective-permute-done.5.refs_6_) | copy-start | bytes 1179652
  46.7 1.7 %collective-permute-start.9 = (bf16[4,32,1536]{2,1,0:T(8,128)(2,1)S(1)}, bf16[4,32,1536]{2,1,0:T(8,128)(2,1)S(1)}, u32[]{:S(2)}, u32[]{:S(2)}) collective-permute-start(bf16[4,32,1536]{2,1,0:T(8,128)(2,1)S(1)} %collective-permute-done.5.refs_6_), channel_id=1, source_target_pairs={{0,1},{1,0},{2,3},{3,2},{4,5},{5,4},{6,7},{7,6},{8,9},{9,8},{10,11... | collective-permute-start | bytes 1179656 | tf_op jit(solution)/shard_map/ppermute | solution.py:367
  46.8 2.2 %collective-permute-start.8 = (bf16[4,32,1536]{2,1,0:T(8,128)(2,1)S(1)}, bf16[4,32,1536]{2,1,0:T(8,128)(2,1)S(1)}, u32[]{:S(2)}, u32[]{:S(2)}) collective-permute-start(bf16[4,32,1536]{2,1,0:T(8,128)(2,1)S(1)} %collective-permute-done.4.refs_5_), channel_id=1, source_target_pairs={{0,1},{1,0},{2,3},{3,2},{4,5},{5,4},{6,7},{7,6},{8,9},{9,8},{10,11... | collective-permute-start | bytes 1179656 | tf_op jit(solution)/shard_map/ppermute | solution.py:367
  107.1 20.5 %copy-start.3 = (bf16[512,1536]{1,0:T(8,128)(2,1)S(1)}, bf16[512,1536]{1,0:T(8,128)(2,1)}, u32[]{:S(2)}) copy-start(bf16[512,1536]{1,0:T(8,128)(2,1)} %get-tuple-element.31) | copy-start | bytes 4718596
  107.1 2.0 %collective-permute-start.29 = (bf16[256,768]{1,0:T(8,128)(2,1)}, bf16[256,768]{1,0:T(8,128)(2,1)S(1)}, u32[]{:S(2)}, u32[]{:S(2)}) collective-permute-start(bf16[256,768]{1,0:T(8,128)(2,1)} %get-tuple-element.34), channel_id=1, source_target_pairs={{0,1},{1,0},{2,3},{3,2},{4,5},{5,4},{6,7},{7,6},{8,9},{9,8},{10,11... | collective-permute-start | bytes 1179656 | tf_op jit(solution)/shard_map/ppermute | solution.py:367
  110.2 7.6 %collective-permute-start.32 = (bf16[4,16,768]{2,1,0:T(8,128)(2,1)S(1)}, bf16[4,16,768]{2,1,0:T(8,128)(2,1)S(1)}, u32[]{:S(2)}, u32[]{:S(2)}) collective-permute-start(bf16[4,16,768]{2,1,0:T(8,128)(2,1)S(1)} %bitcast.119), channel_id=1, source_target_pairs={{0,24},{2,26},{4,28},{6,30},{8,16},{10,18},{12,20},{14,22},{16,8},... | collective-permute-start | bytes 294920 | tf_op jit(solution)/shard_map/ppermute | solution.py:363
  110.6 8.3 %collective-permute-start.30 = (bf16[4,16,768]{2,1,0:T(8,128)(2,1)S(1)}, bf16[4,16,768]{2,1,0:T(8,128)(2,1)S(1)}, u32[]{:S(2)}, u32[]{:S(2)}) collective-permute-start(bf16[4,16,768]{2,1,0:T(8,128)(2,1)S(1)} %bitcast.118), channel_id=1, source_target_pairs={{0,8},{2,10},{4,12},{6,14},{8,0},{10,2},{12,4},{14,6},{16,24},{18,... | collective-permute-start | bytes 294920 | tf_op jit(solution)/shard_map/ppermute | solution.py:363
  110.9 9.0 %collective-permute-start.31 = (bf16[4,16,768]{2,1,0:T(8,128)(2,1)S(1)}, bf16[4,16,768]{2,1,0:T(8,128)(2,1)S(1)}, u32[]{:S(2)}, u32[]{:S(2)}) collective-permute-start(bf16[4,16,768]{2,1,0:T(8,128)(2,1)S(1)} %bitcast.117), channel_id=1, source_target_pairs={{0,16},{2,18},{4,20},{6,22},{8,24},{10,26},{12,28},{14,30},{16,0},... | collective-permute-start | bytes 294920 | tf_op jit(solution)/shard_map/ppermute | solution.py:363
  114.7 12.9 %collective-permute-start.22 = (bf16[512,1536]{1,0:T(8,128)(2,1)}, bf16[512,1536]{1,0:T(8,128)(2,1)S(1)}, u32[]{:S(2)}, u32[]{:S(2)}) collective-permute-start(bf16[512,1536]{1,0:T(8,128)(2,1)} %get-tuple-element.32), channel_id=1, source_target_pairs={{0,1},{1,0},{2,3},{3,2},{4,5},{5,4},{6,7},{7,6},{8,9},{9,8},{10,11... | collective-permute-start | bytes 4718600 | tf_op jit(solution)/shard_map/ppermute | solution.py:367
  120.0 3.9 %collective-permute-start.33 = (bf16[16,768]{1,0:T(8,128)(2,1)S(1)}, bf16[16,768]{1,0:T(8,128)(2,1)S(1)}, u32[]{:S(2)}, u32[]{:S(2)}) collective-permute-start(bf16[16,768]{1,0:T(8,128)(2,1)S(1)} %get-tuple-element.123), channel_id=1, source_target_pairs={{0,2},{2,0},{4,6},{6,4},{8,10},{10,8},{12,14},{14,12},{16,18},{18,... | collective-permute-start | bytes 73736 | tf_op jit(solution)/shard_map/ppermute | solution.py:363
  121.5 4.7 %collective-permute-start.35 = (bf16[16,768]{1,0:T(8,128)(2,1)S(1)}, bf16[16,768]{1,0:T(8,128)(2,1)S(1)}, u32[]{:S(2)}, u32[]{:S(2)}) collective-permute-start(bf16[16,768]{1,0:T(8,128)(2,1)S(1)} %get-tuple-element.124), channel_id=1, source_target_pairs={{0,6},{2,4},{4,2},{6,0},{8,14},{10,12},{12,10},{14,8},{16,22},{18,... | collective-permute-start | bytes 73736 | tf_op jit(solution)/shard_map/ppermute | solution.py:363
  123.0 3.8 %collective-permute-start.34 = (bf16[16,768]{1,0:T(8,128)(2,1)S(1)}, bf16[16,768]{1,0:T(8,128)(2,1)S(1)}, u32[]{:S(2)}, u32[]{:S(2)}) collective-permute-start(bf16[16,768]{1,0:T(8,128)(2,1)S(1)} %get-tuple-element.125), channel_id=1, source_target_pairs={{0,4},{2,6},{4,0},{6,2},{8,12},{10,14},{12,8},{14,10},{16,20},{18,... | collective-permute-start | bytes 73736 | tf_op jit(solution)/shard_map/ppermute | solution.py:363
  123.5 41.9 %collective-permute-start.21 = (bf16[512,3072]{1,0:T(8,128)(2,1)}, bf16[512,3072]{1,0:T(8,128)(2,1)S(1)}, u32[]{:S(2)}, u32[]{:S(2)}) collective-permute-start(bf16[512,3072]{1,0:T(8,128)(2,1)} %get-tuple-element.25), channel_id=1, source_target_pairs={{0,1},{1,0},{2,3},{3,2},{4,5},{5,4},{6,7},{7,6},{8,9},{9,8},{10,11... | collective-permute-start | bytes 9437192 | tf_op jit(solution)/shard_map/ppermute | solution.py:367
  128.0 37.5 %copy-start.2 = (s32[17]{0:T(128)S(1)}, s32[17]{0:T(128)}, u32[]{:S(2)}) copy-start(s32[17]{0:T(128)} %pad_add_fusion.tab_ref) | copy-start | bytes 208
  128.1 13.0 %collective-permute-start.25 = (bf16[4,32,1536]{2,1,0:T(8,128)(2,1)S(1)}, bf16[4,32,1536]{2,1,0:T(8,128)(2,1)S(1)}, u32[]{:S(2)}, u32[]{:S(2)}) collective-permute-start(bf16[4,32,1536]{2,1,0:T(8,128)(2,1)S(1)} %bitcast.109), channel_id=1, source_target_pairs={{0,6},{2,4},{4,2},{6,0},{8,14},{10,12},{12,10},{14,8},{16,22},{18,... | collective-permute-start | bytes 1179656 | tf_op jit(solution)/shard_map/ppermute | solution.py:363
  129.6 16.5 %collective-permute-start.23 = (bf16[4,32,1536]{2,1,0:T(8,128)(2,1)S(1)}, bf16[4,32,1536]{2,1,0:T(8,128)(2,1)S(1)}, u32[]{:S(2)}, u32[]{:S(2)}) collective-permute-start(bf16[4,32,1536]{2,1,0:T(8,128)(2,1)S(1)} %bitcast.108), channel_id=1, source_target_pairs={{0,2},{2,0},{4,6},{6,4},{8,10},{10,8},{12,14},{14,12},{16,18},{18,... | collective-permute-start | bytes 1179656 | tf_op jit(solution)/shard_map/ppermute | solution.py:363
  130.1 16.7 %collective-permute-start.24 = (bf16[4,32,1536]{2,1,0:T(8,128)(2,1)S(1)}, bf16[4,32,1536]{2,1,0:T(8,128)(2,1)S(1)}, u32[]{:S(2)}, u32[]{:S(2)}) collective-permute-start(bf16[4,32,1536]{2,1,0:T(8,128)(2,1)S(1)} %bitcast.107), channel_id=1, source_target_pairs={{0,4},{2,6},{4,0},{6,2},{8,12},{10,14},{12,8},{14,10},{16,20},{18,... | collective-permute-start | bytes 1179656 | tf_op jit(solution)/shard_map/ppermute | solution.py:363
  148.4 6.5 %collective-permute-start.26 = (bf16[32,1536]{1,0:T(8,128)(2,1)}, bf16[32,1536]{1,0:T(8,128)(2,1)S(1)}, u32[]{:S(2)}, u32[]{:S(2)}) collective-permute-start(bf16[32,1536]{1,0:T(8,128)(2,1)} %get-tuple-element.120), channel_id=1, source_target_pairs={{0,8},{2,10},{4,12},{6,14},{8,0},{10,2},{12,4},{14,6},{16,24},{18,... | collective-permute-start | bytes 294920 | tf_op jit(solution)/shard_map/ppermute | solution.py:363
  149.5 7.6 %collective-permute-start.28 = (bf16[32,1536]{1,0:T(8,128)(2,1)S(1)}, bf16[32,1536]{1,0:T(8,128)(2,1)}, u32[]{:S(2)}, u32[]{:S(2)}) collective-permute-start(bf16[32,1536]{1,0:T(8,128)(2,1)S(1)} %get-tuple-element.121), channel_id=1, source_target_pairs={{0,24},{2,26},{4,28},{6,30},{8,16},{10,18},{12,20},{14,22},{16,8},... | collective-permute-start | bytes 294920 | tf_op jit(solution)/shard_map/ppermute | solution.py:363
  150.5 10.4 %collective-permute-start.27 = (bf16[32,1536]{1,0:T(8,128)(2,1)S(1)}, bf16[32,1536]{1,0:T(8,128)(2,1)}, u32[]{:S(2)}, u32[]{:S(2)}) collective-permute-start(bf16[32,1536]{1,0:T(8,128)(2,1)S(1)} %get-tuple-element.122), channel_id=1, source_target_pairs={{0,16},{2,18},{4,20},{6,22},{8,24},{10,26},{12,28},{14,30},{16,0},... | collective-permute-start | bytes 294920 | tf_op jit(solution)/shard_map/ppermute | solution.py:363
  (9 other events, 10.3 us)

commit v2 on v1

v2 whole, which is shorter than its diff:
```python
import functools

import jax
import jax.numpy as jnp
from jax import lax
from jax.experimental import pallas as pl
from jax.experimental.pallas import tpu as pltpu
from jax.sharding import PartitionSpec as P

F32 = jnp.float32
BF = jnp.bfloat16
NT = (((1,), (1,)), ((), ()))
D, FH, EO, TW, NE = 512, 256, 128, 64, 8
HALF = NE // 2
EMB, DENSE = 416, 13
XR = 448
QA = HALF * EO
QD = QA + 128
QC = QD + 512
B1, GA = 72, 80
FG = NE * FH + 128
TILE = 512


def mm(a, b):
    return jnp.dot(a, b, preferred_element_type=F32)


def mm_nt(a, b):
    return lax.dot_general(a, b, NT, preferred_element_type=F32)


def act_pair(half):
    t = jnp.tanh(half)
    q = 1.0 + t
    m = half * q
    return m, q + m * (1.0 - t)


def swap_halves(a, flag):
    return jnp.where(flag, jnp.concatenate([a[HALF:NE], a[0:HALF]], axis=0), a)


def lane_fold(a):
    total = a[:, 0:128]
    for c in range(1, a.shape[1] // 128):
        total = total + a[:, 128 * c : 128 * c + 128]
    return total


def p_order(at, chunks):
    return at if chunks == 1 else at % 4 * 4 + at // 4


def main_kernel(pieces, chunks, batch_rows, tab_ref, *refs):
    emb_ref, dense_ref, lab_ref, far_lab_ref, sizes_ref, vec_ref, far_vec_ref = refs[:7]
    p_refs = (refs[7 : 7 + pieces], refs[7 + pieces : 7 + 2 * pieces])
    q_refs = (refs[7 + 2 * pieces : 7 + 3 * pieces], refs[7 + 3 * pieces : 7 + 4 * pieces])
    refs = refs[7 + 4 * pieces :]
    hg_ref, wat_s = refs[:2]
    dp_refs, dq_refs = refs[2:4], refs[4:6]
    (
        x_s, hid_s, mid_s, sl1_s, out_s, sl2_s, sg_s, fg_s, mix_s,
        w1_s, w1t_s, ga_s, w2t_s, w2_s, b1_s, b2_s, gb_s, tt_s, tw_s, tcol_s, q_s, start_s, end_s, inv_s,
        dwa_s, dw1_s, dw2_s, dtw_s, dcol_s, dlog_s, dsm_s,
    ) = refs[6:]
    n = emb_ref.shape[1]
    fs, osz, ds = FH // chunks, EO // chunks, D // chunks
    step = pl.program_id(0)
    core = tab_ref[0]
    second_core = core == 1

    @pl.when(step == 0)
    def _():
        rows = lax.broadcasted_iota(jnp.int32, (32, n), 0)
        x_s[EMB:XR, :] = jnp.where(rows == DENSE, 1.0, 0.0).astype(BF)
        ones = jnp.where(lax.broadcasted_iota(jnp.int32, (16, n), 0) == 0, 1.0, 0.0).astype(BF)
        hid_s[D : D + 16, :] = ones
        for k in range(NE):
            mid_s[k, FH : FH + 16, :] = ones
        mix_s[2 * EO : 2 * EO + 16, :] = ones
        fg_s[NE * FH + 16 : FG, :] = jnp.zeros((FG - NE * FH - 16, n), BF)
        for ref in (dwa_s, dw1_s, dw2_s, dtw_s, dcol_s, dlog_s):
            ref[...] = jnp.zeros_like(ref)
        gates = []
        for side in range(2):
            base = HALF * FH * side
            at = 0
            for ref in p_refs[side]:
                for c in range(ref.shape[0]):
                    for k in range(HALF):
                        w1_s[ds * at : ds * at + ds, base + FH * k : base + FH * k + FH] = ref[c, k]
                    at += 1
            for k in range(HALF):
                block = w1_s[:, base + FH * k : base + FH * k + FH]
                w1t_s[base + FH * k : base + FH * k + FH, :] = (block.astype(F32).T * 0.5).astype(BF)
            holder = core if side == 0 else 1 - core
            at = 0
            for ref in q_refs[side]:
                for c in range(ref.shape[0]):
                    q_s[tab_ref[1 + at]] = ref[c, :, 0:QD].astype(F32)
                    small = ref[c, :, QA:QD].astype(F32)
                    to = ds * p_order(at, chunks)
                    ga_s[to : to + fs, :] = small
                    ga_s[to + fs : to + ds, :] = pltpu.roll(small, 128 - NE, 1)
                    wat_s[pl.ds(pl.multiple_of(to + holder * fs, fs), fs), :] = ref[c, :, QD : QD + XR]
                    at += 1
            gates.append(swap_halves(ga_s[...].T[GA : GA + NE], second_core))
            w2 = q_s[:, :, 0:QA].reshape(FH, QA) * 0.5
            w2_s[:, QA * side : QA * side + QA] = w2.astype(BF)
            w2t_s[QA * side : QA * side + QA, :] = w2.T.astype(BF)
            b1_s[side] = q_s[:, :, QA:QD].reshape(FH, 128) * 0.5
            last = q_s[:, 0:osz, QA:QD].reshape(EO, 128)
            b2_s[side] = last * 0.5
            tower = last[:, 0:TW]
            rest = jnp.zeros_like(tower)
            both = jnp.concatenate([tower, rest] if side == 0 else [rest, tower], axis=1)
            tw_s[EO * side : EO * side + EO, :] = both.astype(BF)
            tt_s[:, EO * side : EO * side + EO] = (both.T * 0.5).astype(BF)
        gates = jnp.concatenate(gates, axis=0)
        w1t_s[NE * FH : NE * FH + 16, :] = gates.astype(BF)
        pad = jnp.concatenate([gates, jnp.zeros((112, D), F32)], axis=0)
        w1_s[:, NE * FH : FG] = pad.T.astype(BF)
        vecs = [jnp.concatenate([r[...].astype(F32), jnp.zeros((112, 128), F32)], axis=0).T for r in (vec_ref, far_vec_ref)]
        gb_s[...] = jnp.concatenate([swap_halves(v[0:NE, 0:1], second_core) for v in vecs], axis=0)
        b1 = jnp.concatenate([v[0:TW, 1:2] for v in vecs], axis=0)
        head = jnp.concatenate([v[0:TW, 2:3] for v in vecs], axis=0)
        last = jnp.concatenate([v[0:1, 3:4] for v in vecs] * TW, axis=0)
        tcol_s[...] = jnp.concatenate([b1 * 0.5, head, head * 0.5, last], axis=1)
        users = sizes_ref.shape[1]
        counts = sizes_ref[...].astype(F32)
        turned = jnp.concatenate([counts, jnp.zeros((128 - counts.shape[0], users), F32)], axis=0).T
        upto = lax.broadcasted_iota(jnp.int32, (users, users), 1) <= lax.broadcasted_iota(jnp.int32, (users, users), 0)
        ends = mm(jnp.where(upto, 1.0, 0.0).astype(BF), turned.astype(BF))
        starts = ends - turned
        for b in range(counts.shape[0]):
            end_s[b] = jnp.broadcast_to(ends[:, b : b + 1], (users, 128))
            start_s[b] = jnp.broadcast_to(starts[:, b : b + 1], (users, 128))
            inv_s[b] = jnp.broadcast_to(1.0 / turned[:, b : b + 1], (users, 128))

    batch_steps = batch_rows // n
    at_step = core * pl.num_programs(0) + step
    batch = at_step // batch_steps
    first_row = (at_step % batch_steps * n).astype(F32)
    row_weight = []
    for c in range(n // 128):
        row_at = first_row + (lax.broadcasted_iota(jnp.int32, (1, 128), 1) + 128 * c).astype(F32)
        inside = (row_at >= start_s[batch]) & (row_at < end_s[batch])
        row_weight.append(jnp.sum(jnp.where(inside, inv_s[batch], 0.0), axis=0, keepdims=True))
    row_weight = jnp.concatenate(row_weight, axis=1)
    labels = (lab_ref[...].astype(F32), far_lab_ref[...].astype(F32))
    x_s[0:EMB, :] = emb_ref[...]
    x_s[EMB : EMB + DENSE, :] = dense_ref[...]
    x = x_s[...]
    hid = mm(wat_s[...], x).astype(BF)
    hid_s[0:D, :] = hid
    logits = mm(w1t_s[NE * FH : NE * FH + 16, :], hid) + gb_s[...]
    probs = []
    for t in range(2):
        lt = logits[NE * t : NE * t + NE]
        e = jnp.exp(lt - jnp.max(lt, axis=0, keepdims=True))
        probs.append(e / jnp.sum(e, axis=0, keepdims=True))
    mix = [None, None]
    pend = None
    nxt = mm(w1t_s[0:FH, :], hid)
    for k in range(NE + 1):
        h = nxt
        if k < NE - 1:
            nxt = mm(w1t_s[FH * (k + 1) : FH * (k + 2), :], hid)
        if k < NE:
            m, s = act_pair(h + b1_s[k // HALF, :, B1 + k % HALF : B1 + k % HALF + 1])
            mb = m.astype(BF)
            mid_s[k, 0:FH, :] = mb
            sl1_s[FH * k : FH * k + FH, :] = s.astype(BF)
            h2 = mm(w2t_s[EO * k : EO * k + EO, :], mb)
        if pend is not None:
            j = k - 1
            o, s = act_pair(pend + b2_s[j // HALF, :, TW + j % HALF : TW + j % HALF + 1])
            out_s[EO * j : EO * j + EO, :] = o.astype(out_s.dtype)
            sl2_s[EO * j : EO * j + EO, :] = s.astype(sl2_s.dtype)
            for t in range(2):
                term = probs[t][j : j + 1, :] * o
                mix[t] = term if j == 0 else mix[t] + term
        pend = h2
    mix_s[0:EO, :] = mix[0].astype(BF)
    mix_s[EO : 2 * EO, :] = mix[1].astype(BF)
    act, slope = act_pair(mm(tt_s[...], mix_s[0 : 2 * EO, :]) + tcol_s[:, 0:1])
    weighted = act * tcol_s[:, 1:2]
    lgos = []
    for t in range(2):
        logit = jnp.sum(weighted[TW * t : TW * t + TW], axis=0, keepdims=True) + tcol_s[t : t + 1, 3:4]
        lgos.append(row_weight * (0.5 * jnp.tanh(0.5 * logit) + 0.5 - labels[t]))
    lgo = jnp.concatenate([jnp.broadcast_to(lgos[t], (TW, n)) for t in range(2)], axis=0)
    dcol_s[...] += lane_fold(lgo * act)
    dlog_s[...] += lane_fold(jnp.concatenate([jnp.broadcast_to(lgos[t], (8, n)) for t in range(2)], axis=0))
    tg = (lgo * (tcol_s[:, 2:3] * slope)).astype(BF)
    dtw_s[...] += mm_nt(mix_s[...], tg)
    mgh = mm(tw_s[...], tg) * 0.5
    pgs = [[], []]
    mgs = [None] * NE
    for k in range(NE + 2):
        if k < NE:
            o = out_s[EO * k : EO * k + EO, :].astype(F32)
            og = None
            for t in range(2):
                mg = mgh[EO * t : EO * t + EO]
                pgs[t].append(jnp.sum(o * mg, axis=0, keepdims=True))
                term = probs[t][k : k + 1, :] * mg
                og = term if og is None else og + term
            sg = (og * sl2_s[EO * k : EO * k + EO, :].astype(F32)).astype(BF)
            sg_s[EO * k : EO * k + EO, :] = sg
            mgs[k] = mm(w2_s[:, EO * k : EO * k + EO], sg)
        if 1 <= k < NE + 1:
            j = k - 1
            dw2_s[:, EO * j : EO * j + EO] += mm_nt(mid_s[j], sg_s[EO * j : EO * j + EO, :])
            fg = (mgs[j] * sl1_s[FH * j : FH * j + FH, :].astype(F32)).astype(BF)
            fg_s[FH * j : FH * j + FH, :] = fg
        if k >= 2:
            j = k - 2
            dw1_s[:, FH * j : FH * j + FH] += mm_nt(hid_s[...], fg_s[FH * j : FH * j + FH, :])
    lgs = []
    for t in range(2):
        pg = jnp.concatenate(pgs[t], axis=0)
        lgs.append(2.0 * probs[t] * (pg - jnp.sum(probs[t] * pg, axis=0, keepdims=True)))
    fg_s[NE * FH : NE * FH + 16, :] = jnp.concatenate(lgs, axis=0).astype(BF)
    dw1_s[:, NE * FH : FG] += mm_nt(hid_s[...], fg_s[NE * FH : FG, :])
    hg = mm(w1_s[...], fg_s[...]).astype(BF)
    hg_ref[...] = hg
    dwa_s[...] += mm_nt(hg, x)

    @pl.when(step == pl.num_programs(0) - 1)
    def _():
        gate = dw1_s[:, NE * FH : FG].T
        dlog = jnp.sum(dlog_s[...], axis=1, keepdims=True)
        dcol = jnp.sum(dcol_s[...].T, axis=0, keepdims=True)
        for side in range(2):
            ref = dp_refs[side]
            for c in range(chunks):
                for k in range(HALF):
                    base = HALF * FH * side + FH * k
                    ref[c, k] = dw1_s[ds * c : ds * c + ds, base : base + FH].astype(BF)
            own_gate = swap_halves(gate[NE * side : NE * side + NE], second_core)
            gate_rows = jnp.concatenate([own_gate[:, 0:D], jnp.zeros((120, D), F32)], axis=0).T
            b1 = [dw1_s[D : D + 1, FH * k : FH * k + FH] for k in range(HALF * side, HALF * side + HALF)]
            b1 = jnp.concatenate(b1 + [jnp.zeros((124, FH), F32)], axis=0).T
            b2 = [dw2_s[FH : FH + 1, EO * k : EO * k + EO] for k in range(HALF * side, HALF * side + HALF)]
            b2 = jnp.concatenate(b2 + [jnp.zeros((60, EO), F32)], axis=0).T
            tower = dtw_s[EO * side : EO * side + EO, TW * side : TW * side + TW]
            tower = jnp.concatenate([tower, b2], axis=1)
            lanes = slice(TW * side, TW * side + TW)
            blank = jnp.zeros((1, TW), F32)
            lines = [jnp.concatenate([a, blank], axis=1) for a in (dtw_s[2 * EO : 2 * EO + 1, lanes], dcol[:, lanes])]
            gate_b = jnp.sum(jnp.where(lax.broadcasted_iota(jnp.int32, (NE, D + 16), 1) == D, own_gate, 0.0), axis=1, keepdims=True)
            small = jnp.concatenate([gate_b, dlog[8 * side : 8 * side + 8]], axis=0)
            small = jnp.concatenate([jnp.broadcast_to(small, (16, 128)), jnp.zeros((112, 128), F32)], axis=0).T[0:1]
            tail = jnp.concatenate(lines + [small, jnp.zeros((fs - osz - 3, 128), F32)], axis=0)
            b1 = pltpu.roll(b1, B1, 1)
            for c in range(chunks):
                dsm_s[fs * c : fs * c + fs, :] = b1[fs * c : fs * c + fs] + jnp.concatenate([tower[osz * c : osz * c + osz], tail], axis=0)
            ref = dq_refs[side]
            holder = core if side == 0 else 1 - core
            for c in range(chunks):
                where = pl.ds(pl.multiple_of(tab_ref[1 + c] * fs, fs), fs)
                ref[c, :, 0:QA] = dw2_s[where, QA * side : QA * side + QA].astype(BF)
                to = ds * p_order(c, chunks)
                low = pltpu.roll(gate_rows[to : to + fs], GA, 1)
                high = pltpu.roll(gate_rows[to + fs : to + ds], GA + NE, 1)
                ref[c, :, QA:QD] = (dsm_s[where, :] + low + high).astype(BF)
                ref[c, :, QD : QD + XR] = dwa_s[pl.ds(pl.multiple_of(to + holder * fs, fs), fs), :].astype(BF)
                ref[c, :, QD + XR : QC] = jnp.zeros((fs, QC - QD - XR), BF)


def const2(i, c):
    return (0, 0)


def const3(i, c):
    return (0, 0, 0)


def const4(i, c):
    return (0, 0, 0, 0)


def main_call(table, embt, denset, labels, far_labels, sizes, vec, far_vec, p_own, p_other, q_own, q_other):
    rows = embt.shape[1]
    half = rows // 2
    steps = half // TILE
    pieces = len(p_own)
    chunks = sum(a.shape[0] for a in q_own)
    fs, ds = FH // chunks, D // chunks
    batches, users = sizes.shape

    def own(i, c):
        return (0, c[0] * steps + i)

    grads = [(chunks, HALF, ds, FH)] * 2 + [(chunks, fs, QC)] * 2
    spec = pltpu.PrefetchScalarGridSpec(
        num_scalar_prefetch=1,
        grid=(steps,),
        in_specs=[
            pl.BlockSpec((EMB, TILE), own),
            pl.BlockSpec((DENSE, TILE), own),
            pl.BlockSpec((1, TILE), own),
            pl.BlockSpec((1, TILE), own),
        ]
        + [whole()] * (3 + 4 * pieces),
        out_specs=[pl.BlockSpec((D, TILE), lambda i, c: (0, i))] + [whole()] * 5,
        scratch_shapes=[
            pltpu.VMEM((XR, TILE), BF),
            pltpu.VMEM((D + 16, TILE), BF),
            pltpu.VMEM((NE, FH + 16, TILE), BF),
            pltpu.VMEM((NE * FH, TILE), BF),
            pltpu.VMEM((NE * EO, TILE), F32),
            pltpu.VMEM((NE * EO, TILE), F32),
            pltpu.VMEM((NE * EO, TILE), BF),
            pltpu.VMEM((FG, TILE), BF),
            pltpu.VMEM((2 * EO + 16, TILE), BF),
            pltpu.VMEM((D, FG), BF),
            pltpu.VMEM((NE * FH + 16, D), BF),
            pltpu.VMEM((D, 128), F32),
            pltpu.VMEM((NE * EO, FH), BF),
            pltpu.VMEM((FH, NE * EO), BF),
            pltpu.VMEM((2, FH, 128), F32),
            pltpu.VMEM((2, EO, 128), F32),
            pltpu.VMEM((16, 1), F32),
            pltpu.VMEM((2 * TW, 2 * EO), BF),
            pltpu.VMEM((2 * EO, 2 * TW), BF),
            pltpu.VMEM((2 * TW, 4), F32),
            pltpu.VMEM((chunks, fs, QD), F32),
            pltpu.VMEM((batches, users, 128), F32),
            pltpu.VMEM((batches, users, 128), F32),
            pltpu.VMEM((batches, users, 128), F32),
            pltpu.VMEM((D, XR), F32),
            pltpu.VMEM((D + 16, FG), F32),
            pltpu.VMEM((FH + 16, NE * EO), F32),
            pltpu.VMEM((2 * EO + 16, 2 * TW), F32),
            pltpu.VMEM((2 * TW, 128), F32),
            pltpu.VMEM((16, 128), F32),
            pltpu.VMEM((FH, 128), F32),
        ],
    )
    return pl.pallas_call(
        functools.partial(main_kernel, pieces, chunks, rows // batches),
        grid_spec=spec,
        out_shape=[jax.ShapeDtypeStruct((D, half), BF), jax.ShapeDtypeStruct((D, XR), BF)]
        + [jax.ShapeDtypeStruct(a, BF) for a in grads],
        compiler_params=pltpu.CompilerParams(vmem_limit_bytes=48 * 1024 * 1024),
        cost_estimate=pl.CostEstimate(flops=50_000_000_000, bytes_accessed=24_000_000, transcendentals=0),
        name="experts",
    )(table, embt, denset, labels, far_labels, sizes, vec, far_vec, *p_own, *p_other, *q_own, *q_other)


def input_kernel(steps, tab_ref, own_ref, far_ref, wat_ref, token_ref, eg_ref, dg_ref, done_ref, wa_s):
    step = pl.program_id(0)

    @pl.when(step == 0)
    def _():
        done_ref[...] = jnp.zeros_like(done_ref)
        wa_s[...] = wat_ref[...].astype(F32).T.astype(BF)

    def emit(ref):
        eg = mm(wa_s[...], ref[...])
        eg_ref[...] = eg[0:EMB]
        dg_ref[...] = eg[EMB : EMB + DENSE]

    @pl.when(step < steps)
    def _():
        emit(own_ref)

    @pl.when(step >= steps)
    def _():
        emit(far_ref)


def input_call(table, own_hg, far_hg, wat, token):
    half = own_hg.shape[1]
    tile = 2 * TILE
    steps = half // tile

    def place(i, c):
        near = i < steps
        return (0, jnp.where(near, c[0] * steps + i, (1 - c[0]) * steps + i - steps))

    spec = pltpu.PrefetchScalarGridSpec(
        num_scalar_prefetch=1,
        grid=(2 * steps,),
        in_specs=[
            pl.BlockSpec((D, tile), lambda i, c: (0, jnp.minimum(i, steps - 1))),
            pl.BlockSpec((D, tile), lambda i, c: (0, jnp.maximum(i - steps, 0))),
            whole(),
            whole(pl.ANY),
        ],
        out_specs=[pl.BlockSpec((EMB, tile), place), pl.BlockSpec((DENSE, tile), place), pl.BlockSpec((8, 128), const2)],
        scratch_shapes=[pltpu.VMEM((XR, D), BF)],
    )
    return pl.pallas_call(
        functools.partial(input_kernel, steps),
        grid_spec=spec,
        out_shape=[jax.ShapeDtypeStruct((EMB, 2 * half), F32), jax.ShapeDtypeStruct((DENSE, 2 * half), F32), jax.ShapeDtypeStruct((8, 128), F32)],
        compiler_params=pltpu.CompilerParams(vmem_limit_bytes=48 * 1024 * 1024),
        cost_estimate=pl.CostEstimate(flops=6_000_000_000, bytes_accessed=18_000_000, transcendentals=0),
        name="input_grads",
    )(table, own_hg, far_hg, wat, token)


def widen(a):
    return jnp.concatenate([a.astype(F32), jnp.zeros((a.shape[0], 128 - a.shape[1]), F32)], axis=1)


def square(rows):
    count = sum(a.shape[0] for a in rows)
    return jnp.concatenate(rows + [jnp.zeros((128 - count, 128), F32)], axis=0)


def pack_vec(gb_ref, t1_ref, t2_ref, t3_ref):
    return jnp.concatenate([widen(r[...]) for r in (gb_ref, t1_ref, t2_ref, t3_ref)] + [jnp.zeros((12, 128), F32)], axis=0).astype(BF)


def pack_kernel(core_ref, emb_ref, dense_ref, bias_ref, w2_ref, b1_ref, b2_ref, gate_ref, tower_ref, *refs):
    q_ref, vec_ref = refs[4:]
    vec_ref[...] = pack_vec(*refs[:4])
    fs = q_ref.shape[0]
    turned = square([widen(r[...]) for r in (b1_ref, b2_ref, gate_ref, dense_ref, bias_ref)]).T
    lane = lax.broadcasted_iota(jnp.int32, (fs, 128), 1)
    low, high = turned[0:fs], turned[fs : 2 * fs]
    small = jnp.concatenate([widen(tower_ref[...]), jnp.zeros((fs - tower_ref.shape[0], 128), F32)], axis=0)
    small += jnp.where((lane >= TW) & (lane < TW + HALF), pltpu.roll(low, TW - HALF, 1), 0.0)
    small += jnp.where(((lane >= B1) & (lane < B1 + HALF)) | ((lane >= GA) & (lane < GA + NE)), pltpu.roll(low, B1, 1), 0.0)
    small += jnp.where((lane >= GA + NE) & (lane < GA + 2 * NE), pltpu.roll(high, GA, 1), 0.0)
    for k in range(HALF):
        q_ref[:, EO * k : EO * k + EO] = w2_ref[k]
    q_ref[:, QA:QD] = small.astype(BF)
    second_core = core_ref[0] == 1
    lanes = lax.broadcasted_iota(jnp.int32, (2 * fs, 128), 1)
    last = widen(emb_ref[:, 384:EMB]) + jnp.where((lanes >= 32) & (lanes < 33 + DENSE), pltpu.roll(turned[0 : 2 * fs], 16, 1), 0.0)
    for c in range(3):
        block = emb_ref[:, 128 * c : 128 * c + 128]
        q_ref[:, QD + 128 * c : QD + 128 * c + 128] = jnp.where(second_core, block[fs:], block[0:fs])
    q_ref[:, QD + 384 : QC] = jnp.where(second_core, last[fs:], last[0:fs]).astype(BF)


def whole(memory=pltpu.VMEM):
    return pl.BlockSpec(memory_space=memory)


def pack_call(core, *parts):
    fs = parts[3].shape[1]
    return pl.pallas_call(
        pack_kernel,
        in_specs=[whole(pltpu.SMEM)] + [whole() for _ in parts],
        out_specs=[whole(), whole()],
        out_shape=[jax.ShapeDtypeStruct((fs, QC), BF), jax.ShapeDtypeStruct((16, 128), BF)],
        name="pack",
    )(core, *parts)


def sum_kernel(groups, count, *refs):
    ins, outs = refs[:count], refs[-len(groups) :]
    for group, out in zip(groups, outs):
        total = None
        for number, at in group:
            term = (ins[number][...] if at is None else ins[number][at]).astype(F32)
            total = term if total is None else total + term
        out[...] = total.astype(out.dtype)


def sum_call(name, arrays, groups, shapes, token=None, dtype=BF):
    shapes = [jax.ShapeDtypeStruct(a, dtype) for a in shapes]
    extra = [] if token is None else [token]
    return pl.pallas_call(
        functools.partial(sum_kernel, groups, len(arrays)),
        in_specs=[whole() for _ in arrays] + [whole(pl.ANY) for _ in extra],
        out_specs=[whole() for _ in shapes],
        out_shape=shapes,
        compiler_params=pltpu.CompilerParams(vmem_limit_bytes=32 * 1024 * 1024),
        name=name,
    )(*arrays, *extra)


def finish_kernel(scale, core_ref, far_ref, *refs):
    tp, tq = [sum(r[...].astype(F32) for r in refs[4 * j : 4 * j + 4]) * scale for j in range(2)]
    own_part, far_part = tq[:, QD : QD + XR], far_ref[...] * scale
    second_core = core_ref[0] == 1
    ta = jnp.concatenate([jnp.where(second_core, far_part, own_part), jnp.where(second_core, own_part, far_part)], axis=0)
    emb_ref, dense_ref, bias_ref, w1_ref, b1_ref, w2_ref, b2_ref, gate_ref, gb_ref, tower_ref, t1_ref, t2_ref, t3_ref = refs[8:]
    fs = tq.shape[0]
    osz = tower_ref.shape[0]
    w1_ref[...] = tp
    for k in range(HALF):
        w2_ref[k] = tq[:, EO * k : EO * k + EO]
    small = tq[:, QA:QD]
    turned = square([small]).T
    b1_ref[...] = turned[B1 : B1 + HALF, 0:fs]
    b2_ref[...] = turned[TW : TW + HALF, 0:osz]
    gates = turned[GA : GA + NE] + pltpu.roll(turned[GA + NE : GA + 2 * NE], fs, 1)
    gate_ref[...] = gates[:, 0 : 2 * fs]
    tower_ref[...] = small[0:osz, 0:TW]
    t1_ref[...] = small[osz : osz + 1, 0:TW]
    t2_ref[...] = small[osz + 1 : osz + 2, 0:TW]
    gb_ref[...] = small[osz + 2 : osz + 3, 0:NE]
    t3_ref[...] = small[osz + 2 : osz + 3, NE : NE + 1]
    emb_ref[...] = ta[:, 0:EMB]
    last = square([widen(ta[:, 384:XR])]).T
    dense_ref[...] = last[32 : 32 + DENSE, 0 : 2 * fs]
    bias_ref[...] = last[32 + DENSE : 33 + DENSE, 0 : 2 * fs]


def last_kernel(*refs):
    refs[4][...] = sum(r[:, QD : QD + XR].astype(F32) for r in refs[:4])


def last_call(arrays):
    return pl.pallas_call(
        last_kernel,
        in_specs=[whole() for _ in arrays],
        out_specs=whole(),
        out_shape=jax.ShapeDtypeStruct((arrays[0].shape[0], XR), F32),
        name="sum_last",
    )(*arrays)


def finish_call(scale, core, far, arrays, ds, fs, osz):
    shapes = [
        (ds, EMB), (DENSE, ds), (1, ds), (HALF, ds, FH), (HALF, fs), (HALF, fs, EO), (HALF, osz), (NE, ds), (1, NE),
        (osz, TW), (1, TW), (1, TW), (1, 1),
    ]
    return pl.pallas_call(
        functools.partial(finish_kernel, scale),
        in_specs=[whole(pltpu.SMEM), whole()] + [whole() for _ in arrays],
        out_specs=[whole() for _ in shapes],
        out_shape=[jax.ShapeDtypeStruct(a, F32) for a in shapes],
        name="finish",
    )(core, far, *arrays)


def join_kernel(*refs):
    ins, (p_ref, q_ref) = refs[:8], refs[8:]
    for j in range(4):
        p_ref[j] = ins[j][...]
        q_ref[j] = ins[4 + j][...]


def join_call(parts_p, parts_q):
    return pl.pallas_call(
        join_kernel,
        in_specs=[whole() for _ in range(8)],
        out_specs=[whole(), whole()],
        out_shape=[jax.ShapeDtypeStruct((4, *a[0].shape), BF) for a in (parts_p, parts_q)],
        name="join",
    )(*parts_p, *parts_q)


def hop(a, mask, size):
    return lax.ppermute(a, "rows", [(i, i ^ mask) for i in range(size)])


def partner(a):
    return lax.ppermute(a, "task", [(0, 1), (1, 0)])


def add_wide(a, b):
    return a.astype(F32) + b.astype(F32)


def pad_to(a, rows, cols):
    return jnp.pad(a, ((0, rows - a.shape[0]), (0, cols - a.shape[1])))


def body(
    emb, dense, group_sizes, labels, w_emb, w_dense, b_in, expert_w1, expert_b1, expert_w2, expert_b2,
    gate_w, gate_b, tower_w1, tower_b1, tower_w2, tower_b2,
):
    size = lax.axis_size("rows")
    core = lax.axis_index("task")
    place = lax.axis_index("rows")
    user_count = group_sizes.shape[1] * group_sizes.shape[0] * size
    ds, fs, osz = D // size, FH // size, EO // size
    fast = size == 16
    far_labels = partner(labels)
    smalls = (gate_b, tower_b1, tower_w2, tower_b2[None])

    if fast:
        one_core = core[None].astype(jnp.int32)
        gate_t = jnp.transpose(gate_w, (0, 2, 1))[0]
        q_shard, vec = pack_call(
            one_core, w_emb.T, w_dense, b_in[None], expert_w2, expert_b1, expert_b2, gate_t, tower_w1[0], *smalls
        )
        near_p = [expert_w1] + [hop(expert_w1, 4 * a, size) for a in range(1, 4)]
        near_q = [q_shard] + [hop(q_shard, b, size) for b in range(1, 4)]
        zp, zq = join_call(near_p, near_q)
        p_own = [zp] + [hop(zp, b, size) for b in range(1, 4)]
        q_own = [zq] + [hop(zq, 4 * a, size) for a in range(1, 4)]
        order = place ^ jnp.arange(16, dtype=jnp.int32)
    else:
        gather = functools.partial(lax.all_gather, axis_name="rows", axis=0, tiled=True)
        proj = jnp.concatenate([w_emb.T, w_dense.T, b_in[:, None], jnp.zeros((ds, 82), BF)], axis=1)
        w2_all = gather(jnp.transpose(expert_w2, (1, 0, 2)).reshape(fs, QA))
        o_all = gather(jnp.concatenate([tower_w1[0], expert_b2.T], axis=1))
        b1_all, g_all, proj_all = gather(expert_b1.T), gather(gate_w[0]), gather(proj)
        small = jnp.concatenate([pad_to(o_all, FH, B1), pad_to(b1_all, FH, GA - B1), g_all[0:FH], g_all[FH:], jnp.zeros((FH, 32), BF)], axis=1)
        part = jnp.where(core == 0, proj_all[0:FH], proj_all[FH:])
        q_own = [jnp.concatenate([w2_all, small, part], axis=1)[None]]
        p_own = [lax.all_gather(expert_w1, "rows", axis=1, tiled=True)[None]]
        order = jnp.zeros((1,), jnp.int32)
        vec = jnp.concatenate([pad_to(a, 1, 128) for a in smalls] + [jnp.zeros((12, 128), BF)], axis=0)
    p_other = [partner(a) for a in p_own]
    q_other = [partner(a) for a in q_own]
    table = jnp.concatenate([core[None].astype(jnp.int32), order])

    hg, wat, dp_own, dp_far, dq_own, dq_far = main_call(
        table, emb.T, dense.T, labels, far_labels, group_sizes, vec, partner(vec), p_own, p_other, q_own, q_other
    )
    dp_far, dq_far = partner(dp_far), partner(dq_far)
    far_hg = partner(hg)
    scale = 1.0 / user_count
    if fast:
        p_shape, q_shape = (HALF, ds, FH), (fs, QC)
        groups = [[(j, slice(4 * b, 4 * b + 4)), (j + 1, slice(4 * b, 4 * b + 4))] for j in (0, 2) for b in range(1, 4)]
        sums = sum_call("sum_cores", [dp_own, dp_far, dq_own, dq_far], groups, [(4, *p_shape)] * 3 + [(4, *q_shape)] * 3)
        got_p = [hop(sums[b - 1], b, size) for b in range(1, 4)]
        got_q = [hop(sums[2 + a], 4 * a, size) for a in range(1, 4)]
        eg, dg, token = input_call(table, hg, far_hg, wat, sums[0])
        groups = [[(j, k) for j in range(start, start + 5)] for start in (0, 5) for k in range(4)]
        arrays = [dp_own, dp_far, *got_p, dq_own, dq_far, *got_q]
        sums = sum_call("sum_first", arrays, groups, [p_shape] * 4 + [q_shape] * 4, token)
        parts_p = [sums[0]] + [hop(sums[a], 4 * a, size) for a in range(1, 4)]
        parts_q = [sums[4]] + [hop(sums[4 + b], b, size) for b in range(1, 4)]
        far_input = partner(last_call(parts_q))
        out = finish_call(scale, one_core, far_input, parts_p + parts_q, ds, fs, osz)
        g_emb, g_dense, g_bias, g_w1, g_b1, g_w2, g_b2, g_gate, g_gb, g_tower, g_t1, g_t2, g_t3 = out
        return (
            eg.T, dg.T, g_emb.T, g_dense, g_bias[0], g_w1, g_b1, g_w2, g_b2, g_gate.T[None], g_gb, g_tower[None], g_t1, g_t2, g_t3[0],
        )
    eg, dg, _ = input_call(table, hg, far_hg, wat, dp_far)
    scatter = functools.partial(lax.psum_scatter, axis_name="rows", scatter_dimension=0, tiled=True)
    dp, wide = add_wide(dp_own[0], dp_far[0]), add_wide(dq_own[0], dq_far[0])
    small = wide[:, QA:QD]
    near, far = wide[:, QD : QD + XR], partner(wide[:, QD : QD + XR])
    ta = scatter(jnp.concatenate([jnp.where(core == 0, near, far), jnp.where(core == 0, far, near)], axis=0)) * scale
    tp = lax.psum_scatter(dp, "rows", scatter_dimension=1, tiled=True) * scale
    tw2, to, tb1 = scatter(wide[:, 0:QA]) * scale, scatter(small[0:EO, 0:B1]) * scale, scatter(small[:, B1 : B1 + HALF]) * scale
    tg = scatter(jnp.concatenate([small[:, GA : GA + NE], small[:, GA + NE : GA + 2 * NE]], axis=0)) * scale
    ts = lax.psum(small[EO : EO + 3], "rows") * scale
    return (
        eg.T,
        dg.T,
        ta[:, 0:EMB].T,
        ta[:, EMB : EMB + DENSE].T,
        ta[:, EMB + DENSE],
        tp,
        tb1.T,
        jnp.transpose(tw2.reshape(fs, HALF, EO), (1, 0, 2)),
        to[:, TW : TW + HALF].T,
        tg[None],
        ts[2:3, 0:NE],
        to[:, 0:TW][None],
        ts[0:1, 0:TW],
        ts[1:2, 0:TW],
        ts[2, NE : NE + 1],
    )


def solution(mesh):
    in_specs = (
        P("rows", None),
        P("rows", None),
        P("rows", None),
        P("task", "rows"),
        P(None, "rows"),
        P(None, "rows"),
        P("rows"),
        P("task", "rows", None),
        P("task", "rows"),
        P("task", "rows", None),
        P("task", "rows"),
        P("task", "rows", None),
        P("task", None),
        P("task", "rows", None),
        P("task", None),
        P("task", None),
        P("task"),
    )
    out_specs = (
        P("rows", None),
        P("rows", None),
        P(None, "rows"),
        P(None, "rows"),
        P("rows"),
        P("task", "rows", None),
        P("task", "rows"),
        P("task", "rows", None),
        P("task", "rows"),
        P("task", "rows", None),
        P("task", None),
        P("task", "rows", None),
        P("task", None),
        P("task", None),
        P("task"),
    )
    return jax.shard_map(body, mesh=mesh, in_specs=in_specs, out_specs=out_specs, check_vma=False)
```

time: 172 us -> 150 us (0.87)
  other arithmetic: 11.1 us -> 0.08 us
  waiting for transfers between devices: 40.4 us -> 29.4 us
  Pallas kernels: 62.4 us -> 70.4 us
  local copies, waits for them, and re-layouts: 18.4 us -> 12.1 us
  starting transfers between devices: 37.6 us -> 35.7 us
    ppermute x24, waiting for transfers between devices: 37.6 us -> 17.1 us  [hop(): return lax.ppermute(a, 'rows', [(i, i ^ mask) for i in range(size)])]
    ppermute x12 -> x14, waiting for transfers between devices: 2.87 us -> 12.3 us  [partner(): return lax.ppermute(a, 'task', [(0, 1), (1, 0)])]
    pallas_call x2 -> x8, Pallas kernels: 62.4 us -> 70.4 us  [the longest x1 53.9 us: main_call(): pl.pallas_call(functools.partial(main_kernel, pieces, chunks, rows // bat...]
    unnamed x52 -> x50, local copies, waits for them, and re-layouts: 8.21 us -> 12.1 us
    ppermute x24, starting transfers between devices: 35.3 us -> 32.5 us  [hop(): return lax.ppermute(a, 'rows', [(i, i ^ mask) for i in range(size)])]
    slice x8 -> x0, local copies, waits for them, and re-layouts: 2.73 us -> none  [the longest x1 0.69 us: body(): tp[:, EMB + DENSE]]
    reduce_sum x1 -> x0, other arithmetic: 2.7 us -> none  [body(): jnp.sum(jnp.where(inside, inverse[:, None, :], 0.0), axis=2).reshape(1, -1)]
    convert_element_type x7 -> x0, other arithmetic: 2.53 us -> none  [the longest x1 1.09 us: body(): dq = (dq_own.astype(F32) + partner(dq_other).astype(F32)).astype(BF)]
  transfers between devices with their start and end apart: 36 -> 38, of which waited for: 19 -> 13; matrix products, arithmetic and copies ran while one was open for 14% -> 0% of each run, Pallas kernels for 0% -> 7%
where the time goes in v2:
time: 150 us; the launch traced here: 149 us
  Pallas kernels  70.4 us (47%)
  starting transfers between devices  35.7 us (24%)
  waiting for transfers between devices  29.4 us (20%)
  local copies, waits for them, and re-layouts  12.1 us (8%)
  between operations  1.5 us (1%)
    pallas_call x1, Pallas kernels, main_call(): pl.pallas_call(functools.partial(main_kernel, pieces, chunks, rows // bat...  53.9 us
    ppermute x24, starting transfers between devices, hop(): return lax.ppermute(a, 'rows', [(i, i ^ mask) for i in range(size)])  32.5 us
    ppermute x24, waiting for transfers between devices, hop(): return lax.ppermute(a, 'rows', [(i, i ^ mask) for i in range(size)])  17.1 us
    ppermute x14, waiting for transfers between devices, partner(): return lax.ppermute(a, 'task', [(0, 1), (1, 0)])  12.3 us
    unnamed x50, local copies, waits for them, and re-layouts  12.1 us
    pallas_call x1, Pallas kernels, input_call(): pl.pallas_call(functools.partial(input_kernel, steps), grid_spec=spec, ou...  9.24 us
    ppermute x14, starting transfers between devices, partner(): return lax.ppermute(a, 'task', [(0, 1), (1, 0)])  3.18 us
  transfers between devices with their start and end apart: 38, of which 13 were waited for; matrix products, arithmetic and copies ran while one was open for 0% of the time, Pallas kernels for 7%

profile of v2, /device:TPU:0, one launch (start us, length us, event | category | flops | bytes accessed | tf_op | source)
XLA Modules:
  0.0 149.2 jit_solution(4028895784726134846)
XLA Ops:
  1.3 1.6 %pack.1 = (bf16[16,1152]{1,0:T(8,128)(2,1)}, bf16[16,128]{1,0:T(8,128)(2,1)}) custom-call(s32[1]{0:T(128)} %bitcast.core_ref, bf16[32,416]{1,0:T(8,128)(2,1)} %bitcast.21, bf16[13,32]{1,0:T(8,128)(2,1)} %dense_ref.1, bf16[1,32]{1,0:T(2,128)(2,1)} %bitcast.24, bf16[4,16,128]{2,1,0:T(8,128)(2,1)} %w2_ref.1, bf16[4,16]{1,0:T(4,128)(2,1)} %b1_ref.1, ...), custom_call_target="tpu_custom_call" | custom-call | tf_op jit(solution)/shard_map/pack/pallas_call | solution.py:449
  2.9 2.9 %collective-permute-start.5 = (bf16[16,1152]{1,0:T(8,128)(2,1)}, bf16[16,1152]{1,0:T(8,128)(2,1)S(1)}, u32[]{:S(2)}, u32[]{:S(2)}) collective-permute-start(bf16[16,1152]{1,0:T(8,128)(2,1)} %get-tuple-element.56.refs_4_), channel_id=1, source_target_pairs={{0,2},{2,0},{4,6},{6,4},{8,10},{10,8},{12,14},{14,12},{16,18},{18,... | collective-permute-start | bytes 110600 | tf_op jit(solution)/shard_map/ppermute | solution.py:555
  5.9 1.6 %collective-permute-start.2 = (bf16[4,32,256]{2,1,0:T(8,128)(2,1)}, bf16[4,32,256]{2,1,0:T(8,128)(2,1)S(1)}, u32[]{:S(2)}, u32[]{:S(2)}) collective-permute-start(bf16[4,32,256]{2,1,0:T(8,128)(2,1)} %refs_0_.3), channel_id=1, source_target_pairs={{0,8},{2,10},{4,12},{6,14},{8,0},{10,2},{12,4},{14,6},{16,24},{18,... | collective-permute-start | bytes 196616 | tf_op jit(solution)/shard_map/ppermute | solution.py:555
  7.5 2.6 %collective-permute-start.3 = (bf16[4,32,256]{2,1,0:T(8,128)(2,1)}, bf16[4,32,256]{2,1,0:T(8,128)(2,1)S(1)}, u32[]{:S(2)}, u32[]{:S(2)}) collective-permute-start(bf16[4,32,256]{2,1,0:T(8,128)(2,1)} %refs_0_.3), channel_id=1, source_target_pairs={{0,16},{2,18},{4,20},{6,22},{8,24},{10,26},{12,28},{14,30},{16,0},... | collective-permute-start | bytes 196616 | tf_op jit(solution)/shard_map/ppermute | solution.py:555
  10.3 1.5 %collective-permute-start.6 = (bf16[16,1152]{1,0:T(8,128)(2,1)}, bf16[16,1152]{1,0:T(8,128)(2,1)S(1)}, u32[]{:S(2)}, u32[]{:S(2)}) collective-permute-start(bf16[16,1152]{1,0:T(8,128)(2,1)} %get-tuple-element.56.refs_4_), channel_id=1, source_target_pairs={{0,4},{2,6},{4,0},{6,2},{8,12},{10,14},{12,8},{14,10},{16,20},{18,... | collective-permute-start | bytes 110600 | tf_op jit(solution)/shard_map/ppermute | solution.py:555
  12.0 2.7 %collective-permute-done.6.refs_6_ = bf16[16,1152]{1,0:T(8,128)(2,1)S(1)} collective-permute-done((bf16[16,1152]{1,0:T(8,128)(2,1)}, bf16[16,1152]{1,0:T(8,128)(2,1)S(1)}, u32[]{:S(2)}, u32[]{:S(2)}) %collective-permute-start.6) | collective-permute-done | bytes 36896 | tf_op jit(solution)/shard_map/ppermute | solution.py:555
  14.8 2.1 %collective-permute-done.7.refs_7_ = bf16[16,1152]{1,0:T(8,128)(2,1)S(1)} collective-permute-done((bf16[16,1152]{1,0:T(8,128)(2,1)}, bf16[16,1152]{1,0:T(8,128)(2,1)S(1)}, u32[]{:S(2)}, u32[]{:S(2)}) %collective-permute-start.7) | collective-permute-done | bytes 36896 | tf_op jit(solution)/shard_map/ppermute | solution.py:555
  16.9 0.6 copy-done.22
  17.5 0.6 copy-done.16
  18.1 1.7 %join.1 = (bf16[4,4,32,256]{3,2,1,0:T(8,128)(2,1)}, bf16[4,16,1152]{2,1,0:T(8,128)(2,1)}) custom-call(bf16[4,32,256]{2,1,0:T(8,128)(2,1)} %refs_0_.3, bf16[4,32,256]{2,1,0:T(8,128)(2,1)} %copy-done.14, bf16[4,32,256]{2,1,0:T(8,128)(2,1)} %copy-done.15, bf16[4,32,256]{2,1,0:T(8,128)(2,1)} %copy-done.16, bf16[16,1152]{1,0:T(8,128)(2,1)} %get-tuple-element.56.refs_4_, ...), custom_call_target="tpu_custom_call" | custom-call | tf_op jit(solution)/shard_map/join/pallas_call | solution.py:545
  19.9 0.7 collective-permute-start.15
  20.6 3.5 %collective-permute-start.16 = (bf16[4,16,1152]{2,1,0:T(8,128)(2,1)}, bf16[4,16,1152]{2,1,0:T(8,128)(2,1)S(1)}, u32[]{:S(2)}, u32[]{:S(2)}) collective-permute-start(bf16[4,16,1152]{2,1,0:T(8,128)(2,1)} %get-tuple-element.58.refs_15_), channel_id=1, source_target_pairs={{0,16},{2,18},{4,20},{6,22},{8,24},{10,26},{12,28},{14,30},{16,0},... | collective-permute-start | bytes 442376 | tf_op jit(solution)/shard_map/ppermute | solution.py:555
  24.8 1.0 collective-permute-done.1.refs_6_
  26.7 2.6 %collective-permute-start.10 = (bf16[4,4,32,256]{3,2,1,0:T(8,128)(2,1)}, bf16[4,4,32,256]{3,2,1,0:T(8,128)(2,1)S(1)}, u32[]{:S(2)}, u32[]{:S(2)}) collective-permute-start(bf16[4,4,32,256]{3,2,1,0:T(8,128)(2,1)} %get-tuple-element.57.refs_7_), channel_id=1, source_target_pairs={{0,6},{2,4},{4,2},{6,0},{8,14},{10,12},{12,10},{14,8},{16,22},{18,... | collective-permute-start | bytes 786440 | tf_op jit(solution)/shard_map/ppermute | solution.py:555
  29.3 4.1 %collective-permute-done.16.refs_17_ = bf16[4,16,1152]{2,1,0:T(8,128)(2,1)S(1)} collective-permute-done((bf16[4,16,1152]{2,1,0:T(8,128)(2,1)}, bf16[4,16,1152]{2,1,0:T(8,128)(2,1)S(1)}, u32[]{:S(2)}, u32[]{:S(2)}) %collective-permute-start.16) | collective-permute-done | bytes 147488 | tf_op jit(solution)/shard_map/ppermute | solution.py:555
  33.9 1.1 collective-permute-done.18.refs_19_
  35.5 5.0 %collective-permute-done.9.refs_9_ = bf16[4,4,32,256]{3,2,1,0:T(8,128)(2,1)S(1)} collective-permute-done((bf16[4,4,32,256]{3,2,1,0:T(8,128)(2,1)}, bf16[4,4,32,256]{3,2,1,0:T(8,128)(2,1)S(1)}, u32[]{:S(2)}, u32[]{:S(2)}) %collective-permute-start.9) | collective-permute-done | bytes 262176 | tf_op jit(solution)/shard_map/ppermute | solution.py:555
  41.6 1.0 collective-permute-done.20.refs_21_
  42.8 0.9 copy-done.5
  43.8 0.9 copy-done.6
  44.7 0.9 copy-done.7
  45.6 0.7 copy-done.8
  46.3 0.7 copy-done.9
  47.0 0.7 copy-done.10
  47.7 53.9 %experts.1 = (bf16[512,3072]{1,0:T(8,128)(2,1)}, bf16[512,448]{1,0:T(8,128)(2,1)S(1)}, bf16[16,4,32,256]{3,2,1,0:T(8,128)(2,1)}, bf16[16,4,32,256]{3,2,1,0:T(8,1...) custom-call(s32[17]{0:T(128)S(1)} %pad_add_fusion.tab_ref, bf16[416,6144]{1,0:T(8,128)(2,1)} %bitcast.25, ...), custom_call_target="tpu_custom_call" | custom-call | flops 49999998976 | bytes 24000000 | tf_op jit(solution)/shard_map/experts/pallas_call | solution.py:343
  102.3 6.7 %collective-permute-done.24.refs_3_.refs_6_ = bf16[16,16,1152]{2,1,0:T(8,128)(2,1)S(1)} collective-permute-done((bf16[16,16,1152]{2,1,0:T(8,128)(2,1)S(1)}, bf16[16,16,1152]{2,1,0:T(8,128)(2,1)S(1)}, u32[]{:S(2)}, u32[]{:S(2)}) %collective-permute-start.24) | collective-permute-done | bytes 589856 | tf_op jit(solution)/shard_map/ppermute | solution.py:559
  109.0 0.9 collective-permute-done.23.refs_1_
  109.9 1.2 copy-done
  111.8 1.5 %collective-permute-start.25 = (bf16[4,4,32,256]{3,2,1,0:T(8,128)(2,1)S(1)}, bf16[4,4,32,256]{3,2,1,0:T(8,128)(2,1)S(1)}, u32[]{:S(2)}, u32[]{:S(2)}) collective-permute-start(bf16[4,4,32,256]{3,2,1,0:T(8,128)(2,1)S(1)} %get-tuple-element.65.token_ref), channel_id=1, source_target_pairs={{0,2},{2,0},{4,6},{6,4},{8,10},{10,8},{12,14},{14,12},{16,18},{18,... | collective-permute-start | bytes 786440 | tf_op jit(solution)/shard_map/ppermute | solution.py:555
  113.8 1.5 collective-permute-start.27
  115.3 2.1 %collective-permute-done.28.refs_7_ = bf16[4,16,1152]{2,1,0:T(8,128)(2,1)S(1)} collective-permute-done((bf16[4,16,1152]{2,1,0:T(8,128)(2,1)S(1)}, bf16[4,16,1152]{2,1,0:T(8,128)(2,1)S(1)}, u32[]{:S(2)}, u32[]{:S(2)}) %collective-permute-start.28) | collective-permute-done | bytes 147488 | tf_op jit(solution)/shard_map/ppermute | solution.py:555
  117.4 2.4 %collective-permute-start.29 = (bf16[4,16,1152]{2,1,0:T(8,128)(2,1)S(1)}, bf16[4,16,1152]{2,1,0:T(8,128)(2,1)S(1)}, u32[]{:S(2)}, u32[]{:S(2)}) collective-permute-start(bf16[4,16,1152]{2,1,0:T(8,128)(2,1)S(1)} %get-tuple-element.71), channel_id=1, source_target_pairs={{0,16},{2,18},{4,20},{6,22},{8,24},{10,26},{12,28},{14,30},{16,0},... | collective-permute-start | bytes 442376 | tf_op jit(solution)/shard_map/ppermute | solution.py:555
  119.8 1.2 collective-permute-start.30
  121.4 1.9 %copy-done.4 = bf16[512,3072]{1,0:T(8,128)(2,1)S(1)} copy-done((bf16[512,3072]{1,0:T(8,128)(2,1)S(1)}, bf16[512,3072]{1,0:T(8,128)(2,1)}, u32[]{:S(2)}) %copy-start.4) | copy-done | bytes 3145752
  123.3 9.2 %input_grads.1 = (f32[416,6144]{1,0:T(8,128)}, f32[13,6144]{1,0:T(8,128)}, f32[8,128]{1,0:T(8,128)S(1)}) custom-call(s32[17]{0:T(128)S(1)} %pad_add_fusion.tab_ref, bf16[512,3072]{1,0:T(8,128)(2,1)S(1)} %copy-done.4, bf16[512,3072]{1,0:T(8,128)(2,1)} %copy-done.24, bf16[512,448]{1,0:T(8,128)(2,1)S(1)} %get-tuple-element.60.wat_ref, ...), custom_call_target="tpu_custom_call" | custom-call | flops 6000000000 | bytes 18000000 | tf_op jit(solution)/shard_map/input_grads/pallas_call | solution.py:397
  132.9 0.6 copy-done.2
  133.5 0.6 copy-done.3
  134.1 1.5 %collective-permute-start.31 = (bf16[16,1152]{1,0:T(8,128)(2,1)S(1)}, bf16[16,1152]{1,0:T(8,128)(2,1)S(1)}, u32[]{:S(2)}, u32[]{:S(2)}) collective-permute-start(bf16[16,1152]{1,0:T(8,128)(2,1)S(1)} %get-tuple-element.75), channel_id=1, source_target_pairs={{0,2},{2,0},{4,6},{6,4},{8,10},{10,8},{12,14},{14,12},{16,18},{18,... | collective-permute-start | bytes 110600 | tf_op jit(solution)/shard_map/ppermute | solution.py:555
  136.1 1.5 collective-permute-start.33
  137.6 1.7 %collective-permute-start.35 = (bf16[4,32,256]{2,1,0:T(8,128)(2,1)S(1)}, bf16[4,32,256]{2,1,0:T(8,128)(2,1)S(1)}, u32[]{:S(2)}, u32[]{:S(2)}) collective-permute-start(bf16[4,32,256]{2,1,0:T(8,128)(2,1)S(1)} %get-tuple-element.79), channel_id=1, source_target_pairs={{0,8},{2,10},{4,12},{6,14},{8,0},{10,2},{12,4},{14,6},{16,24},{18,... | collective-permute-start | bytes 196616 | tf_op jit(solution)/shard_map/ppermute | solution.py:555
  139.3 1.2 collective-permute-start.36
  140.5 1.5 %collective-permute-start.37 = (bf16[4,32,256]{2,1,0:T(8,128)(2,1)S(1)}, bf16[4,32,256]{2,1,0:T(8,128)(2,1)S(1)}, u32[]{:S(2)}, u32[]{:S(2)}) collective-permute-start(bf16[4,32,256]{2,1,0:T(8,128)(2,1)S(1)} %get-tuple-element.81), channel_id=1, source_target_pairs={{0,24},{2,26},{4,28},{6,30},{8,16},{10,18},{12,20},{14,22},{16,8},... | collective-permute-start | bytes 196616 | tf_op jit(solution)/shard_map/ppermute | solution.py:555
  142.1 0.6 copy-done.12
  142.7 1.4 sum_last.1
  144.1 1.4 collective-permute-done.34.far_ref
  145.5 1.1 collective-permute-done.36.refs_2_
  146.7 0.6 copy-done.18
  147.3 1.9 %finish.1 = (f32[32,416]{1,0:T(8,128)}, f32[13,32]{1,0:T(8,128)}, f32[1,32]{1,0:T(1,128)}, f32[4,32,256]{2,1,0:T(8,128)}, f32[4,16]{1,0:T(4,128)}, /*index=5*/f3...) custom-call(s32[1]{0:T(128)} %bitcast.core_ref, ...), custom_call_target="tpu_custom_call" | custom-call | tf_op jit(solution)/shard_map/finish/pallas_call | solution.py:528
  (88 shorter events, 7.6 us)
Async XLA Ops:
  2.9 8.8 %collective-permute-start.5 = (bf16[16,1152]{1,0:T(8,128)(2,1)}, bf16[16,1152]{1,0:T(8,128)(2,1)S(1)}, u32[]{:S(2)}, u32[]{:S(2)}) collective-permute-start(bf16[16,1152]{1,0:T(8,128)(2,1)} %get-tuple-element.56.refs_4_), channel_id=1, source_target_pairs={{0,2},{2,0},{4,6},{6,4},{8,10},{10,8},{12,14},{14,12},{16,18},{18,... | collective-permute-start | bytes 110600 | tf_op jit(solution)/shard_map/ppermute | solution.py:555
  5.9 11.0 %collective-permute-start.2 = (bf16[4,32,256]{2,1,0:T(8,128)(2,1)}, bf16[4,32,256]{2,1,0:T(8,128)(2,1)S(1)}, u32[]{:S(2)}, u32[]{:S(2)}) collective-permute-start(bf16[4,32,256]{2,1,0:T(8,128)(2,1)} %refs_0_.3), channel_id=1, source_target_pairs={{0,8},{2,10},{4,12},{6,14},{8,0},{10,2},{12,4},{14,6},{16,24},{18,... | collective-permute-start | bytes 196616 | tf_op jit(solution)/shard_map/ppermute | solution.py:555
  7.5 9.4 %collective-permute-start.3 = (bf16[4,32,256]{2,1,0:T(8,128)(2,1)}, bf16[4,32,256]{2,1,0:T(8,128)(2,1)S(1)}, u32[]{:S(2)}, u32[]{:S(2)}) collective-permute-start(bf16[4,32,256]{2,1,0:T(8,128)(2,1)} %refs_0_.3), channel_id=1, source_target_pairs={{0,16},{2,18},{4,20},{6,22},{8,24},{10,26},{12,28},{14,30},{16,0},... | collective-permute-start | bytes 196616 | tf_op jit(solution)/shard_map/ppermute | solution.py:555
  10.0 6.8 %collective-permute-start.4 = (bf16[4,32,256]{2,1,0:T(8,128)(2,1)}, bf16[4,32,256]{2,1,0:T(8,128)(2,1)S(1)}, u32[]{:S(2)}, u32[]{:S(2)}) collective-permute-start(bf16[4,32,256]{2,1,0:T(8,128)(2,1)} %refs_0_.3), channel_id=1, source_target_pairs={{0,24},{2,26},{4,28},{6,30},{8,16},{10,18},{12,20},{14,22},{16,8},... | collective-permute-start | bytes 196616 | tf_op jit(solution)/shard_map/ppermute | solution.py:555
  10.3 4.5 %collective-permute-start.6 = (bf16[16,1152]{1,0:T(8,128)(2,1)}, bf16[16,1152]{1,0:T(8,128)(2,1)S(1)}, u32[]{:S(2)}, u32[]{:S(2)}) collective-permute-start(bf16[16,1152]{1,0:T(8,128)(2,1)} %get-tuple-element.56.refs_4_), channel_id=1, source_target_pairs={{0,4},{2,6},{4,0},{6,2},{8,12},{10,14},{12,8},{14,10},{16,20},{18,... | collective-permute-start | bytes 110600 | tf_op jit(solution)/shard_map/ppermute | solution.py:555
  11.8 5.1 %copy-start.20 = (bf16[16,1152]{1,0:T(8,128)(2,1)}, bf16[16,1152]{1,0:T(8,128)(2,1)S(1)}, u32[]{:S(2)}) copy-start(bf16[16,1152]{1,0:T(8,128)(2,1)S(1)} %collective-permute-done.5.refs_5_) | copy-start | bytes 110596
  11.8 5.1 %collective-permute-start.7 = (bf16[16,1152]{1,0:T(8,128)(2,1)}, bf16[16,1152]{1,0:T(8,128)(2,1)S(1)}, u32[]{:S(2)}, u32[]{:S(2)}) collective-permute-start(bf16[16,1152]{1,0:T(8,128)(2,1)} %get-tuple-element.56.refs_4_), channel_id=1, source_target_pairs={{0,6},{2,4},{4,2},{6,0},{8,14},{10,12},{12,10},{14,8},{16,22},{18,... | collective-permute-start | bytes 110600 | tf_op jit(solution)/shard_map/ppermute | solution.py:555
  14.8 2.1 %copy-start.21 = (bf16[16,1152]{1,0:T(8,128)(2,1)}, bf16[16,1152]{1,0:T(8,128)(2,1)S(1)}, u32[]{:S(2)}) copy-start(bf16[16,1152]{1,0:T(8,128)(2,1)S(1)} %collective-permute-done.6.refs_6_) | copy-start | bytes 110596
  19.9 6.8 %collective-permute-start.15 = (bf16[4,16,1152]{2,1,0:T(8,128)(2,1)}, bf16[4,16,1152]{2,1,0:T(8,128)(2,1)S(1)}, u32[]{:S(2)}, u32[]{:S(2)}) collective-permute-start(bf16[4,16,1152]{2,1,0:T(8,128)(2,1)} %get-tuple-element.58.refs_15_), channel_id=1, source_target_pairs={{0,8},{2,10},{4,12},{6,14},{8,0},{10,2},{12,4},{14,6},{16,24},{18,... | collective-permute-start | bytes 442376 | tf_op jit(solution)/shard_map/ppermute | solution.py:555
  20.6 12.8 %collective-permute-start.16 = (bf16[4,16,1152]{2,1,0:T(8,128)(2,1)}, bf16[4,16,1152]{2,1,0:T(8,128)(2,1)S(1)}, u32[]{:S(2)}, u32[]{:S(2)}) collective-permute-start(bf16[4,16,1152]{2,1,0:T(8,128)(2,1)} %get-tuple-element.58.refs_15_), channel_id=1, source_target_pairs={{0,16},{2,18},{4,20},{6,22},{8,24},{10,26},{12,28},{14,30},{16,0},... | collective-permute-start | bytes 442376 | tf_op jit(solution)/shard_map/ppermute | solution.py:555
  24.0 9.4 %collective-permute-start.17 = (bf16[4,16,1152]{2,1,0:T(8,128)(2,1)}, bf16[4,16,1152]{2,1,0:T(8,128)(2,1)S(1)}, u32[]{:S(2)}, u32[]{:S(2)}) collective-permute-start(bf16[4,16,1152]{2,1,0:T(8,128)(2,1)} %get-tuple-element.58.refs_15_), channel_id=1, source_target_pairs={{0,24},{2,26},{4,28},{6,30},{8,16},{10,18},{12,20},{14,22},{16,8},... | collective-permute-start | bytes 442376 | tf_op jit(solution)/shard_map/ppermute | solution.py:555
  24.3 2.1 %collective-permute-start = (s32[1,6144]{1,0:T(1,128)}, s32[1,6144]{1,0:T(1,128)S(1)}, u32[]{:S(2)}, u32[]{:S(2)}) collective-permute-start(s32[1,6144]{1,0:T(1,128)} %refs_2_.3), channel_id=1, source_target_pairs={{0,1},{1,0},{2,3},{3,2},{4,5},{5,4},{6,7},{7,6},{8,9},{9,8},{10,11... | collective-permute-start | bytes 73736 | tf_op jit(solution)/shard_map/ppermute | solution.py:559
  24.3 1.5 %collective-permute-start.1 = (bf16[16,128]{1,0:T(8,128)(2,1)}, bf16[16,128]{1,0:T(8,128)(2,1)S(1)}, u32[]{:S(2)}, u32[]{:S(2)}) collective-permute-start(bf16[16,128]{1,0:T(8,128)(2,1)} %get-tuple-element.55.refs_5_), channel_id=1, source_target_pairs={{0,1},{1,0},{2,3},{3,2},{4,5},{5,4},{6,7},{7,6},{8,9},{9,8},{10,11... | collective-permute-start | bytes 12296 | tf_op jit(solution)/shard_map/ppermute | solution.py:559
  25.8 9.3 %collective-permute-start.8 = (bf16[4,4,32,256]{3,2,1,0:T(8,128)(2,1)}, bf16[4,4,32,256]{3,2,1,0:T(8,128)(2,1)S(1)}, u32[]{:S(2)}, u32[]{:S(2)}) collective-permute-start(bf16[4,4,32,256]{3,2,1,0:T(8,128)(2,1)} %get-tuple-element.57.refs_7_), channel_id=1, source_target_pairs={{0,2},{2,0},{4,6},{6,4},{8,10},{10,8},{12,14},{14,12},{16,18},{18,... | collective-permute-start | bytes 786440 | tf_op jit(solution)/shard_map/ppermute | solution.py:555
  26.3 14.1 %collective-permute-start.9 = (bf16[4,4,32,256]{3,2,1,0:T(8,128)(2,1)}, bf16[4,4,32,256]{3,2,1,0:T(8,128)(2,1)S(1)}, u32[]{:S(2)}, u32[]{:S(2)}) collective-permute-start(bf16[4,4,32,256]{3,2,1,0:T(8,128)(2,1)} %get-tuple-element.57.refs_7_), channel_id=1, source_target_pairs={{0,4},{2,6},{4,0},{6,2},{8,12},{10,14},{12,8},{14,10},{16,20},{18,... | collective-permute-start | bytes 786440 | tf_op jit(solution)/shard_map/ppermute | solution.py:555
  26.7 13.8 %collective-permute-start.10 = (bf16[4,4,32,256]{3,2,1,0:T(8,128)(2,1)}, bf16[4,4,32,256]{3,2,1,0:T(8,128)(2,1)S(1)}, u32[]{:S(2)}, u32[]{:S(2)}) collective-permute-start(bf16[4,4,32,256]{3,2,1,0:T(8,128)(2,1)} %get-tuple-element.57.refs_7_), channel_id=1, source_target_pairs={{0,6},{2,4},{4,2},{6,0},{8,14},{10,12},{12,10},{14,8},{16,22},{18,... | collective-permute-start | bytes 786440 | tf_op jit(solution)/shard_map/ppermute | solution.py:555
  33.4 1.6 %collective-permute-start.18 = (bf16[4,16,1152]{2,1,0:T(8,128)(2,1)}, bf16[4,16,1152]{2,1,0:T(8,128)(2,1)S(1)}, u32[]{:S(2)}, u32[]{:S(2)}) collective-permute-start(bf16[4,16,1152]{2,1,0:T(8,128)(2,1)} %get-tuple-element.58.refs_15_), channel_id=1, source_target_pairs={{0,1},{1,0},{2,3},{3,2},{4,5},{5,4},{6,7},{7,6},{8,9},{9,8},{10,11... | collective-permute-start | bytes 442376 | tf_op jit(solution)/shard_map/ppermute | solution.py:559
  33.4 7.6 %collective-permute-start.11 = (bf16[4,4,32,256]{3,2,1,0:T(8,128)(2,1)}, bf16[4,4,32,256]{3,2,1,0:T(8,128)(2,1)S(1)}, u32[]{:S(2)}, u32[]{:S(2)}) collective-permute-start(bf16[4,4,32,256]{3,2,1,0:T(8,128)(2,1)} %get-tuple-element.57.refs_7_), channel_id=1, source_target_pairs={{0,1},{1,0},{2,3},{3,2},{4,5},{5,4},{6,7},{7,6},{8,9},{9,8},{10,11... | collective-permute-start | bytes 786440 | tf_op jit(solution)/shard_map/ppermute | solution.py:559
  35.0 6.1 %collective-permute-start.19 = (bf16[4,16,1152]{2,1,0:T(8,128)(2,1)S(1)}, bf16[4,16,1152]{2,1,0:T(8,128)(2,1)S(1)}, u32[]{:S(2)}, u32[]{:S(2)}) collective-permute-start(bf16[4,16,1152]{2,1,0:T(8,128)(2,1)S(1)} %collective-permute-done.15.refs_16_), channel_id=1, source_target_pairs={{0,1},{1,0},{2,3},{3,2},{4,5},{5,4},{6,7},{7,6},{8,9},{9,8},{10,11... | collective-permute-start | bytes 442376 | tf_op jit(solution)/shard_map/ppermute | solution.py:559
  35.1 7.6 %collective-permute-start.12 = (bf16[4,4,32,256]{3,2,1,0:T(8,128)(2,1)S(1)}, bf16[4,4,32,256]{3,2,1,0:T(8,128)(2,1)S(1)}, u32[]{:S(2)}, u32[]{:S(2)}) collective-permute-start(bf16[4,4,32,256]{3,2,1,0:T(8,128)(2,1)S(1)} %collective-permute-done.8.refs_8_), channel_id=1, source_target_pairs={{0,1},{1,0},{2,3},{3,2},{4,5},{5,4},{6,7},{7,6},{8,9},{9,8},{10,11... | collective-permute-start | bytes 786440 | tf_op jit(solution)/shard_map/ppermute | solution.py:559
  40.4 2.3 %collective-permute-start.13 = (bf16[4,4,32,256]{3,2,1,0:T(8,128)(2,1)S(1)}, bf16[4,4,32,256]{3,2,1,0:T(8,128)(2,1)S(1)}, u32[]{:S(2)}, u32[]{:S(2)}) collective-permute-start(bf16[4,4,32,256]{3,2,1,0:T(8,128)(2,1)S(1)} %collective-permute-done.9.refs_9_), channel_id=1, source_target_pairs={{0,1},{1,0},{2,3},{3,2},{4,5},{5,4},{6,7},{7,6},{8,9},{9,8},{10,11... | collective-permute-start | bytes 786440 | tf_op jit(solution)/shard_map/ppermute | solution.py:559
  40.5 2.3 %collective-permute-start.14 = (bf16[4,4,32,256]{3,2,1,0:T(8,128)(2,1)S(1)}, bf16[4,4,32,256]{3,2,1,0:T(8,128)(2,1)S(1)}, u32[]{:S(2)}, u32[]{:S(2)}) collective-permute-start(bf16[4,4,32,256]{3,2,1,0:T(8,128)(2,1)S(1)} %collective-permute-done.10.refs_10_), channel_id=1, source_target_pairs={{0,1},{1,0},{2,3},{3,2},{4,5},{5,4},{6,7},{7,6},{8,9},{9,8},{10,11... | collective-permute-start | bytes 786440 | tf_op jit(solution)/shard_map/ppermute | solution.py:559
  41.0 1.6 %collective-permute-start.20 = (bf16[4,16,1152]{2,1,0:T(8,128)(2,1)S(1)}, bf16[4,16,1152]{2,1,0:T(8,128)(2,1)S(1)}, u32[]{:S(2)}, u32[]{:S(2)}) collective-permute-start(bf16[4,16,1152]{2,1,0:T(8,128)(2,1)S(1)} %collective-permute-done.16.refs_17_), channel_id=1, source_target_pairs={{0,1},{1,0},{2,3},{3,2},{4,5},{5,4},{6,7},{7,6},{8,9},{9,8},{10,11... | collective-permute-start | bytes 442376 | tf_op jit(solution)/shard_map/ppermute | solution.py:559
  41.0 1.7 %collective-permute-start.21 = (bf16[4,16,1152]{2,1,0:T(8,128)(2,1)S(1)}, bf16[4,16,1152]{2,1,0:T(8,128)(2,1)S(1)}, u32[]{:S(2)}, u32[]{:S(2)}) collective-permute-start(bf16[4,16,1152]{2,1,0:T(8,128)(2,1)S(1)} %collective-permute-done.17.refs_18_), channel_id=1, source_target_pairs={{0,1},{1,0},{2,3},{3,2},{4,5},{5,4},{6,7},{7,6},{8,9},{9,8},{10,11... | collective-permute-start | bytes 442376 | tf_op jit(solution)/shard_map/ppermute | solution.py:559
  42.8 1.0 copy-start.5
  101.6 18.1 %collective-permute-start.22 = (bf16[512,3072]{1,0:T(8,128)(2,1)}, bf16[512,3072]{1,0:T(8,128)(2,1)S(1)}, u32[]{:S(2)}, u32[]{:S(2)}) collective-permute-start(bf16[512,3072]{1,0:T(8,128)(2,1)} %get-tuple-element.59.own_ref), channel_id=1, source_target_pairs={{0,1},{1,0},{2,3},{3,2},{4,5},{5,4},{6,7},{7,6},{8,9},{9,8},{10,11... | collective-permute-start | bytes 9437192 | tf_op jit(solution)/shard_map/ppermute | solution.py:559
  101.8 8.1 %collective-permute-start.23 = (bf16[16,4,32,256]{3,2,1,0:T(8,128)(2,1)}, bf16[16,4,32,256]{3,2,1,0:T(8,128)(2,1)S(1)}, u32[]{:S(2)}, u32[]{:S(2)}) collective-permute-start(bf16[16,4,32,256]{3,2,1,0:T(8,128)(2,1)} %get-tuple-element.62), channel_id=1, source_target_pairs={{0,1},{1,0},{2,3},{3,2},{4,5},{5,4},{6,7},{7,6},{8,9},{9,8},{10,11... | collective-permute-start | bytes 3145736 | tf_op jit(solution)/shard_map/ppermute | solution.py:559
  102.2 6.8 %collective-permute-start.24 = (bf16[16,16,1152]{2,1,0:T(8,128)(2,1)S(1)}, bf16[16,16,1152]{2,1,0:T(8,128)(2,1)S(1)}, u32[]{:S(2)}, u32[]{:S(2)}) collective-permute-start(bf16[16,16,1152]{2,1,0:T(8,128)(2,1)S(1)} %get-tuple-element.64), channel_id=1, source_target_pairs={{0,1},{1,0},{2,3},{3,2},{4,5},{5,4},{6,7},{7,6},{8,9},{9,8},{10,11... | collective-permute-start | bytes 1769480 | tf_op jit(solution)/shard_map/ppermute | solution.py:559
  109.9 1.2 copy-start
  111.4 6.0 %collective-permute-start.28 = (bf16[4,16,1152]{2,1,0:T(8,128)(2,1)S(1)}, bf16[4,16,1152]{2,1,0:T(8,128)(2,1)S(1)}, u32[]{:S(2)}, u32[]{:S(2)}) collective-permute-start(bf16[4,16,1152]{2,1,0:T(8,128)(2,1)S(1)} %get-tuple-element.70), channel_id=1, source_target_pairs={{0,8},{2,10},{4,12},{6,14},{8,0},{10,2},{12,4},{14,6},{16,24},{18,... | collective-permute-start | bytes 442376 | tf_op jit(solution)/shard_map/ppermute | solution.py:555
  111.8 20.7 %collective-permute-start.25 = (bf16[4,4,32,256]{3,2,1,0:T(8,128)(2,1)S(1)}, bf16[4,4,32,256]{3,2,1,0:T(8,128)(2,1)S(1)}, u32[]{:S(2)}, u32[]{:S(2)}) collective-permute-start(bf16[4,4,32,256]{3,2,1,0:T(8,128)(2,1)S(1)} %get-tuple-element.65.token_ref), channel_id=1, source_target_pairs={{0,2},{2,0},{4,6},{6,4},{8,10},{10,8},{12,14},{14,12},{16,18},{18,... | collective-permute-start | bytes 786440 | tf_op jit(solution)/shard_map/ppermute | solution.py:555
  113.3 19.2 %collective-permute-start.26 = (bf16[4,4,32,256]{3,2,1,0:T(8,128)(2,1)S(1)}, bf16[4,4,32,256]{3,2,1,0:T(8,128)(2,1)S(1)}, u32[]{:S(2)}, u32[]{:S(2)}) collective-permute-start(bf16[4,4,32,256]{3,2,1,0:T(8,128)(2,1)S(1)} %get-tuple-element.68), channel_id=1, source_target_pairs={{0,4},{2,6},{4,0},{6,2},{8,12},{10,14},{12,8},{14,10},{16,20},{18,... | collective-permute-start | bytes 786440 | tf_op jit(solution)/shard_map/ppermute | solution.py:555
  113.8 18.8 %collective-permute-start.27 = (bf16[4,4,32,256]{3,2,1,0:T(8,128)(2,1)S(1)}, bf16[4,4,32,256]{3,2,1,0:T(8,128)(2,1)S(1)}, u32[]{:S(2)}, u32[]{:S(2)}) collective-permute-start(bf16[4,4,32,256]{3,2,1,0:T(8,128)(2,1)S(1)} %get-tuple-element.69), channel_id=1, source_target_pairs={{0,6},{2,4},{4,2},{6,0},{8,14},{10,12},{12,10},{14,8},{16,22},{18,... | collective-permute-start | bytes 786440 | tf_op jit(solution)/shard_map/ppermute | solution.py:555
  117.4 15.2 %collective-permute-start.29 = (bf16[4,16,1152]{2,1,0:T(8,128)(2,1)S(1)}, bf16[4,16,1152]{2,1,0:T(8,128)(2,1)S(1)}, u32[]{:S(2)}, u32[]{:S(2)}) collective-permute-start(bf16[4,16,1152]{2,1,0:T(8,128)(2,1)S(1)} %get-tuple-element.71), channel_id=1, source_target_pairs={{0,16},{2,18},{4,20},{6,22},{8,24},{10,26},{12,28},{14,30},{16,0},... | collective-permute-start | bytes 442376 | tf_op jit(solution)/shard_map/ppermute | solution.py:555
  119.8 1.6 %copy-start.24 = (bf16[512,3072]{1,0:T(8,128)(2,1)}, bf16[512,3072]{1,0:T(8,128)(2,1)S(1)}, u32[]{:S(2)}) copy-start(bf16[512,3072]{1,0:T(8,128)(2,1)S(1)} %collective-permute-done.22.far_ref) | copy-start | bytes 9437188
  119.8 12.8 %collective-permute-start.30 = (bf16[4,16,1152]{2,1,0:T(8,128)(2,1)S(1)}, bf16[4,16,1152]{2,1,0:T(8,128)(2,1)S(1)}, u32[]{:S(2)}, u32[]{:S(2)}) collective-permute-start(bf16[4,16,1152]{2,1,0:T(8,128)(2,1)S(1)} %get-tuple-element.72), channel_id=1, source_target_pairs={{0,24},{2,26},{4,28},{6,30},{8,16},{10,18},{12,20},{14,22},{16,8},... | collective-permute-start | bytes 442376 | tf_op jit(solution)/shard_map/ppermute | solution.py:555
  121.4 1.9 %copy-start.4 = (bf16[512,3072]{1,0:T(8,128)(2,1)S(1)}, bf16[512,3072]{1,0:T(8,128)(2,1)}, u32[]{:S(2)}) copy-start(bf16[512,3072]{1,0:T(8,128)(2,1)} %get-tuple-element.59.own_ref) | copy-start | bytes 9437188
  123.3 9.3 %copy-start.1 = (bf16[16,4,32,256]{3,2,1,0:T(8,128)(2,1)S(1)}, bf16[16,4,32,256]{3,2,1,0:T(8,128)(2,1)}, u32[]{:S(2)}) copy-start(bf16[16,4,32,256]{3,2,1,0:T(8,128)(2,1)} %get-tuple-element.61.refs_0_) | copy-start | bytes 3145732
  134.1 6.4 %collective-permute-start.31 = (bf16[16,1152]{1,0:T(8,128)(2,1)S(1)}, bf16[16,1152]{1,0:T(8,128)(2,1)S(1)}, u32[]{:S(2)}, u32[]{:S(2)}) collective-permute-start(bf16[16,1152]{1,0:T(8,128)(2,1)S(1)} %get-tuple-element.75), channel_id=1, source_target_pairs={{0,2},{2,0},{4,6},{6,4},{8,10},{10,8},{12,14},{14,12},{16,18},{18,... | collective-permute-start | bytes 110600 | tf_op jit(solution)/shard_map/ppermute | solution.py:555
  135.6 6.5 %collective-permute-start.32 = (bf16[16,1152]{1,0:T(8,128)(2,1)S(1)}, bf16[16,1152]{1,0:T(8,128)(2,1)S(1)}, u32[]{:S(2)}, u32[]{:S(2)}) collective-permute-start(bf16[16,1152]{1,0:T(8,128)(2,1)S(1)} %get-tuple-element.76), channel_id=1, source_target_pairs={{0,4},{2,6},{4,0},{6,2},{8,12},{10,14},{12,8},{14,10},{16,20},{18,... | collective-permute-start | bytes 110600 | tf_op jit(solution)/shard_map/ppermute | solution.py:555
  136.1 6.0 %collective-permute-start.33 = (bf16[16,1152]{1,0:T(8,128)(2,1)S(1)}, bf16[16,1152]{1,0:T(8,128)(2,1)S(1)}, u32[]{:S(2)}, u32[]{:S(2)}) collective-permute-start(bf16[16,1152]{1,0:T(8,128)(2,1)S(1)} %get-tuple-element.77), channel_id=1, source_target_pairs={{0,6},{2,4},{4,2},{6,0},{8,14},{10,12},{12,10},{14,8},{16,22},{18,... | collective-permute-start | bytes 110600 | tf_op jit(solution)/shard_map/ppermute | solution.py:555
  137.6 8.0 %collective-permute-start.35 = (bf16[4,32,256]{2,1,0:T(8,128)(2,1)S(1)}, bf16[4,32,256]{2,1,0:T(8,128)(2,1)S(1)}, u32[]{:S(2)}, u32[]{:S(2)}) collective-permute-start(bf16[4,32,256]{2,1,0:T(8,128)(2,1)S(1)} %get-tuple-element.79), channel_id=1, source_target_pairs={{0,8},{2,10},{4,12},{6,14},{8,0},{10,2},{12,4},{14,6},{16,24},{18,... | collective-permute-start | bytes 196616 | tf_op jit(solution)/shard_map/ppermute | solution.py:555
  139.3 7.3 %collective-permute-start.36 = (bf16[4,32,256]{2,1,0:T(8,128)(2,1)S(1)}, bf16[4,32,256]{2,1,0:T(8,128)(2,1)S(1)}, u32[]{:S(2)}, u32[]{:S(2)}) collective-permute-start(bf16[4,32,256]{2,1,0:T(8,128)(2,1)S(1)} %get-tuple-element.80), channel_id=1, source_target_pairs={{0,16},{2,18},{4,20},{6,22},{8,24},{10,26},{12,28},{14,30},{16,0},... | collective-permute-start | bytes 196616 | tf_op jit(solution)/shard_map/ppermute | solution.py:555
  140.5 1.6 %copy-start.11 = (bf16[16,1152]{1,0:T(8,128)(2,1)}, bf16[16,1152]{1,0:T(8,128)(2,1)S(1)}, u32[]{:S(2)}) copy-start(bf16[16,1152]{1,0:T(8,128)(2,1)S(1)} %collective-permute-done.31.refs_1_.refs_5_) | copy-start | bytes 110596
  140.5 6.1 %collective-permute-start.37 = (bf16[4,32,256]{2,1,0:T(8,128)(2,1)S(1)}, bf16[4,32,256]{2,1,0:T(8,128)(2,1)S(1)}, u32[]{:S(2)}, u32[]{:S(2)}) collective-permute-start(bf16[4,32,256]{2,1,0:T(8,128)(2,1)S(1)} %get-tuple-element.81), channel_id=1, source_target_pairs={{0,24},{2,26},{4,28},{6,30},{8,16},{10,18},{12,20},{14,22},{16,8},... | collective-permute-start | bytes 196616 | tf_op jit(solution)/shard_map/ppermute | solution.py:555
  144.1 1.4 collective-permute-start.34
  145.5 1.1 copy-start.23
  145.5 1.1 copy-start.17
  (15 other events, 10.2 us)

commit v3 on v2

v3 whole, which is shorter than its diff:
```python
import functools

import jax
import jax.numpy as jnp
from jax import lax
from jax.experimental import pallas as pl
from jax.experimental.pallas import tpu as pltpu
from jax.sharding import PartitionSpec as P

F32 = jnp.float32
BF = jnp.bfloat16
NT = (((1,), (1,)), ((), ()))
D, FH, EO, TW, NE = 512, 256, 128, 64, 8
HALF = NE // 2
EMB, DENSE = 416, 13
XR = 448
QA = HALF * FH
QS = QA + HALF * EO
UC = QS + 128
B1, GA = 72, 80
FG = NE * FH + 128
TILE = 512


def mm(a, b):
    return jnp.dot(a, b, preferred_element_type=F32)


def mm_nt(a, b):
    return lax.dot_general(a, b, NT, preferred_element_type=F32)


def act_pair(half):
    t = jnp.tanh(half)
    q = 1.0 + t
    m = half * q
    return m, q + m * (1.0 - t)


def swap_halves(a, flag):
    return jnp.where(flag, jnp.concatenate([a[HALF:NE], a[0:HALF]], axis=0), a)


def lane_fold(a):
    total = a[:, 0:128]
    for c in range(1, a.shape[1] // 128):
        total = total + a[:, 128 * c : 128 * c + 128]
    return total


def chunk_at(n, chunks, flag):
    if chunks == 1 or n // 4 in (0, 3):
        return n
    return n + 4 * flag if n // 4 == 1 else n - 4 * flag


def main_kernel(pieces, chunks, tab_ref, *refs):
    emb_ref, dense_ref, lab_ref, far_lab_ref, row_ref, vec_ref, far_vec_ref = refs[:7]
    u_refs = (refs[7 : 7 + pieces], refs[7 + pieces : 7 + 2 * pieces])
    hg_ref, wat_s, *du_refs = refs[7 + 2 * pieces : 11 + 2 * pieces]
    (
        x_s, hid_s, mid_s, sl1_s, out_s, sl2_s, sg_s, fg_s, mix_s,
        w1_s, w1t_s, ga_s, w2t_s, w2_s, b1_s, b2_s, gb_s, tt_s, tw_s, tcol_s, q_s,
        dwa_s, dw1_s, dw2_s, dtw_s, dcol_s, dlog_s, dsm_s, u_s, sem,
    ) = refs[11 + 2 * pieces :]
    n = emb_ref.shape[1]
    fs, osz, ds = FH // chunks, EO // chunks, D // chunks
    step = pl.program_id(0)
    core = tab_ref[0]
    second_core = core == 1

    @pl.when(step == 0)
    def _():
        copies = [[], []]
        for side in range(2):
            at = 0
            for j, ref in enumerate(u_refs[side]):
                copies[side].append(pltpu.make_async_copy(ref, u_s.at[side, pl.ds(at, ref.shape[0])], sem.at[pieces * side + j]))
                copies[side][-1].start()
                at += ref.shape[0]
        rows = lax.broadcasted_iota(jnp.int32, (32, n), 0)
        x_s[EMB:XR, :] = jnp.where(rows == DENSE, 1.0, 0.0).astype(BF)
        ones = jnp.where(lax.broadcasted_iota(jnp.int32, (16, n), 0) == 0, 1.0, 0.0).astype(BF)
        hid_s[D : D + 16, :] = ones
        for k in range(NE):
            mid_s[k, FH : FH + 16, :] = ones
        mix_s[2 * EO : 2 * EO + 16, :] = ones
        fg_s[NE * FH + 16 : FG, :] = jnp.zeros((FG - NE * FH - 16, n), BF)
        for ref in (dwa_s, dw1_s, dw2_s, dtw_s, dcol_s, dlog_s):
            ref[...] = jnp.zeros_like(ref)
        gates = []
        for side in range(2):
            for copy in copies[side]:
                copy.wait()
            base = HALF * FH * side
            holder = core if side == 0 else 1 - core
            for c in range(chunks):
                at = chunk_at(c, chunks, holder)
                to = pl.multiple_of(ds * at, ds)
                w1_s[pl.ds(to, ds), base : base + QA] = u_s[side, c, :, 0:QA]
                q_s[tab_ref[1 + at]] = u_s[side, c, 0:fs, QA:UC].astype(F32)
                small = u_s[side, c, 0:fs, QS:UC].astype(F32)
                ga_s[pl.ds(to, fs), :] = small
                ga_s[pl.ds(pl.multiple_of(to + fs, fs), fs), :] = pltpu.roll(small, 128 - NE, 1)
                wat_s[pl.ds(pl.multiple_of(to + holder * fs, fs), fs), :] = u_s[side, c, fs:ds, QA : QA + XR]
            for k in range(HALF):
                block = w1_s[:, base + FH * k : base + FH * k + FH]
                w1t_s[base + FH * k : base + FH * k + FH, :] = (block.astype(F32).T * 0.5).astype(BF)
            gates.append(swap_halves(ga_s[...].T[GA : GA + NE], second_core))
            cols = HALF * EO
            w2 = q_s[:, :, 0:cols].reshape(FH, cols) * 0.5
            w2_s[:, cols * side : cols * side + cols] = w2.astype(BF)
            w2t_s[cols * side : cols * side + cols, :] = w2.T.astype(BF)
            b1_s[side] = q_s[:, :, cols : cols + 128].reshape(FH, 128) * 0.5
            last = q_s[:, 0:osz, cols : cols + 128].reshape(EO, 128)
            b2_s[side] = last * 0.5
            tower = last[:, 0:TW]
            rest = jnp.zeros_like(tower)
            both = jnp.concatenate([tower, rest] if side == 0 else [rest, tower], axis=1)
            tw_s[EO * side : EO * side + EO, :] = both.astype(BF)
            tt_s[:, EO * side : EO * side + EO] = (both.T * 0.5).astype(BF)
        gates = jnp.concatenate(gates, axis=0)
        w1t_s[NE * FH : NE * FH + 16, :] = gates.astype(BF)
        pad = jnp.concatenate([gates, jnp.zeros((112, D), F32)], axis=0)
        w1_s[:, NE * FH : FG] = pad.T.astype(BF)
        vecs = [jnp.concatenate([r[...].astype(F32), jnp.zeros((112, 128), F32)], axis=0).T for r in (vec_ref, far_vec_ref)]
        gb_s[...] = jnp.concatenate([swap_halves(v[0:NE, 0:1], second_core) for v in vecs], axis=0)
        b1 = jnp.concatenate([v[0:TW, 1:2] for v in vecs], axis=0)
        head = jnp.concatenate([v[0:TW, 2:3] for v in vecs], axis=0)
        last = jnp.concatenate([v[0:1, 3:4] for v in vecs] * TW, axis=0)
        tcol_s[...] = jnp.concatenate([b1 * 0.5, head, head * 0.5, last], axis=1)

    row_weight = row_ref[...]
    labels = (lab_ref[...].astype(F32), far_lab_ref[...].astype(F32))
    x_s[0:EMB, :] = emb_ref[...]
    x_s[EMB : EMB + DENSE, :] = dense_ref[...]
    x = x_s[...]
    hid = mm(wat_s[...], x).astype(BF)
    hid_s[0:D, :] = hid
    logits = mm(w1t_s[NE * FH : NE * FH + 16, :], hid) + gb_s[...]
    probs = []
    for t in range(2):
        lt = logits[NE * t : NE * t + NE]
        e = jnp.exp(lt - jnp.max(lt, axis=0, keepdims=True))
        probs.append(e / jnp.sum(e, axis=0, keepdims=True))
    mix = [None, None]
    pend = None
    nxt = mm(w1t_s[0:FH, :], hid)
    for k in range(NE + 1):
        h = nxt
        if k < NE - 1:
            nxt = mm(w1t_s[FH * (k + 1) : FH * (k + 2), :], hid)
        if k < NE:
            m, s = act_pair(h + b1_s[k // HALF, :, B1 + k % HALF : B1 + k % HALF + 1])
            mb = m.astype(BF)
            mid_s[k, 0:FH, :] = mb
            sl1_s[FH * k : FH * k + FH, :] = s.astype(BF)
            h2 = mm(w2t_s[EO * k : EO * k + EO, :], mb)
        if pend is not None:
            j = k - 1
            o, s = act_pair(pend + b2_s[j // HALF, :, TW + j % HALF : TW + j % HALF + 1])
            out_s[EO * j : EO * j + EO, :] = o.astype(out_s.dtype)
            sl2_s[EO * j : EO * j + EO, :] = s.astype(sl2_s.dtype)
            for t in range(2):
                term = probs[t][j : j + 1, :] * o
                mix[t] = term if j == 0 else mix[t] + term
        pend = h2
    mix_s[0:EO, :] = mix[0].astype(BF)
    mix_s[EO : 2 * EO, :] = mix[1].astype(BF)
    act, slope = act_pair(mm(tt_s[...], mix_s[0 : 2 * EO, :]) + tcol_s[:, 0:1])
    weighted = act * tcol_s[:, 1:2]
    lgos = []
    for t in range(2):
        logit = jnp.sum(weighted[TW * t : TW * t + TW], axis=0, keepdims=True) + tcol_s[t : t + 1, 3:4]
        lgos.append(row_weight * (0.5 * jnp.tanh(0.5 * logit) + 0.5 - labels[t]))
    lgo = jnp.concatenate([jnp.broadcast_to(lgos[t], (TW, n)) for t in range(2)], axis=0)
    dcol_s[...] += lane_fold(lgo * act)
    dlog_s[...] += lane_fold(jnp.concatenate([jnp.broadcast_to(lgos[t], (8, n)) for t in range(2)], axis=0))
    tg = (lgo * (tcol_s[:, 2:3] * slope)).astype(BF)
    dtw_s[...] += mm_nt(mix_s[...], tg)
    mgh = mm(tw_s[...], tg) * 0.5
    pgs = [[], []]
    mgs = [None] * NE
    for k in range(NE + 2):
        if k < NE:
            o = out_s[EO * k : EO * k + EO, :].astype(F32)
            og = None
            for t in range(2):
                mg = mgh[EO * t : EO * t + EO]
                pgs[t].append(jnp.sum(o * mg, axis=0, keepdims=True))
                term = probs[t][k : k + 1, :] * mg
                og = term if og is None else og + term
            sg = (og * sl2_s[EO * k : EO * k + EO, :].astype(F32)).astype(BF)
            sg_s[EO * k : EO * k + EO, :] = sg
            mgs[k] = mm(w2_s[:, EO * k : EO * k + EO], sg)
        if 1 <= k < NE + 1:
            j = k - 1
            dw2_s[:, EO * j : EO * j + EO] += mm_nt(mid_s[j], sg_s[EO * j : EO * j + EO, :])
            fg = (mgs[j] * sl1_s[FH * j : FH * j + FH, :].astype(F32)).astype(BF)
            fg_s[FH * j : FH * j + FH, :] = fg
        if k >= 2:
            j = k - 2
            dw1_s[:, FH * j : FH * j + FH] += mm_nt(hid_s[...], fg_s[FH * j : FH * j + FH, :])
    lgs = []
    for t in range(2):
        pg = jnp.concatenate(pgs[t], axis=0)
        lgs.append(2.0 * probs[t] * (pg - jnp.sum(probs[t] * pg, axis=0, keepdims=True)))
    fg_s[NE * FH : NE * FH + 16, :] = jnp.concatenate(lgs, axis=0).astype(BF)
    dw1_s[:, NE * FH : FG] += mm_nt(hid_s[...], fg_s[NE * FH : FG, :])
    hg = mm(w1_s[...], fg_s[...]).astype(BF)
    hg_ref[...] = hg
    dwa_s[...] += mm_nt(hg, x)

    @pl.when(step == pl.num_programs(0) - 1)
    def _():
        gate = dw1_s[:, NE * FH : FG].T
        dlog = jnp.sum(dlog_s[...], axis=1, keepdims=True)
        dcol = jnp.sum(dcol_s[...].T, axis=0, keepdims=True)
        for side in range(2):
            own_gate = swap_halves(gate[NE * side : NE * side + NE], second_core)
            ga_s[...] = jnp.concatenate([own_gate[:, 0:D], jnp.zeros((120, D), F32)], axis=0).T
            b1 = [dw1_s[D : D + 1, FH * k : FH * k + FH] for k in range(HALF * side, HALF * side + HALF)]
            b1 = jnp.concatenate(b1 + [jnp.zeros((124, FH), F32)], axis=0).T
            b2 = [dw2_s[FH : FH + 1, EO * k : EO * k + EO] for k in range(HALF * side, HALF * side + HALF)]
            b2 = jnp.concatenate(b2 + [jnp.zeros((60, EO), F32)], axis=0).T
            tower = dtw_s[EO * side : EO * side + EO, TW * side : TW * side + TW]
            tower = jnp.concatenate([tower, b2], axis=1)
            lanes = slice(TW * side, TW * side + TW)
            blank = jnp.zeros((1, TW), F32)
            lines = [jnp.concatenate([a, blank], axis=1) for a in (dtw_s[2 * EO : 2 * EO + 1, lanes], dcol[:, lanes])]
            gate_b = jnp.sum(jnp.where(lax.broadcasted_iota(jnp.int32, (NE, D + 16), 1) == D, own_gate, 0.0), axis=1, keepdims=True)
            small = jnp.concatenate([gate_b, dlog[8 * side : 8 * side + 8]], axis=0)
            small = jnp.concatenate([jnp.broadcast_to(small, (16, 128)), jnp.zeros((112, 128), F32)], axis=0).T[0:1]
            tail = jnp.concatenate(lines + [small, jnp.zeros((fs - osz - 3, 128), F32)], axis=0)
            b1 = pltpu.roll(b1, B1, 1)
            for c in range(chunks):
                dsm_s[fs * c : fs * c + fs, :] = b1[fs * c : fs * c + fs] + jnp.concatenate([tower[osz * c : osz * c + osz], tail], axis=0)
            ref = du_refs[side]
            holder = core if side == 0 else 1 - core
            cols = HALF * EO
            for c in range(chunks):
                at = chunk_at(c, chunks, holder)
                to = pl.multiple_of(ds * at, ds)
                where = pl.ds(pl.multiple_of(tab_ref[1 + at] * fs, fs), fs)
                ref[c, :, 0:QA] = dw1_s[pl.ds(to, ds), QA * side : QA * side + QA].astype(BF)
                ref[c, 0:fs, QA:QS] = dw2_s[where, cols * side : cols * side + cols].astype(BF)
                low = pltpu.roll(ga_s[pl.ds(to, fs), :], GA, 1)
                high = pltpu.roll(ga_s[pl.ds(pl.multiple_of(to + fs, fs), fs), :], GA + NE, 1)
                ref[c, 0:fs, QS:UC] = (dsm_s[where, :] + low + high).astype(BF)
                lower = dwa_s[pl.ds(pl.multiple_of(to + holder * fs, fs), fs), :]
                ref[c, fs:ds, QA:UC] = jnp.concatenate([lower, jnp.zeros((fs, UC - QA - XR), F32)], axis=1).astype(BF)


def weight_kernel(batch_rows, tab_ref, sizes_ref, token_ref, out_ref, start_s, end_s, inv_s):
    users = sizes_ref.shape[1]
    counts = sizes_ref[...].astype(F32)
    turned = jnp.concatenate([counts, jnp.zeros((128 - counts.shape[0], users), F32)], axis=0).T
    upto = lax.broadcasted_iota(jnp.int32, (users, users), 1) <= lax.broadcasted_iota(jnp.int32, (users, users), 0)
    ends = mm(jnp.where(upto, 1.0, 0.0).astype(BF), turned.astype(BF))
    starts = ends - turned
    for b in range(counts.shape[0]):
        end_s[b] = jnp.broadcast_to(ends[:, b : b + 1], (users, 128))
        start_s[b] = jnp.broadcast_to(starts[:, b : b + 1], (users, 128))
        inv_s[b] = jnp.broadcast_to(1.0 / turned[:, b : b + 1], (users, 128))
    steps = out_ref.shape[1] // TILE
    for step in range(steps):
        at_step = tab_ref[0] * steps + step
        batch = at_step // (batch_rows // TILE)
        first_row = (at_step % (batch_rows // TILE) * TILE).astype(F32)
        for c in range(TILE // 128):
            row_at = first_row + (lax.broadcasted_iota(jnp.int32, (1, 128), 1) + 128 * c).astype(F32)
            inside = (row_at >= start_s[batch]) & (row_at < end_s[batch])
            at = TILE * step + 128 * c
            out_ref[:, at : at + 128] = jnp.sum(jnp.where(inside, inv_s[batch], 0.0), axis=0, keepdims=True)


def weight_call(table, sizes, rows, token):
    batches, users = sizes.shape
    return pl.pallas_call(
        functools.partial(weight_kernel, rows // batches),
        in_specs=[whole(pltpu.SMEM), whole(), whole(pl.ANY)],
        out_specs=whole(),
        out_shape=jax.ShapeDtypeStruct((1, rows // 2), F32),
        scratch_shapes=[pltpu.VMEM((batches, users, 128), F32)] * 3,
        cost_estimate=pl.CostEstimate(flops=3_000_000_000, bytes_accessed=1_000_000, transcendentals=0),
        name="row_weights",
    )(table, sizes, token)


def const2(i, c):
    return (0, 0)


def main_call(table, embt, denset, labels, far_labels, row_weights, vec, far_vec, own_u, far_u):
    rows = embt.shape[1]
    half = rows // 2
    steps = half // TILE
    pieces = len(own_u)
    chunks = sum(a.shape[0] for a in own_u)
    fs, ds = FH // chunks, D // chunks

    def own(i, c):
        return (0, c[0] * steps + i)

    grads = [(chunks, ds, UC)] * 2
    spec = pltpu.PrefetchScalarGridSpec(
        num_scalar_prefetch=1,
        grid=(steps,),
        in_specs=[
            pl.BlockSpec((EMB, TILE), own),
            pl.BlockSpec((DENSE, TILE), own),
            pl.BlockSpec((1, TILE), own),
            pl.BlockSpec((1, TILE), own),
            pl.BlockSpec((1, TILE), lambda i, c: (0, i)),
            whole(),
            whole(),
        ]
        + [whole(pl.ANY) for _ in (*own_u, *far_u)],
        out_specs=[pl.BlockSpec((D, TILE), lambda i, c: (0, i))] + [whole()] * 3,
        scratch_shapes=[
            pltpu.VMEM((XR, TILE), BF),
            pltpu.VMEM((D + 16, TILE), BF),
            pltpu.VMEM((NE, FH + 16, TILE), BF),
            pltpu.VMEM((NE * FH, TILE), BF),
            pltpu.VMEM((NE * EO, TILE), F32),
            pltpu.VMEM((NE * EO, TILE), F32),
            pltpu.VMEM((NE * EO, TILE), BF),
            pltpu.VMEM((FG, TILE), BF),
            pltpu.VMEM((2 * EO + 16, TILE), BF),
            pltpu.VMEM((D, FG), BF),
            pltpu.VMEM((NE * FH + 16, D), BF),
            pltpu.VMEM((D, 128), F32),
            pltpu.VMEM((NE * EO, FH), BF),
            pltpu.VMEM((FH, NE * EO), BF),
            pltpu.VMEM((2, FH, 128), F32),
            pltpu.VMEM((2, EO, 128), F32),
            pltpu.VMEM((16, 1), F32),
            pltpu.VMEM((2 * TW, 2 * EO), BF),
            pltpu.VMEM((2 * EO, 2 * TW), BF),
            pltpu.VMEM((2 * TW, 4), F32),
            pltpu.VMEM((chunks, fs, UC - QA), F32),
            pltpu.VMEM((D, XR), F32),
            pltpu.VMEM((D + 16, FG), F32),
            pltpu.VMEM((FH + 16, NE * EO), F32),
            pltpu.VMEM((2 * EO + 16, 2 * TW), F32),
            pltpu.VMEM((2 * TW, 128), F32),
            pltpu.VMEM((16, 128), F32),
            pltpu.VMEM((FH, 128), F32),
            pltpu.VMEM((2, chunks, ds, UC), BF),
            pltpu.SemaphoreType.DMA((2 * pieces,)),
        ],
    )
    return pl.pallas_call(
        functools.partial(main_kernel, pieces, chunks),
        grid_spec=spec,
        out_shape=[jax.ShapeDtypeStruct((D, half), BF), jax.ShapeDtypeStruct((D, XR), BF)]
        + [jax.ShapeDtypeStruct(a, BF) for a in grads],
        compiler_params=pltpu.CompilerParams(vmem_limit_bytes=48 * 1024 * 1024),
        cost_estimate=pl.CostEstimate(flops=50_000_000_000, bytes_accessed=24_000_000, transcendentals=0),
        name="experts",
    )(table, embt, denset, labels, far_labels, row_weights, vec, far_vec, *own_u, *far_u)


def input_kernel(tab_ref, hg_ref, wat_ref, *refs):
    eg_ref, dg_ref, done_ref, wa_s = refs[-4:]

    @pl.when(pl.program_id(0) == 0)
    def _():
        wa_s[...] = wat_ref[...].astype(F32).T.astype(BF)
        done_ref[...] = jnp.zeros_like(done_ref)

    eg = mm(wa_s[...], hg_ref[...])
    eg_ref[...] = eg[0:EMB]
    dg_ref[...] = eg[EMB : EMB + DENSE]


def input_call(table, hg, wat, token, other, name):
    half = hg.shape[1]
    tile = 2 * TILE
    steps = half // tile

    def place(i, c):
        return (0, (c[0] if other is None else 1 - c[0]) * steps + i)

    extra = [token] + (list(other) if other is not None else [])
    spec = pltpu.PrefetchScalarGridSpec(
        num_scalar_prefetch=1,
        grid=(steps,),
        in_specs=[pl.BlockSpec((D, tile), lambda i, c: (0, i)), pl.BlockSpec((D, XR), const2, pipeline_mode=pl.Buffered(1))]
        + [whole(pl.ANY) for _ in extra],
        out_specs=[pl.BlockSpec((EMB, tile), place), pl.BlockSpec((DENSE, tile), place), pl.BlockSpec((8, 128), const2)],
        scratch_shapes=[pltpu.VMEM((XR, D), BF)],
    )
    return pl.pallas_call(
        input_kernel,
        grid_spec=spec,
        out_shape=[jax.ShapeDtypeStruct((EMB, 2 * half), F32), jax.ShapeDtypeStruct((DENSE, 2 * half), F32), jax.ShapeDtypeStruct((8, 128), F32)],
        input_output_aliases={} if other is None else {4: 0, 5: 1},
        compiler_params=pltpu.CompilerParams(vmem_limit_bytes=32 * 1024 * 1024),
        cost_estimate=pl.CostEstimate(flops=4_000_000_000, bytes_accessed=9_000_000, transcendentals=0),
        name=name,
    )(table, hg, wat, *extra)


def widen(a):
    return jnp.concatenate([a.astype(F32), jnp.zeros((a.shape[0], 128 - a.shape[1]), F32)], axis=1)


def square(rows):
    count = sum(a.shape[0] for a in rows)
    return jnp.concatenate(rows + [jnp.zeros((128 - count, 128), F32)], axis=0)


def pack_vec(gb_ref, t1_ref, t2_ref, t3_ref):
    return jnp.concatenate([widen(r[...]) for r in (gb_ref, t1_ref, t2_ref, t3_ref)] + [jnp.zeros((12, 128), F32)], axis=0).astype(BF)


def pack_kernel(core_ref, emb_ref, dense_ref, bias_ref, w1_ref, w2_ref, b1_ref, b2_ref, gate_ref, tower_ref, *refs):
    u_ref, vec_ref = refs[4:]
    vec_ref[...] = pack_vec(*refs[:4])
    fs = u_ref.shape[0] // 2
    turned = square([widen(r[...]) for r in (b1_ref, b2_ref, gate_ref, dense_ref, bias_ref)]).T
    lane = lax.broadcasted_iota(jnp.int32, (fs, 128), 1)
    low, high = turned[0:fs], turned[fs : 2 * fs]
    small = jnp.concatenate([widen(tower_ref[...]), jnp.zeros((fs - tower_ref.shape[0], 128), F32)], axis=0)
    small += jnp.where((lane >= TW) & (lane < TW + HALF), pltpu.roll(low, TW - HALF, 1), 0.0)
    small += jnp.where(((lane >= B1) & (lane < B1 + HALF)) | ((lane >= GA) & (lane < GA + NE)), pltpu.roll(low, B1, 1), 0.0)
    small += jnp.where((lane >= GA + NE) & (lane < GA + 2 * NE), pltpu.roll(high, GA, 1), 0.0)
    for k in range(HALF):
        u_ref[:, FH * k : FH * k + FH] = w1_ref[k]
        u_ref[0:fs, QA + EO * k : QA + EO * k + EO] = w2_ref[k]
    u_ref[0:fs, QS:UC] = small.astype(BF)
    second_core = core_ref[0] == 1
    lanes = lax.broadcasted_iota(jnp.int32, (2 * fs, 128), 1)
    last = widen(emb_ref[:, 384:EMB]) + jnp.where((lanes >= 32) & (lanes < 33 + DENSE), pltpu.roll(turned[0 : 2 * fs], 16, 1), 0.0)
    for c in range(3):
        block = emb_ref[:, 128 * c : 128 * c + 128]
        u_ref[fs:, QA + 128 * c : QA + 128 * c + 128] = jnp.where(second_core, block[fs:], block[0:fs])
    u_ref[fs:, QA + 384 : QA + 512] = jnp.where(second_core, last[fs:], last[0:fs]).astype(BF)
    u_ref[fs:, QA + 512 : UC] = jnp.zeros((fs, UC - QA - 512), BF)


def whole(memory=pltpu.VMEM):
    return pl.BlockSpec(memory_space=memory)


def pack_call(core, *parts):
    ds = parts[3].shape[1]
    return pl.pallas_call(
        pack_kernel,
        in_specs=[whole(pltpu.SMEM)] + [whole() for _ in parts],
        out_specs=[whole(), whole()],
        out_shape=[jax.ShapeDtypeStruct((ds, UC), BF), jax.ShapeDtypeStruct((16, 128), BF)],
        name="pack",
    )(core, *parts)


def sum_kernel(groups, count, *refs):
    ins, outs = refs[:count], refs[-len(groups) :]
    for group, out in zip(groups, outs):
        total = None
        for number, at in group:
            term = ins[number][at].astype(F32)
            total = term if total is None else total + term
        out[...] = total.astype(out.dtype)


def sum_call(name, arrays, groups, shapes, token=None, through=None):
    extra = [a for a in (token, through) if a is not None]
    lead = [] if through is None else [through]
    return pl.pallas_call(
        functools.partial(sum_kernel, groups, len(arrays)),
        in_specs=[whole() for _ in arrays] + [whole(pl.ANY) for _ in extra],
        out_specs=[whole(pl.ANY) for _ in lead] + [whole() for _ in shapes],
        out_shape=[jax.ShapeDtypeStruct(a.shape, a.dtype) for a in lead] + [jax.ShapeDtypeStruct(a, BF) for a in shapes],
        input_output_aliases={len(arrays) + len(extra) - 1: 0} if lead else {},
        compiler_params=pltpu.CompilerParams(vmem_limit_bytes=32 * 1024 * 1024),
        name=name,
    )(*arrays, *extra)


def finish_kernel(scale, core_ref, token_ref, far_ref, *refs):
    total = sum(r[...].astype(F32) for r in refs[:4]) * scale
    ds = total.shape[0]
    fs = ds // 2
    own_part, far_part = total[fs:, QA : QA + XR], far_ref[...] * scale
    second_core = core_ref[0] == 1
    ta = jnp.concatenate([jnp.where(second_core, far_part, own_part), jnp.where(second_core, own_part, far_part)], axis=0)
    emb_ref, dense_ref, bias_ref, w1_ref, b1_ref, w2_ref, b2_ref, gate_ref, gb_ref, tower_ref, t1_ref, t2_ref, t3_ref = refs[4:]
    osz = tower_ref.shape[0]
    for k in range(HALF):
        w1_ref[k] = total[:, FH * k : FH * k + FH]
        w2_ref[k] = total[0:fs, QA + EO * k : QA + EO * k + EO]
    small = total[0:fs, QS:UC]
    turned = square([small]).T
    b1_ref[...] = turned[B1 : B1 + HALF, 0:fs]
    b2_ref[...] = turned[TW : TW + HALF, 0:osz]
    gates = turned[GA : GA + NE] + pltpu.roll(turned[GA + NE : GA + 2 * NE], fs, 1)
    gate_ref[...] = gates[:, 0 : 2 * fs]
    tower_ref[...] = small[0:osz, 0:TW]
    t1_ref[...] = small[osz : osz + 1, 0:TW]
    t2_ref[...] = small[osz + 1 : osz + 2, 0:TW]
    gb_ref[...] = small[osz + 2 : osz + 3, 0:NE]
    t3_ref[...] = small[osz + 2 : osz + 3, NE : NE + 1]
    emb_ref[...] = ta[:, 0:EMB]
    last = square([widen(ta[:, 384:XR])]).T
    dense_ref[...] = last[32 : 32 + DENSE, 0 : 2 * fs]
    bias_ref[...] = last[32 + DENSE : 33 + DENSE, 0 : 2 * fs]


def last_kernel(*refs):
    fs = refs[4].shape[0]
    refs[4][...] = sum(r[fs:, QA : QA + XR].astype(F32) for r in refs[:4])


def last_call(arrays):
    return pl.pallas_call(
        last_kernel,
        in_specs=[whole() for _ in arrays],
        out_specs=whole(),
        out_shape=jax.ShapeDtypeStruct((arrays[0].shape[0] // 2, XR), F32),
        name="sum_last",
    )(*arrays)


def finish_call(scale, core, token, far, arrays, ds, fs, osz):
    shapes = [
        (ds, EMB), (DENSE, ds), (1, ds), (HALF, ds, FH), (HALF, fs), (HALF, fs, EO), (HALF, osz), (NE, ds), (1, NE),
        (osz, TW), (1, TW), (1, TW), (1, 1),
    ]
    return pl.pallas_call(
        functools.partial(finish_kernel, scale),
        in_specs=[whole(pltpu.SMEM), whole(pl.ANY), whole()] + [whole() for _ in arrays],
        out_specs=[whole() for _ in shapes],
        out_shape=[jax.ShapeDtypeStruct(a, F32) for a in shapes],
        name="finish",
    )(core, token, far, *arrays)


def join_kernel(token_ref, *refs):
    for j in range(4):
        refs[4][j] = refs[j][...]


def join_call(parts, token):
    return pl.pallas_call(
        join_kernel,
        in_specs=[whole(pl.ANY)] + [whole() for _ in parts],
        out_specs=whole(),
        out_shape=jax.ShapeDtypeStruct((4, *parts[0].shape), BF),
        name="join",
    )(token, *parts)


def hop(a, mask, size):
    return lax.ppermute(a, "rows", [(i, i ^ mask) for i in range(size)])


def cross(a, masks, size):
    pairs = [(2 * i + t, 2 * (i ^ masks[t]) + t) for i in range(size) for t in range(2)]
    return lax.ppermute(a, ("rows", "task"), pairs)


def partner(a):
    return lax.ppermute(a, "task", [(0, 1), (1, 0)])


def add_wide(a, b):
    return a.astype(F32) + b.astype(F32)


def pad_to(a, rows, cols):
    return jnp.pad(a, ((0, rows - a.shape[0]), (0, cols - a.shape[1])))


def body(
    emb, dense, group_sizes, labels, w_emb, w_dense, b_in, expert_w1, expert_b1, expert_w2, expert_b2,
    gate_w, gate_b, tower_w1, tower_b1, tower_w2, tower_b2,
):
    size = lax.axis_size("rows")
    core = lax.axis_index("task")
    place = lax.axis_index("rows")
    user_count = group_sizes.shape[1] * group_sizes.shape[0] * size
    ds, fs, osz = D // size, FH // size, EO // size
    fast = size == 16
    far_labels = partner(labels)
    smalls = (gate_b, tower_b1, tower_w2, tower_b2[None])

    if fast:
        one_core = core[None].astype(jnp.int32)
        gate_t = jnp.transpose(gate_w, (0, 2, 1))[0]
        shard, vec = pack_call(
            one_core, w_emb.T, w_dense, b_in[None], expert_w1, expert_w2, expert_b1, expert_b2, gate_t, tower_w1[0], *smalls
        )
        row_weights = weight_call(one_core, group_sizes, emb.shape[0], vec)
        near = join_call([shard] + [hop(shard, 4 * a, size) for a in range(1, 4)], row_weights)
        near = jnp.concatenate([near, cross(near, (1, 2), size)], axis=0)
        own_u = [near, cross(near, (2, 1), size)]
        steps = jnp.arange(16, dtype=jnp.int32)
        order = place ^ (steps % 4 * 4 + steps // 4)
    else:
        gather = functools.partial(lax.all_gather, axis_name="rows", axis=0, tiled=True)
        proj = jnp.concatenate([w_emb.T, w_dense.T, b_in[:, None], jnp.zeros((ds, 82), BF)], axis=1)
        w1_all = gather(jnp.transpose(expert_w1, (1, 0, 2)).reshape(ds, QA))
        w2_all = gather(jnp.transpose(expert_w2, (1, 0, 2)).reshape(fs, HALF * EO))
        o_all = gather(jnp.concatenate([tower_w1[0], expert_b2.T], axis=1))
        b1_all, g_all, proj_all = gather(expert_b1.T), gather(gate_w[0]), gather(proj)
        small = jnp.concatenate([pad_to(o_all, FH, B1), pad_to(b1_all, FH, GA - B1), g_all[0:FH], g_all[FH:], jnp.zeros((FH, 32), BF)], axis=1)
        part = jnp.where(core == 0, proj_all[0:FH], proj_all[FH:])
        lower = jnp.concatenate([part, jnp.zeros((FH, UC - QA - 512), BF)], axis=1)
        own_u = [jnp.concatenate([w1_all, jnp.concatenate([jnp.concatenate([w2_all, small], axis=1), lower], axis=0)], axis=1)[None]]
        order = jnp.zeros((1,), jnp.int32)
        vec = jnp.concatenate([pad_to(a, 1, 128) for a in smalls] + [jnp.zeros((12, 128), BF)], axis=0)
        row_weights = weight_call(core[None].astype(jnp.int32), group_sizes, emb.shape[0], vec)
    far_u = [partner(a) for a in own_u]
    table = jnp.concatenate([core[None].astype(jnp.int32), order])

    hg, wat, du_own, du_far = main_call(table, emb.T, dense.T, labels, far_labels, row_weights, vec, partner(vec), own_u, far_u)
    du_far = partner(du_far)
    scale = 1.0 / user_count
    if fast:
        hg, part = sum_call("sum_cores", [du_own, du_far], [[(0, slice(8, 16)), (1, slice(8, 16))]], [(8, ds, UC)], through=hg)
        got = cross(part, (2, 1), size)
        eg, dg, token = input_call(table, hg, wat, part, None, "input_own")
        far_hg = partner(hg)
        groups = [[(j, slice(4 * b, 4 * b + 4)) for j in range(3)] for b in (1, 0)]
        part, rest = sum_call("sum_first", [du_own, du_far, got], groups, [(4, ds, UC)] * 2, token)
        got = cross(part, (1, 2), size)
        eg, dg, token = input_call(table, far_hg, wat, part, (eg, dg), "input_far")
        sums = sum_call("sum_second", [rest, got], [[(0, k), (1, k)] for k in range(4)], [(ds, UC)] * 4, token)
        parts = [sums[0]] + [hop(sums[a], 4 * a, size) for a in range(1, 4)]
        far_input = partner(last_call(parts))
        out = finish_call(scale, one_core, sums[0], far_input, parts, ds, fs, osz)
        g_emb, g_dense, g_bias, g_w1, g_b1, g_w2, g_b2, g_gate, g_gb, g_tower, g_t1, g_t2, g_t3 = out
        return (
            eg.T, dg.T, g_emb.T, g_dense, g_bias[0], g_w1, g_b1, g_w2, g_b2, g_gate.T[None], g_gb, g_tower[None], g_t1, g_t2, g_t3[0],
        )
    eg, dg, token = input_call(table, hg, wat, du_far, None, "input_own")
    eg, dg, _ = input_call(table, partner(hg), wat, token, (eg, dg), "input_far")
    scatter = functools.partial(lax.psum_scatter, axis_name="rows", scatter_dimension=0, tiled=True)
    wide = add_wide(du_own[0], du_far[0])
    upper, near = wide[0:FH, QA:UC], wide[FH:, QA : QA + XR]
    far, small = partner(near), upper[:, HALF * EO :]
    ta = scatter(jnp.concatenate([jnp.where(core == 0, near, far), jnp.where(core == 0, far, near)], axis=0)) * scale
    tp = jnp.transpose((scatter(wide[:, 0:QA]) * scale).reshape(ds, HALF, FH), (1, 0, 2))
    tw2, to, tb1 = scatter(upper[:, 0 : HALF * EO]) * scale, scatter(small[0:EO, 0:B1]) * scale, scatter(small[:, B1 : B1 + HALF]) * scale
    tg = scatter(jnp.concatenate([small[:, GA : GA + NE], small[:, GA + NE : GA + 2 * NE]], axis=0)) * scale
    ts = lax.psum(small[EO : EO + 3], "rows") * scale
    return (
        eg.T,
        dg.T,
        ta[:, 0:EMB].T,
        ta[:, EMB : EMB + DENSE].T,
        ta[:, EMB + DENSE],
        tp,
        tb1.T,
        jnp.transpose(tw2.reshape(fs, HALF, EO), (1, 0, 2)),
        to[:, TW : TW + HALF].T,
        tg[None],
        ts[2:3, 0:NE],
        to[:, 0:TW][None],
        ts[0:1, 0:TW],
        ts[1:2, 0:TW],
        ts[2, NE : NE + 1],
    )


def solution(mesh):
    in_specs = (
        P("rows", None),
        P("rows", None),
        P("rows", None),
        P("task", "rows"),
        P(None, "rows"),
        P(None, "rows"),
        P("rows"),
        P("task", "rows", None),
        P("task", "rows"),
        P("task", "rows", None),
        P("task", "rows"),
        P("task", "rows", None),
        P("task", None),
        P("task", "rows", None),
        P("task", None),
        P("task", None),
        P("task"),
    )
    out_specs = (
        P("rows", None),
        P("rows", None),
        P(None, "rows"),
        P(None, "rows"),
        P("rows"),
        P("task", "rows", None),
        P("task", "rows"),
        P("task", "rows", None),
        P("task", "rows"),
        P("task", "rows", None),
        P("task", None),
        P("task", "rows", None),
        P("task", None),
        P("task", None),
        P("task"),
    )
    return jax.shard_map(body, mesh=mesh, in_specs=in_specs, out_specs=out_specs, check_vma=False)
```

time: 150 us -> 144 us (0.960)
  starting transfers between devices: 35.7 us -> 17.3 us
  waiting for transfers between devices: 29.4 us -> 42.6 us
  local copies, waits for them, and re-layouts: 12.1 us -> 4.85 us
  Pallas kernels: 70.4 us -> 75.9 us
    ppermute x0 -> x4, waiting for transfers between devices: none -> 24.8 us  [cross(): return lax.ppermute(a, ('rows', 'task'), pairs)]
    ppermute x24 -> x6, starting transfers between devices: 32.5 us -> 10.1 us  [hop(): return lax.ppermute(a, 'rows', [(i, i ^ mask) for i in range(size)])]
    unnamed x50 -> x24, local copies, waits for them, and re-layouts: 12.1 us -> 4.85 us
    ppermute x0 -> x4, starting transfers between devices: none -> 6.14 us  [cross(): return lax.ppermute(a, ('rows', 'task'), pairs)]
    ppermute x24 -> x6, waiting for transfers between devices: 17.1 us -> 11 us  [hop(): return lax.ppermute(a, 'rows', [(i, i ^ mask) for i in range(size)])]
    ppermute x14 -> x7, waiting for transfers between devices: 12.3 us -> 6.81 us  [partner(): return lax.ppermute(a, 'task', [(0, 1), (1, 0)])]
    pallas_call x3 -> x5, Pallas kernels: 64.9 us -> 70 us  [the longest x1 53.6 us: main_call(): pl.pallas_call(functools.partial(main_kernel, pieces, chunks), grid_spec=...]
    ppermute x14 -> x7, starting transfers between devices: 3.18 us -> 1.05 us  [partner(): return lax.ppermute(a, 'task', [(0, 1), (1, 0)])]
  transfers between devices with their start and end apart: 38 -> 17, of which waited for: 13 -> 10; matrix products, arithmetic and copies ran while one was open for 0% -> 0% of each run, Pallas kernels for 7% -> 10%
where the time goes in v3:
time: 144 us; the launch traced here: 143 us
  Pallas kernels  75.9 us (53%)
  waiting for transfers between devices  42.6 us (30%)
  starting transfers between devices  17.3 us (12%)
  local copies, waits for them, and re-layouts  4.85 us (3%)
  between operations  1.54 us (1%)
    pallas_call x1, Pallas kernels, main_call(): pl.pallas_call(functools.partial(main_kernel, pieces, chunks), grid_spec=...  53.6 us
    ppermute x4, waiting for transfers between devices, cross(): return lax.ppermute(a, ('rows', 'task'), pairs)  24.8 us
    pallas_call x2, Pallas kernels, input_call(): pl.pallas_call(input_kernel, grid_spec=spec, out_shape=[jax.ShapeDtypeStr...  11.1 us
    ppermute x6, waiting for transfers between devices, hop(): return lax.ppermute(a, 'rows', [(i, i ^ mask) for i in range(size)])  11 us
    ppermute x6, starting transfers between devices, hop(): return lax.ppermute(a, 'rows', [(i, i ^ mask) for i in range(size)])  10.1 us
    ppermute x7, waiting for transfers between devices, partner(): return lax.ppermute(a, 'task', [(0, 1), (1, 0)])  6.81 us
    ppermute x4, starting transfers between devices, cross(): return lax.ppermute(a, ('rows', 'task'), pairs)  6.14 us
    unnamed x24, local copies, waits for them, and re-layouts  4.85 us
  transfers between devices with their start and end apart: 17, of which 10 were waited for; matrix products, arithmetic and copies ran while one was open for 0% of the time, Pallas kernels for 10%

profile of v3, /device:TPU:0, one launch (start us, length us, event | category | flops | bytes accessed | tf_op | source)
XLA Modules:
  0.0 143.3 jit_solution(18066545896567910922)
XLA Ops:
  1.3 1.7 %pack.1 = (bf16[32,1664]{1,0:T(8,128)(2,1)}, bf16[16,128]{1,0:T(8,128)(2,1)}) custom-call(s32[1]{0:T(128)} %bitcast.core_ref.tab_ref, bf16[32,416]{1,0:T(8,128)(2,1)} %bitcast.21, bf16[13,32]{1,0:T(8,128)(2,1)} %dense_ref.1, bf16[1,32]{1,0:T(2,128)(2,1)} %bitcast.24, bf16[4,32,256]{2,1,0:T(8,128)(2,1)} %w1_ref.1, bf16[4,16,128]{2,1,0:T(8,128)(2,1)} %w2_ref.1, ...), custom_call_target="tpu_custom_call" | custom-call | tf_op jit(solution)/shard_map/pack/pallas_call | solution.py:449
  3.0 5.0 %collective-permute-start.4 = (bf16[32,1664]{1,0:T(8,128)(2,1)}, bf16[32,1664]{1,0:T(8,128)(2,1)S(1)}, u32[]{:S(2)}, u32[]{:S(2)}) collective-permute-start(bf16[32,1664]{1,0:T(8,128)(2,1)} %get-tuple-element.49.refs_0_), channel_id=1, source_target_pairs={{0,24},{2,26},{4,28},{6,30},{8,16},{10,18},{12,20},{14,22},{16,8},... | collective-permute-start | bytes 319496 | tf_op jit(solution)/shard_map/ppermute | solution.py:556
  8.0 0.0 collective-permute-start.3
  8.0 0.6 collective-permute-start.2
  8.7 3.4 %row_weights.1.token_ref.refs_4_ = f32[1,3072]{1,0:T(1,128)} custom-call(s32[1]{0:T(128)} %bitcast.core_ref.tab_ref, s32[3,512]{1,0:T(4,128)} %sizes_ref.1, bf16[16,128]{1,0:T(8,128)(2,1)} %get-tuple-element.48.token_ref.refs_5_), custom_call_target="tpu_custom_call" | custom-call | flops 3000000000 | bytes 1000000 | tf_op jit(solution)/shard_map/row_weights/pallas_call | solution.py:279
  12.1 0.0 collective-permute-done.4.refs_3_
  12.1 5.1 %collective-permute-done.3.refs_2_ = bf16[32,1664]{1,0:T(8,128)(2,1)S(1)} collective-permute-done((bf16[32,1664]{1,0:T(8,128)(2,1)}, bf16[32,1664]{1,0:T(8,128)(2,1)S(1)}, u32[]{:S(2)}, u32[]{:S(2)}) %collective-permute-start.3) | collective-permute-done | bytes 106528 | tf_op jit(solution)/shard_map/ppermute | solution.py:556
  17.2 0.6 copy-done.9
  17.8 0.6 copy-done.10
  18.5 1.8 %join.1 = bf16[4,32,1664]{2,1,0:T(8,128)(2,1)} custom-call(f32[1,3072]{1,0:T(1,128)} %row_weights.1.token_ref.refs_4_, bf16[32,1664]{1,0:T(8,128)(2,1)} %get-tuple-element.49.refs_0_, bf16[32,1664]{1,0:T(8,128)(2,1)} %copy-done.10, bf16[32,1664]{1,0:T(8,128)(2,1)} %copy-done.9, bf16[32,1664]{1,0:T(8,128)(2,1)} %copy-done.8), custom_call_target="tpu_custom_call" | custom-call | tf_op jit(solution)/shard_map/join/pallas_call | solution.py:546
  20.3 1.5 %collective-permute-start.5 = (bf16[4,32,1664]{2,1,0:T(8,128)(2,1)}, bf16[4,32,1664]{2,1,0:T(8,128)(2,1)S(1)}, u32[]{:S(2)}, u32[]{:S(2)}) collective-permute-start(bf16[4,32,1664]{2,1,0:T(8,128)(2,1)} %join.1), channel_id=1, source_target_pairs={{0,2},{1,5},{2,0},{3,7},{4,6},{5,1},{6,4},{7,3},{8,10},{9,13},{10,... | collective-permute-start | bytes 1277960 | tf_op jit(solution)/shard_map/ppermute | solution.py:561
  21.8 6.8 %collective-permute-done.5 = bf16[4,32,1664]{2,1,0:T(8,128)(2,1)S(1)} collective-permute-done((bf16[4,32,1664]{2,1,0:T(8,128)(2,1)}, bf16[4,32,1664]{2,1,0:T(8,128)(2,1)S(1)}, u32[]{:S(2)}, u32[]{:S(2)}) %collective-permute-start.5) | collective-permute-done | bytes 426016 | tf_op jit(solution)/shard_map/ppermute | solution.py:561
  28.7 1.1 pad_maximum_fusion.refs_7_
  29.8 1.6 %collective-permute-start.6 = (bf16[8,32,1664]{2,1,0:T(8,128)(2,1)S(1)}, bf16[8,32,1664]{2,1,0:T(8,128)(2,1)S(1)}, u32[]{:S(2)}, u32[]{:S(2)}) collective-permute-start(bf16[8,32,1664]{2,1,0:T(8,128)(2,1)S(1)} %pad_maximum_fusion.refs_7_), channel_id=1, source_target_pairs={{0,4},{1,3},{2,6},{3,1},{4,0},{5,7},{6,2},{7,5},{8,12},{9,11},{10,... | collective-permute-start | bytes 2555912 | tf_op jit(solution)/shard_map/ppermute | solution.py:561
  31.3 0.0 collective-permute-start.7
  31.3 11.2 %collective-permute-done.6.refs_8_ = bf16[8,32,1664]{2,1,0:T(8,128)(2,1)S(1)} collective-permute-done((bf16[8,32,1664]{2,1,0:T(8,128)(2,1)S(1)}, bf16[8,32,1664]{2,1,0:T(8,128)(2,1)S(1)}, u32[]{:S(2)}, u32[]{:S(2)}) %collective-permute-start.6) | collective-permute-done | bytes 852000 | tf_op jit(solution)/shard_map/ppermute | solution.py:561
  42.5 0.5 collective-permute-start.1
  43.0 0.1 collective-permute-start
  43.1 0.1 pad_add_fusion.tab_ref
  43.2 1.7 %collective-permute-done.1.refs_6_ = bf16[16,128]{1,0:T(8,128)(2,1)S(1)} collective-permute-done((bf16[16,128]{1,0:T(8,128)(2,1)S(1)}, bf16[16,128]{1,0:T(8,128)(2,1)S(1)}, u32[]{:S(2)}, u32[]{:S(2)}) %collective-permute-start.1) | collective-permute-done | bytes 4128 | tf_op jit(solution)/shard_map/ppermute | solution.py:565
  44.9 0.0 collective-permute-done.refs_3_
  44.9 0.0 collective-permute-done.7.refs_9_
  44.9 0.7 copy-done.1
  45.7 0.9 copy-done.2
  46.6 53.6 %experts.1 = (bf16[512,3072]{1,0:T(8,128)(2,1)}, bf16[512,448]{1,0:T(8,128)(2,1)S(1)}, bf16[16,32,1664]{2,1,0:T(8,128)(2,1)S(1)}, bf16[16,32,1664]{2,1,0:T(8,128)(2,1)}) custom-call(s32[17]{0:T(128)S(1)} %pad_add_fusion.tab_ref, bf16[416,6144]{1,0:T(8,128)(2,1)} %bitcast.25, bf16[13,6144]{1,0:T(8,128)(2,1)S(1)} %bitcast.20, s32[1,6144]{1,0:T(1,128)S(1)} %copy-done.3, ...), custom_call_target="tpu_custom_call" | custom-call | flops 49999998976 | bytes 24000000 | tf_op jit(solution)/shard_map/experts/pallas_call | solution.py:353
  100.2 0.2 collective-permute-start.9
  100.5 3.6 %collective-permute-done.9.refs_1_ = bf16[16,32,1664]{2,1,0:T(8,128)(2,1)S(1)} collective-permute-done((bf16[16,32,1664]{2,1,0:T(8,128)(2,1)}, bf16[16,32,1664]{2,1,0:T(8,128)(2,1)S(1)}, u32[]{:S(2)}, u32[]{:S(2)}) %collective-permute-start.9) | collective-permute-done | bytes 1703968 | tf_op jit(solution)/shard_map/ppermute | solution.py:565
  104.1 0.2 sum_cores.1
  104.3 0.2 collective-permute-start.10
  104.6 1.5 %collective-permute-start.11 = (bf16[8,32,1664]{2,1,0:T(8,128)(2,1)S(1)}, bf16[8,32,1664]{2,1,0:T(8,128)(2,1)S(1)}, u32[]{:S(2)}, u32[]{:S(2)}) collective-permute-start(bf16[8,32,1664]{2,1,0:T(8,128)(2,1)S(1)} %get-tuple-element.55.refs_0_), channel_id=1, source_target_pairs={{0,4},{1,3},{2,6},{3,1},{4,0},{5,7},{6,2},{7,5},{8,12},{9,11},{10,... | collective-permute-start | bytes 2555912 | tf_op jit(solution)/shard_map/ppermute | solution.py:561
  106.1 6.5 %input_own.1 = (f32[416,6144]{1,0:T(8,128)}, f32[13,6144]{1,0:T(8,128)}, f32[8,128]{1,0:T(8,128)S(1)}) custom-call(s32[17]{0:T(128)S(1)} %pad_add_fusion.tab_ref, bf16[512,3072]{1,0:T(8,128)(2,1)} %get-tuple-element.53.hg_ref, bf16[512,448]{1,0:T(8,128)(2,1)S(1)} %get-tuple-element.54.wat_ref, bf16[8,32,1664]{2,1,0:T(8,128)(2,1)S(1)} %get-tuple-element.55.refs_0_), custom_call_target="tpu_custom_call" | custom-call | flops 4000000000 | bytes 9000000 | tf_op jit(solution)/shard_map/input_own/pallas_call | solution.py:394
  112.6 4.7 %collective-permute-done.11.refs_2_ = bf16[8,32,1664]{2,1,0:T(8,128)(2,1)S(1)} collective-permute-done((bf16[8,32,1664]{2,1,0:T(8,128)(2,1)S(1)}, bf16[8,32,1664]{2,1,0:T(8,128)(2,1)S(1)}, u32[]{:S(2)}, u32[]{:S(2)}) %collective-permute-start.11) | collective-permute-done | bytes 852000 | tf_op jit(solution)/shard_map/ppermute | solution.py:561
  117.2 0.3 sum_first.1
  117.6 1.6 %collective-permute-start.12 = (bf16[4,32,1664]{2,1,0:T(8,128)(2,1)S(1)}, bf16[4,32,1664]{2,1,0:T(8,128)(2,1)S(1)}, u32[]{:S(2)}, u32[]{:S(2)}) collective-permute-start(bf16[4,32,1664]{2,1,0:T(8,128)(2,1)S(1)} %get-tuple-element.57.refs_0_), channel_id=1, source_target_pairs={{0,2},{1,5},{2,0},{3,7},{4,6},{5,1},{6,4},{7,3},{8,10},{9,13},{10,... | collective-permute-start | bytes 1277960 | tf_op jit(solution)/shard_map/ppermute | solution.py:561
  119.1 4.6 %input_far.1 = (f32[416,6144]{1,0:T(8,128)}, f32[13,6144]{1,0:T(8,128)}, f32[8,128]{1,0:T(8,128)S(1)}) custom-call(s32[17]{0:T(128)S(1)} %pad_add_fusion.tab_ref, bf16[512,3072]{1,0:T(8,128)(2,1)S(1)} %collective-permute-done.10.hg_ref, bf16[512,448]{1,0:T(8,128)(2,1)S(1)} %get-tuple-element.54.wat_ref, ...), custom_call_target="tpu_custom_call", output_to_operand_aliasing={{0}: (4, {}), {1}: (5, {})} | custom-call | flops 4000000000 | bytes 9000000 | tf_op jit(solution)/shard_map/input_far/pallas_call | solution.py:394
  123.7 2.0 %collective-permute-done.12.refs_1_ = bf16[4,32,1664]{2,1,0:T(8,128)(2,1)S(1)} collective-permute-done((bf16[4,32,1664]{2,1,0:T(8,128)(2,1)S(1)}, bf16[4,32,1664]{2,1,0:T(8,128)(2,1)S(1)}, u32[]{:S(2)}, u32[]{:S(2)}) %collective-permute-start.12) | collective-permute-done | bytes 426016 | tf_op jit(solution)/shard_map/ppermute | solution.py:561
  125.8 0.1 sum_second.1
  125.9 0.6 copy-done
  126.5 3.0 %collective-permute-start.14 = (bf16[32,1664]{1,0:T(8,128)(2,1)S(1)}, bf16[32,1664]{1,0:T(8,128)(2,1)S(1)}, u32[]{:S(2)}, u32[]{:S(2)}) collective-permute-start(bf16[32,1664]{1,0:T(8,128)(2,1)S(1)} %get-tuple-element.66), channel_id=1, source_target_pairs={{0,16},{2,18},{4,20},{6,22},{8,24},{10,26},{12,28},{14,30},{16,0},... | collective-permute-start | bytes 319496 | tf_op jit(solution)/shard_map/ppermute | solution.py:556
  129.6 1.3 collective-permute-start.15
  130.9 0.4 collective-permute-done.13.refs_1_
  131.3 5.5 %collective-permute-done.14.refs_2_ = bf16[32,1664]{1,0:T(8,128)(2,1)S(1)} collective-permute-done((bf16[32,1664]{1,0:T(8,128)(2,1)S(1)}, bf16[32,1664]{1,0:T(8,128)(2,1)S(1)}, u32[]{:S(2)}, u32[]{:S(2)}) %collective-permute-start.14) | collective-permute-done | bytes 106528 | tf_op jit(solution)/shard_map/ppermute | solution.py:556
  136.8 0.6 copy-done.6
  137.5 0.1 copy-done.7
  137.5 1.7 %sum_last.1 = f32[16,448]{1,0:T(8,128)} custom-call(bf16[32,1664]{1,0:T(8,128)(2,1)} %copy-done, bf16[32,1664]{1,0:T(8,128)(2,1)} %copy-done.5, bf16[32,1664]{1,0:T(8,128)(2,1)} %copy-done.6, bf16[32,1664]{1,0:T(8,128)(2,1)} %copy-done.7), custom_call_target="tpu_custom_call" | custom-call | tf_op jit(solution)/shard_map/sum_last/pallas_call | solution.py:517
  139.2 1.4 collective-permute-done.16.far_ref
  140.6 0.6 copy-done.11
  141.2 1.9 %finish.1 = (f32[32,416]{1,0:T(8,128)}, f32[13,32]{1,0:T(8,128)}, f32[1,32]{1,0:T(1,128)}, f32[4,32,256]{2,1,0:T(8,128)}, f32[4,16]{1,0:T(4,128)}, /*index=5*/f3...) custom-call(s32[1]{0:T(128)} %bitcast.core_ref.tab_ref, ...), custom_call_target="tpu_custom_call" | custom-call | tf_op jit(solution)/shard_map/finish/pallas_call | solution.py:531
  (24 shorter events, 0.1 us)
Async XLA Ops:
  3.0 9.2 %collective-permute-start.4 = (bf16[32,1664]{1,0:T(8,128)(2,1)}, bf16[32,1664]{1,0:T(8,128)(2,1)S(1)}, u32[]{:S(2)}, u32[]{:S(2)}) collective-permute-start(bf16[32,1664]{1,0:T(8,128)(2,1)} %get-tuple-element.49.refs_0_), channel_id=1, source_target_pairs={{0,24},{2,26},{4,28},{6,30},{8,16},{10,18},{12,20},{14,22},{16,8},... | collective-permute-start | bytes 319496 | tf_op jit(solution)/shard_map/ppermute | solution.py:556
  8.0 9.2 %collective-permute-start.3 = (bf16[32,1664]{1,0:T(8,128)(2,1)}, bf16[32,1664]{1,0:T(8,128)(2,1)S(1)}, u32[]{:S(2)}, u32[]{:S(2)}) collective-permute-start(bf16[32,1664]{1,0:T(8,128)(2,1)} %get-tuple-element.49.refs_0_), channel_id=1, source_target_pairs={{0,16},{2,18},{4,20},{6,22},{8,24},{10,26},{12,28},{14,30},{16,0},... | collective-permute-start | bytes 319496 | tf_op jit(solution)/shard_map/ppermute | solution.py:556
  8.0 9.2 %collective-permute-start.2 = (bf16[32,1664]{1,0:T(8,128)(2,1)}, bf16[32,1664]{1,0:T(8,128)(2,1)S(1)}, u32[]{:S(2)}, u32[]{:S(2)}) collective-permute-start(bf16[32,1664]{1,0:T(8,128)(2,1)} %get-tuple-element.49.refs_0_), channel_id=1, source_target_pairs={{0,8},{2,10},{4,12},{6,14},{8,0},{10,2},{12,4},{14,6},{16,24},{18,... | collective-permute-start | bytes 319496 | tf_op jit(solution)/shard_map/ppermute | solution.py:556
  8.7 33.9 %copy-start.4 = (bf16[16,128]{1,0:T(8,128)(2,1)S(1)}, bf16[16,128]{1,0:T(8,128)(2,1)}, u32[]{:S(2)}) copy-start(bf16[16,128]{1,0:T(8,128)(2,1)} %get-tuple-element.48.token_ref.refs_5_) | copy-start | bytes 12292
  8.7 34.4 %copy-start.3 = (s32[1,6144]{1,0:T(1,128)S(1)}, s32[1,6144]{1,0:T(1,128)}, u32[]{:S(2)}) copy-start(s32[1,6144]{1,0:T(1,128)} %refs_2_.3) | copy-start | bytes 73732
  12.1 5.1 %copy-start.8 = (bf16[32,1664]{1,0:T(8,128)(2,1)}, bf16[32,1664]{1,0:T(8,128)(2,1)S(1)}, u32[]{:S(2)}) copy-start(bf16[32,1664]{1,0:T(8,128)(2,1)S(1)} %collective-permute-done.4.refs_3_) | copy-start | bytes 319492
  17.2 0.6 copy-start.9
  17.8 0.6 copy-start.10
  20.3 8.3 %collective-permute-start.5 = (bf16[4,32,1664]{2,1,0:T(8,128)(2,1)}, bf16[4,32,1664]{2,1,0:T(8,128)(2,1)S(1)}, u32[]{:S(2)}, u32[]{:S(2)}) collective-permute-start(bf16[4,32,1664]{2,1,0:T(8,128)(2,1)} %join.1), channel_id=1, source_target_pairs={{0,2},{1,5},{2,0},{3,7},{4,6},{5,1},{6,4},{7,3},{8,10},{9,13},{10,... | collective-permute-start | bytes 1277960 | tf_op jit(solution)/shard_map/ppermute | solution.py:561
  29.8 12.8 %collective-permute-start.6 = (bf16[8,32,1664]{2,1,0:T(8,128)(2,1)S(1)}, bf16[8,32,1664]{2,1,0:T(8,128)(2,1)S(1)}, u32[]{:S(2)}, u32[]{:S(2)}) collective-permute-start(bf16[8,32,1664]{2,1,0:T(8,128)(2,1)S(1)} %pad_maximum_fusion.refs_7_), channel_id=1, source_target_pairs={{0,4},{1,3},{2,6},{3,1},{4,0},{5,7},{6,2},{7,5},{8,12},{9,11},{10,... | collective-permute-start | bytes 2555912 | tf_op jit(solution)/shard_map/ppermute | solution.py:561
  31.3 13.6 %collective-permute-start.7 = (bf16[8,32,1664]{2,1,0:T(8,128)(2,1)S(1)}, bf16[8,32,1664]{2,1,0:T(8,128)(2,1)S(1)}, u32[]{:S(2)}, u32[]{:S(2)}) collective-permute-start(bf16[8,32,1664]{2,1,0:T(8,128)(2,1)S(1)} %pad_maximum_fusion.refs_7_), channel_id=1, source_target_pairs={{0,1},{1,0},{2,3},{3,2},{4,5},{5,4},{6,7},{7,6},{8,9},{9,8},{10,11... | collective-permute-start | bytes 2555912 | tf_op jit(solution)/shard_map/ppermute | solution.py:565
  42.5 2.4 %collective-permute-start.8 = (bf16[8,32,1664]{2,1,0:T(8,128)(2,1)S(1)}, bf16[8,32,1664]{2,1,0:T(8,128)(2,1)S(1)}, u32[]{:S(2)}, u32[]{:S(2)}) collective-permute-start(bf16[8,32,1664]{2,1,0:T(8,128)(2,1)S(1)} %collective-permute-done.6.refs_8_), channel_id=1, source_target_pairs={{0,1},{1,0},{2,3},{3,2},{4,5},{5,4},{6,7},{7,6},{8,9},{9,8},{10,11... | collective-permute-start | bytes 2555912 | tf_op jit(solution)/shard_map/ppermute | solution.py:565
  42.5 2.4 %collective-permute-start.1 = (bf16[16,128]{1,0:T(8,128)(2,1)S(1)}, bf16[16,128]{1,0:T(8,128)(2,1)S(1)}, u32[]{:S(2)}, u32[]{:S(2)}) collective-permute-start(bf16[16,128]{1,0:T(8,128)(2,1)S(1)} %copy-done.4), channel_id=1, source_target_pairs={{0,1},{1,0},{2,3},{3,2},{4,5},{5,4},{6,7},{7,6},{8,9},{9,8},{10,11... | collective-permute-start | bytes 12296 | tf_op jit(solution)/shard_map/ppermute | solution.py:565
  43.0 1.9 %collective-permute-start = (s32[1,6144]{1,0:T(1,128)S(1)}, s32[1,6144]{1,0:T(1,128)S(1)}, u32[]{:S(2)}, u32[]{:S(2)}) collective-permute-start(s32[1,6144]{1,0:T(1,128)S(1)} %copy-done.3), channel_id=1, source_target_pairs={{0,1},{1,0},{2,3},{3,2},{4,5},{5,4},{6,7},{7,6},{8,9},{9,8},{10,11... | collective-permute-start | bytes 73736 | tf_op jit(solution)/shard_map/ppermute | solution.py:565
  44.9 0.7 copy-start.1
  45.7 0.9 copy-start.2
  100.2 3.9 %collective-permute-start.9 = (bf16[16,32,1664]{2,1,0:T(8,128)(2,1)}, bf16[16,32,1664]{2,1,0:T(8,128)(2,1)S(1)}, u32[]{:S(2)}, u32[]{:S(2)}) collective-permute-start(bf16[16,32,1664]{2,1,0:T(8,128)(2,1)} %get-tuple-element.51), channel_id=1, source_target_pairs={{0,1},{1,0},{2,3},{3,2},{4,5},{5,4},{6,7},{7,6},{8,9},{9,8},{10,11... | collective-permute-start | bytes 5111816 | tf_op jit(solution)/shard_map/ppermute | solution.py:565
  104.3 14.8 %collective-permute-start.10 = (bf16[512,3072]{1,0:T(8,128)(2,1)}, bf16[512,3072]{1,0:T(8,128)(2,1)S(1)}, u32[]{:S(2)}, u32[]{:S(2)}) collective-permute-start(bf16[512,3072]{1,0:T(8,128)(2,1)} %get-tuple-element.53.hg_ref), channel_id=1, source_target_pairs={{0,1},{1,0},{2,3},{3,2},{4,5},{5,4},{6,7},{7,6},{8,9},{9,8},{10,11... | collective-permute-start | bytes 9437192 | tf_op jit(solution)/shard_map/ppermute | solution.py:565
  104.6 12.7 %collective-permute-start.11 = (bf16[8,32,1664]{2,1,0:T(8,128)(2,1)S(1)}, bf16[8,32,1664]{2,1,0:T(8,128)(2,1)S(1)}, u32[]{:S(2)}, u32[]{:S(2)}) collective-permute-start(bf16[8,32,1664]{2,1,0:T(8,128)(2,1)S(1)} %get-tuple-element.55.refs_0_), channel_id=1, source_target_pairs={{0,4},{1,3},{2,6},{3,1},{4,0},{5,7},{6,2},{7,5},{8,12},{9,11},{10,... | collective-permute-start | bytes 2555912 | tf_op jit(solution)/shard_map/ppermute | solution.py:561
  117.6 8.2 %collective-permute-start.12 = (bf16[4,32,1664]{2,1,0:T(8,128)(2,1)S(1)}, bf16[4,32,1664]{2,1,0:T(8,128)(2,1)S(1)}, u32[]{:S(2)}, u32[]{:S(2)}) collective-permute-start(bf16[4,32,1664]{2,1,0:T(8,128)(2,1)S(1)} %get-tuple-element.57.refs_0_), channel_id=1, source_target_pairs={{0,2},{1,5},{2,0},{3,7},{4,6},{5,1},{6,4},{7,3},{8,10},{9,13},{10,... | collective-permute-start | bytes 1277960 | tf_op jit(solution)/shard_map/ppermute | solution.py:561
  125.9 0.6 copy-start
  126.5 4.7 %collective-permute-start.13 = (bf16[32,1664]{1,0:T(8,128)(2,1)S(1)}, bf16[32,1664]{1,0:T(8,128)(2,1)S(1)}, u32[]{:S(2)}, u32[]{:S(2)}) collective-permute-start(bf16[32,1664]{1,0:T(8,128)(2,1)S(1)} %get-tuple-element.65), channel_id=1, source_target_pairs={{0,8},{2,10},{4,12},{6,14},{8,0},{10,2},{12,4},{14,6},{16,24},{18,... | collective-permute-start | bytes 319496 | tf_op jit(solution)/shard_map/ppermute | solution.py:556
  126.5 10.3 %collective-permute-start.14 = (bf16[32,1664]{1,0:T(8,128)(2,1)S(1)}, bf16[32,1664]{1,0:T(8,128)(2,1)S(1)}, u32[]{:S(2)}, u32[]{:S(2)}) collective-permute-start(bf16[32,1664]{1,0:T(8,128)(2,1)S(1)} %get-tuple-element.66), channel_id=1, source_target_pairs={{0,16},{2,18},{4,20},{6,22},{8,24},{10,26},{12,28},{14,30},{16,0},... | collective-permute-start | bytes 319496 | tf_op jit(solution)/shard_map/ppermute | solution.py:556
  129.6 7.3 %collective-permute-start.15 = (bf16[32,1664]{1,0:T(8,128)(2,1)S(1)}, bf16[32,1664]{1,0:T(8,128)(2,1)S(1)}, u32[]{:S(2)}, u32[]{:S(2)}) collective-permute-start(bf16[32,1664]{1,0:T(8,128)(2,1)S(1)} %get-tuple-element.67), channel_id=1, source_target_pairs={{0,24},{2,26},{4,28},{6,30},{8,16},{10,18},{12,20},{14,22},{16,8},... | collective-permute-start | bytes 319496 | tf_op jit(solution)/shard_map/ppermute | solution.py:556
  131.3 5.6 %copy-start.5 = (bf16[32,1664]{1,0:T(8,128)(2,1)}, bf16[32,1664]{1,0:T(8,128)(2,1)S(1)}, u32[]{:S(2)}) copy-start(bf16[32,1664]{1,0:T(8,128)(2,1)S(1)} %collective-permute-done.13.refs_1_) | copy-start | bytes 319492
  136.8 0.6 copy-start.6
  136.8 0.7 copy-start.7
  139.2 1.4 collective-permute-start.16
  140.6 0.6 copy-start.11

commit v4 on v3

--- a/solution.py
+++ b/solution.py
@@ -19,7 +19,8 @@
 UC = QS + 128
 B1, GA = 72, 80
 FG = NE * FH + 128
-TILE = 512
+TILE = 1024
+SUB = 512
 
 
 def mm(a, b):
@@ -28,6 +29,10 @@
 
 def mm_nt(a, b):
     return lax.dot_general(a, b, NT, preferred_element_type=F32)
+
+
+def act_narrow(half):
+    return act_pair(half.astype(BF))
 
 
 def act_pair(half):
@@ -54,16 +59,31 @@
     return n + 4 * flag if n // 4 == 1 else n - 4 * flag
 
 
+LAG = 4
+
+
+def take_turns(chains, lag):
+    going = [(chain, lag * j) for j, chain in enumerate(chains)]
+    while going:
+        left = []
+        for chain, wait in going:
+            if wait > 0:
+                left.append((chain, wait - 1))
+            elif next(chain, True) is None:
+                left.append((chain, 0))
+        going = left
+
+
 def main_kernel(pieces, chunks, tab_ref, *refs):
     emb_ref, dense_ref, lab_ref, far_lab_ref, row_ref, vec_ref, far_vec_ref = refs[:7]
     u_refs = (refs[7 : 7 + pieces], refs[7 + pieces : 7 + 2 * pieces])
-    hg_ref, wat_s, *du_refs = refs[7 + 2 * pieces : 11 + 2 * pieces]
+    hg_ref, wat_s, du_own_ref, *du_far_refs = refs[7 + 2 * pieces : 12 + 2 * pieces]
     (
         x_s, hid_s, mid_s, sl1_s, out_s, sl2_s, sg_s, fg_s, mix_s,
         w1_s, w1t_s, ga_s, w2t_s, w2_s, b1_s, b2_s, gb_s, tt_s, tw_s, tcol_s, q_s,
         dwa_s, dw1_s, dw2_s, dtw_s, dcol_s, dlog_s, dsm_s, u_s, sem,
-    ) = refs[11 + 2 * pieces :]
-    n = emb_ref.shape[1]
+    ) = refs[12 + 2 * pieces :]
+    n = SUB
     fs, osz, ds = FH // chunks, EO // chunks, D // chunks
     step = pl.program_id(0)
     core = tab_ref[0]
@@ -79,13 +99,14 @@
                 copies[side][-1].start()
                 at += ref.shape[0]
         rows = lax.broadcasted_iota(jnp.int32, (32, n), 0)
-        x_s[EMB:XR, :] = jnp.where(rows == DENSE, 1.0, 0.0).astype(BF)
         ones = jnp.where(lax.broadcasted_iota(jnp.int32, (16, n), 0) == 0, 1.0, 0.0).astype(BF)
-        hid_s[D : D + 16, :] = ones
-        for k in range(NE):
-            mid_s[k, FH : FH + 16, :] = ones
-        mix_s[2 * EO : 2 * EO + 16, :] = ones
-        fg_s[NE * FH + 16 : FG, :] = jnp.zeros((FG - NE * FH - 16, n), BF)
+        for h in range(TILE // SUB):
+            x_s[h, EMB:XR, :] = jnp.where(rows == DENSE, 1.0, 0.0).astype(BF)
+            hid_s[h, D : D + 16, :] = ones
+            for k in range(NE):
+                mid_s[h, k, FH : FH + 16, :] = ones
+            mix_s[h, 2 * EO : 2 * EO + 16, :] = ones
+            fg_s[h, NE * FH + 16 : FG, :] = jnp.zeros((FG - NE * FH - 16, n), BF)
         for ref in (dwa_s, dw1_s, dw2_s, dtw_s, dcol_s, dlog_s):
             ref[...] = jnp.zeros_like(ref)
         gates = []
@@ -130,86 +151,97 @@
         last = jnp.concatenate([v[0:1, 3:4] for v in vecs] * TW, axis=0)
         tcol_s[...] = jnp.concatenate([b1 * 0.5, head, head * 0.5, last], axis=1)
 
-    row_weight = row_ref[...]
-    labels = (lab_ref[...].astype(F32), far_lab_ref[...].astype(F32))
-    x_s[0:EMB, :] = emb_ref[...]
-    x_s[EMB : EMB + DENSE, :] = dense_ref[...]
-    x = x_s[...]
-    hid = mm(wat_s[...], x).astype(BF)
-    hid_s[0:D, :] = hid
-    logits = mm(w1t_s[NE * FH : NE * FH + 16, :], hid) + gb_s[...]
-    probs = []
-    for t in range(2):
-        lt = logits[NE * t : NE * t + NE]
-        e = jnp.exp(lt - jnp.max(lt, axis=0, keepdims=True))
-        probs.append(e / jnp.sum(e, axis=0, keepdims=True))
-    mix = [None, None]
-    pend = None
-    nxt = mm(w1t_s[0:FH, :], hid)
-    for k in range(NE + 1):
-        h = nxt
-        if k < NE - 1:
-            nxt = mm(w1t_s[FH * (k + 1) : FH * (k + 2), :], hid)
-        if k < NE:
-            m, s = act_pair(h + b1_s[k // HALF, :, B1 + k % HALF : B1 + k % HALF + 1])
-            mb = m.astype(BF)
-            mid_s[k, 0:FH, :] = mb
-            sl1_s[FH * k : FH * k + FH, :] = s.astype(BF)
-            h2 = mm(w2t_s[EO * k : EO * k + EO, :], mb)
-        if pend is not None:
-            j = k - 1
-            o, s = act_pair(pend + b2_s[j // HALF, :, TW + j % HALF : TW + j % HALF + 1])
-            out_s[EO * j : EO * j + EO, :] = o.astype(out_s.dtype)
-            sl2_s[EO * j : EO * j + EO, :] = s.astype(sl2_s.dtype)
-            for t in range(2):
-                term = probs[t][j : j + 1, :] * o
-                mix[t] = term if j == 0 else mix[t] + term
-        pend = h2
-    mix_s[0:EO, :] = mix[0].astype(BF)
-    mix_s[EO : 2 * EO, :] = mix[1].astype(BF)
-    act, slope = act_pair(mm(tt_s[...], mix_s[0 : 2 * EO, :]) + tcol_s[:, 0:1])
-    weighted = act * tcol_s[:, 1:2]
-    lgos = []
-    for t in range(2):
-        logit = jnp.sum(weighted[TW * t : TW * t + TW], axis=0, keepdims=True) + tcol_s[t : t + 1, 3:4]
-        lgos.append(row_weight * (0.5 * jnp.tanh(0.5 * logit) + 0.5 - labels[t]))
-    lgo = jnp.concatenate([jnp.broadcast_to(lgos[t], (TW, n)) for t in range(2)], axis=0)
-    dcol_s[...] += lane_fold(lgo * act)
-    dlog_s[...] += lane_fold(jnp.concatenate([jnp.broadcast_to(lgos[t], (8, n)) for t in range(2)], axis=0))
-    tg = (lgo * (tcol_s[:, 2:3] * slope)).astype(BF)
-    dtw_s[...] += mm_nt(mix_s[...], tg)
-    mgh = mm(tw_s[...], tg) * 0.5
-    pgs = [[], []]
-    mgs = [None] * NE
-    for k in range(NE + 2):
-        if k < NE:
-            o = out_s[EO * k : EO * k + EO, :].astype(F32)
-            og = None
-            for t in range(2):
-                mg = mgh[EO * t : EO * t + EO]
-                pgs[t].append(jnp.sum(o * mg, axis=0, keepdims=True))
-                term = probs[t][k : k + 1, :] * mg
-                og = term if og is None else og + term
-            sg = (og * sl2_s[EO * k : EO * k + EO, :].astype(F32)).astype(BF)
-            sg_s[EO * k : EO * k + EO, :] = sg
-            mgs[k] = mm(w2_s[:, EO * k : EO * k + EO], sg)
-        if 1 <= k < NE + 1:
-            j = k - 1
-            dw2_s[:, EO * j : EO * j + EO] += mm_nt(mid_s[j], sg_s[EO * j : EO * j + EO, :])
-            fg = (mgs[j] * sl1_s[FH * j : FH * j + FH, :].astype(F32)).astype(BF)
-            fg_s[FH * j : FH * j + FH, :] = fg
-        if k >= 2:
-            j = k - 2
-            dw1_s[:, FH * j : FH * j + FH] += mm_nt(hid_s[...], fg_s[FH * j : FH * j + FH, :])
-    lgs = []
-    for t in range(2):
-        pg = jnp.concatenate(pgs[t], axis=0)
-        lgs.append(2.0 * probs[t] * (pg - jnp.sum(probs[t] * pg, axis=0, keepdims=True)))
-    fg_s[NE * FH : NE * FH + 16, :] = jnp.concatenate(lgs, axis=0).astype(BF)
-    dw1_s[:, NE * FH : FG] += mm_nt(hid_s[...], fg_s[NE * FH : FG, :])
-    hg = mm(w1_s[...], fg_s[...]).astype(BF)
-    hg_ref[...] = hg
-    dwa_s[...] += mm_nt(hg, x)
+    def chain(h):
+        at = slice(SUB * h, SUB * h + SUB)
+        x_s[h, 0:EMB, :] = emb_ref[:, at]
+        x_s[h, EMB : EMB + DENSE, :] = dense_ref[:, at]
+        hid = mm(wat_s[...], x_s[h]).astype(BF)
+        hid_s[h, 0:D, :] = hid
+        yield
+        logits = mm(w1t_s[NE * FH : NE * FH + 16, :], hid) + gb_s[...]
+        probs = []
+        for t in range(2):
+            lt = logits[NE * t : NE * t + NE]
+            e = jnp.exp(lt - jnp.max(lt, axis=0, keepdims=True))
+            probs.append(e / jnp.sum(e, axis=0, keepdims=True))
+        mix = [None, None]
+        pend = None
+        nxt = mm(w1t_s[0:FH, :], hid)
+        yield
+        for k in range(NE + 1):
+            pre = nxt
+            if k < NE - 1:
+                nxt = mm(w1t_s[FH * (k + 1) : FH * (k + 2), :], hid)
+            if k < NE:
+                m, s = act_narrow(pre + b1_s[k // HALF, :, B1 + k % HALF : B1 + k % HALF + 1])
+                mid_s[h, k, 0:FH, :] = m
+                sl1_s[h, FH * k : FH * k + FH, :] = s
+                pre2 = mm(w2t_s[EO * k : EO * k + EO, :], m)
+            if pend is not None:
+                j = k - 1
+                o, s = act_narrow(pend + b2_s[j // HALF, :, TW + j % HALF : TW + j % HALF + 1])
+                out_s[h, EO * j : EO * j + EO, :] = o
+                sl2_s[h, EO * j : EO * j + EO, :] = s
+                o = o.astype(F32)
+                for t in range(2):
+                    term = probs[t][j : j + 1, :] * o
+                    mix[t] = term if j == 0 else mix[t] + term
+            pend = pre2
+            yield
+        mix_s[h, 0:EO, :] = mix[0].astype(BF)
+        mix_s[h, EO : 2 * EO, :] = mix[1].astype(BF)
+        act, slope = act_pair(mm(tt_s[...], mix_s[h, 0 : 2 * EO, :]) + tcol_s[:, 0:1])
+        weighted = act * tcol_s[:, 1:2]
+        lgos = []
+        for t in range(2):
+            logit = jnp.sum(weighted[TW * t : TW * t + TW], axis=0, keepdims=True) + tcol_s[t : t + 1, 3:4]
+            label = (lab_ref, far_lab_ref)[t][:, at].astype(F32)
+            lgos.append(row_ref[:, at] * (0.5 * jnp.tanh(0.5 * logit) + 0.5 - label))
+        lgo = jnp.concatenate([jnp.broadcast_to(lgos[t], (TW, SUB)) for t in range(2)], axis=0)
+        dcol_s[...] += lane_fold(lgo * act)
+        dlog_s[...] += lane_fold(jnp.concatenate([jnp.broadcast_to(lgos[t], (8, SUB)) for t in range(2)], axis=0))
+        tg = (lgo * (tcol_s[:, 2:3] * slope)).astype(BF)
+        yield
+        dtw_s[...] += mm_nt(mix_s[h], tg)
+        mgh = mm(tw_s[...], tg) * 0.5
+        yield
+        pgs = [[], []]
+        mgs = [None] * NE
+        for k in range(NE + 2):
+            if k < NE:
+                o = out_s[h, EO * k : EO * k + EO, :]
+                og = None
+                for t in range(2):
+                    mg = mgh[EO * t : EO * t + EO]
+                    pgs[t].append(jnp.sum((o * mg.astype(BF)).astype(F32), axis=0, keepdims=True))
+                    term = probs[t][k : k + 1, :] * mg
+                    og = term if og is None else og + term
+                sg = og.astype(BF) * sl2_s[h, EO * k : EO * k + EO, :]
+                sg_s[h, EO * (k % 2) : EO * (k % 2) + EO, :] = sg
+                mgs[k] = mm(w2_s[:, EO * k : EO * k + EO], sg)
+            if 1 <= k < NE + 1:
+                j = k - 1
+                dw2_s[:, EO * j : EO * j + EO] += mm_nt(mid_s[h, j], sg_s[h, EO * (j % 2) : EO * (j % 2) + EO, :])
+                fg = mgs[j].astype(BF) * sl1_s[h, FH * j : FH * j + FH, :]
+                fg_s[h, FH * j : FH * j + FH, :] = fg
+            if k >= 2:
+                j = k - 2
+                dw1_s[:, FH * j : FH * j + FH] += mm_nt(hid_s[h], fg_s[h, FH * j : FH * j + FH, :])
+            yield
+        lgs = []
+        for t in range(2):
+            pg = jnp.concatenate(pgs[t], axis=0)
+            lgs.append(2.0 * probs[t] * (pg - jnp.sum(probs[t] * pg, axis=0, keepdims=True)))
+        fg_s[h, NE * FH : NE * FH + 16, :] = jnp.concatenate(lgs, axis=0).astype(BF)
+        yield
+        dw1_s[:, NE * FH : FG] += mm_nt(hid_s[h], fg_s[h, NE * FH : FG, :])
+        hg = mm(w1_s[...], fg_s[h]).astype(BF)
+        hg_ref[:, at] = hg
+        yield
+        dwa_s[...] += mm_nt(hg, x_s[h])
+        yield
+
+    take_turns([chain(h) for h in range(TILE // SUB)], LAG)
 
     @pl.when(step == pl.num_programs(0) - 1)
     def _():
@@ -235,11 +267,13 @@
             b1 = pltpu.roll(b1, B1, 1)
             for c in range(chunks):
                 dsm_s[fs * c : fs * c + fs, :] = b1[fs * c : fs * c + fs] + jnp.concatenate([tower[osz * c : osz * c + osz], tail], axis=0)
-            ref = du_refs[side]
             holder = core if side == 0 else 1 - core
             cols = HALF * EO
-            for c in range(chunks):
-                at = chunk_at(c, chunks, holder)
+            for n in range(chunks):
+                ref, c = du_own_ref, n
+                if side == 1:
+                    ref, c = du_far_refs[n * 2 // chunks], n % max(chunks // 2, 1)
+                at = chunk_at(n, chunks, holder)
                 to = pl.multiple_of(ds * at, ds)
                 where = pl.ds(pl.multiple_of(tab_ref[1 + at] * fs, fs), fs)
                 ref[c, :, 0:QA] = dw1_s[pl.ds(to, ds), QA * side : QA * side + QA].astype(BF)
@@ -251,27 +285,28 @@
                 ref[c, fs:ds, QA:UC] = jnp.concatenate([lower, jnp.zeros((fs, UC - QA - XR), F32)], axis=1).astype(BF)
 
 
-def weight_kernel(batch_rows, tab_ref, sizes_ref, token_ref, out_ref, start_s, end_s, inv_s):
-    users = sizes_ref.shape[1]
-    counts = sizes_ref[...].astype(F32)
-    turned = jnp.concatenate([counts, jnp.zeros((128 - counts.shape[0], users), F32)], axis=0).T
-    upto = lax.broadcasted_iota(jnp.int32, (users, users), 1) <= lax.broadcasted_iota(jnp.int32, (users, users), 0)
-    ends = mm(jnp.where(upto, 1.0, 0.0).astype(BF), turned.astype(BF))
-    starts = ends - turned
-    for b in range(counts.shape[0]):
-        end_s[b] = jnp.broadcast_to(ends[:, b : b + 1], (users, 128))
+def weight_kernel(batch_rows, tab_ref, sizes_ref, token_ref, out_ref, start_s):
+    batches, users = sizes_ref.shape
+    counts = jnp.concatenate([sizes_ref[...].astype(F32), jnp.zeros((16 - batches, users), F32)], axis=0)
+    turned = jnp.concatenate([counts, jnp.zeros((112, users), F32)], axis=0).T
+    before = lax.broadcasted_iota(jnp.int32, (users, users), 1) < lax.broadcasted_iota(jnp.int32, (users, users), 0)
+    starts = mm(jnp.where(before, 1.0, 0.0).astype(BF), turned.astype(BF))
+    for b in range(batches):
         start_s[b] = jnp.broadcast_to(starts[:, b : b + 1], (users, 128))
-        inv_s[b] = jnp.broadcast_to(1.0 / turned[:, b : b + 1], (users, 128))
-    steps = out_ref.shape[1] // TILE
+    first = lax.broadcasted_iota(jnp.int32, counts.shape, 1) == 0
+    rises = counts - jnp.where(first, 0.0, pltpu.roll(counts, 1, 1))
+    line = lax.broadcasted_iota(jnp.int32, counts.shape, 0)
+    steps = out_ref.shape[1] // SUB
     for step in range(steps):
         at_step = tab_ref[0] * steps + step
-        batch = at_step // (batch_rows // TILE)
-        first_row = (at_step % (batch_rows // TILE) * TILE).astype(F32)
-        for c in range(TILE // 128):
-            row_at = first_row + (lax.broadcasted_iota(jnp.int32, (1, 128), 1) + 128 * c).astype(F32)
-            inside = (row_at >= start_s[batch]) & (row_at < end_s[batch])
-            at = TILE * step + 128 * c
-            out_ref[:, at : at + 128] = jnp.sum(jnp.where(inside, inv_s[batch], 0.0), axis=0, keepdims=True)
+        batch = at_step // (batch_rows // SUB)
+        first_row = (at_step % (batch_rows // SUB) * SUB).astype(F32)
+        begins = start_s[batch]
+        places = first_row + lax.broadcasted_iota(jnp.int32, (1, 128), 1).astype(F32)
+        begun = [jnp.where(begins <= places + 128.0 * c, 1.0, 0.0).astype(BF) for c in range(SUB // 128)]
+        rise = jnp.where(line == batch, rises, 0.0).astype(BF)
+        size = jnp.sum(mm(rise, jnp.concatenate(begun, axis=1)), axis=0, keepdims=True)
+        out_ref[:, SUB * step : SUB * step + SUB] = 1.0 / size
 
 
 def weight_call(table, sizes, rows, token):
@@ -281,7 +316,7 @@
         in_specs=[whole(pltpu.SMEM), whole(), whole(pl.ANY)],
         out_specs=whole(),
         out_shape=jax.ShapeDtypeStruct((1, rows // 2), F32),
-        scratch_shapes=[pltpu.VMEM((batches, users, 128), F32)] * 3,
+        scratch_shapes=[pltpu.VMEM((batches, users, 128), F32)],
         cost_estimate=pl.CostEstimate(flops=3_000_000_000, bytes_accessed=1_000_000, transcendentals=0),
         name="row_weights",
     )(table, sizes, token)
@@ -302,7 +337,8 @@
     def own(i, c):
         return (0, c[0] * steps + i)
 
-    grads = [(chunks, ds, UC)] * 2
+    grads = [(chunks, ds, UC)] + [(max(chunks // 2, 1), ds, UC)] * 2
+    parts = TILE // SUB
     spec = pltpu.PrefetchScalarGridSpec(
         num_scalar_prefetch=1,
         grid=(steps,),
@@ -315,18 +351,18 @@
             whole(),
             whole(),
         ]
-        + [whole(pl.ANY) for _ in (*own_u, *far_u)],
-        out_specs=[pl.BlockSpec((D, TILE), lambda i, c: (0, i))] + [whole()] * 3,
+        + [whole(pltpu.HBM) for _ in (*own_u, *far_u)],
+        out_specs=[pl.BlockSpec((D, TILE), lambda i, c: (0, i))] + [whole()] * 4,
         scratch_shapes=[
-            pltpu.VMEM((XR, TILE), BF),
-            pltpu.VMEM((D + 16, TILE), BF),
-            pltpu.VMEM((NE, FH + 16, TILE), BF),
-            pltpu.VMEM((NE * FH, TILE), BF),
-            pltpu.VMEM((NE * EO, TILE), F32),
-            pltpu.VMEM((NE * EO, TILE), F32),
-            pltpu.VMEM((NE * EO, TILE), BF),
-            pltpu.VMEM((FG, TILE), BF),
-            pltpu.VMEM((2 * EO + 16, TILE), BF),
+            pltpu.VMEM((parts, XR, SUB), BF),
+            pltpu.VMEM((parts, D + 16, SUB), BF),
+            pltpu.VMEM((parts, NE, FH + 16, SUB), BF),
+            pltpu.VMEM((parts, NE * FH, SUB), BF),
+            pltpu.VMEM((parts, NE * EO, SUB), BF),
+            pltpu.VMEM((parts, NE * EO, SUB), BF),
+            pltpu.VMEM((parts, 2 * EO, SUB), BF),
+            pltpu.VMEM((parts, FG, SUB), BF),
+            pltpu.VMEM((parts, 2 * EO + 16, SUB), BF),
             pltpu.VMEM((D, FG), BF),
             pltpu.VMEM((NE * FH + 16, D), BF),
             pltpu.VMEM((D, 128), F32),
@@ -376,7 +412,7 @@
 
 def input_call(table, hg, wat, token, other, name):
     half = hg.shape[1]
-    tile = 2 * TILE
+    tile = TILE
     steps = half // tile
 
     def place(i, c):
@@ -479,14 +515,15 @@
     )(*arrays, *extra)
 
 
-def finish_kernel(scale, core_ref, token_ref, far_ref, *refs):
+def finish_kernel(scale, core_ref, token_ref, *refs):
     total = sum(r[...].astype(F32) for r in refs[:4]) * scale
     ds = total.shape[0]
     fs = ds // 2
-    own_part, far_part = total[fs:, QA : QA + XR], far_ref[...] * scale
+    own_part = total[fs:, QA : QA + XR]
+    far_part = sum(r[...].astype(F32) for r in refs[4:8])[:, 0:XR] * scale
     second_core = core_ref[0] == 1
     ta = jnp.concatenate([jnp.where(second_core, far_part, own_part), jnp.where(second_core, own_part, far_part)], axis=0)
-    emb_ref, dense_ref, bias_ref, w1_ref, b1_ref, w2_ref, b2_ref, gate_ref, gb_ref, tower_ref, t1_ref, t2_ref, t3_ref = refs[4:]
+    emb_ref, dense_ref, bias_ref, w1_ref, b1_ref, w2_ref, b2_ref, gate_ref, gb_ref, tower_ref, t1_ref, t2_ref, t3_ref = refs[8:]
     osz = tower_ref.shape[0]
     for k in range(HALF):
         w1_ref[k] = total[:, FH * k : FH * k + FH]
@@ -508,48 +545,18 @@
     bias_ref[...] = last[32 + DENSE : 33 + DENSE, 0 : 2 * fs]
 
 
-def last_kernel(*refs):
-    fs = refs[4].shape[0]
-    refs[4][...] = sum(r[fs:, QA : QA + XR].astype(F32) for r in refs[:4])
-
-
-def last_call(arrays):
-    return pl.pallas_call(
-        last_kernel,
-        in_specs=[whole() for _ in arrays],
-        out_specs=whole(),
-        out_shape=jax.ShapeDtypeStruct((arrays[0].shape[0] // 2, XR), F32),
-        name="sum_last",
-    )(*arrays)
-
-
-def finish_call(scale, core, token, far, arrays, ds, fs, osz):
+def finish_call(scale, core, token, arrays, ds, fs, osz):
     shapes = [
         (ds, EMB), (DENSE, ds), (1, ds), (HALF, ds, FH), (HALF, fs), (HALF, fs, EO), (HALF, osz), (NE, ds), (1, NE),
         (osz, TW), (1, TW), (1, TW), (1, 1),
     ]
     return pl.pallas_call(
         functools.partial(finish_kernel, scale),
-        in_specs=[whole(pltpu.SMEM), whole(pl.ANY), whole()] + [whole() for _ in arrays],
+        in_specs=[whole(pltpu.SMEM), whole(pl.ANY)] + [whole() for _ in arrays],
         out_specs=[whole() for _ in shapes],
         out_shape=[jax.ShapeDtypeStruct(a, F32) for a in shapes],
         name="finish",
-    )(core, token, far, *arrays)
-
-
-def join_kernel(token_ref, *refs):
-    for j in range(4):
-        refs[4][j] = refs[j][...]
-
-
-def join_call(parts, token):
-    return pl.pallas_call(
-        join_kernel,
-        in_specs=[whole(pl.ANY)] + [whole() for _ in parts],
-        out_specs=whole(),
-        out_shape=jax.ShapeDtypeStruct((4, *parts[0].shape), BF),
-        name="join",
-    )(token, *parts)
+    )(core, token, *arrays)
 
 
 def hop(a, mask, size):
@@ -593,9 +600,9 @@
             one_core, w_emb.T, w_dense, b_in[None], expert_w1, expert_w2, expert_b1, expert_b2, gate_t, tower_w1[0], *smalls
         )
         row_weights = weight_call(one_core, group_sizes, emb.shape[0], vec)
-        near = join_call([shard] + [hop(shard, 4 * a, size) for a in range(1, 4)], row_weights)
-        near = jnp.concatenate([near, cross(near, (1, 2), size)], axis=0)
-        own_u = [near, cross(near, (2, 1), size)]
+        near = jnp.stack([shard] + [hop(shard, 4 * a, size) for a in range(1, 4)])
+        once = cross(near, (1, 2), size)
+        own_u = [near, once, cross(near, (2, 1), size), cross(once, (2, 1), size)]
         steps = jnp.arange(16, dtype=jnp.int32)
         order = place ^ (steps % 4 * 4 + steps // 4)
     else:
@@ -615,30 +622,30 @@
     far_u = [partner(a) for a in own_u]
     table = jnp.concatenate([core[None].astype(jnp.int32), order])
 
-    hg, wat, du_own, du_far = main_call(table, emb.T, dense.T, labels, far_labels, row_weights, vec, partner(vec), own_u, far_u)
-    du_far = partner(du_far)
+    hg, wat, du_own, du_low, du_high = main_call(table, emb.T, dense.T, labels, far_labels, row_weights, vec, partner(vec), own_u, far_u)
+    du_high = partner(du_high)
     scale = 1.0 / user_count
     if fast:
-        hg, part = sum_call("sum_cores", [du_own, du_far], [[(0, slice(8, 16)), (1, slice(8, 16))]], [(8, ds, UC)], through=hg)
+        hg, part = sum_call("sum_cores", [du_own, du_high], [[(0, slice(8, 16)), (1, slice(0, 8))]], [(8, ds, UC)], through=hg)
         got = cross(part, (2, 1), size)
+        du_low, far_hg = partner(du_low), partner(hg)
         eg, dg, token = input_call(table, hg, wat, part, None, "input_own")
-        far_hg = partner(hg)
         groups = [[(j, slice(4 * b, 4 * b + 4)) for j in range(3)] for b in (1, 0)]
-        part, rest = sum_call("sum_first", [du_own, du_far, got], groups, [(4, ds, UC)] * 2, token)
+        part, rest = sum_call("sum_first", [du_own, du_low, got], groups, [(4, ds, UC)] * 2, token)
         got = cross(part, (1, 2), size)
         eg, dg, token = input_call(table, far_hg, wat, part, (eg, dg), "input_far")
         sums = sum_call("sum_second", [rest, got], [[(0, k), (1, k)] for k in range(4)], [(ds, UC)] * 4, token)
         parts = [sums[0]] + [hop(sums[a], 4 * a, size) for a in range(1, 4)]
-        far_input = partner(last_call(parts))
-        out = finish_call(scale, one_core, sums[0], far_input, parts, ds, fs, osz)
+        parts += [partner(a[fs:, QA : QA + 512]) for a in parts]
+        out = finish_call(scale, one_core, sums[0], parts, ds, fs, osz)
         g_emb, g_dense, g_bias, g_w1, g_b1, g_w2, g_b2, g_gate, g_gb, g_tower, g_t1, g_t2, g_t3 = out
         return (
             eg.T, dg.T, g_emb.T, g_dense, g_bias[0], g_w1, g_b1, g_w2, g_b2, g_gate.T[None], g_gb, g_tower[None], g_t1, g_t2, g_t3[0],
         )
-    eg, dg, token = input_call(table, hg, wat, du_far, None, "input_own")
+    eg, dg, token = input_call(table, hg, wat, du_high, None, "input_own")
     eg, dg, _ = input_call(table, partner(hg), wat, token, (eg, dg), "input_far")
     scatter = functools.partial(lax.psum_scatter, axis_name="rows", scatter_dimension=0, tiled=True)
-    wide = add_wide(du_own[0], du_far[0])
+    wide = add_wide(du_own[0], partner(du_low)[0])
     upper, near = wide[0:FH, QA:UC], wide[FH:, QA : QA + XR]
     far, small = partner(near), upper[:, HALF * EO :]
     ta = scatter(jnp.concatenate([jnp.where(core == 0, near, far), jnp.where(core == 0, far, near)], axis=0)) * scale

time: 144 us -> 134 us (0.931)
  Pallas kernels: 75.9 us -> 66.2 us
    pallas_call x1, Pallas kernels: 53.6 us -> 48.2 us  [main_call(): pl.pallas_call(functools.partial(main_kernel, pieces, chunks), grid_spec=...]
    pallas_call x2 -> x0, Pallas kernels: 3.51 us -> none  [the longest x1 1.83 us: join_call(): pl.pallas_call(join_kernel, in_specs=[whole(pl.ANY)] + [whole() for _ in...]
    ppermute x6, waiting for transfers between devices: 11 us -> 14.2 us  [hop(): return lax.ppermute(a, 'rows', [(i, i ^ mask) for i in range(size)])]
    ppermute x7 -> x13, waiting for transfers between devices: 6.81 us -> 3.64 us  [partner(): return lax.ppermute(a, 'task', [(0, 1), (1, 0)])]
    ppermute x7 -> x13, starting transfers between devices: 1.05 us -> 3.35 us  [partner(): return lax.ppermute(a, 'task', [(0, 1), (1, 0)])]
    ppermute x4 -> x5, starting transfers between devices: 6.14 us -> 4.83 us  [cross(): return lax.ppermute(a, ('rows', 'task'), pairs)]
    unnamed x24 -> x28, local copies, waits for them, and re-layouts: 4.85 us -> 4.04 us
    ppermute x4 -> x5, waiting for transfers between devices: 24.8 us -> 24.8 us  [cross(): return lax.ppermute(a, ('rows', 'task'), pairs)]
  transfers between devices with their start and end apart: 17 -> 24, of which waited for: 10 -> 12; matrix products, arithmetic and copies ran while one was open for 0% -> 0% of each run, Pallas kernels for 10% -> 11%
where the time goes in v4:
time: 134 us
  Pallas kernels  66.2 us (49%)
  waiting for transfers between devices  42.7 us (32%)
  starting transfers between devices  18.3 us (14%)
  local copies, waits for them, and re-layouts  4.05 us (3%)
  between operations  1.65 us (1%)
    pallas_call x1, Pallas kernels, main_call(): pl.pallas_call(functools.partial(main_kernel, pieces, chunks), grid_spec=...  48.2 us
    ppermute x5, waiting for transfers between devices, cross(): return lax.ppermute(a, ('rows', 'task'), pairs)  24.8 us
    ppermute x6, waiting for transfers between devices, hop(): return lax.ppermute(a, 'rows', [(i, i ^ mask) for i in range(size)])  14.2 us
    pallas_call x2, Pallas kernels, input_call(): pl.pallas_call(input_kernel, grid_spec=spec, out_shape=[jax.ShapeDtypeStr...  11.1 us
    ppermute x6, starting transfers between devices, hop(): return lax.ppermute(a, 'rows', [(i, i ^ mask) for i in range(size)])  10.1 us
    ppermute x5, starting transfers between devices, cross(): return lax.ppermute(a, ('rows', 'task'), pairs)  4.83 us
    unnamed x28, local copies, waits for them, and re-layouts  4.04 us
    ppermute x13, waiting for transfers between devices, partner(): return lax.ppermute(a, 'task', [(0, 1), (1, 0)])  3.64 us
  transfers between devices with their start and end apart: 24, of which 12 were waited for; matrix products, arithmetic and copies ran while one was open for 0% of the time, Pallas kernels for 11%

profile of v4, /device:TPU:0, one launch (start us, length us, event | category | flops | bytes accessed | tf_op | source)
XLA Modules:
  0.0 134.0 jit_solution(14731080745403033742)
XLA Ops:
  1.3 1.7 %pack.1 = (bf16[32,1664]{1,0:T(8,128)(2,1)}, bf16[16,128]{1,0:T(8,128)(2,1)}) custom-call(s32[1]{0:T(128)} %bitcast.core_ref.tab_ref, bf16[32,416]{1,0:T(8,128)(2,1)} %bitcast.29, bf16[13,32]{1,0:T(8,128)(2,1)} %dense_ref.1, bf16[1,32]{1,0:T(2,128)(2,1)} %bitcast.32, bf16[4,32,256]{2,1,0:T(8,128)(2,1)} %w1_ref.1, bf16[4,16,128]{2,1,0:T(8,128)(2,1)} %w2_ref.1, ...), custom_call_target="tpu_custom_call" | custom-call | tf_op jit(solution)/shard_map/pack/pallas_call | solution.py:485
  3.0 5.0 %collective-permute-start.4 = (bf16[32,1664]{1,0:T(8,128)(2,1)}, bf16[32,1664]{1,0:T(8,128)(2,1)S(1)}, u32[]{:S(2)}, u32[]{:S(2)}) collective-permute-start(bf16[32,1664]{1,0:T(8,128)(2,1)} %get-tuple-element.50), channel_id=1, source_target_pairs={{0,24},{2,26},{4,28},{6,30},{8,16},{10,18},{12,20},{14,22},{16,8},... | collective-permute-start | bytes 319496 | tf_op jit(solution)/shard_map/ppermute | solution.py:563
  8.0 0.6 collective-permute-start.2
  8.7 3.5 %collective-permute-done.4 = bf16[32,1664]{1,0:T(8,128)(2,1)S(1)} collective-permute-done((bf16[32,1664]{1,0:T(8,128)(2,1)}, bf16[32,1664]{1,0:T(8,128)(2,1)S(1)}, u32[]{:S(2)}, u32[]{:S(2)}) %collective-permute-start.4) | collective-permute-done | bytes 106528 | tf_op jit(solution)/shard_map/ppermute | solution.py:563
  12.1 5.1 %collective-permute-done.3 = bf16[32,1664]{1,0:T(8,128)(2,1)S(1)} collective-permute-done((bf16[32,1664]{1,0:T(8,128)(2,1)}, bf16[32,1664]{1,0:T(8,128)(2,1)S(1)}, u32[]{:S(2)}, u32[]{:S(2)}) %collective-permute-start.3) | collective-permute-done | bytes 106528 | tf_op jit(solution)/shard_map/ppermute | solution.py:563
  17.2 1.0 pad_maximum_fusion.refs_7_
  18.2 1.6 %collective-permute-start.5 = (bf16[4,32,1664]{2,1,0:T(8,128)(2,1)S(1)}, bf16[4,32,1664]{2,1,0:T(8,128)(2,1)S(1)}, u32[]{:S(2)}, u32[]{:S(2)}) collective-permute-start(bf16[4,32,1664]{2,1,0:T(8,128)(2,1)S(1)} %pad_maximum_fusion.refs_7_), channel_id=1, source_target_pairs={{0,2},{1,5},{2,0},{3,7},{4,6},{5,1},{6,4},{7,3},{8,10},{9,13},{10,... | collective-permute-start | bytes 1277960 | tf_op jit(solution)/shard_map/ppermute | solution.py:568
  19.8 1.5 %collective-permute-start.6 = (bf16[4,32,1664]{2,1,0:T(8,128)(2,1)S(1)}, bf16[4,32,1664]{2,1,0:T(8,128)(2,1)S(1)}, u32[]{:S(2)}, u32[]{:S(2)}) collective-permute-start(bf16[4,32,1664]{2,1,0:T(8,128)(2,1)S(1)} %pad_maximum_fusion.refs_7_), channel_id=1, source_target_pairs={{0,4},{1,3},{2,6},{3,1},{4,0},{5,7},{6,2},{7,5},{8,12},{9,11},{10,... | collective-permute-start | bytes 1277960 | tf_op jit(solution)/shard_map/ppermute | solution.py:568
  21.3 9.6 %collective-permute-done.5.refs_8_ = bf16[4,32,1664]{2,1,0:T(8,128)(2,1)S(1)} collective-permute-done((bf16[4,32,1664]{2,1,0:T(8,128)(2,1)S(1)}, bf16[4,32,1664]{2,1,0:T(8,128)(2,1)S(1)}, u32[]{:S(2)}, u32[]{:S(2)}) %collective-permute-start.5) | collective-permute-done | bytes 426016 | tf_op jit(solution)/shard_map/ppermute | solution.py:568
  30.9 0.1 collective-permute-start.7
  31.0 0.5 collective-permute-start.8
  31.5 0.0 collective-permute-start.9
  31.6 0.5 collective-permute-start.10
  32.0 7.0 %collective-permute-done.7.refs_10_ = bf16[4,32,1664]{2,1,0:T(8,128)(2,1)S(1)} collective-permute-done((bf16[4,32,1664]{2,1,0:T(8,128)(2,1)S(1)}, bf16[4,32,1664]{2,1,0:T(8,128)(2,1)S(1)}, u32[]{:S(2)}, u32[]{:S(2)}) %collective-permute-start.7) | collective-permute-done | bytes 426016 | tf_op jit(solution)/shard_map/ppermute | solution.py:568
  39.0 2.7 %row_weights.1.refs_4_ = f32[1,3072]{1,0:T(1,128)} custom-call(s32[1]{0:T(128)} %bitcast.core_ref.tab_ref, s32[3,512]{1,0:T(4,128)} %sizes_ref.1, bf16[16,128]{1,0:T(8,128)(2,1)} %get-tuple-element.49.token_ref.refs_5_), custom_call_target="tpu_custom_call" | custom-call | flops 3000000000 | bytes 1000000 | tf_op jit(solution)/shard_map/row_weights/pallas_call | solution.py:314
  41.8 0.6 collective-permute-start
  42.3 0.1 pad_add_fusion.tab_ref
  42.4 0.8 collective-permute-done.refs_3_
  43.2 0.0 copy-start.3
  43.2 0.9 copy-done.3
  44.2 0.7 copy-done.6
  44.9 48.2 %experts.1 = (bf16[512,3072]{1,0:T(8,128)(2,1)}, bf16[512,448]{1,0:T(8,128)(2,1)S(1)}, bf16[16,32,1664]{2,1,0:T(8,128)(2,1)}, bf16[8,32,1664]{2,1,0:T(8,128)(2,1)S(1)}, bf16[8,32,1664]{2,1,0:T(8,128)(2,1)S(1)}) custom-call(s32[17]{0:T(128)S(1)} %pad_add_fusion.tab_ref, bf16[416,6144]{1,0:T(8,128)(2,1)} %bitcast.33, bf16[13,6144]{1,0:T(8,128)(2,1)S(1)} %bitcast.24, ...), custom_call_target="tpu_custom_call" | custom-call | flops 49999998976 | bytes 24000000 | tf_op jit(solution)/shard_map/experts/pallas_call | solution.py:389
  93.1 0.4 collective-permute-start.12
  93.5 2.0 %collective-permute-done.12.refs_1_ = bf16[8,32,1664]{2,1,0:T(8,128)(2,1)S(1)} collective-permute-done((bf16[8,32,1664]{2,1,0:T(8,128)(2,1)S(1)}, bf16[8,32,1664]{2,1,0:T(8,128)(2,1)S(1)}, u32[]{:S(2)}, u32[]{:S(2)}) %collective-permute-start.12) | collective-permute-done | bytes 852000 | tf_op jit(solution)/shard_map/ppermute | solution.py:572
  95.5 1.5 %copy-done = bf16[16,32,1664]{2,1,0:T(8,128)(2,1)S(1)} copy-done((bf16[16,32,1664]{2,1,0:T(8,128)(2,1)S(1)}, bf16[16,32,1664]{2,1,0:T(8,128)(2,1)}, u32[]{:S(2)}) %copy-start) | copy-done | bytes 1703960
  97.0 0.2 sum_cores.1
  97.2 0.4 collective-permute-start.13
  97.6 0.2 collective-permute-start.14
  97.8 0.1 collective-permute-start.15
  97.9 6.5 %input_own.1 = (f32[416,6144]{1,0:T(8,128)}, f32[13,6144]{1,0:T(8,128)}, f32[8,128]{1,0:T(8,128)S(1)}) custom-call(s32[17]{0:T(128)S(1)} %pad_add_fusion.tab_ref, bf16[512,3072]{1,0:T(8,128)(2,1)} %get-tuple-element.54.hg_ref, bf16[512,448]{1,0:T(8,128)(2,1)S(1)} %get-tuple-element.55.wat_ref, bf16[8,32,1664]{2,1,0:T(8,128)(2,1)S(1)} %get-tuple-element.57.refs_0_), custom_call_target="tpu_custom_call" | custom-call | flops 4000000000 | bytes 9000000 | tf_op jit(solution)/shard_map/input_own/pallas_call | solution.py:430
  104.4 6.1 %collective-permute-done.15.refs_2_ = bf16[8,32,1664]{2,1,0:T(8,128)(2,1)S(1)} collective-permute-done((bf16[8,32,1664]{2,1,0:T(8,128)(2,1)S(1)}, bf16[8,32,1664]{2,1,0:T(8,128)(2,1)S(1)}, u32[]{:S(2)}, u32[]{:S(2)}) %collective-permute-start.15) | collective-permute-done | bytes 852000 | tf_op jit(solution)/shard_map/ppermute | solution.py:568
  110.5 0.3 sum_first.1
  110.8 1.6 %collective-permute-start.16 = (bf16[4,32,1664]{2,1,0:T(8,128)(2,1)S(1)}, bf16[4,32,1664]{2,1,0:T(8,128)(2,1)S(1)}, u32[]{:S(2)}, u32[]{:S(2)}) collective-permute-start(bf16[4,32,1664]{2,1,0:T(8,128)(2,1)S(1)} %get-tuple-element.59.refs_0_), channel_id=1, source_target_pairs={{0,2},{1,5},{2,0},{3,7},{4,6},{5,1},{6,4},{7,3},{8,10},{9,13},{10,... | collective-permute-start | bytes 1277960 | tf_op jit(solution)/shard_map/ppermute | solution.py:568
  112.3 4.6 %input_far.1 = (f32[416,6144]{1,0:T(8,128)}, f32[13,6144]{1,0:T(8,128)}, f32[8,128]{1,0:T(8,128)S(1)}) custom-call(s32[17]{0:T(128)S(1)} %pad_add_fusion.tab_ref, bf16[512,3072]{1,0:T(8,128)(2,1)S(1)} %collective-permute-done.13.hg_ref, bf16[512,448]{1,0:T(8,128)(2,1)S(1)} %get-tuple-element.55.wat_ref, ...), custom_call_target="tpu_custom_call", output_to_operand_aliasing={{0}: (4, {}), {1}: (5, {})} | custom-call | flops 4000000000 | bytes 9000000 | tf_op jit(solution)/shard_map/input_far/pallas_call | solution.py:430
  116.9 2.0 %collective-permute-done.16.refs_1_ = bf16[4,32,1664]{2,1,0:T(8,128)(2,1)S(1)} collective-permute-done((bf16[4,32,1664]{2,1,0:T(8,128)(2,1)S(1)}, bf16[4,32,1664]{2,1,0:T(8,128)(2,1)S(1)}, u32[]{:S(2)}, u32[]{:S(2)}) %collective-permute-start.16) | collective-permute-done | bytes 426016 | tf_op jit(solution)/shard_map/ppermute | solution.py:568
  119.0 0.1 sum_second.1
  119.1 0.4 collective-permute-start.17
  119.5 2.7 %collective-permute-start.18 = (bf16[32,1664]{1,0:T(8,128)(2,1)S(1)}, bf16[32,1664]{1,0:T(8,128)(2,1)S(1)}, u32[]{:S(2)}, u32[]{:S(2)}) collective-permute-start(bf16[32,1664]{1,0:T(8,128)(2,1)S(1)} %get-tuple-element.68), channel_id=1, source_target_pairs={{0,16},{2,18},{4,20},{6,22},{8,24},{10,26},{12,28},{14,30},{16,0},... | collective-permute-start | bytes 319496 | tf_op jit(solution)/shard_map/ppermute | solution.py:563
  122.2 1.3 collective-permute-start.19
  123.5 0.4 collective-permute-done.17.refs_1_
  123.9 0.2 collective-permute-start.21
  124.1 5.3 %collective-permute-done.18.refs_2_ = bf16[32,1664]{1,0:T(8,128)(2,1)S(1)} collective-permute-done((bf16[32,1664]{1,0:T(8,128)(2,1)S(1)}, bf16[32,1664]{1,0:T(8,128)(2,1)S(1)}, u32[]{:S(2)}, u32[]{:S(2)}) %collective-permute-start.18) | collective-permute-done | bytes 106528 | tf_op jit(solution)/shard_map/ppermute | solution.py:563
  129.5 0.5 collective-permute-start.23
  130.1 0.6 collective-permute-done.22.refs_6_
  130.6 0.2 collective-permute-done.23.refs_7_
  130.9 0.3 copy-done.12
  131.2 0.6 copy-done.13
  131.8 1.9 %finish.1 = (f32[32,416]{1,0:T(8,128)}, f32[13,32]{1,0:T(8,128)}, f32[1,32]{1,0:T(1,128)}, f32[4,32,256]{2,1,0:T(8,128)}, f32[4,16]{1,0:T(4,128)}, /*index=5*/f3...) custom-call(s32[1]{0:T(128)} %bitcast.core_ref.tab_ref, ...), custom_call_target="tpu_custom_call" | custom-call | tf_op jit(solution)/shard_map/finish/pallas_call | solution.py:553
  (44 shorter events, 0.1 us)
Async XLA Ops:
  3.0 9.2 %collective-permute-start.4 = (bf16[32,1664]{1,0:T(8,128)(2,1)}, bf16[32,1664]{1,0:T(8,128)(2,1)S(1)}, u32[]{:S(2)}, u32[]{:S(2)}) collective-permute-start(bf16[32,1664]{1,0:T(8,128)(2,1)} %get-tuple-element.50), channel_id=1, source_target_pairs={{0,24},{2,26},{4,28},{6,30},{8,16},{10,18},{12,20},{14,22},{16,8},... | collective-permute-start | bytes 319496 | tf_op jit(solution)/shard_map/ppermute | solution.py:563
  8.0 9.2 %collective-permute-start.3 = (bf16[32,1664]{1,0:T(8,128)(2,1)}, bf16[32,1664]{1,0:T(8,128)(2,1)S(1)}, u32[]{:S(2)}, u32[]{:S(2)}) collective-permute-start(bf16[32,1664]{1,0:T(8,128)(2,1)} %get-tuple-element.50), channel_id=1, source_target_pairs={{0,16},{2,18},{4,20},{6,22},{8,24},{10,26},{12,28},{14,30},{16,0},... | collective-permute-start | bytes 319496 | tf_op jit(solution)/shard_map/ppermute | solution.py:563
  8.0 9.2 %collective-permute-start.2 = (bf16[32,1664]{1,0:T(8,128)(2,1)}, bf16[32,1664]{1,0:T(8,128)(2,1)S(1)}, u32[]{:S(2)}, u32[]{:S(2)}) collective-permute-start(bf16[32,1664]{1,0:T(8,128)(2,1)} %get-tuple-element.50), channel_id=1, source_target_pairs={{0,8},{2,10},{4,12},{6,14},{8,0},{10,2},{12,4},{14,6},{16,24},{18,... | collective-permute-start | bytes 319496 | tf_op jit(solution)/shard_map/ppermute | solution.py:563
  18.2 12.7 %collective-permute-start.5 = (bf16[4,32,1664]{2,1,0:T(8,128)(2,1)S(1)}, bf16[4,32,1664]{2,1,0:T(8,128)(2,1)S(1)}, u32[]{:S(2)}, u32[]{:S(2)}) collective-permute-start(bf16[4,32,1664]{2,1,0:T(8,128)(2,1)S(1)} %pad_maximum_fusion.refs_7_), channel_id=1, source_target_pairs={{0,2},{1,5},{2,0},{3,7},{4,6},{5,1},{6,4},{7,3},{8,10},{9,13},{10,... | collective-permute-start | bytes 1277960 | tf_op jit(solution)/shard_map/ppermute | solution.py:568
  19.8 11.8 %collective-permute-start.6 = (bf16[4,32,1664]{2,1,0:T(8,128)(2,1)S(1)}, bf16[4,32,1664]{2,1,0:T(8,128)(2,1)S(1)}, u32[]{:S(2)}, u32[]{:S(2)}) collective-permute-start(bf16[4,32,1664]{2,1,0:T(8,128)(2,1)S(1)} %pad_maximum_fusion.refs_7_), channel_id=1, source_target_pairs={{0,4},{1,3},{2,6},{3,1},{4,0},{5,7},{6,2},{7,5},{8,12},{9,11},{10,... | collective-permute-start | bytes 1277960 | tf_op jit(solution)/shard_map/ppermute | solution.py:568
  30.9 8.1 %collective-permute-start.7 = (bf16[4,32,1664]{2,1,0:T(8,128)(2,1)S(1)}, bf16[4,32,1664]{2,1,0:T(8,128)(2,1)S(1)}, u32[]{:S(2)}, u32[]{:S(2)}) collective-permute-start(bf16[4,32,1664]{2,1,0:T(8,128)(2,1)S(1)} %collective-permute-done.5.refs_8_), channel_id=1, source_target_pairs={{0,4},{1,3},{2,6},{3,1},{4,0},{5,7},{6,2},{7,5},{8,12},{9,11},{10,... | collective-permute-start | bytes 1277960 | tf_op jit(solution)/shard_map/ppermute | solution.py:568
  31.0 10.8 %collective-permute-start.1 = (bf16[16,128]{1,0:T(8,128)(2,1)}, bf16[16,128]{1,0:T(8,128)(2,1)S(1)}, u32[]{:S(2)}, u32[]{:S(2)}) collective-permute-start(bf16[16,128]{1,0:T(8,128)(2,1)} %get-tuple-element.49.token_ref.refs_5_), channel_id=1, source_target_pairs={{0,1},{1,0},{2,3},{3,2},{4,5},{5,4},{6,7},{7,6},{8,9},{9,8},{10,11... | collective-permute-start | bytes 12296 | tf_op jit(solution)/shard_map/ppermute | solution.py:572
  31.0 10.8 %copy-start.4 = (s32[1,6144]{1,0:T(1,128)S(1)}, s32[1,6144]{1,0:T(1,128)}, u32[]{:S(2)}) copy-start(s32[1,6144]{1,0:T(1,128)} %refs_2_.3) | copy-start | bytes 73732
  31.0 12.2 %copy-start.5 = (bf16[16,128]{1,0:T(8,128)(2,1)S(1)}, bf16[16,128]{1,0:T(8,128)(2,1)}, u32[]{:S(2)}) copy-start(bf16[16,128]{1,0:T(8,128)(2,1)} %get-tuple-element.49.token_ref.refs_5_) | copy-start | bytes 12292
  31.0 12.2 %collective-permute-start.8 = (bf16[4,32,1664]{2,1,0:T(8,128)(2,1)S(1)}, bf16[4,32,1664]{2,1,0:T(8,128)(2,1)S(1)}, u32[]{:S(2)}, u32[]{:S(2)}) collective-permute-start(bf16[4,32,1664]{2,1,0:T(8,128)(2,1)S(1)} %pad_maximum_fusion.refs_7_), channel_id=1, source_target_pairs={{0,1},{1,0},{2,3},{3,2},{4,5},{5,4},{6,7},{7,6},{8,9},{9,8},{10,11... | collective-permute-start | bytes 1277960 | tf_op jit(solution)/shard_map/ppermute | solution.py:572
  31.5 11.7 %collective-permute-start.9 = (bf16[4,32,1664]{2,1,0:T(8,128)(2,1)S(1)}, bf16[4,32,1664]{2,1,0:T(8,128)(2,1)S(1)}, u32[]{:S(2)}, u32[]{:S(2)}) collective-permute-start(bf16[4,32,1664]{2,1,0:T(8,128)(2,1)S(1)} %collective-permute-done.5.refs_8_), channel_id=1, source_target_pairs={{0,1},{1,0},{2,3},{3,2},{4,5},{5,4},{6,7},{7,6},{8,9},{9,8},{10,11... | collective-permute-start | bytes 1277960 | tf_op jit(solution)/shard_map/ppermute | solution.py:572
  31.6 11.6 %collective-permute-start.10 = (bf16[4,32,1664]{2,1,0:T(8,128)(2,1)S(1)}, bf16[4,32,1664]{2,1,0:T(8,128)(2,1)S(1)}, u32[]{:S(2)}, u32[]{:S(2)}) collective-permute-start(bf16[4,32,1664]{2,1,0:T(8,128)(2,1)S(1)} %collective-permute-done.6.refs_9_), channel_id=1, source_target_pairs={{0,1},{1,0},{2,3},{3,2},{4,5},{5,4},{6,7},{7,6},{8,9},{9,8},{10,11... | collective-permute-start | bytes 1277960 | tf_op jit(solution)/shard_map/ppermute | solution.py:572
  39.0 4.2 %collective-permute-start.11 = (bf16[4,32,1664]{2,1,0:T(8,128)(2,1)S(1)}, bf16[4,32,1664]{2,1,0:T(8,128)(2,1)S(1)}, u32[]{:S(2)}, u32[]{:S(2)}) collective-permute-start(bf16[4,32,1664]{2,1,0:T(8,128)(2,1)S(1)} %collective-permute-done.7.refs_10_), channel_id=1, source_target_pairs={{0,1},{1,0},{2,3},{3,2},{4,5},{5,4},{6,7},{7,6},{8,9},{9,8},{10,11... | collective-permute-start | bytes 1277960 | tf_op jit(solution)/shard_map/ppermute | solution.py:572
  41.8 1.4 %collective-permute-start = (s32[1,6144]{1,0:T(1,128)S(1)}, s32[1,6144]{1,0:T(1,128)S(1)}, u32[]{:S(2)}, u32[]{:S(2)}) collective-permute-start(s32[1,6144]{1,0:T(1,128)S(1)} %copy-done.4), channel_id=1, source_target_pairs={{0,1},{1,0},{2,3},{3,2},{4,5},{5,4},{6,7},{7,6},{8,9},{9,8},{10,11... | collective-permute-start | bytes 73736 | tf_op jit(solution)/shard_map/ppermute | solution.py:572
  43.2 0.9 copy-start.3
  44.2 0.7 copy-start.6
  93.1 2.4 %collective-permute-start.12 = (bf16[8,32,1664]{2,1,0:T(8,128)(2,1)S(1)}, bf16[8,32,1664]{2,1,0:T(8,128)(2,1)S(1)}, u32[]{:S(2)}, u32[]{:S(2)}) collective-permute-start(bf16[8,32,1664]{2,1,0:T(8,128)(2,1)S(1)} %get-tuple-element.52), channel_id=1, source_target_pairs={{0,1},{1,0},{2,3},{3,2},{4,5},{5,4},{6,7},{7,6},{8,9},{9,8},{10,11... | collective-permute-start | bytes 2555912 | tf_op jit(solution)/shard_map/ppermute | solution.py:572
  95.5 1.5 %copy-start = (bf16[16,32,1664]{2,1,0:T(8,128)(2,1)S(1)}, bf16[16,32,1664]{2,1,0:T(8,128)(2,1)}, u32[]{:S(2)}) copy-start(bf16[16,32,1664]{2,1,0:T(8,128)(2,1)} %get-tuple-element.51.refs_0_) | copy-start | bytes 5111812
  97.2 15.2 %collective-permute-start.13 = (bf16[512,3072]{1,0:T(8,128)(2,1)}, bf16[512,3072]{1,0:T(8,128)(2,1)S(1)}, u32[]{:S(2)}, u32[]{:S(2)}) collective-permute-start(bf16[512,3072]{1,0:T(8,128)(2,1)} %get-tuple-element.54.hg_ref), channel_id=1, source_target_pairs={{0,1},{1,0},{2,3},{3,2},{4,5},{5,4},{6,7},{7,6},{8,9},{9,8},{10,11... | collective-permute-start | bytes 9437192 | tf_op jit(solution)/shard_map/ppermute | solution.py:572
  97.6 6.8 %collective-permute-start.14 = (bf16[8,32,1664]{2,1,0:T(8,128)(2,1)S(1)}, bf16[8,32,1664]{2,1,0:T(8,128)(2,1)S(1)}, u32[]{:S(2)}, u32[]{:S(2)}) collective-permute-start(bf16[8,32,1664]{2,1,0:T(8,128)(2,1)S(1)} %get-tuple-element.56), channel_id=1, source_target_pairs={{0,1},{1,0},{2,3},{3,2},{4,5},{5,4},{6,7},{7,6},{8,9},{9,8},{10,11... | collective-permute-start | bytes 2555912 | tf_op jit(solution)/shard_map/ppermute | solution.py:572
  97.8 12.7 %collective-permute-start.15 = (bf16[8,32,1664]{2,1,0:T(8,128)(2,1)S(1)}, bf16[8,32,1664]{2,1,0:T(8,128)(2,1)S(1)}, u32[]{:S(2)}, u32[]{:S(2)}) collective-permute-start(bf16[8,32,1664]{2,1,0:T(8,128)(2,1)S(1)} %get-tuple-element.57.refs_0_), channel_id=1, source_target_pairs={{0,4},{1,3},{2,6},{3,1},{4,0},{5,7},{6,2},{7,5},{8,12},{9,11},{10,... | collective-permute-start | bytes 2555912 | tf_op jit(solution)/shard_map/ppermute | solution.py:568
  97.9 12.6 %copy-start.1 = (bf16[16,32,1664]{2,1,0:T(8,128)(2,1)S(1)}, bf16[16,32,1664]{2,1,0:T(8,128)(2,1)}, u32[]{:S(2)}) copy-start(bf16[16,32,1664]{2,1,0:T(8,128)(2,1)} %get-tuple-element.51.refs_0_) | copy-start | bytes 5111812
  110.8 8.2 %collective-permute-start.16 = (bf16[4,32,1664]{2,1,0:T(8,128)(2,1)S(1)}, bf16[4,32,1664]{2,1,0:T(8,128)(2,1)S(1)}, u32[]{:S(2)}, u32[]{:S(2)}) collective-permute-start(bf16[4,32,1664]{2,1,0:T(8,128)(2,1)S(1)} %get-tuple-element.59.refs_0_), channel_id=1, source_target_pairs={{0,2},{1,5},{2,0},{3,7},{4,6},{5,1},{6,4},{7,3},{8,10},{9,13},{10,... | collective-permute-start | bytes 1277960 | tf_op jit(solution)/shard_map/ppermute | solution.py:568
  119.1 11.8 %copy-start.2 = (bf16[32,1664]{1,0:T(8,128)(2,1)}, bf16[32,1664]{1,0:T(8,128)(2,1)S(1)}, u32[]{:S(2)}) copy-start(bf16[32,1664]{1,0:T(8,128)(2,1)S(1)} %get-tuple-element.66.token_ref.refs_0_) | copy-start | bytes 319492
  119.1 4.8 %collective-permute-start.17 = (bf16[32,1664]{1,0:T(8,128)(2,1)S(1)}, bf16[32,1664]{1,0:T(8,128)(2,1)S(1)}, u32[]{:S(2)}, u32[]{:S(2)}) collective-permute-start(bf16[32,1664]{1,0:T(8,128)(2,1)S(1)} %get-tuple-element.67), channel_id=1, source_target_pairs={{0,8},{2,10},{4,12},{6,14},{8,0},{10,2},{12,4},{14,6},{16,24},{18,... | collective-permute-start | bytes 319496 | tf_op jit(solution)/shard_map/ppermute | solution.py:563
  119.5 10.0 %collective-permute-start.18 = (bf16[32,1664]{1,0:T(8,128)(2,1)S(1)}, bf16[32,1664]{1,0:T(8,128)(2,1)S(1)}, u32[]{:S(2)}, u32[]{:S(2)}) collective-permute-start(bf16[32,1664]{1,0:T(8,128)(2,1)S(1)} %get-tuple-element.68), channel_id=1, source_target_pairs={{0,16},{2,18},{4,20},{6,22},{8,24},{10,26},{12,28},{14,30},{16,0},... | collective-permute-start | bytes 319496 | tf_op jit(solution)/shard_map/ppermute | solution.py:563
  122.2 7.2 %collective-permute-start.19 = (bf16[32,1664]{1,0:T(8,128)(2,1)S(1)}, bf16[32,1664]{1,0:T(8,128)(2,1)S(1)}, u32[]{:S(2)}, u32[]{:S(2)}) collective-permute-start(bf16[32,1664]{1,0:T(8,128)(2,1)S(1)} %get-tuple-element.69), channel_id=1, source_target_pairs={{0,24},{2,26},{4,28},{6,30},{8,16},{10,18},{12,20},{14,22},{16,8},... | collective-permute-start | bytes 319496 | tf_op jit(solution)/shard_map/ppermute | solution.py:563
  123.5 6.5 %collective-permute-start.20 = (bf16[16,512]{1,0:T(8,128)(2,1)S(1)}, bf16[16,512]{1,0:T(8,128)(2,1)S(1)}, u32[]{:S(2)}, u32[]{:S(2)}) collective-permute-start(bf16[16,512]{1,0:T(8,128)(2,1)S(1)} %slice.12), channel_id=1, source_target_pairs={{0,1},{1,0},{2,3},{3,2},{4,5},{5,4},{6,7},{7,6},{8,9},{9,8},{10,11... | collective-permute-start | bytes 49160 | tf_op jit(solution)/shard_map/ppermute | solution.py:572
  123.9 7.0 %copy-start.7 = (bf16[32,1664]{1,0:T(8,128)(2,1)}, bf16[32,1664]{1,0:T(8,128)(2,1)S(1)}, u32[]{:S(2)}) copy-start(bf16[32,1664]{1,0:T(8,128)(2,1)S(1)} %collective-permute-done.17.refs_1_) | copy-start | bytes 319492
  123.9 6.2 %collective-permute-start.21 = (bf16[16,512]{1,0:T(8,128)(2,1)S(1)}, bf16[16,512]{1,0:T(8,128)(2,1)S(1)}, u32[]{:S(2)}, u32[]{:S(2)}) collective-permute-start(bf16[16,512]{1,0:T(8,128)(2,1)S(1)} %slice.16), channel_id=1, source_target_pairs={{0,1},{1,0},{2,3},{3,2},{4,5},{5,4},{6,7},{7,6},{8,9},{9,8},{10,11... | collective-permute-start | bytes 49160 | tf_op jit(solution)/shard_map/ppermute | solution.py:572
  129.5 1.4 %copy-start.8 = (bf16[32,1664]{1,0:T(8,128)(2,1)}, bf16[32,1664]{1,0:T(8,128)(2,1)S(1)}, u32[]{:S(2)}) copy-start(bf16[32,1664]{1,0:T(8,128)(2,1)S(1)} %collective-permute-done.18.refs_2_) | copy-start | bytes 319492
  129.5 1.2 collective-permute-start.22
  129.5 1.4 %copy-start.9 = (bf16[32,1664]{1,0:T(8,128)(2,1)}, bf16[32,1664]{1,0:T(8,128)(2,1)S(1)}, u32[]{:S(2)}) copy-start(bf16[32,1664]{1,0:T(8,128)(2,1)S(1)} %collective-permute-done.19.refs_3_) | copy-start | bytes 319492
  129.5 1.4 %collective-permute-start.23 = (bf16[16,512]{1,0:T(8,128)(2,1)S(1)}, bf16[16,512]{1,0:T(8,128)(2,1)S(1)}, u32[]{:S(2)}, u32[]{:S(2)}) collective-permute-start(bf16[16,512]{1,0:T(8,128)(2,1)S(1)} %slice.18), channel_id=1, source_target_pairs={{0,1},{1,0},{2,3},{3,2},{4,5},{5,4},{6,7},{7,6},{8,9},{9,8},{10,11... | collective-permute-start | bytes 49160 | tf_op jit(solution)/shard_map/ppermute | solution.py:572
  130.0 0.9 copy-start.10
  130.1 0.9 copy-start.11
  130.6 0.6 copy-start.12
  131.2 0.6 copy-start.13

commit v5 on v4

--- a/solution.py
+++ b/solution.py
@@ -74,15 +74,15 @@
         going = left
 
 
-def main_kernel(pieces, chunks, tab_ref, *refs):
-    emb_ref, dense_ref, lab_ref, far_lab_ref, row_ref, vec_ref, far_vec_ref = refs[:7]
-    u_refs = (refs[7 : 7 + pieces], refs[7 + pieces : 7 + 2 * pieces])
-    hg_ref, wat_s, du_own_ref, *du_far_refs = refs[7 + 2 * pieces : 12 + 2 * pieces]
+def main_kernel(pieces, chunks, rows, batch_rows, tab_ref, *refs):
+    emb_ref, dense_ref, line_ref, far_line_ref = refs[:4]
+    u_refs = (refs[4 : 4 + pieces], refs[4 + pieces : 4 + 2 * pieces])
+    hg_ref, wat_s, *du_refs = refs[4 + 2 * pieces : 10 + 2 * pieces]
     (
         x_s, hid_s, mid_s, sl1_s, out_s, sl2_s, sg_s, fg_s, mix_s,
         w1_s, w1t_s, ga_s, w2t_s, w2_s, b1_s, b2_s, gb_s, tt_s, tw_s, tcol_s, q_s,
-        dwa_s, dw1_s, dw2_s, dtw_s, dcol_s, dlog_s, dsm_s, u_s, sem,
-    ) = refs[12 + 2 * pieces :]
+        dwa_s, dw1_s, dw2_s, dtw_s, dcol_s, dlog_s, dsm_s, dense_s, start_s, row_s, sem,
+    ) = refs[10 + 2 * pieces :]
     n = SUB
     fs, osz, ds = FH // chunks, EO // chunks, D // chunks
     step = pl.program_id(0)
@@ -91,17 +91,14 @@
 
     @pl.when(step == 0)
     def _():
-        copies = [[], []]
-        for side in range(2):
-            at = 0
-            for j, ref in enumerate(u_refs[side]):
-                copies[side].append(pltpu.make_async_copy(ref, u_s.at[side, pl.ds(at, ref.shape[0])], sem.at[pieces * side + j]))
-                copies[side][-1].start()
-                at += ref.shape[0]
-        rows = lax.broadcasted_iota(jnp.int32, (32, n), 0)
+        half = dense_s.shape[1]
+        mine = dense_ref.at[:, pl.ds(pl.multiple_of(core * half, half), half)]
+        dense_copy = pltpu.make_async_copy(mine, dense_s, sem)
+        dense_copy.start()
+        row_number = lax.broadcasted_iota(jnp.int32, (32, n), 0)
         ones = jnp.where(lax.broadcasted_iota(jnp.int32, (16, n), 0) == 0, 1.0, 0.0).astype(BF)
         for h in range(TILE // SUB):
-            x_s[h, EMB:XR, :] = jnp.where(rows == DENSE, 1.0, 0.0).astype(BF)
+            x_s[h, EMB:XR, :] = jnp.where(row_number == DENSE, 1.0, 0.0).astype(BF)
             hid_s[h, D : D + 16, :] = ones
             for k in range(NE):
                 mid_s[h, k, FH : FH + 16, :] = ones
@@ -109,21 +106,24 @@
             fg_s[h, NE * FH + 16 : FG, :] = jnp.zeros((FG - NE * FH - 16, n), BF)
         for ref in (dwa_s, dw1_s, dw2_s, dtw_s, dcol_s, dlog_s):
             ref[...] = jnp.zeros_like(ref)
+        users = start_s.shape[1]
+        sizes = [line_ref[:, rows + 512 + users * b : rows + 512 + users * b + users] for b in range(start_s.shape[0])]
+        fill_weights(core, batch_rows, jnp.concatenate(sizes, axis=0), start_s, row_s)
+        dense_copy.wait()
         gates = []
         for side in range(2):
-            for copy in copies[side]:
-                copy.wait()
             base = HALF * FH * side
             holder = core if side == 0 else 1 - core
             for c in range(chunks):
+                ref, c_in = u_refs[side][c * pieces // chunks], c % (chunks // pieces)
                 at = chunk_at(c, chunks, holder)
                 to = pl.multiple_of(ds * at, ds)
-                w1_s[pl.ds(to, ds), base : base + QA] = u_s[side, c, :, 0:QA]
-                q_s[tab_ref[1 + at]] = u_s[side, c, 0:fs, QA:UC].astype(F32)
-                small = u_s[side, c, 0:fs, QS:UC].astype(F32)
+                w1_s[pl.ds(to, ds), base : base + QA] = ref[c_in, :, 0:QA]
+                q_s[tab_ref[1 + at]] = ref[c_in, 0:fs, QA:UC].astype(F32)
+                small = ref[c_in, 0:fs, QS:UC].astype(F32)
                 ga_s[pl.ds(to, fs), :] = small
                 ga_s[pl.ds(pl.multiple_of(to + fs, fs), fs), :] = pltpu.roll(small, 128 - NE, 1)
-                wat_s[pl.ds(pl.multiple_of(to + holder * fs, fs), fs), :] = u_s[side, c, fs:ds, QA : QA + XR]
+                wat_s[pl.ds(pl.multiple_of(to + holder * fs, fs), fs), :] = ref[c_in, fs:ds, QA : QA + XR]
             for k in range(HALF):
                 block = w1_s[:, base + FH * k : base + FH * k + FH]
                 w1t_s[base + FH * k : base + FH * k + FH, :] = (block.astype(F32).T * 0.5).astype(BF)
@@ -144,7 +144,7 @@
         w1t_s[NE * FH : NE * FH + 16, :] = gates.astype(BF)
         pad = jnp.concatenate([gates, jnp.zeros((112, D), F32)], axis=0)
         w1_s[:, NE * FH : FG] = pad.T.astype(BF)
-        vecs = [jnp.concatenate([r[...].astype(F32), jnp.zeros((112, 128), F32)], axis=0).T for r in (vec_ref, far_vec_ref)]
+        vecs = [square([r[:, rows + 128 * j : rows + 128 * j + 128] for j in range(4)]).T for r in (line_ref, far_line_ref)]
         gb_s[...] = jnp.concatenate([swap_halves(v[0:NE, 0:1], second_core) for v in vecs], axis=0)
         b1 = jnp.concatenate([v[0:TW, 1:2] for v in vecs], axis=0)
         head = jnp.concatenate([v[0:TW, 2:3] for v in vecs], axis=0)
@@ -154,7 +154,7 @@
     def chain(h):
         at = slice(SUB * h, SUB * h + SUB)
         x_s[h, 0:EMB, :] = emb_ref[:, at]
-        x_s[h, EMB : EMB + DENSE, :] = dense_ref[:, at]
+        x_s[h, EMB : EMB + DENSE, :] = dense_s[:, pl.ds(pl.multiple_of(step * TILE + SUB * h, SUB), SUB)]
         hid = mm(wat_s[...], x_s[h]).astype(BF)
         hid_s[h, 0:D, :] = hid
         yield
@@ -195,8 +195,8 @@
         lgos = []
         for t in range(2):
             logit = jnp.sum(weighted[TW * t : TW * t + TW], axis=0, keepdims=True) + tcol_s[t : t + 1, 3:4]
-            label = (lab_ref, far_lab_ref)[t][:, at].astype(F32)
-            lgos.append(row_ref[:, at] * (0.5 * jnp.tanh(0.5 * logit) + 0.5 - label))
+            label = (line_ref, far_line_ref)[t][:, pl.ds(pl.multiple_of((core * pl.num_programs(0) + step) * TILE + SUB * h, SUB), SUB)]
+            lgos.append(row_s[:, pl.ds(pl.multiple_of(step * TILE + SUB * h, SUB), SUB)] * (0.5 * jnp.tanh(0.5 * logit) + 0.5 - label))
         lgo = jnp.concatenate([jnp.broadcast_to(lgos[t], (TW, SUB)) for t in range(2)], axis=0)
         dcol_s[...] += lane_fold(lgo * act)
         dlog_s[...] += lane_fold(jnp.concatenate([jnp.broadcast_to(lgos[t], (8, SUB)) for t in range(2)], axis=0))
@@ -270,9 +270,7 @@
             holder = core if side == 0 else 1 - core
             cols = HALF * EO
             for n in range(chunks):
-                ref, c = du_own_ref, n
-                if side == 1:
-                    ref, c = du_far_refs[n * 2 // chunks], n % max(chunks // 2, 1)
+                ref, c = du_refs[2 * side + n * 2 // chunks], n % max(chunks // 2, 1)
                 at = chunk_at(n, chunks, holder)
                 to = pl.multiple_of(ds * at, ds)
                 where = pl.ds(pl.multiple_of(tab_ref[1 + at] * fs, fs), fs)
@@ -285,9 +283,9 @@
                 ref[c, fs:ds, QA:UC] = jnp.concatenate([lower, jnp.zeros((fs, UC - QA - XR), F32)], axis=1).astype(BF)
 
 
-def weight_kernel(batch_rows, tab_ref, sizes_ref, token_ref, out_ref, start_s):
-    batches, users = sizes_ref.shape
-    counts = jnp.concatenate([sizes_ref[...].astype(F32), jnp.zeros((16 - batches, users), F32)], axis=0)
+def fill_weights(core, batch_rows, sizes, start_s, out_ref):
+    batches, users = sizes.shape
+    counts = jnp.concatenate([sizes.astype(F32), jnp.zeros((16 - batches, users), F32)], axis=0)
     turned = jnp.concatenate([counts, jnp.zeros((112, users), F32)], axis=0).T
     before = lax.broadcasted_iota(jnp.int32, (users, users), 1) < lax.broadcasted_iota(jnp.int32, (users, users), 0)
     starts = mm(jnp.where(before, 1.0, 0.0).astype(BF), turned.astype(BF))
@@ -298,7 +296,7 @@
     line = lax.broadcasted_iota(jnp.int32, counts.shape, 0)
     steps = out_ref.shape[1] // SUB
     for step in range(steps):
-        at_step = tab_ref[0] * steps + step
+        at_step = core * steps + step
         batch = at_step // (batch_rows // SUB)
         first_row = (at_step % (batch_rows // SUB) * SUB).astype(F32)
         begins = start_s[batch]
@@ -309,24 +307,11 @@
         out_ref[:, SUB * step : SUB * step + SUB] = 1.0 / size
 
 
-def weight_call(table, sizes, rows, token):
-    batches, users = sizes.shape
-    return pl.pallas_call(
-        functools.partial(weight_kernel, rows // batches),
-        in_specs=[whole(pltpu.SMEM), whole(), whole(pl.ANY)],
-        out_specs=whole(),
-        out_shape=jax.ShapeDtypeStruct((1, rows // 2), F32),
-        scratch_shapes=[pltpu.VMEM((batches, users, 128), F32)],
-        cost_estimate=pl.CostEstimate(flops=3_000_000_000, bytes_accessed=1_000_000, transcendentals=0),
-        name="row_weights",
-    )(table, sizes, token)
-
-
 def const2(i, c):
     return (0, 0)
 
 
-def main_call(table, embt, denset, labels, far_labels, row_weights, vec, far_vec, own_u, far_u):
+def main_call(table, embt, denset, line, far_line, sizes_shape, own_u, far_u):
     rows = embt.shape[1]
     half = rows // 2
     steps = half // TILE
@@ -337,22 +322,19 @@
     def own(i, c):
         return (0, c[0] * steps + i)
 
-    grads = [(chunks, ds, UC)] + [(max(chunks // 2, 1), ds, UC)] * 2
+    grads = [(max(chunks // 2, 1), ds, UC)] * 4
     parts = TILE // SUB
     spec = pltpu.PrefetchScalarGridSpec(
         num_scalar_prefetch=1,
         grid=(steps,),
         in_specs=[
             pl.BlockSpec((EMB, TILE), own),
-            pl.BlockSpec((DENSE, TILE), own),
-            pl.BlockSpec((1, TILE), own),
-            pl.BlockSpec((1, TILE), own),
-            pl.BlockSpec((1, TILE), lambda i, c: (0, i)),
+            whole(pltpu.HBM),
             whole(),
             whole(),
         ]
-        + [whole(pltpu.HBM) for _ in (*own_u, *far_u)],
-        out_specs=[pl.BlockSpec((D, TILE), lambda i, c: (0, i))] + [whole()] * 4,
+        + [whole() for _ in (*own_u, *far_u)],
+        out_specs=[pl.BlockSpec((D, TILE), lambda i, c: (0, i))] + [whole()] * 5,
         scratch_shapes=[
             pltpu.VMEM((parts, XR, SUB), BF),
             pltpu.VMEM((parts, D + 16, SUB), BF),
@@ -382,19 +364,21 @@
             pltpu.VMEM((2 * TW, 128), F32),
             pltpu.VMEM((16, 128), F32),
             pltpu.VMEM((FH, 128), F32),
-            pltpu.VMEM((2, chunks, ds, UC), BF),
-            pltpu.SemaphoreType.DMA((2 * pieces,)),
+            pltpu.VMEM((DENSE, half), BF),
+            pltpu.VMEM((*sizes_shape, 128), F32),
+            pltpu.VMEM((1, half), F32),
+            pltpu.SemaphoreType.DMA(()),
         ],
     )
     return pl.pallas_call(
-        functools.partial(main_kernel, pieces, chunks),
+        functools.partial(main_kernel, pieces, chunks, rows, rows // sizes_shape[0]),
         grid_spec=spec,
         out_shape=[jax.ShapeDtypeStruct((D, half), BF), jax.ShapeDtypeStruct((D, XR), BF)]
         + [jax.ShapeDtypeStruct(a, BF) for a in grads],
         compiler_params=pltpu.CompilerParams(vmem_limit_bytes=48 * 1024 * 1024),
         cost_estimate=pl.CostEstimate(flops=50_000_000_000, bytes_accessed=24_000_000, transcendentals=0),
         name="experts",
-    )(table, embt, denset, labels, far_labels, row_weights, vec, far_vec, *own_u, *far_u)
+    )(table, embt, denset, line, far_line, *own_u, *far_u)
 
 
 def input_kernel(tab_ref, hg_ref, wat_ref, *refs):
@@ -447,13 +431,15 @@
     return jnp.concatenate(rows + [jnp.zeros((128 - count, 128), F32)], axis=0)
 
 
-def pack_vec(gb_ref, t1_ref, t2_ref, t3_ref):
-    return jnp.concatenate([widen(r[...]) for r in (gb_ref, t1_ref, t2_ref, t3_ref)] + [jnp.zeros((12, 128), F32)], axis=0).astype(BF)
-
-
 def pack_kernel(core_ref, emb_ref, dense_ref, bias_ref, w1_ref, w2_ref, b1_ref, b2_ref, gate_ref, tower_ref, *refs):
-    u_ref, vec_ref = refs[4:]
-    vec_ref[...] = pack_vec(*refs[:4])
+    sizes_ref, label_ref, u_ref, line_ref = refs[4:]
+    rows = label_ref.shape[1]
+    line_ref[:, 0:rows] = label_ref[...].astype(F32)
+    for j in range(4):
+        line_ref[:, rows + 128 * j : rows + 128 * j + 128] = widen(refs[j][...])
+    users = sizes_ref.shape[1]
+    for b in range(sizes_ref.shape[0]):
+        line_ref[:, rows + 512 + users * b : rows + 512 + users * b + users] = sizes_ref[b : b + 1, :].astype(F32)
     fs = u_ref.shape[0] // 2
     turned = square([widen(r[...]) for r in (b1_ref, b2_ref, gate_ref, dense_ref, bias_ref)]).T
     lane = lax.broadcasted_iota(jnp.int32, (fs, 128), 1)
@@ -486,7 +472,7 @@
         pack_kernel,
         in_specs=[whole(pltpu.SMEM)] + [whole() for _ in parts],
         out_specs=[whole(), whole()],
-        out_shape=[jax.ShapeDtypeStruct((ds, UC), BF), jax.ShapeDtypeStruct((16, 128), BF)],
+        out_shape=[jax.ShapeDtypeStruct((ds, UC), BF), jax.ShapeDtypeStruct((1, parts[-1].shape[1] + 512 + parts[-2].size), F32)],
         name="pack",
     )(core, *parts)
 
@@ -510,7 +496,7 @@
         out_specs=[whole(pl.ANY) for _ in lead] + [whole() for _ in shapes],
         out_shape=[jax.ShapeDtypeStruct(a.shape, a.dtype) for a in lead] + [jax.ShapeDtypeStruct(a, BF) for a in shapes],
         input_output_aliases={len(arrays) + len(extra) - 1: 0} if lead else {},
-        compiler_params=pltpu.CompilerParams(vmem_limit_bytes=32 * 1024 * 1024),
+        compiler_params=pltpu.CompilerParams(vmem_limit_bytes=16 * 1024 * 1024),
         name=name,
     )(*arrays, *extra)
 
@@ -555,6 +541,7 @@
         in_specs=[whole(pltpu.SMEM), whole(pl.ANY)] + [whole() for _ in arrays],
         out_specs=[whole() for _ in shapes],
         out_shape=[jax.ShapeDtypeStruct(a, F32) for a in shapes],
+        compiler_params=pltpu.CompilerParams(vmem_limit_bytes=8 * 1024 * 1024),
         name="finish",
     )(core, token, *arrays)
 
@@ -590,16 +577,14 @@
     user_count = group_sizes.shape[1] * group_sizes.shape[0] * size
     ds, fs, osz = D // size, FH // size, EO // size
     fast = size == 16
-    far_labels = partner(labels)
     smalls = (gate_b, tower_b1, tower_w2, tower_b2[None])
 
     if fast:
         one_core = core[None].astype(jnp.int32)
         gate_t = jnp.transpose(gate_w, (0, 2, 1))[0]
-        shard, vec = pack_call(
-            one_core, w_emb.T, w_dense, b_in[None], expert_w1, expert_w2, expert_b1, expert_b2, gate_t, tower_w1[0], *smalls
+        shard, line = pack_call(
+            one_core, w_emb.T, w_dense, b_in[None], expert_w1, expert_w2, expert_b1, expert_b2, gate_t, tower_w1[0], *smalls, group_sizes, labels
         )
-        row_weights = weight_call(one_core, group_sizes, emb.shape[0], vec)
         near = jnp.stack([shard] + [hop(shard, 4 * a, size) for a in range(1, 4)])
         once = cross(near, (1, 2), size)
         own_u = [near, once, cross(near, (2, 1), size), cross(once, (2, 1), size)]
@@ -617,21 +602,21 @@
         lower = jnp.concatenate([part, jnp.zeros((FH, UC - QA - 512), BF)], axis=1)
         own_u = [jnp.concatenate([w1_all, jnp.concatenate([jnp.concatenate([w2_all, small], axis=1), lower], axis=0)], axis=1)[None]]
         order = jnp.zeros((1,), jnp.int32)
-        vec = jnp.concatenate([pad_to(a, 1, 128) for a in smalls] + [jnp.zeros((12, 128), BF)], axis=0)
-        row_weights = weight_call(core[None].astype(jnp.int32), group_sizes, emb.shape[0], vec)
+        line = [labels.astype(F32)] + [pad_to(a, 1, 128).astype(F32) for a in smalls]
+        line = jnp.concatenate(line + [group_sizes.astype(F32).reshape(1, -1)], axis=1)
     far_u = [partner(a) for a in own_u]
     table = jnp.concatenate([core[None].astype(jnp.int32), order])
 
-    hg, wat, du_own, du_low, du_high = main_call(table, emb.T, dense.T, labels, far_labels, row_weights, vec, partner(vec), own_u, far_u)
+    hg, wat, own_low, own_high, du_low, du_high = main_call(table, emb.T, dense.T, line, partner(line), group_sizes.shape, own_u, far_u)
     du_high = partner(du_high)
     scale = 1.0 / user_count
     if fast:
-        hg, part = sum_call("sum_cores", [du_own, du_high], [[(0, slice(8, 16)), (1, slice(0, 8))]], [(8, ds, UC)], through=hg)
+        hg, part = sum_call("sum_cores", [own_high, du_high], [[(0, slice(0, 8)), (1, slice(0, 8))]], [(8, ds, UC)], through=hg)
         got = cross(part, (2, 1), size)
         du_low, far_hg = partner(du_low), partner(hg)
         eg, dg, token = input_call(table, hg, wat, part, None, "input_own")
         groups = [[(j, slice(4 * b, 4 * b + 4)) for j in range(3)] for b in (1, 0)]
-        part, rest = sum_call("sum_first", [du_own, du_low, got], groups, [(4, ds, UC)] * 2, token)
+        part, rest = sum_call("sum_first", [own_low, du_low, got], groups, [(4, ds, UC)] * 2, token)
         got = cross(part, (1, 2), size)
         eg, dg, token = input_call(table, far_hg, wat, part, (eg, dg), "input_far")
         sums = sum_call("sum_second", [rest, got], [[(0, k), (1, k)] for k in range(4)], [(ds, UC)] * 4, token)
@@ -645,7 +630,7 @@
     eg, dg, token = input_call(table, hg, wat, du_high, None, "input_own")
     eg, dg, _ = input_call(table, partner(hg), wat, token, (eg, dg), "input_far")
     scatter = functools.partial(lax.psum_scatter, axis_name="rows", scatter_dimension=0, tiled=True)
-    wide = add_wide(du_own[0], partner(du_low)[0])
+    wide = add_wide(own_low[0], partner(du_low)[0])
     upper, near = wide[0:FH, QA:UC], wide[FH:, QA : QA + XR]
     far, small = partner(near), upper[:, HALF * EO :]
     ta = scatter(jnp.concatenate([jnp.where(core == 0, near, far), jnp.where(core == 0, far, near)], axis=0)) * scale

time: 134 us -> 127 us (0.948)
  Pallas kernels: 66.2 us -> 61.4 us
  local copies, waits for them, and re-layouts: 4.05 us -> 1.69 us
    pallas_call x2 -> x1, Pallas kernels: 50.9 us -> 47 us  [main_call(): pl.pallas_call(functools.partial(main_kernel, pieces, chunks, rows, rows...]
    unnamed x28 -> x4, local copies, waits for them, and re-layouts: 4.04 us -> 1.68 us
    ppermute x13 -> x12, starting transfers between devices: 3.35 us -> 2.55 us  [partner(): return lax.ppermute(a, 'task', [(0, 1), (1, 0)])]
    ppermute x13 -> x12, waiting for transfers between devices: 3.64 us -> 4.42 us  [partner(): return lax.ppermute(a, 'task', [(0, 1), (1, 0)])]
  transfers between devices with their start and end apart: 24 -> 23, of which waited for: 12 -> 13; matrix products, arithmetic and copies ran while one was open for 0% -> 0% of each run, Pallas kernels for 11% -> 9%
where the time goes in v5:
time: 127 us
  Pallas kernels  61.4 us (48%)
  waiting for transfers between devices  43.9 us (35%)
  starting transfers between devices  17.5 us (14%)
  local copies, waits for them, and re-layouts  1.69 us (1%)
  between operations  1.53 us (1%)
    pallas_call x1, Pallas kernels, main_call(): pl.pallas_call(functools.partial(main_kernel, pieces, chunks, rows, rows...  47 us
    ppermute x5, waiting for transfers between devices, cross(): return lax.ppermute(a, ('rows', 'task'), pairs)  25.3 us
    ppermute x6, waiting for transfers between devices, hop(): return lax.ppermute(a, 'rows', [(i, i ^ mask) for i in range(size)])  14.2 us
    pallas_call x2, Pallas kernels, input_call(): pl.pallas_call(input_kernel, grid_spec=spec, out_shape=[jax.ShapeDtypeStr...  11.1 us
    ppermute x6, starting transfers between devices, hop(): return lax.ppermute(a, 'rows', [(i, i ^ mask) for i in range(size)])  10.1 us
    ppermute x5, starting transfers between devices, cross(): return lax.ppermute(a, ('rows', 'task'), pairs)  4.8 us
    ppermute x12, waiting for transfers between devices, partner(): return lax.ppermute(a, 'task', [(0, 1), (1, 0)])  4.42 us
    ppermute x12, starting transfers between devices, partner(): return lax.ppermute(a, 'task', [(0, 1), (1, 0)])  2.55 us
  transfers between devices with their start and end apart: 23, of which 13 were waited for; matrix products, arithmetic and copies ran while one was open for 0% of the time, Pallas kernels for 9%

profile of v5, /device:TPU:0, one launch (start us, length us, event | category | flops | bytes accessed | tf_op | source)
XLA Modules:
  0.0 127.1 jit_solution(15189707080665815419)
XLA Ops:
  1.3 1.7 %pack.1 = (bf16[32,1664]{1,0:T(8,128)(2,1)}, f32[1,8192]{1,0:T(1,128)}) custom-call(s32[1]{0:T(128)} %bitcast.core_ref, bf16[32,416]{1,0:T(8,128)(2,1)} %bitcast.29, bf16[13,32]{1,0:T(8,128)(2,1)} %dense_ref.1, bf16[1,32]{1,0:T(2,128)(2,1)} %bitcast.32, bf16[4,32,256]{2,1,0:T(8,128)(2,1)} %w1_ref.1, bf16[4,16,128]{2,1,0:T(8,128)(2,1)} %w2_ref.1, ...), custom_call_target="tpu_custom_call" | custom-call | tf_op jit(solution)/shard_map/pack/pallas_call | solution.py:471
  3.0 5.0 %collective-permute-start.3 = (bf16[32,1664]{1,0:T(8,128)(2,1)}, bf16[32,1664]{1,0:T(8,128)(2,1)S(1)}, u32[]{:S(2)}, u32[]{:S(2)}) collective-permute-start(bf16[32,1664]{1,0:T(8,128)(2,1)} %get-tuple-element.51), channel_id=1, source_target_pairs={{0,24},{2,26},{4,28},{6,30},{8,16},{10,18},{12,20},{14,22},{16,8},... | collective-permute-start | bytes 319496 | tf_op jit(solution)/shard_map/ppermute | solution.py:550
  8.1 0.0 collective-permute-start.2
  8.1 0.6 collective-permute-start.1
  8.7 3.5 %collective-permute-done.3 = bf16[32,1664]{1,0:T(8,128)(2,1)S(1)} collective-permute-done((bf16[32,1664]{1,0:T(8,128)(2,1)}, bf16[32,1664]{1,0:T(8,128)(2,1)S(1)}, u32[]{:S(2)}, u32[]{:S(2)}) %collective-permute-start.3) | collective-permute-done | bytes 106528 | tf_op jit(solution)/shard_map/ppermute | solution.py:550
  12.2 5.1 %collective-permute-done.2 = bf16[32,1664]{1,0:T(8,128)(2,1)S(1)} collective-permute-done((bf16[32,1664]{1,0:T(8,128)(2,1)}, bf16[32,1664]{1,0:T(8,128)(2,1)S(1)}, u32[]{:S(2)}, u32[]{:S(2)}) %collective-permute-start.2) | collective-permute-done | bytes 106528 | tf_op jit(solution)/shard_map/ppermute | solution.py:550
  17.3 0.0 collective-permute-done.1
  17.3 1.0 pad_maximum_fusion.refs_4_
  18.2 1.6 %collective-permute-start.4 = (bf16[4,32,1664]{2,1,0:T(8,128)(2,1)S(1)}, bf16[4,32,1664]{2,1,0:T(8,128)(2,1)S(1)}, u32[]{:S(2)}, u32[]{:S(2)}) collective-permute-start(bf16[4,32,1664]{2,1,0:T(8,128)(2,1)S(1)} %pad_maximum_fusion.refs_4_), channel_id=1, source_target_pairs={{0,2},{1,5},{2,0},{3,7},{4,6},{5,1},{6,4},{7,3},{8,10},{9,13},{10,... | collective-permute-start | bytes 1277960 | tf_op jit(solution)/shard_map/ppermute | solution.py:555
  19.8 1.5 %collective-permute-start.5 = (bf16[4,32,1664]{2,1,0:T(8,128)(2,1)S(1)}, bf16[4,32,1664]{2,1,0:T(8,128)(2,1)S(1)}, u32[]{:S(2)}, u32[]{:S(2)}) collective-permute-start(bf16[4,32,1664]{2,1,0:T(8,128)(2,1)S(1)} %pad_maximum_fusion.refs_4_), channel_id=1, source_target_pairs={{0,4},{1,3},{2,6},{3,1},{4,0},{5,7},{6,2},{7,5},{8,12},{9,11},{10,... | collective-permute-start | bytes 1277960 | tf_op jit(solution)/shard_map/ppermute | solution.py:555
  21.3 9.6 %collective-permute-done.4.refs_5_ = bf16[4,32,1664]{2,1,0:T(8,128)(2,1)S(1)} collective-permute-done((bf16[4,32,1664]{2,1,0:T(8,128)(2,1)S(1)}, bf16[4,32,1664]{2,1,0:T(8,128)(2,1)S(1)}, u32[]{:S(2)}, u32[]{:S(2)}) %collective-permute-start.4) | collective-permute-done | bytes 426016 | tf_op jit(solution)/shard_map/ppermute | solution.py:555
  31.0 0.1 collective-permute-start.6
  31.0 0.5 collective-permute-start.8
  31.6 0.0 collective-permute-done.5.refs_6_
  31.6 0.0 collective-permute-start.9
  31.6 7.5 %collective-permute-done.6.refs_7_ = bf16[4,32,1664]{2,1,0:T(8,128)(2,1)S(1)} collective-permute-done((bf16[4,32,1664]{2,1,0:T(8,128)(2,1)S(1)}, bf16[4,32,1664]{2,1,0:T(8,128)(2,1)S(1)}, u32[]{:S(2)}, u32[]{:S(2)}) %collective-permute-start.6) | collective-permute-done | bytes 426016 | tf_op jit(solution)/shard_map/ppermute | solution.py:555
  39.1 0.5 collective-permute-start
  39.6 0.1 pad_add_fusion.tab_ref
  39.7 1.1 collective-permute-done.refs_3_
  40.7 0.0 collective-permute-done.9.refs_10_
  40.7 0.0 collective-permute-done.8.refs_9_
  40.8 0.1 collective-permute-done.10.refs_11_
  40.9 0.9 copy-done
  41.8 0.8 copy-done.1
  42.6 47.0 %experts.1 = (bf16[512,3072]{1,0:T(8,128)(2,1)}, bf16[512,448]{1,0:T(8,128)(2,1)S(1)}, bf16[8,32,1664]{2,1,0:T(8,128)(2,1)S(1)}, bf16[8,32,1664]{2,1,0:T(8,128)(...) custom-call(s32[17]{0:T(128)S(1)} %pad_add_fusion.tab_ref, bf16[416,6144]{1,0:T(8,128)(2,1)} %bitcast.33, ...), custom_call_target="tpu_custom_call" | custom-call | flops 49999998976 | bytes 24000000 | tf_op jit(solution)/shard_map/experts/pallas_call | solution.py:373
  89.6 0.3 collective-permute-start.11
  89.9 2.4 %collective-permute-done.11.refs_1_ = bf16[8,32,1664]{2,1,0:T(8,128)(2,1)S(1)} collective-permute-done((bf16[8,32,1664]{2,1,0:T(8,128)(2,1)}, bf16[8,32,1664]{2,1,0:T(8,128)(2,1)S(1)}, u32[]{:S(2)}, u32[]{:S(2)}) %collective-permute-start.11) | collective-permute-done | bytes 852000 | tf_op jit(solution)/shard_map/ppermute | solution.py:559
  92.3 0.2 sum_cores.1
  92.5 0.3 collective-permute-start.12
  92.8 0.3 collective-permute-start.13
  93.1 0.1 collective-permute-start.14
  93.2 6.5 %input_own.1 = (f32[416,6144]{1,0:T(8,128)}, f32[13,6144]{1,0:T(8,128)}, f32[8,128]{1,0:T(8,128)S(1)}) custom-call(s32[17]{0:T(128)S(1)} %pad_add_fusion.tab_ref, bf16[512,3072]{1,0:T(8,128)(2,1)} %get-tuple-element.55.hg_ref, bf16[512,448]{1,0:T(8,128)(2,1)S(1)} %get-tuple-element.56.wat_ref, bf16[8,32,1664]{2,1,0:T(8,128)(2,1)S(1)} %get-tuple-element.59.refs_0_), custom_call_target="tpu_custom_call" | custom-call | flops 4000000000 | bytes 9000000 | tf_op jit(solution)/shard_map/input_own/pallas_call | solution.py:414
  99.7 6.1 %collective-permute-done.14.refs_2_ = bf16[8,32,1664]{2,1,0:T(8,128)(2,1)S(1)} collective-permute-done((bf16[8,32,1664]{2,1,0:T(8,128)(2,1)S(1)}, bf16[8,32,1664]{2,1,0:T(8,128)(2,1)S(1)}, u32[]{:S(2)}, u32[]{:S(2)}) %collective-permute-start.14) | collective-permute-done | bytes 852000 | tf_op jit(solution)/shard_map/ppermute | solution.py:555
  105.8 0.4 sum_first.1
  106.1 1.6 %collective-permute-start.15 = (bf16[4,32,1664]{2,1,0:T(8,128)(2,1)S(1)}, bf16[4,32,1664]{2,1,0:T(8,128)(2,1)S(1)}, u32[]{:S(2)}, u32[]{:S(2)}) collective-permute-start(bf16[4,32,1664]{2,1,0:T(8,128)(2,1)S(1)} %get-tuple-element.61.refs_0_), channel_id=1, source_target_pairs={{0,2},{1,5},{2,0},{3,7},{4,6},{5,1},{6,4},{7,3},{8,10},{9,13},{10,... | collective-permute-start | bytes 1277960 | tf_op jit(solution)/shard_map/ppermute | solution.py:555
  107.7 4.6 %input_far.1 = (f32[416,6144]{1,0:T(8,128)}, f32[13,6144]{1,0:T(8,128)}, f32[8,128]{1,0:T(8,128)S(1)}) custom-call(s32[17]{0:T(128)S(1)} %pad_add_fusion.tab_ref, bf16[512,3072]{1,0:T(8,128)(2,1)S(1)} %collective-permute-done.12.hg_ref, bf16[512,448]{1,0:T(8,128)(2,1)S(1)} %get-tuple-element.56.wat_ref, ...), custom_call_target="tpu_custom_call", output_to_operand_aliasing={{0}: (4, {}), {1}: (5, {})} | custom-call | flops 4000000000 | bytes 9000000 | tf_op jit(solution)/shard_map/input_far/pallas_call | solution.py:414
  112.3 2.0 %collective-permute-done.15.refs_1_ = bf16[4,32,1664]{2,1,0:T(8,128)(2,1)S(1)} collective-permute-done((bf16[4,32,1664]{2,1,0:T(8,128)(2,1)S(1)}, bf16[4,32,1664]{2,1,0:T(8,128)(2,1)S(1)}, u32[]{:S(2)}, u32[]{:S(2)}) %collective-permute-start.15) | collective-permute-done | bytes 426016 | tf_op jit(solution)/shard_map/ppermute | solution.py:555
  114.3 0.1 sum_second.1
  114.4 0.4 collective-permute-start.16
  114.8 2.7 %collective-permute-start.17 = (bf16[32,1664]{1,0:T(8,128)(2,1)S(1)}, bf16[32,1664]{1,0:T(8,128)(2,1)S(1)}, u32[]{:S(2)}, u32[]{:S(2)}) collective-permute-start(bf16[32,1664]{1,0:T(8,128)(2,1)S(1)} %get-tuple-element.70), channel_id=1, source_target_pairs={{0,16},{2,18},{4,20},{6,22},{8,24},{10,26},{12,28},{14,30},{16,0},... | collective-permute-start | bytes 319496 | tf_op jit(solution)/shard_map/ppermute | solution.py:550
  117.6 1.3 %collective-permute-start.18 = (bf16[32,1664]{1,0:T(8,128)(2,1)S(1)}, bf16[32,1664]{1,0:T(8,128)(2,1)S(1)}, u32[]{:S(2)}, u32[]{:S(2)}) collective-permute-start(bf16[32,1664]{1,0:T(8,128)(2,1)S(1)} %get-tuple-element.71), channel_id=1, source_target_pairs={{0,24},{2,26},{4,28},{6,30},{8,16},{10,18},{12,20},{14,22},{16,8},... | collective-permute-start | bytes 319496 | tf_op jit(solution)/shard_map/ppermute | solution.py:550
  118.9 0.4 collective-permute-done.16.refs_1_
  119.3 0.2 collective-permute-start.20
  119.4 5.3 %collective-permute-done.17.refs_2_ = bf16[32,1664]{1,0:T(8,128)(2,1)S(1)} collective-permute-done((bf16[32,1664]{1,0:T(8,128)(2,1)S(1)}, bf16[32,1664]{1,0:T(8,128)(2,1)S(1)}, u32[]{:S(2)}, u32[]{:S(2)}) %collective-permute-start.17) | collective-permute-done | bytes 106528 | tf_op jit(solution)/shard_map/ppermute | solution.py:550
  124.7 0.5 collective-permute-start.22
  125.2 0.7 collective-permute-done.21.refs_6_
  125.9 0.2 collective-permute-done.22.refs_7_
  126.1 0.8 finish.1
  (17 shorter events, 0.0 us)
Async XLA Ops:
  3.0 9.2 %collective-permute-start.3 = (bf16[32,1664]{1,0:T(8,128)(2,1)}, bf16[32,1664]{1,0:T(8,128)(2,1)S(1)}, u32[]{:S(2)}, u32[]{:S(2)}) collective-permute-start(bf16[32,1664]{1,0:T(8,128)(2,1)} %get-tuple-element.51), channel_id=1, source_target_pairs={{0,24},{2,26},{4,28},{6,30},{8,16},{10,18},{12,20},{14,22},{16,8},... | collective-permute-start | bytes 319496 | tf_op jit(solution)/shard_map/ppermute | solution.py:550
  8.1 9.2 %collective-permute-start.2 = (bf16[32,1664]{1,0:T(8,128)(2,1)}, bf16[32,1664]{1,0:T(8,128)(2,1)S(1)}, u32[]{:S(2)}, u32[]{:S(2)}) collective-permute-start(bf16[32,1664]{1,0:T(8,128)(2,1)} %get-tuple-element.51), channel_id=1, source_target_pairs={{0,16},{2,18},{4,20},{6,22},{8,24},{10,26},{12,28},{14,30},{16,0},... | collective-permute-start | bytes 319496 | tf_op jit(solution)/shard_map/ppermute | solution.py:550
  8.1 9.2 %collective-permute-start.1 = (bf16[32,1664]{1,0:T(8,128)(2,1)}, bf16[32,1664]{1,0:T(8,128)(2,1)S(1)}, u32[]{:S(2)}, u32[]{:S(2)}) collective-permute-start(bf16[32,1664]{1,0:T(8,128)(2,1)} %get-tuple-element.51), channel_id=1, source_target_pairs={{0,8},{2,10},{4,12},{6,14},{8,0},{10,2},{12,4},{14,6},{16,24},{18,... | collective-permute-start | bytes 319496 | tf_op jit(solution)/shard_map/ppermute | solution.py:550
  18.2 12.7 %collective-permute-start.4 = (bf16[4,32,1664]{2,1,0:T(8,128)(2,1)S(1)}, bf16[4,32,1664]{2,1,0:T(8,128)(2,1)S(1)}, u32[]{:S(2)}, u32[]{:S(2)}) collective-permute-start(bf16[4,32,1664]{2,1,0:T(8,128)(2,1)S(1)} %pad_maximum_fusion.refs_4_), channel_id=1, source_target_pairs={{0,2},{1,5},{2,0},{3,7},{4,6},{5,1},{6,4},{7,3},{8,10},{9,13},{10,... | collective-permute-start | bytes 1277960 | tf_op jit(solution)/shard_map/ppermute | solution.py:555
  19.8 11.7 %collective-permute-start.5 = (bf16[4,32,1664]{2,1,0:T(8,128)(2,1)S(1)}, bf16[4,32,1664]{2,1,0:T(8,128)(2,1)S(1)}, u32[]{:S(2)}, u32[]{:S(2)}) collective-permute-start(bf16[4,32,1664]{2,1,0:T(8,128)(2,1)S(1)} %pad_maximum_fusion.refs_4_), channel_id=1, source_target_pairs={{0,4},{1,3},{2,6},{3,1},{4,0},{5,7},{6,2},{7,5},{8,12},{9,11},{10,... | collective-permute-start | bytes 1277960 | tf_op jit(solution)/shard_map/ppermute | solution.py:555
  31.0 8.1 %collective-permute-start.6 = (bf16[4,32,1664]{2,1,0:T(8,128)(2,1)S(1)}, bf16[4,32,1664]{2,1,0:T(8,128)(2,1)S(1)}, u32[]{:S(2)}, u32[]{:S(2)}) collective-permute-start(bf16[4,32,1664]{2,1,0:T(8,128)(2,1)S(1)} %collective-permute-done.4.refs_5_), channel_id=1, source_target_pairs={{0,4},{1,3},{2,6},{3,1},{4,0},{5,7},{6,2},{7,5},{8,12},{9,11},{10,... | collective-permute-start | bytes 1277960 | tf_op jit(solution)/shard_map/ppermute | solution.py:555
  31.0 9.7 %collective-permute-start.7 = (bf16[4,32,1664]{2,1,0:T(8,128)(2,1)S(1)}, bf16[4,32,1664]{2,1,0:T(8,128)(2,1)S(1)}, u32[]{:S(2)}, u32[]{:S(2)}) collective-permute-start(bf16[4,32,1664]{2,1,0:T(8,128)(2,1)S(1)} %pad_maximum_fusion.refs_4_), channel_id=1, source_target_pairs={{0,1},{1,0},{2,3},{3,2},{4,5},{5,4},{6,7},{7,6},{8,9},{9,8},{10,11... | collective-permute-start | bytes 1277960 | tf_op jit(solution)/shard_map/ppermute | solution.py:559
  31.0 9.7 %collective-permute-start.8 = (bf16[4,32,1664]{2,1,0:T(8,128)(2,1)S(1)}, bf16[4,32,1664]{2,1,0:T(8,128)(2,1)S(1)}, u32[]{:S(2)}, u32[]{:S(2)}) collective-permute-start(bf16[4,32,1664]{2,1,0:T(8,128)(2,1)S(1)} %collective-permute-done.4.refs_5_), channel_id=1, source_target_pairs={{0,1},{1,0},{2,3},{3,2},{4,5},{5,4},{6,7},{7,6},{8,9},{9,8},{10,11... | collective-permute-start | bytes 1277960 | tf_op jit(solution)/shard_map/ppermute | solution.py:559
  31.6 9.2 %collective-permute-start.9 = (bf16[4,32,1664]{2,1,0:T(8,128)(2,1)S(1)}, bf16[4,32,1664]{2,1,0:T(8,128)(2,1)S(1)}, u32[]{:S(2)}, u32[]{:S(2)}) collective-permute-start(bf16[4,32,1664]{2,1,0:T(8,128)(2,1)S(1)} %collective-permute-done.5.refs_6_), channel_id=1, source_target_pairs={{0,1},{1,0},{2,3},{3,2},{4,5},{5,4},{6,7},{7,6},{8,9},{9,8},{10,11... | collective-permute-start | bytes 1277960 | tf_op jit(solution)/shard_map/ppermute | solution.py:559
  39.1 1.8 %collective-permute-start.10 = (bf16[4,32,1664]{2,1,0:T(8,128)(2,1)S(1)}, bf16[4,32,1664]{2,1,0:T(8,128)(2,1)S(1)}, u32[]{:S(2)}, u32[]{:S(2)}) collective-permute-start(bf16[4,32,1664]{2,1,0:T(8,128)(2,1)S(1)} %collective-permute-done.6.refs_7_), channel_id=1, source_target_pairs={{0,1},{1,0},{2,3},{3,2},{4,5},{5,4},{6,7},{7,6},{8,9},{9,8},{10,11... | collective-permute-start | bytes 1277960 | tf_op jit(solution)/shard_map/ppermute | solution.py:559
  39.1 1.7 %collective-permute-start = (f32[1,8192]{1,0:T(1,128)}, f32[1,8192]{1,0:T(1,128)S(1)}, u32[]{:S(2)}, u32[]{:S(2)}) collective-permute-start(f32[1,8192]{1,0:T(1,128)} %get-tuple-element.50.refs_2_), channel_id=1, source_target_pairs={{0,1},{1,0},{2,3},{3,2},{4,5},{5,4},{6,7},{7,6},{8,9},{9,8},{10,11... | collective-permute-start | bytes 98312 | tf_op jit(solution)/shard_map/ppermute | solution.py:559
  40.9 0.9 copy-start
  41.8 0.8 copy-start.1
  89.6 2.7 %collective-permute-start.11 = (bf16[8,32,1664]{2,1,0:T(8,128)(2,1)}, bf16[8,32,1664]{2,1,0:T(8,128)(2,1)S(1)}, u32[]{:S(2)}, u32[]{:S(2)}) collective-permute-start(bf16[8,32,1664]{2,1,0:T(8,128)(2,1)} %get-tuple-element.53), channel_id=1, source_target_pairs={{0,1},{1,0},{2,3},{3,2},{4,5},{5,4},{6,7},{7,6},{8,9},{9,8},{10,11... | collective-permute-start | bytes 2555912 | tf_op jit(solution)/shard_map/ppermute | solution.py:559
  92.5 15.2 %collective-permute-start.12 = (bf16[512,3072]{1,0:T(8,128)(2,1)}, bf16[512,3072]{1,0:T(8,128)(2,1)S(1)}, u32[]{:S(2)}, u32[]{:S(2)}) collective-permute-start(bf16[512,3072]{1,0:T(8,128)(2,1)} %get-tuple-element.55.hg_ref), channel_id=1, source_target_pairs={{0,1},{1,0},{2,3},{3,2},{4,5},{5,4},{6,7},{7,6},{8,9},{9,8},{10,11... | collective-permute-start | bytes 9437192 | tf_op jit(solution)/shard_map/ppermute | solution.py:559
  92.8 6.9 %collective-permute-start.13 = (bf16[8,32,1664]{2,1,0:T(8,128)(2,1)}, bf16[8,32,1664]{2,1,0:T(8,128)(2,1)S(1)}, u32[]{:S(2)}, u32[]{:S(2)}) collective-permute-start(bf16[8,32,1664]{2,1,0:T(8,128)(2,1)} %get-tuple-element.58), channel_id=1, source_target_pairs={{0,1},{1,0},{2,3},{3,2},{4,5},{5,4},{6,7},{7,6},{8,9},{9,8},{10,11... | collective-permute-start | bytes 2555912 | tf_op jit(solution)/shard_map/ppermute | solution.py:559
  93.1 12.7 %collective-permute-start.14 = (bf16[8,32,1664]{2,1,0:T(8,128)(2,1)S(1)}, bf16[8,32,1664]{2,1,0:T(8,128)(2,1)S(1)}, u32[]{:S(2)}, u32[]{:S(2)}) collective-permute-start(bf16[8,32,1664]{2,1,0:T(8,128)(2,1)S(1)} %get-tuple-element.59.refs_0_), channel_id=1, source_target_pairs={{0,4},{1,3},{2,6},{3,1},{4,0},{5,7},{6,2},{7,5},{8,12},{9,11},{10,... | collective-permute-start | bytes 2555912 | tf_op jit(solution)/shard_map/ppermute | solution.py:555
  106.1 8.2 %collective-permute-start.15 = (bf16[4,32,1664]{2,1,0:T(8,128)(2,1)S(1)}, bf16[4,32,1664]{2,1,0:T(8,128)(2,1)S(1)}, u32[]{:S(2)}, u32[]{:S(2)}) collective-permute-start(bf16[4,32,1664]{2,1,0:T(8,128)(2,1)S(1)} %get-tuple-element.61.refs_0_), channel_id=1, source_target_pairs={{0,2},{1,5},{2,0},{3,7},{4,6},{5,1},{6,4},{7,3},{8,10},{9,13},{10,... | collective-permute-start | bytes 1277960 | tf_op jit(solution)/shard_map/ppermute | solution.py:555
  114.4 4.8 %collective-permute-start.16 = (bf16[32,1664]{1,0:T(8,128)(2,1)S(1)}, bf16[32,1664]{1,0:T(8,128)(2,1)S(1)}, u32[]{:S(2)}, u32[]{:S(2)}) collective-permute-start(bf16[32,1664]{1,0:T(8,128)(2,1)S(1)} %get-tuple-element.69), channel_id=1, source_target_pairs={{0,8},{2,10},{4,12},{6,14},{8,0},{10,2},{12,4},{14,6},{16,24},{18,... | collective-permute-start | bytes 319496 | tf_op jit(solution)/shard_map/ppermute | solution.py:550
  114.8 9.9 %collective-permute-start.17 = (bf16[32,1664]{1,0:T(8,128)(2,1)S(1)}, bf16[32,1664]{1,0:T(8,128)(2,1)S(1)}, u32[]{:S(2)}, u32[]{:S(2)}) collective-permute-start(bf16[32,1664]{1,0:T(8,128)(2,1)S(1)} %get-tuple-element.70), channel_id=1, source_target_pairs={{0,16},{2,18},{4,20},{6,22},{8,24},{10,26},{12,28},{14,30},{16,0},... | collective-permute-start | bytes 319496 | tf_op jit(solution)/shard_map/ppermute | solution.py:550
  117.6 7.1 %collective-permute-start.18 = (bf16[32,1664]{1,0:T(8,128)(2,1)S(1)}, bf16[32,1664]{1,0:T(8,128)(2,1)S(1)}, u32[]{:S(2)}, u32[]{:S(2)}) collective-permute-start(bf16[32,1664]{1,0:T(8,128)(2,1)S(1)} %get-tuple-element.71), channel_id=1, source_target_pairs={{0,24},{2,26},{4,28},{6,30},{8,16},{10,18},{12,20},{14,22},{16,8},... | collective-permute-start | bytes 319496 | tf_op jit(solution)/shard_map/ppermute | solution.py:550
  118.9 6.3 %collective-permute-start.19 = (bf16[16,512]{1,0:T(8,128)(2,1)S(1)}, bf16[16,512]{1,0:T(8,128)(2,1)S(1)}, u32[]{:S(2)}, u32[]{:S(2)}) collective-permute-start(bf16[16,512]{1,0:T(8,128)(2,1)S(1)} %slice.12), channel_id=1, source_target_pairs={{0,1},{1,0},{2,3},{3,2},{4,5},{5,4},{6,7},{7,6},{8,9},{9,8},{10,11... | collective-permute-start | bytes 49160 | tf_op jit(solution)/shard_map/ppermute | solution.py:559
  119.3 6.0 %collective-permute-start.20 = (bf16[16,512]{1,0:T(8,128)(2,1)S(1)}, bf16[16,512]{1,0:T(8,128)(2,1)S(1)}, u32[]{:S(2)}, u32[]{:S(2)}) collective-permute-start(bf16[16,512]{1,0:T(8,128)(2,1)S(1)} %slice.16), channel_id=1, source_target_pairs={{0,1},{1,0},{2,3},{3,2},{4,5},{5,4},{6,7},{7,6},{8,9},{9,8},{10,11... | collective-permute-start | bytes 49160 | tf_op jit(solution)/shard_map/ppermute | solution.py:559
  124.7 1.2 collective-permute-start.21
  124.7 1.3 %collective-permute-start.22 = (bf16[16,512]{1,0:T(8,128)(2,1)S(1)}, bf16[16,512]{1,0:T(8,128)(2,1)S(1)}, u32[]{:S(2)}, u32[]{:S(2)}) collective-permute-start(bf16[16,512]{1,0:T(8,128)(2,1)S(1)} %slice.18), channel_id=1, source_target_pairs={{0,1},{1,0},{2,3},{3,2},{4,5},{5,4},{6,7},{7,6},{8,9},{9,8},{10,11... | collective-permute-start | bytes 49160 | tf_op jit(solution)/shard_map/ppermute | solution.py:559

commit v6 on v5

--- a/solution.py
+++ b/solution.py
@@ -74,14 +74,14 @@
         going = left
 
 
-def main_kernel(pieces, chunks, rows, batch_rows, tab_ref, *refs):
+def main_kernel(pieces, chunks, batch_rows, tab_ref, *refs):
     emb_ref, dense_ref, line_ref, far_line_ref = refs[:4]
     u_refs = (refs[4 : 4 + pieces], refs[4 + pieces : 4 + 2 * pieces])
     hg_ref, wat_s, *du_refs = refs[4 + 2 * pieces : 10 + 2 * pieces]
     (
         x_s, hid_s, mid_s, sl1_s, out_s, sl2_s, sg_s, fg_s, mix_s,
         w1_s, w1t_s, ga_s, w2t_s, w2_s, b1_s, b2_s, gb_s, tt_s, tw_s, tcol_s, q_s,
-        dwa_s, dw1_s, dw2_s, dtw_s, dcol_s, dlog_s, dsm_s, dense_s, start_s, row_s, sem,
+        dwa_s, dw1_s, dw2_s, dtw_s, dcol_s, dlog_s, dsm_s, start_s, row_s,
     ) = refs[10 + 2 * pieces :]
     n = SUB
     fs, osz, ds = FH // chunks, EO // chunks, D // chunks
@@ -91,10 +91,6 @@
 
     @pl.when(step == 0)
     def _():
-        half = dense_s.shape[1]
-        mine = dense_ref.at[:, pl.ds(pl.multiple_of(core * half, half), half)]
-        dense_copy = pltpu.make_async_copy(mine, dense_s, sem)
-        dense_copy.start()
         row_number = lax.broadcasted_iota(jnp.int32, (32, n), 0)
         ones = jnp.where(lax.broadcasted_iota(jnp.int32, (16, n), 0) == 0, 1.0, 0.0).astype(BF)
         for h in range(TILE // SUB):
@@ -107,9 +103,9 @@
         for ref in (dwa_s, dw1_s, dw2_s, dtw_s, dcol_s, dlog_s):
             ref[...] = jnp.zeros_like(ref)
         users = start_s.shape[1]
-        sizes = [line_ref[:, rows + 512 + users * b : rows + 512 + users * b + users] for b in range(start_s.shape[0])]
+        after = row_s.shape[1] + 512
+        sizes = [line_ref[:, after + users * b : after + users * b + users] for b in range(start_s.shape[0])]
         fill_weights(core, batch_rows, jnp.concatenate(sizes, axis=0), start_s, row_s)
-        dense_copy.wait()
         gates = []
         for side in range(2):
             base = HALF * FH * side
@@ -144,7 +140,8 @@
         w1t_s[NE * FH : NE * FH + 16, :] = gates.astype(BF)
         pad = jnp.concatenate([gates, jnp.zeros((112, D), F32)], axis=0)
         w1_s[:, NE * FH : FG] = pad.T.astype(BF)
-        vecs = [square([r[:, rows + 128 * j : rows + 128 * j + 128] for j in range(4)]).T for r in (line_ref, far_line_ref)]
+        half = row_s.shape[1]
+        vecs = [square([r[:, half + 128 * j : half + 128 * j + 128] for j in range(4)]).T for r in (line_ref, far_line_ref)]
         gb_s[...] = jnp.concatenate([swap_halves(v[0:NE, 0:1], second_core) for v in vecs], axis=0)
         b1 = jnp.concatenate([v[0:TW, 1:2] for v in vecs], axis=0)
         head = jnp.concatenate([v[0:TW, 2:3] for v in vecs], axis=0)
@@ -154,7 +151,7 @@
     def chain(h):
         at = slice(SUB * h, SUB * h + SUB)
         x_s[h, 0:EMB, :] = emb_ref[:, at]
-        x_s[h, EMB : EMB + DENSE, :] = dense_s[:, pl.ds(pl.multiple_of(step * TILE + SUB * h, SUB), SUB)]
+        x_s[h, EMB : EMB + DENSE, :] = dense_ref[:, pl.ds(pl.multiple_of(step * TILE + SUB * h, SUB), SUB)]
         hid = mm(wat_s[...], x_s[h]).astype(BF)
         hid_s[h, 0:D, :] = hid
         yield
@@ -195,7 +192,7 @@
         lgos = []
         for t in range(2):
             logit = jnp.sum(weighted[TW * t : TW * t + TW], axis=0, keepdims=True) + tcol_s[t : t + 1, 3:4]
-            label = (line_ref, far_line_ref)[t][:, pl.ds(pl.multiple_of((core * pl.num_programs(0) + step) * TILE + SUB * h, SUB), SUB)]
+            label = (line_ref, far_line_ref)[t][:, pl.ds(pl.multiple_of(step * TILE + SUB * h, SUB), SUB)]
             lgos.append(row_s[:, pl.ds(pl.multiple_of(step * TILE + SUB * h, SUB), SUB)] * (0.5 * jnp.tanh(0.5 * logit) + 0.5 - label))
         lgo = jnp.concatenate([jnp.broadcast_to(lgos[t], (TW, SUB)) for t in range(2)], axis=0)
         dcol_s[...] += lane_fold(lgo * act)
@@ -329,7 +326,7 @@
         grid=(steps,),
         in_specs=[
             pl.BlockSpec((EMB, TILE), own),
-            whole(pltpu.HBM),
+            whole(),
             whole(),
             whole(),
         ]
@@ -364,14 +361,12 @@
             pltpu.VMEM((2 * TW, 128), F32),
             pltpu.VMEM((16, 128), F32),
             pltpu.VMEM((FH, 128), F32),
-            pltpu.VMEM((DENSE, half), BF),
             pltpu.VMEM((*sizes_shape, 128), F32),
             pltpu.VMEM((1, half), F32),
-            pltpu.SemaphoreType.DMA(()),
         ],
     )
     return pl.pallas_call(
-        functools.partial(main_kernel, pieces, chunks, rows, rows // sizes_shape[0]),
+        functools.partial(main_kernel, pieces, chunks, rows // sizes_shape[0]),
         grid_spec=spec,
         out_shape=[jax.ShapeDtypeStruct((D, half), BF), jax.ShapeDtypeStruct((D, XR), BF)]
         + [jax.ShapeDtypeStruct(a, BF) for a in grads],
@@ -563,6 +558,14 @@
     return a.astype(F32) + b.astype(F32)
 
 
+def halves(line, denset, core):
+    rows = denset.shape[1]
+    half = rows // 2
+    own_line = jnp.concatenate([lax.dynamic_slice(line, (0, core * half), (1, half)), line[:, rows:]], axis=1)
+    sent_line = jnp.concatenate([lax.dynamic_slice(line, (0, (1 - core) * half), (1, half)), line[:, rows : rows + 512]], axis=1)
+    return own_line, partner(sent_line), lax.dynamic_slice(denset, (0, core * half), (DENSE, half))
+
+
 def pad_to(a, rows, cols):
     return jnp.pad(a, ((0, rows - a.shape[0]), (0, cols - a.shape[1])))
 
@@ -586,6 +589,8 @@
             one_core, w_emb.T, w_dense, b_in[None], expert_w1, expert_w2, expert_b1, expert_b2, gate_t, tower_w1[0], *smalls, group_sizes, labels
         )
         near = jnp.stack([shard] + [hop(shard, 4 * a, size) for a in range(1, 4)])
+        own_line, far_line, own_dense = halves(line, dense.T, core)
+        near, own_line, far_line, own_dense = lax.optimization_barrier((near, own_line, far_line, own_dense))
         once = cross(near, (1, 2), size)
         own_u = [near, once, cross(near, (2, 1), size), cross(once, (2, 1), size)]
         steps = jnp.arange(16, dtype=jnp.int32)
@@ -604,10 +609,11 @@
         order = jnp.zeros((1,), jnp.int32)
         line = [labels.astype(F32)] + [pad_to(a, 1, 128).astype(F32) for a in smalls]
         line = jnp.concatenate(line + [group_sizes.astype(F32).reshape(1, -1)], axis=1)
+        own_line, far_line, own_dense = halves(line, dense.T, core)
     far_u = [partner(a) for a in own_u]
     table = jnp.concatenate([core[None].astype(jnp.int32), order])
 
-    hg, wat, own_low, own_high, du_low, du_high = main_call(table, emb.T, dense.T, line, partner(line), group_sizes.shape, own_u, far_u)
+    hg, wat, own_low, own_high, du_low, du_high = main_call(table, emb.T, own_dense, own_line, far_line, group_sizes.shape, own_u, far_u)
     du_high = partner(du_high)
     scale = 1.0 / user_count
     if fast:

time: 127 us -> 125 us (0.984)
  waiting for transfers between devices: 43.9 us -> 42.3 us
    ppermute x6, waiting for transfers between devices: 14.2 us -> 11.8 us  [hop(): return lax.ppermute(a, 'rows', [(i, i ^ mask) for i in range(size)])]
    unnamed x4 -> x2, local copies, waits for them, and re-layouts: 1.68 us -> 0.01 us
    slice x0 -> x2, local copies, waits for them, and re-layouts: none -> 1.38 us  [the longest x1 0.7 us: halves(): line[:, rows:]]
  transfers between devices with their start and end apart: 23 -> 23, of which waited for: 13 -> 12; matrix products, arithmetic and copies ran while one was open for 0% -> 3% of each run, Pallas kernels for 9% -> 9%
where the time goes in v6:
time: 125 us
  Pallas kernels  60.7 us (49%)
  waiting for transfers between devices  42.3 us (34%)
  starting transfers between devices  16.9 us (14%)
  local copies, waits for them, and re-layouts  2.15 us (2%)
  between operations  1.61 us (1%)
    pallas_call x1, Pallas kernels, main_call(): pl.pallas_call(functools.partial(main_kernel, pieces, chunks, rows // siz...  46.5 us
    ppermute x5, waiting for transfers between devices, cross(): return lax.ppermute(a, ('rows', 'task'), pairs)  25.3 us
    ppermute x6, waiting for transfers between devices, hop(): return lax.ppermute(a, 'rows', [(i, i ^ mask) for i in range(size)])  11.8 us
    pallas_call x2, Pallas kernels, input_call(): pl.pallas_call(input_kernel, grid_spec=spec, out_shape=[jax.ShapeDtypeStr...  11.1 us
    ppermute x6, starting transfers between devices, hop(): return lax.ppermute(a, 'rows', [(i, i ^ mask) for i in range(size)])  10.1 us
    ppermute x12, waiting for transfers between devices, partner(): return lax.ppermute(a, 'task', [(0, 1), (1, 0)])  5.12 us
    ppermute x5, starting transfers between devices, cross(): return lax.ppermute(a, ('rows', 'task'), pairs)  4.78 us
  transfers between devices with their start and end apart: 23, of which 12 were waited for; matrix products, arithmetic and copies ran while one was open for 3% of the time, Pallas kernels for 9%

profile of v6, /device:TPU:0, one launch (start us, length us, event | category | flops | bytes accessed | tf_op | source)
XLA Modules:
  0.0 124.7 jit_solution(15647672791056152497)
XLA Ops:
  0.7 0.0 copy-start
  1.4 1.7 %pack.1 = (bf16[32,1664]{1,0:T(8,128)(2,1)}, f32[1,8192]{1,0:T(1,128)}) custom-call(s32[1]{0:T(128)} %bitcast.core_ref, bf16[32,416]{1,0:T(8,128)(2,1)} %bitcast.29, bf16[13,32]{1,0:T(8,128)(2,1)} %dense_ref.1, bf16[1,32]{1,0:T(2,128)(2,1)} %bitcast.32, bf16[4,32,256]{2,1,0:T(8,128)(2,1)} %w1_ref.1, bf16[4,16,128]{2,1,0:T(8,128)(2,1)} %w2_ref.1, ...), custom_call_target="tpu_custom_call" | custom-call | tf_op jit(solution)/shard_map/pack/pallas_call | solution.py:466
  3.1 5.0 %collective-permute-start.2 = (bf16[32,1664]{1,0:T(8,128)(2,1)}, bf16[32,1664]{1,0:T(8,128)(2,1)S(1)}, u32[]{:S(2)}, u32[]{:S(2)}) collective-permute-start(bf16[32,1664]{1,0:T(8,128)(2,1)} %get-tuple-element.54), channel_id=1, source_target_pairs={{0,24},{2,26},{4,28},{6,30},{8,16},{10,18},{12,20},{14,22},{16,8},... | collective-permute-start | bytes 319496 | tf_op jit(solution)/shard_map/ppermute | solution.py:545
  8.1 0.0 collective-permute-start.1
  8.1 0.6 collective-permute-start
  8.8 0.7 slice.19
  9.5 0.7 constant_dynamic-slice_fusion
  10.2 0.1 collective-permute-start.3
  10.3 0.7 slice.18
  11.0 1.2 collective-permute-done.2
  12.2 5.1 %collective-permute-done.1 = bf16[32,1664]{1,0:T(8,128)(2,1)S(1)} collective-permute-done((bf16[32,1664]{1,0:T(8,128)(2,1)}, bf16[32,1664]{1,0:T(8,128)(2,1)S(1)}, u32[]{:S(2)}, u32[]{:S(2)}) %collective-permute-start.1) | collective-permute-done | bytes 106528 | tf_op jit(solution)/shard_map/ppermute | solution.py:545
  17.3 0.0 collective-permute-done
  17.3 1.0 pad_maximum_fusion.refs_4_
  18.3 0.0 collective-permute-done.3.refs_3_
  18.3 1.6 %collective-permute-start.4 = (bf16[4,32,1664]{2,1,0:T(8,128)(2,1)S(1)}, bf16[4,32,1664]{2,1,0:T(8,128)(2,1)S(1)}, u32[]{:S(2)}, u32[]{:S(2)}) collective-permute-start(bf16[4,32,1664]{2,1,0:T(8,128)(2,1)S(1)} %pad_maximum_fusion.refs_4_), channel_id=1, source_target_pairs={{0,2},{1,5},{2,0},{3,7},{4,6},{5,1},{6,4},{7,3},{8,10},{9,13},{10,... | collective-permute-start | bytes 1277960 | tf_op jit(solution)/shard_map/ppermute | solution.py:550
  19.9 1.5 %collective-permute-start.5 = (bf16[4,32,1664]{2,1,0:T(8,128)(2,1)S(1)}, bf16[4,32,1664]{2,1,0:T(8,128)(2,1)S(1)}, u32[]{:S(2)}, u32[]{:S(2)}) collective-permute-start(bf16[4,32,1664]{2,1,0:T(8,128)(2,1)S(1)} %pad_maximum_fusion.refs_4_), channel_id=1, source_target_pairs={{0,4},{1,3},{2,6},{3,1},{4,0},{5,7},{6,2},{7,5},{8,12},{9,11},{10,... | collective-permute-start | bytes 1277960 | tf_op jit(solution)/shard_map/ppermute | solution.py:550
  21.4 9.6 %collective-permute-done.4.refs_5_ = bf16[4,32,1664]{2,1,0:T(8,128)(2,1)S(1)} collective-permute-done((bf16[4,32,1664]{2,1,0:T(8,128)(2,1)S(1)}, bf16[4,32,1664]{2,1,0:T(8,128)(2,1)S(1)}, u32[]{:S(2)}, u32[]{:S(2)}) %collective-permute-start.4) | collective-permute-done | bytes 426016 | tf_op jit(solution)/shard_map/ppermute | solution.py:550
  31.0 0.1 collective-permute-start.6
  31.1 0.5 collective-permute-start.8
  31.6 0.0 collective-permute-start.9
  31.6 7.5 %collective-permute-done.6.refs_7_ = bf16[4,32,1664]{2,1,0:T(8,128)(2,1)S(1)} collective-permute-done((bf16[4,32,1664]{2,1,0:T(8,128)(2,1)S(1)}, bf16[4,32,1664]{2,1,0:T(8,128)(2,1)S(1)}, u32[]{:S(2)}, u32[]{:S(2)}) %collective-permute-start.6) | collective-permute-done | bytes 426016 | tf_op jit(solution)/shard_map/ppermute | solution.py:550
  39.2 0.1 pad_add_fusion.tab_ref
  39.3 1.8 %collective-permute-done.10.refs_11_ = bf16[4,32,1664]{2,1,0:T(8,128)(2,1)} collective-permute-done((bf16[4,32,1664]{2,1,0:T(8,128)(2,1)S(1)}, bf16[4,32,1664]{2,1,0:T(8,128)(2,1)}, u32[]{:S(2)}, u32[]{:S(2)}) %collective-permute-start.10) | collective-permute-done | bytes 426016 | tf_op jit(solution)/shard_map/ppermute | solution.py:554
  41.1 46.5 %experts.1 = (bf16[512,3072]{1,0:T(8,128)(2,1)}, bf16[512,448]{1,0:T(8,128)(2,1)S(1)}, bf16[8,32,1664]{2,1,0:T(8,128)(2,1)S(1)}, bf16[8,32,1664]{2,1,0:T(8,128)(...) custom-call(s32[17]{0:T(128)S(1)} %pad_add_fusion.tab_ref, bf16[416,6144]{1,0:T(8,128)(2,1)} %bitcast.33, ...), custom_call_target="tpu_custom_call" | custom-call | flops 49999998976 | bytes 24000000 | tf_op jit(solution)/shard_map/experts/pallas_call | solution.py:368
  87.5 0.1 collective-permute-start.11
  87.6 2.5 %collective-permute-done.11.refs_1_ = bf16[8,32,1664]{2,1,0:T(8,128)(2,1)S(1)} collective-permute-done((bf16[8,32,1664]{2,1,0:T(8,128)(2,1)}, bf16[8,32,1664]{2,1,0:T(8,128)(2,1)S(1)}, u32[]{:S(2)}, u32[]{:S(2)}) %collective-permute-start.11) | collective-permute-done | bytes 852000 | tf_op jit(solution)/shard_map/ppermute | solution.py:554
  90.1 0.2 sum_cores.1
  90.3 0.2 collective-permute-start.12
  90.5 0.4 collective-permute-start.13
  90.9 0.1 collective-permute-start.14
  91.0 6.5 %input_own.1 = (f32[416,6144]{1,0:T(8,128)}, f32[13,6144]{1,0:T(8,128)}, f32[8,128]{1,0:T(8,128)S(1)}) custom-call(s32[17]{0:T(128)S(1)} %pad_add_fusion.tab_ref, bf16[512,3072]{1,0:T(8,128)(2,1)} %get-tuple-element.63.hg_ref, bf16[512,448]{1,0:T(8,128)(2,1)S(1)} %get-tuple-element.64.wat_ref, bf16[8,32,1664]{2,1,0:T(8,128)(2,1)S(1)} %get-tuple-element.67.refs_0_), custom_call_target="tpu_custom_call" | custom-call | flops 4000000000 | bytes 9000000 | tf_op jit(solution)/shard_map/input_own/pallas_call | solution.py:409
  97.5 0.0 collective-permute-done.13.refs_1_
  97.5 6.1 %collective-permute-done.14.refs_2_ = bf16[8,32,1664]{2,1,0:T(8,128)(2,1)S(1)} collective-permute-done((bf16[8,32,1664]{2,1,0:T(8,128)(2,1)S(1)}, bf16[8,32,1664]{2,1,0:T(8,128)(2,1)S(1)}, u32[]{:S(2)}, u32[]{:S(2)}) %collective-permute-start.14) | collective-permute-done | bytes 852000 | tf_op jit(solution)/shard_map/ppermute | solution.py:550
  103.6 0.3 sum_first.1
  103.9 1.6 %collective-permute-start.15 = (bf16[4,32,1664]{2,1,0:T(8,128)(2,1)S(1)}, bf16[4,32,1664]{2,1,0:T(8,128)(2,1)S(1)}, u32[]{:S(2)}, u32[]{:S(2)}) collective-permute-start(bf16[4,32,1664]{2,1,0:T(8,128)(2,1)S(1)} %get-tuple-element.69.refs_0_), channel_id=1, source_target_pairs={{0,2},{1,5},{2,0},{3,7},{4,6},{5,1},{6,4},{7,3},{8,10},{9,13},{10,... | collective-permute-start | bytes 1277960 | tf_op jit(solution)/shard_map/ppermute | solution.py:550
  105.4 4.6 %input_far.1 = (f32[416,6144]{1,0:T(8,128)}, f32[13,6144]{1,0:T(8,128)}, f32[8,128]{1,0:T(8,128)S(1)}) custom-call(s32[17]{0:T(128)S(1)} %pad_add_fusion.tab_ref, bf16[512,3072]{1,0:T(8,128)(2,1)S(1)} %collective-permute-done.12.hg_ref, bf16[512,448]{1,0:T(8,128)(2,1)S(1)} %get-tuple-element.64.wat_ref, ...), custom_call_target="tpu_custom_call", output_to_operand_aliasing={{0}: (4, {}), {1}: (5, {})} | custom-call | flops 4000000000 | bytes 9000000 | tf_op jit(solution)/shard_map/input_far/pallas_call | solution.py:409
  110.0 2.1 %collective-permute-done.15.refs_1_ = bf16[4,32,1664]{2,1,0:T(8,128)(2,1)S(1)} collective-permute-done((bf16[4,32,1664]{2,1,0:T(8,128)(2,1)S(1)}, bf16[4,32,1664]{2,1,0:T(8,128)(2,1)S(1)}, u32[]{:S(2)}, u32[]{:S(2)}) %collective-permute-start.15) | collective-permute-done | bytes 426016 | tf_op jit(solution)/shard_map/ppermute | solution.py:550
  112.1 0.1 sum_second.1
  112.2 0.4 collective-permute-start.16
  112.6 2.7 %collective-permute-start.17 = (bf16[32,1664]{1,0:T(8,128)(2,1)S(1)}, bf16[32,1664]{1,0:T(8,128)(2,1)S(1)}, u32[]{:S(2)}, u32[]{:S(2)}) collective-permute-start(bf16[32,1664]{1,0:T(8,128)(2,1)S(1)} %get-tuple-element.78), channel_id=1, source_target_pairs={{0,16},{2,18},{4,20},{6,22},{8,24},{10,26},{12,28},{14,30},{16,0},... | collective-permute-start | bytes 319496 | tf_op jit(solution)/shard_map/ppermute | solution.py:545
  115.3 1.3 %collective-permute-start.18 = (bf16[32,1664]{1,0:T(8,128)(2,1)S(1)}, bf16[32,1664]{1,0:T(8,128)(2,1)S(1)}, u32[]{:S(2)}, u32[]{:S(2)}) collective-permute-start(bf16[32,1664]{1,0:T(8,128)(2,1)S(1)} %get-tuple-element.79), channel_id=1, source_target_pairs={{0,24},{2,26},{4,28},{6,30},{8,16},{10,18},{12,20},{14,22},{16,8},... | collective-permute-start | bytes 319496 | tf_op jit(solution)/shard_map/ppermute | solution.py:545
  116.6 0.4 collective-permute-done.16.refs_1_
  117.0 0.2 collective-permute-start.20
  117.2 5.2 %collective-permute-done.17.refs_2_ = bf16[32,1664]{1,0:T(8,128)(2,1)S(1)} collective-permute-done((bf16[32,1664]{1,0:T(8,128)(2,1)S(1)}, bf16[32,1664]{1,0:T(8,128)(2,1)S(1)}, u32[]{:S(2)}, u32[]{:S(2)}) %collective-permute-start.17) | collective-permute-done | bytes 106528 | tf_op jit(solution)/shard_map/ppermute | solution.py:545
  122.4 0.5 collective-permute-start.22
  122.9 0.7 collective-permute-done.21.refs_6_
  123.5 0.2 collective-permute-done.22.refs_7_
  123.7 0.8 finish.1
  (21 shorter events, 0.1 us)
Async XLA Ops:
  0.7 10.4 %copy-start = (bf16[6144,13]{0,1:T(8,128)(2,1)S(1)}, bf16[6144,13]{0,1:T(8,128)(2,1)}, u32[]{:S(2)}) copy-start(bf16[6144,13]{0,1:T(8,128)(2,1)} %param.18) | copy-start | bytes 479236
  3.1 9.2 %collective-permute-start.2 = (bf16[32,1664]{1,0:T(8,128)(2,1)}, bf16[32,1664]{1,0:T(8,128)(2,1)S(1)}, u32[]{:S(2)}, u32[]{:S(2)}) collective-permute-start(bf16[32,1664]{1,0:T(8,128)(2,1)} %get-tuple-element.54), channel_id=1, source_target_pairs={{0,24},{2,26},{4,28},{6,30},{8,16},{10,18},{12,20},{14,22},{16,8},... | collective-permute-start | bytes 319496 | tf_op jit(solution)/shard_map/ppermute | solution.py:545
  8.1 9.2 %collective-permute-start.1 = (bf16[32,1664]{1,0:T(8,128)(2,1)}, bf16[32,1664]{1,0:T(8,128)(2,1)S(1)}, u32[]{:S(2)}, u32[]{:S(2)}) collective-permute-start(bf16[32,1664]{1,0:T(8,128)(2,1)} %get-tuple-element.54), channel_id=1, source_target_pairs={{0,16},{2,18},{4,20},{6,22},{8,24},{10,26},{12,28},{14,30},{16,0},... | collective-permute-start | bytes 319496 | tf_op jit(solution)/shard_map/ppermute | solution.py:545
  8.1 9.2 %collective-permute-start = (bf16[32,1664]{1,0:T(8,128)(2,1)}, bf16[32,1664]{1,0:T(8,128)(2,1)S(1)}, u32[]{:S(2)}, u32[]{:S(2)}) collective-permute-start(bf16[32,1664]{1,0:T(8,128)(2,1)} %get-tuple-element.54), channel_id=1, source_target_pairs={{0,8},{2,10},{4,12},{6,14},{8,0},{10,2},{12,4},{14,6},{16,24},{18,... | collective-permute-start | bytes 319496 | tf_op jit(solution)/shard_map/ppermute | solution.py:545
  10.2 8.1 %collective-permute-start.3 = (f32[1,3584]{1,0:T(1,128)S(1)}, f32[1,3584]{1,0:T(1,128)S(1)}, u32[]{:S(2)}, u32[]{:S(2)}) collective-permute-start(f32[1,3584]{1,0:T(1,128)S(1)} %pad_maximum_fusion.2), channel_id=1, source_target_pairs={{0,1},{1,0},{2,3},{3,2},{4,5},{5,4},{6,7},{7,6},{8,9},{9,8},{10,11... | collective-permute-start | bytes 43016 | tf_op jit(solution)/shard_map/ppermute | solution.py:554
  18.3 12.7 %collective-permute-start.4 = (bf16[4,32,1664]{2,1,0:T(8,128)(2,1)S(1)}, bf16[4,32,1664]{2,1,0:T(8,128)(2,1)S(1)}, u32[]{:S(2)}, u32[]{:S(2)}) collective-permute-start(bf16[4,32,1664]{2,1,0:T(8,128)(2,1)S(1)} %pad_maximum_fusion.refs_4_), channel_id=1, source_target_pairs={{0,2},{1,5},{2,0},{3,7},{4,6},{5,1},{6,4},{7,3},{8,10},{9,13},{10,... | collective-permute-start | bytes 1277960 | tf_op jit(solution)/shard_map/ppermute | solution.py:550
  19.9 11.7 %collective-permute-start.5 = (bf16[4,32,1664]{2,1,0:T(8,128)(2,1)S(1)}, bf16[4,32,1664]{2,1,0:T(8,128)(2,1)S(1)}, u32[]{:S(2)}, u32[]{:S(2)}) collective-permute-start(bf16[4,32,1664]{2,1,0:T(8,128)(2,1)S(1)} %pad_maximum_fusion.refs_4_), channel_id=1, source_target_pairs={{0,4},{1,3},{2,6},{3,1},{4,0},{5,7},{6,2},{7,5},{8,12},{9,11},{10,... | collective-permute-start | bytes 1277960 | tf_op jit(solution)/shard_map/ppermute | solution.py:550
  31.0 8.1 %collective-permute-start.6 = (bf16[4,32,1664]{2,1,0:T(8,128)(2,1)S(1)}, bf16[4,32,1664]{2,1,0:T(8,128)(2,1)S(1)}, u32[]{:S(2)}, u32[]{:S(2)}) collective-permute-start(bf16[4,32,1664]{2,1,0:T(8,128)(2,1)S(1)} %collective-permute-done.4.refs_5_), channel_id=1, source_target_pairs={{0,4},{1,3},{2,6},{3,1},{4,0},{5,7},{6,2},{7,5},{8,12},{9,11},{10,... | collective-permute-start | bytes 1277960 | tf_op jit(solution)/shard_map/ppermute | solution.py:550
  31.1 8.1 %collective-permute-start.7 = (bf16[4,32,1664]{2,1,0:T(8,128)(2,1)S(1)}, bf16[4,32,1664]{2,1,0:T(8,128)(2,1)S(1)}, u32[]{:S(2)}, u32[]{:S(2)}) collective-permute-start(bf16[4,32,1664]{2,1,0:T(8,128)(2,1)S(1)} %pad_maximum_fusion.refs_4_), channel_id=1, source_target_pairs={{0,1},{1,0},{2,3},{3,2},{4,5},{5,4},{6,7},{7,6},{8,9},{9,8},{10,11... | collective-permute-start | bytes 1277960 | tf_op jit(solution)/shard_map/ppermute | solution.py:554
  31.1 8.1 %collective-permute-start.8 = (bf16[4,32,1664]{2,1,0:T(8,128)(2,1)S(1)}, bf16[4,32,1664]{2,1,0:T(8,128)(2,1)S(1)}, u32[]{:S(2)}, u32[]{:S(2)}) collective-permute-start(bf16[4,32,1664]{2,1,0:T(8,128)(2,1)S(1)} %collective-permute-done.4.refs_5_), channel_id=1, source_target_pairs={{0,1},{1,0},{2,3},{3,2},{4,5},{5,4},{6,7},{7,6},{8,9},{9,8},{10,11... | collective-permute-start | bytes 1277960 | tf_op jit(solution)/shard_map/ppermute | solution.py:554
  31.6 7.6 %collective-permute-start.9 = (bf16[4,32,1664]{2,1,0:T(8,128)(2,1)S(1)}, bf16[4,32,1664]{2,1,0:T(8,128)(2,1)S(1)}, u32[]{:S(2)}, u32[]{:S(2)}) collective-permute-start(bf16[4,32,1664]{2,1,0:T(8,128)(2,1)S(1)} %collective-permute-done.5.refs_6_), channel_id=1, source_target_pairs={{0,1},{1,0},{2,3},{3,2},{4,5},{5,4},{6,7},{7,6},{8,9},{9,8},{10,11... | collective-permute-start | bytes 1277960 | tf_op jit(solution)/shard_map/ppermute | solution.py:554
  39.2 1.9 %collective-permute-start.10 = (bf16[4,32,1664]{2,1,0:T(8,128)(2,1)S(1)}, bf16[4,32,1664]{2,1,0:T(8,128)(2,1)}, u32[]{:S(2)}, u32[]{:S(2)}) collective-permute-start(bf16[4,32,1664]{2,1,0:T(8,128)(2,1)S(1)} %collective-permute-done.6.refs_7_), channel_id=1, source_target_pairs={{0,1},{1,0},{2,3},{3,2},{4,5},{5,4},{6,7},{7,6},{8,9},{9,8},{10,11... | collective-permute-start | bytes 1277960 | tf_op jit(solution)/shard_map/ppermute | solution.py:554
  87.5 2.6 %collective-permute-start.11 = (bf16[8,32,1664]{2,1,0:T(8,128)(2,1)}, bf16[8,32,1664]{2,1,0:T(8,128)(2,1)S(1)}, u32[]{:S(2)}, u32[]{:S(2)}) collective-permute-start(bf16[8,32,1664]{2,1,0:T(8,128)(2,1)} %get-tuple-element.61), channel_id=1, source_target_pairs={{0,1},{1,0},{2,3},{3,2},{4,5},{5,4},{6,7},{7,6},{8,9},{9,8},{10,11... | collective-permute-start | bytes 2555912 | tf_op jit(solution)/shard_map/ppermute | solution.py:554
  90.3 15.1 %collective-permute-start.12 = (bf16[512,3072]{1,0:T(8,128)(2,1)}, bf16[512,3072]{1,0:T(8,128)(2,1)S(1)}, u32[]{:S(2)}, u32[]{:S(2)}) collective-permute-start(bf16[512,3072]{1,0:T(8,128)(2,1)} %get-tuple-element.63.hg_ref), channel_id=1, source_target_pairs={{0,1},{1,0},{2,3},{3,2},{4,5},{5,4},{6,7},{7,6},{8,9},{9,8},{10,11... | collective-permute-start | bytes 9437192 | tf_op jit(solution)/shard_map/ppermute | solution.py:554
  90.5 7.0 %collective-permute-start.13 = (bf16[8,32,1664]{2,1,0:T(8,128)(2,1)}, bf16[8,32,1664]{2,1,0:T(8,128)(2,1)S(1)}, u32[]{:S(2)}, u32[]{:S(2)}) collective-permute-start(bf16[8,32,1664]{2,1,0:T(8,128)(2,1)} %get-tuple-element.66), channel_id=1, source_target_pairs={{0,1},{1,0},{2,3},{3,2},{4,5},{5,4},{6,7},{7,6},{8,9},{9,8},{10,11... | collective-permute-start | bytes 2555912 | tf_op jit(solution)/shard_map/ppermute | solution.py:554
  90.9 12.7 %collective-permute-start.14 = (bf16[8,32,1664]{2,1,0:T(8,128)(2,1)S(1)}, bf16[8,32,1664]{2,1,0:T(8,128)(2,1)S(1)}, u32[]{:S(2)}, u32[]{:S(2)}) collective-permute-start(bf16[8,32,1664]{2,1,0:T(8,128)(2,1)S(1)} %get-tuple-element.67.refs_0_), channel_id=1, source_target_pairs={{0,4},{1,3},{2,6},{3,1},{4,0},{5,7},{6,2},{7,5},{8,12},{9,11},{10,... | collective-permute-start | bytes 2555912 | tf_op jit(solution)/shard_map/ppermute | solution.py:550
  103.9 8.2 %collective-permute-start.15 = (bf16[4,32,1664]{2,1,0:T(8,128)(2,1)S(1)}, bf16[4,32,1664]{2,1,0:T(8,128)(2,1)S(1)}, u32[]{:S(2)}, u32[]{:S(2)}) collective-permute-start(bf16[4,32,1664]{2,1,0:T(8,128)(2,1)S(1)} %get-tuple-element.69.refs_0_), channel_id=1, source_target_pairs={{0,2},{1,5},{2,0},{3,7},{4,6},{5,1},{6,4},{7,3},{8,10},{9,13},{10,... | collective-permute-start | bytes 1277960 | tf_op jit(solution)/shard_map/ppermute | solution.py:550
  112.2 4.8 %collective-permute-start.16 = (bf16[32,1664]{1,0:T(8,128)(2,1)S(1)}, bf16[32,1664]{1,0:T(8,128)(2,1)S(1)}, u32[]{:S(2)}, u32[]{:S(2)}) collective-permute-start(bf16[32,1664]{1,0:T(8,128)(2,1)S(1)} %get-tuple-element.77), channel_id=1, source_target_pairs={{0,8},{2,10},{4,12},{6,14},{8,0},{10,2},{12,4},{14,6},{16,24},{18,... | collective-permute-start | bytes 319496 | tf_op jit(solution)/shard_map/ppermute | solution.py:545
  112.6 9.8 %collective-permute-start.17 = (bf16[32,1664]{1,0:T(8,128)(2,1)S(1)}, bf16[32,1664]{1,0:T(8,128)(2,1)S(1)}, u32[]{:S(2)}, u32[]{:S(2)}) collective-permute-start(bf16[32,1664]{1,0:T(8,128)(2,1)S(1)} %get-tuple-element.78), channel_id=1, source_target_pairs={{0,16},{2,18},{4,20},{6,22},{8,24},{10,26},{12,28},{14,30},{16,0},... | collective-permute-start | bytes 319496 | tf_op jit(solution)/shard_map/ppermute | solution.py:545
  115.3 7.0 %collective-permute-start.18 = (bf16[32,1664]{1,0:T(8,128)(2,1)S(1)}, bf16[32,1664]{1,0:T(8,128)(2,1)S(1)}, u32[]{:S(2)}, u32[]{:S(2)}) collective-permute-start(bf16[32,1664]{1,0:T(8,128)(2,1)S(1)} %get-tuple-element.79), channel_id=1, source_target_pairs={{0,24},{2,26},{4,28},{6,30},{8,16},{10,18},{12,20},{14,22},{16,8},... | collective-permute-start | bytes 319496 | tf_op jit(solution)/shard_map/ppermute | solution.py:545
  116.6 6.2 %collective-permute-start.19 = (bf16[16,512]{1,0:T(8,128)(2,1)S(1)}, bf16[16,512]{1,0:T(8,128)(2,1)S(1)}, u32[]{:S(2)}, u32[]{:S(2)}) collective-permute-start(bf16[16,512]{1,0:T(8,128)(2,1)S(1)} %slice.20), channel_id=1, source_target_pairs={{0,1},{1,0},{2,3},{3,2},{4,5},{5,4},{6,7},{7,6},{8,9},{9,8},{10,11... | collective-permute-start | bytes 49160 | tf_op jit(solution)/shard_map/ppermute | solution.py:554
  117.0 5.9 %collective-permute-start.20 = (bf16[16,512]{1,0:T(8,128)(2,1)S(1)}, bf16[16,512]{1,0:T(8,128)(2,1)S(1)}, u32[]{:S(2)}, u32[]{:S(2)}) collective-permute-start(bf16[16,512]{1,0:T(8,128)(2,1)S(1)} %slice.24), channel_id=1, source_target_pairs={{0,1},{1,0},{2,3},{3,2},{4,5},{5,4},{6,7},{7,6},{8,9},{9,8},{10,11... | collective-permute-start | bytes 49160 | tf_op jit(solution)/shard_map/ppermute | solution.py:554
  122.3 1.2 collective-permute-start.21
  122.4 1.3 %collective-permute-start.22 = (bf16[16,512]{1,0:T(8,128)(2,1)S(1)}, bf16[16,512]{1,0:T(8,128)(2,1)S(1)}, u32[]{:S(2)}, u32[]{:S(2)}) collective-permute-start(bf16[16,512]{1,0:T(8,128)(2,1)S(1)} %slice.26), channel_id=1, source_target_pairs={{0,1},{1,0},{2,3},{3,2},{4,5},{5,4},{6,7},{7,6},{8,9},{9,8},{10,11... | collective-permute-start | bytes 49160 | tf_op jit(solution)/shard_map/ppermute | solution.py:554

commit v7 on v6

--- a/solution.py
+++ b/solution.py
@@ -77,12 +77,13 @@
 def main_kernel(pieces, chunks, batch_rows, tab_ref, *refs):
     emb_ref, dense_ref, line_ref, far_line_ref = refs[:4]
     u_refs = (refs[4 : 4 + pieces], refs[4 + pieces : 4 + 2 * pieces])
-    hg_ref, wat_s, *du_refs = refs[4 + 2 * pieces : 10 + 2 * pieces]
+    quarters = min(4, chunks)
+    hg_ref, wat_s, *du_refs = refs[4 + 2 * pieces : 6 + 2 * pieces + 2 * quarters]
     (
         x_s, hid_s, mid_s, sl1_s, out_s, sl2_s, sg_s, fg_s, mix_s,
         w1_s, w1t_s, ga_s, w2t_s, w2_s, b1_s, b2_s, gb_s, tt_s, tw_s, tcol_s, q_s,
         dwa_s, dw1_s, dw2_s, dtw_s, dcol_s, dlog_s, dsm_s, start_s, row_s,
-    ) = refs[10 + 2 * pieces :]
+    ) = refs[6 + 2 * pieces + 2 * quarters :]
     n = SUB
     fs, osz, ds = FH // chunks, EO // chunks, D // chunks
     step = pl.program_id(0)
@@ -267,7 +268,7 @@
             holder = core if side == 0 else 1 - core
             cols = HALF * EO
             for n in range(chunks):
-                ref, c = du_refs[2 * side + n * 2 // chunks], n % max(chunks // 2, 1)
+                ref, c = du_refs[quarters * side + n * quarters // chunks], n % (chunks // quarters)
                 at = chunk_at(n, chunks, holder)
                 to = pl.multiple_of(ds * at, ds)
                 where = pl.ds(pl.multiple_of(tab_ref[1 + at] * fs, fs), fs)
@@ -319,7 +320,8 @@
     def own(i, c):
         return (0, c[0] * steps + i)
 
-    grads = [(max(chunks // 2, 1), ds, UC)] * 4
+    quarters = min(4, chunks)
+    grads = [(chunks // quarters, ds, UC)] * (2 * quarters)
     parts = TILE // SUB
     spec = pltpu.PrefetchScalarGridSpec(
         num_scalar_prefetch=1,
@@ -331,7 +333,7 @@
             whole(),
         ]
         + [whole() for _ in (*own_u, *far_u)],
-        out_specs=[pl.BlockSpec((D, TILE), lambda i, c: (0, i))] + [whole()] * 5,
+        out_specs=[pl.BlockSpec((D, TILE), lambda i, c: (0, i))] + [whole()] * (1 + 2 * quarters),
         scratch_shapes=[
             pltpu.VMEM((parts, XR, SUB), BF),
             pltpu.VMEM((parts, D + 16, SUB), BF),
@@ -613,19 +615,23 @@
     far_u = [partner(a) for a in own_u]
     table = jnp.concatenate([core[None].astype(jnp.int32), order])
 
-    hg, wat, own_low, own_high, du_low, du_high = main_call(table, emb.T, own_dense, own_line, far_line, group_sizes.shape, own_u, far_u)
-    du_high = partner(du_high)
+    hg, wat, *grads = main_call(table, emb.T, own_dense, own_line, far_line, group_sizes.shape, own_u, far_u)
+    own, far = grads[: len(grads) // 2], grads[len(grads) // 2 :]
     scale = 1.0 / user_count
     if fast:
-        hg, part = sum_call("sum_cores", [own_high, du_high], [[(0, slice(0, 8)), (1, slice(0, 8))]], [(8, ds, UC)], through=hg)
-        got = cross(part, (2, 1), size)
-        du_low, far_hg = partner(du_low), partner(hg)
-        eg, dg, token = input_call(table, hg, wat, part, None, "input_own")
-        groups = [[(j, slice(4 * b, 4 * b + 4)) for j in range(3)] for b in (1, 0)]
-        part, rest = sum_call("sum_first", [own_low, du_low, got], groups, [(4, ds, UC)] * 2, token)
-        got = cross(part, (1, 2), size)
-        eg, dg, token = input_call(table, far_hg, wat, part, (eg, dg), "input_far")
-        sums = sum_call("sum_second", [rest, got], [[(0, k), (1, k)] for k in range(4)], [(ds, UC)] * 4, token)
+        quarter, every = (4, ds, UC), slice(0, 4)
+        (third,) = sum_call("sum_fourth", [own[3], partner(far[3])], [[(0, every), (1, every)]], [quarter])
+        got_third = cross(third, (2, 1), size)
+        hg, second = sum_call("sum_third", [own[2], partner(far[2])], [[(0, every), (1, every)]], [quarter], third, hg)
+        got_second = cross(second, (2, 1), size)
+        far_first, far_hg = partner(far[1]), partner(hg)
+        eg, dg, token = input_call(table, hg, wat, second, None, "input_own")
+        (first,) = sum_call("sum_second", [own[1], far_first, got_third], [[(j, every) for j in range(3)]], [quarter], token)
+        got_first = cross(first, (1, 2), size)
+        far_none = partner(far[0])
+        eg, dg, token = input_call(table, far_hg, wat, first, (eg, dg), "input_far")
+        groups = [[(j, k) for j in range(4)] for k in range(4)]
+        sums = sum_call("sum_first", [own[0], far_none, got_second, got_first], groups, [(ds, UC)] * 4, token)
         parts = [sums[0]] + [hop(sums[a], 4 * a, size) for a in range(1, 4)]
         parts += [partner(a[fs:, QA : QA + 512]) for a in parts]
         out = finish_call(scale, one_core, sums[0], parts, ds, fs, osz)
@@ -633,10 +639,10 @@
         return (
             eg.T, dg.T, g_emb.T, g_dense, g_bias[0], g_w1, g_b1, g_w2, g_b2, g_gate.T[None], g_gb, g_tower[None], g_t1, g_t2, g_t3[0],
         )
-    eg, dg, token = input_call(table, hg, wat, du_high, None, "input_own")
+    eg, dg, token = input_call(table, hg, wat, far[0], None, "input_own")
     eg, dg, _ = input_call(table, partner(hg), wat, token, (eg, dg), "input_far")
     scatter = functools.partial(lax.psum_scatter, axis_name="rows", scatter_dimension=0, tiled=True)
-    wide = add_wide(own_low[0], partner(du_low)[0])
+    wide = add_wide(own[0][0], partner(far[0])[0])
     upper, near = wide[0:FH, QA:UC], wide[FH:, QA : QA + XR]
     far, small = partner(near), upper[:, HALF * EO :]
     ta = scatter(jnp.concatenate([jnp.where(core == 0, near, far), jnp.where(core == 0, far, near)], axis=0)) * scale

time: 125 us -> 122 us (0.976)
  waiting for transfers between devices: 42.3 us -> 37.2 us
  starting transfers between devices: 16.9 us -> 19.1 us
    ppermute x5 -> x6, waiting for transfers between devices: 25.3 us -> 19.2 us  [cross(): return lax.ppermute(a, ('rows', 'task'), pairs)]
    ppermute x6, waiting for transfers between devices: 11.8 us -> 13.5 us  [hop(): return lax.ppermute(a, 'rows', [(i, i ^ mask) for i in range(size)])]
    ppermute x12 -> x14, starting transfers between devices: 1.95 us -> 3.5 us  [partner(): return lax.ppermute(a, 'task', [(0, 1), (1, 0)])]
    ppermute x12 -> x14, waiting for transfers between devices: 5.12 us -> 4.41 us  [partner(): return lax.ppermute(a, 'task', [(0, 1), (1, 0)])]
    ppermute x5 -> x6, starting transfers between devices: 4.78 us -> 5.48 us  [cross(): return lax.ppermute(a, ('rows', 'task'), pairs)]
  transfers between devices with their start and end apart: 23 -> 26, of which waited for: 12 -> 12; matrix products, arithmetic and copies ran while one was open for 3% -> 3% of each run, Pallas kernels for 9% -> 9%
where the time goes in v7:
time: 122 us
  Pallas kernels  60.4 us (50%)
  waiting for transfers between devices  37.2 us (30%)
  starting transfers between devices  19.1 us (16%)
  local copies, waits for them, and re-layouts  2.15 us (2%)
  between operations  1.63 us (1%)
    pallas_call x1, Pallas kernels, main_call(): pl.pallas_call(functools.partial(main_kernel, pieces, chunks, rows // siz...  46.2 us
    ppermute x6, waiting for transfers between devices, cross(): return lax.ppermute(a, ('rows', 'task'), pairs)  19.2 us
    ppermute x6, waiting for transfers between devices, hop(): return lax.ppermute(a, 'rows', [(i, i ^ mask) for i in range(size)])  13.5 us
    pallas_call x2, Pallas kernels, input_call(): pl.pallas_call(input_kernel, grid_spec=spec, out_shape=[jax.ShapeDtypeStr...  11.1 us
    ppermute x6, starting transfers between devices, hop(): return lax.ppermute(a, 'rows', [(i, i ^ mask) for i in range(size)])  10.1 us
    ppermute x6, starting transfers between devices, cross(): return lax.ppermute(a, ('rows', 'task'), pairs)  5.48 us
    ppermute x14, waiting for transfers between devices, partner(): return lax.ppermute(a, 'task', [(0, 1), (1, 0)])  4.41 us
    ppermute x14, starting transfers between devices, partner(): return lax.ppermute(a, 'task', [(0, 1), (1, 0)])  3.5 us
  transfers between devices with their start and end apart: 26, of which 12 were waited for; matrix products, arithmetic and copies ran while one was open for 3% of the time, Pallas kernels for 9%

profile of v7, /device:TPU:0, one launch (start us, length us, event | category | flops | bytes accessed | tf_op | source)
XLA Modules:
  0.0 121.6 jit_solution(18062530591971528392)
XLA Ops:
  0.7 0.0 copy-start
  1.4 1.7 %pack.1 = (bf16[32,1664]{1,0:T(8,128)(2,1)}, f32[1,8192]{1,0:T(1,128)}) custom-call(s32[1]{0:T(128)} %bitcast.core_ref, bf16[32,416]{1,0:T(8,128)(2,1)} %bitcast.29, bf16[13,32]{1,0:T(8,128)(2,1)} %dense_ref.1, bf16[1,32]{1,0:T(2,128)(2,1)} %bitcast.32, bf16[4,32,256]{2,1,0:T(8,128)(2,1)} %w1_ref.1, bf16[4,16,128]{2,1,0:T(8,128)(2,1)} %w2_ref.1, ...), custom_call_target="tpu_custom_call" | custom-call | tf_op jit(solution)/shard_map/pack/pallas_call | solution.py:468
  3.1 5.0 %collective-permute-start.2 = (bf16[32,1664]{1,0:T(8,128)(2,1)}, bf16[32,1664]{1,0:T(8,128)(2,1)S(1)}, u32[]{:S(2)}, u32[]{:S(2)}) collective-permute-start(bf16[32,1664]{1,0:T(8,128)(2,1)} %get-tuple-element.56), channel_id=1, source_target_pairs={{0,24},{2,26},{4,28},{6,30},{8,16},{10,18},{12,20},{14,22},{16,8},... | collective-permute-start | bytes 319496 | tf_op jit(solution)/shard_map/ppermute | solution.py:547
  8.1 0.0 collective-permute-start.1
  8.1 0.6 collective-permute-start
  8.8 0.7 slice.19
  9.5 0.7 constant_dynamic-slice_fusion
  10.2 0.1 collective-permute-start.3
  10.3 0.7 slice.18
  11.0 1.2 collective-permute-done.2
  12.2 5.1 %collective-permute-done.1 = bf16[32,1664]{1,0:T(8,128)(2,1)S(1)} collective-permute-done((bf16[32,1664]{1,0:T(8,128)(2,1)}, bf16[32,1664]{1,0:T(8,128)(2,1)S(1)}, u32[]{:S(2)}, u32[]{:S(2)}) %collective-permute-start.1) | collective-permute-done | bytes 106528 | tf_op jit(solution)/shard_map/ppermute | solution.py:547
  17.3 1.0 pad_maximum_fusion.refs_4_
  18.3 1.6 %collective-permute-start.4 = (bf16[4,32,1664]{2,1,0:T(8,128)(2,1)S(1)}, bf16[4,32,1664]{2,1,0:T(8,128)(2,1)S(1)}, u32[]{:S(2)}, u32[]{:S(2)}) collective-permute-start(bf16[4,32,1664]{2,1,0:T(8,128)(2,1)S(1)} %pad_maximum_fusion.refs_4_), channel_id=1, source_target_pairs={{0,2},{1,5},{2,0},{3,7},{4,6},{5,1},{6,4},{7,3},{8,10},{9,13},{10,... | collective-permute-start | bytes 1277960 | tf_op jit(solution)/shard_map/ppermute | solution.py:552
  19.9 1.5 %collective-permute-start.5 = (bf16[4,32,1664]{2,1,0:T(8,128)(2,1)S(1)}, bf16[4,32,1664]{2,1,0:T(8,128)(2,1)S(1)}, u32[]{:S(2)}, u32[]{:S(2)}) collective-permute-start(bf16[4,32,1664]{2,1,0:T(8,128)(2,1)S(1)} %pad_maximum_fusion.refs_4_), channel_id=1, source_target_pairs={{0,4},{1,3},{2,6},{3,1},{4,0},{5,7},{6,2},{7,5},{8,12},{9,11},{10,... | collective-permute-start | bytes 1277960 | tf_op jit(solution)/shard_map/ppermute | solution.py:552
  21.4 9.6 %collective-permute-done.4.refs_5_ = bf16[4,32,1664]{2,1,0:T(8,128)(2,1)S(1)} collective-permute-done((bf16[4,32,1664]{2,1,0:T(8,128)(2,1)S(1)}, bf16[4,32,1664]{2,1,0:T(8,128)(2,1)S(1)}, u32[]{:S(2)}, u32[]{:S(2)}) %collective-permute-start.4) | collective-permute-done | bytes 426016 | tf_op jit(solution)/shard_map/ppermute | solution.py:552
  31.0 0.1 collective-permute-start.6
  31.1 0.5 collective-permute-start.8
  31.6 0.0 collective-permute-start.9
  31.6 7.5 %collective-permute-done.6.refs_7_ = bf16[4,32,1664]{2,1,0:T(8,128)(2,1)S(1)} collective-permute-done((bf16[4,32,1664]{2,1,0:T(8,128)(2,1)S(1)}, bf16[4,32,1664]{2,1,0:T(8,128)(2,1)S(1)}, u32[]{:S(2)}, u32[]{:S(2)}) %collective-permute-start.6) | collective-permute-done | bytes 426016 | tf_op jit(solution)/shard_map/ppermute | solution.py:552
  39.2 0.1 pad_add_fusion.tab_ref
  39.3 1.8 %collective-permute-done.10.refs_11_ = bf16[4,32,1664]{2,1,0:T(8,128)(2,1)} collective-permute-done((bf16[4,32,1664]{2,1,0:T(8,128)(2,1)S(1)}, bf16[4,32,1664]{2,1,0:T(8,128)(2,1)}, u32[]{:S(2)}, u32[]{:S(2)}) %collective-permute-start.10) | collective-permute-done | bytes 426016 | tf_op jit(solution)/shard_map/ppermute | solution.py:556
  41.1 46.2 %experts.1 = (bf16[512,3072]{1,0:T(8,128)(2,1)}, bf16[512,448]{1,0:T(8,128)(2,1)}, bf16[4,32,1664]{2,1,0:T(8,128)(2,1)S(1)}, bf16[4,32,1664]{2,1,0:T(8,128)(2,1)...) custom-call(s32[17]{0:T(128)S(1)} %pad_add_fusion.tab_ref, ...), custom_call_target="tpu_custom_call" | custom-call | flops 49999998976 | bytes 24000000 | tf_op jit(solution)/shard_map/experts/pallas_call | solution.py:370
  87.2 0.2 collective-permute-start.12
  87.4 0.4 collective-permute-start.11
  87.8 1.3 %collective-permute-done.12.refs_1_ = bf16[4,32,1664]{2,1,0:T(8,128)(2,1)S(1)} collective-permute-done((bf16[4,32,1664]{2,1,0:T(8,128)(2,1)S(1)}, bf16[4,32,1664]{2,1,0:T(8,128)(2,1)S(1)}, u32[]{:S(2)}, u32[]{:S(2)}) %collective-permute-start.12) | collective-permute-done | bytes 426016 | tf_op jit(solution)/shard_map/ppermute | solution.py:556
  89.1 0.1 sum_fourth.1.refs_2_
  89.2 0.5 collective-permute-done.11.refs_1_
  89.7 0.1 sum_third.1
  89.8 0.2 collective-permute-start.13
  90.0 0.4 collective-permute-start.14
  90.3 0.1 collective-permute-start.15
  90.4 1.3 %collective-permute-start.16 = (bf16[4,32,1664]{2,1,0:T(8,128)(2,1)S(1)}, bf16[4,32,1664]{2,1,0:T(8,128)(2,1)S(1)}, u32[]{:S(2)}, u32[]{:S(2)}) collective-permute-start(bf16[4,32,1664]{2,1,0:T(8,128)(2,1)S(1)} %get-tuple-element.78), channel_id=1, source_target_pairs={{0,1},{1,0},{2,3},{3,2},{4,5},{5,4},{6,7},{7,6},{8,9},{9,8},{10,11... | collective-permute-start | bytes 1277960 | tf_op jit(solution)/shard_map/ppermute | solution.py:556
  91.7 0.7 collective-permute-start.17
  92.4 6.5 %input_own.1 = (f32[416,6144]{1,0:T(8,128)}, f32[13,6144]{1,0:T(8,128)}, f32[8,128]{1,0:T(8,128)S(1)}) custom-call(s32[17]{0:T(128)S(1)} %pad_add_fusion.tab_ref, bf16[512,3072]{1,0:T(8,128)(2,1)} %get-tuple-element.67.hg_ref, bf16[512,448]{1,0:T(8,128)(2,1)S(1)} %copy-done.1, bf16[4,32,1664]{2,1,0:T(8,128)(2,1)S(1)} %get-tuple-element.71.refs_0_), custom_call_target="tpu_custom_call" | custom-call | flops 4000000000 | bytes 9000000 | tf_op jit(solution)/shard_map/input_own/pallas_call | solution.py:411
  98.9 0.2 sum_second.1.refs_0_
  99.0 1.6 %collective-permute-start.18 = (bf16[4,32,1664]{2,1,0:T(8,128)(2,1)S(1)}, bf16[4,32,1664]{2,1,0:T(8,128)(2,1)S(1)}, u32[]{:S(2)}, u32[]{:S(2)}) collective-permute-start(bf16[4,32,1664]{2,1,0:T(8,128)(2,1)S(1)} %sum_second.1.refs_0_), channel_id=1, source_target_pairs={{0,2},{1,5},{2,0},{3,7},{4,6},{5,1},{6,4},{7,3},{8,10},{9,13},{10,... | collective-permute-start | bytes 1277960 | tf_op jit(solution)/shard_map/ppermute | solution.py:552
  100.6 4.6 %input_far.1 = (f32[416,6144]{1,0:T(8,128)}, f32[13,6144]{1,0:T(8,128)}, f32[8,128]{1,0:T(8,128)S(1)}) custom-call(s32[17]{0:T(128)S(1)} %pad_add_fusion.tab_ref, bf16[512,3072]{1,0:T(8,128)(2,1)S(1)} %collective-permute-done.13.hg_ref, bf16[512,448]{1,0:T(8,128)(2,1)S(1)} %copy-done.1, ...), custom_call_target="tpu_custom_call", output_to_operand_aliasing={{0}: (4, {}), {1}: (5, {})} | custom-call | flops 4000000000 | bytes 9000000 | tf_op jit(solution)/shard_map/input_far/pallas_call | solution.py:411
  105.2 2.0 %collective-permute-done.18.refs_3_ = bf16[4,32,1664]{2,1,0:T(8,128)(2,1)S(1)} collective-permute-done((bf16[4,32,1664]{2,1,0:T(8,128)(2,1)S(1)}, bf16[4,32,1664]{2,1,0:T(8,128)(2,1)S(1)}, u32[]{:S(2)}, u32[]{:S(2)}) %collective-permute-start.18) | collective-permute-done | bytes 426016 | tf_op jit(solution)/shard_map/ppermute | solution.py:552
  107.2 0.2 sum_first.1
  107.5 0.4 collective-permute-start.19
  107.9 2.7 %collective-permute-start.20 = (bf16[32,1664]{1,0:T(8,128)(2,1)S(1)}, bf16[32,1664]{1,0:T(8,128)(2,1)S(1)}, u32[]{:S(2)}, u32[]{:S(2)}) collective-permute-start(bf16[32,1664]{1,0:T(8,128)(2,1)S(1)} %get-tuple-element.82), channel_id=1, source_target_pairs={{0,16},{2,18},{4,20},{6,22},{8,24},{10,26},{12,28},{14,30},{16,0},... | collective-permute-start | bytes 319496 | tf_op jit(solution)/shard_map/ppermute | solution.py:547
  110.6 1.3 %collective-permute-start.21 = (bf16[32,1664]{1,0:T(8,128)(2,1)S(1)}, bf16[32,1664]{1,0:T(8,128)(2,1)S(1)}, u32[]{:S(2)}, u32[]{:S(2)}) collective-permute-start(bf16[32,1664]{1,0:T(8,128)(2,1)S(1)} %get-tuple-element.83), channel_id=1, source_target_pairs={{0,24},{2,26},{4,28},{6,30},{8,16},{10,18},{12,20},{14,22},{16,8},... | collective-permute-start | bytes 319496 | tf_op jit(solution)/shard_map/ppermute | solution.py:547
  111.9 2.4 %collective-permute-done.19.refs_1_ = bf16[32,1664]{1,0:T(8,128)(2,1)S(1)} collective-permute-done((bf16[32,1664]{1,0:T(8,128)(2,1)S(1)}, bf16[32,1664]{1,0:T(8,128)(2,1)S(1)}, u32[]{:S(2)}, u32[]{:S(2)}) %collective-permute-start.19) | collective-permute-done | bytes 106528 | tf_op jit(solution)/shard_map/ppermute | solution.py:547
  114.3 4.9 %collective-permute-done.20.refs_2_ = bf16[32,1664]{1,0:T(8,128)(2,1)S(1)} collective-permute-done((bf16[32,1664]{1,0:T(8,128)(2,1)S(1)}, bf16[32,1664]{1,0:T(8,128)(2,1)S(1)}, u32[]{:S(2)}, u32[]{:S(2)}) %collective-permute-start.20) | collective-permute-done | bytes 106528 | tf_op jit(solution)/shard_map/ppermute | solution.py:547
  119.2 0.5 collective-permute-start.25
  119.7 0.7 collective-permute-done.24.refs_6_
  120.4 0.2 collective-permute-done.25.refs_7_
  120.5 0.8 finish.1
  (32 shorter events, 0.1 us)
Async XLA Ops:
  0.7 10.4 %copy-start = (bf16[6144,13]{0,1:T(8,128)(2,1)S(1)}, bf16[6144,13]{0,1:T(8,128)(2,1)}, u32[]{:S(2)}) copy-start(bf16[6144,13]{0,1:T(8,128)(2,1)} %param.18) | copy-start | bytes 479236
  3.1 9.2 %collective-permute-start.2 = (bf16[32,1664]{1,0:T(8,128)(2,1)}, bf16[32,1664]{1,0:T(8,128)(2,1)S(1)}, u32[]{:S(2)}, u32[]{:S(2)}) collective-permute-start(bf16[32,1664]{1,0:T(8,128)(2,1)} %get-tuple-element.56), channel_id=1, source_target_pairs={{0,24},{2,26},{4,28},{6,30},{8,16},{10,18},{12,20},{14,22},{16,8},... | collective-permute-start | bytes 319496 | tf_op jit(solution)/shard_map/ppermute | solution.py:547
  8.1 9.2 %collective-permute-start.1 = (bf16[32,1664]{1,0:T(8,128)(2,1)}, bf16[32,1664]{1,0:T(8,128)(2,1)S(1)}, u32[]{:S(2)}, u32[]{:S(2)}) collective-permute-start(bf16[32,1664]{1,0:T(8,128)(2,1)} %get-tuple-element.56), channel_id=1, source_target_pairs={{0,16},{2,18},{4,20},{6,22},{8,24},{10,26},{12,28},{14,30},{16,0},... | collective-permute-start | bytes 319496 | tf_op jit(solution)/shard_map/ppermute | solution.py:547
  8.1 9.2 %collective-permute-start = (bf16[32,1664]{1,0:T(8,128)(2,1)}, bf16[32,1664]{1,0:T(8,128)(2,1)S(1)}, u32[]{:S(2)}, u32[]{:S(2)}) collective-permute-start(bf16[32,1664]{1,0:T(8,128)(2,1)} %get-tuple-element.56), channel_id=1, source_target_pairs={{0,8},{2,10},{4,12},{6,14},{8,0},{10,2},{12,4},{14,6},{16,24},{18,... | collective-permute-start | bytes 319496 | tf_op jit(solution)/shard_map/ppermute | solution.py:547
  10.2 8.1 %collective-permute-start.3 = (f32[1,3584]{1,0:T(1,128)S(1)}, f32[1,3584]{1,0:T(1,128)S(1)}, u32[]{:S(2)}, u32[]{:S(2)}) collective-permute-start(f32[1,3584]{1,0:T(1,128)S(1)} %pad_maximum_fusion.2), channel_id=1, source_target_pairs={{0,1},{1,0},{2,3},{3,2},{4,5},{5,4},{6,7},{7,6},{8,9},{9,8},{10,11... | collective-permute-start | bytes 43016 | tf_op jit(solution)/shard_map/ppermute | solution.py:556
  18.3 12.7 %collective-permute-start.4 = (bf16[4,32,1664]{2,1,0:T(8,128)(2,1)S(1)}, bf16[4,32,1664]{2,1,0:T(8,128)(2,1)S(1)}, u32[]{:S(2)}, u32[]{:S(2)}) collective-permute-start(bf16[4,32,1664]{2,1,0:T(8,128)(2,1)S(1)} %pad_maximum_fusion.refs_4_), channel_id=1, source_target_pairs={{0,2},{1,5},{2,0},{3,7},{4,6},{5,1},{6,4},{7,3},{8,10},{9,13},{10,... | collective-permute-start | bytes 1277960 | tf_op jit(solution)/shard_map/ppermute | solution.py:552
  19.9 11.7 %collective-permute-start.5 = (bf16[4,32,1664]{2,1,0:T(8,128)(2,1)S(1)}, bf16[4,32,1664]{2,1,0:T(8,128)(2,1)S(1)}, u32[]{:S(2)}, u32[]{:S(2)}) collective-permute-start(bf16[4,32,1664]{2,1,0:T(8,128)(2,1)S(1)} %pad_maximum_fusion.refs_4_), channel_id=1, source_target_pairs={{0,4},{1,3},{2,6},{3,1},{4,0},{5,7},{6,2},{7,5},{8,12},{9,11},{10,... | collective-permute-start | bytes 1277960 | tf_op jit(solution)/shard_map/ppermute | solution.py:552
  31.0 8.1 %collective-permute-start.6 = (bf16[4,32,1664]{2,1,0:T(8,128)(2,1)S(1)}, bf16[4,32,1664]{2,1,0:T(8,128)(2,1)S(1)}, u32[]{:S(2)}, u32[]{:S(2)}) collective-permute-start(bf16[4,32,1664]{2,1,0:T(8,128)(2,1)S(1)} %collective-permute-done.4.refs_5_), channel_id=1, source_target_pairs={{0,4},{1,3},{2,6},{3,1},{4,0},{5,7},{6,2},{7,5},{8,12},{9,11},{10,... | collective-permute-start | bytes 1277960 | tf_op jit(solution)/shard_map/ppermute | solution.py:552
  31.1 8.1 %collective-permute-start.7 = (bf16[4,32,1664]{2,1,0:T(8,128)(2,1)S(1)}, bf16[4,32,1664]{2,1,0:T(8,128)(2,1)S(1)}, u32[]{:S(2)}, u32[]{:S(2)}) collective-permute-start(bf16[4,32,1664]{2,1,0:T(8,128)(2,1)S(1)} %pad_maximum_fusion.refs_4_), channel_id=1, source_target_pairs={{0,1},{1,0},{2,3},{3,2},{4,5},{5,4},{6,7},{7,6},{8,9},{9,8},{10,11... | collective-permute-start | bytes 1277960 | tf_op jit(solution)/shard_map/ppermute | solution.py:556
  31.1 8.1 %collective-permute-start.8 = (bf16[4,32,1664]{2,1,0:T(8,128)(2,1)S(1)}, bf16[4,32,1664]{2,1,0:T(8,128)(2,1)S(1)}, u32[]{:S(2)}, u32[]{:S(2)}) collective-permute-start(bf16[4,32,1664]{2,1,0:T(8,128)(2,1)S(1)} %collective-permute-done.4.refs_5_), channel_id=1, source_target_pairs={{0,1},{1,0},{2,3},{3,2},{4,5},{5,4},{6,7},{7,6},{8,9},{9,8},{10,11... | collective-permute-start | bytes 1277960 | tf_op jit(solution)/shard_map/ppermute | solution.py:556
  31.6 7.6 %collective-permute-start.9 = (bf16[4,32,1664]{2,1,0:T(8,128)(2,1)S(1)}, bf16[4,32,1664]{2,1,0:T(8,128)(2,1)S(1)}, u32[]{:S(2)}, u32[]{:S(2)}) collective-permute-start(bf16[4,32,1664]{2,1,0:T(8,128)(2,1)S(1)} %collective-permute-done.5.refs_6_), channel_id=1, source_target_pairs={{0,1},{1,0},{2,3},{3,2},{4,5},{5,4},{6,7},{7,6},{8,9},{9,8},{10,11... | collective-permute-start | bytes 1277960 | tf_op jit(solution)/shard_map/ppermute | solution.py:556
  39.2 1.9 %collective-permute-start.10 = (bf16[4,32,1664]{2,1,0:T(8,128)(2,1)S(1)}, bf16[4,32,1664]{2,1,0:T(8,128)(2,1)}, u32[]{:S(2)}, u32[]{:S(2)}) collective-permute-start(bf16[4,32,1664]{2,1,0:T(8,128)(2,1)S(1)} %collective-permute-done.6.refs_7_), channel_id=1, source_target_pairs={{0,1},{1,0},{2,3},{3,2},{4,5},{5,4},{6,7},{7,6},{8,9},{9,8},{10,11... | collective-permute-start | bytes 1277960 | tf_op jit(solution)/shard_map/ppermute | solution.py:556
  39.2 1.8 %copy-start.2 = (bf16[4,32,1664]{2,1,0:T(8,128)(2,1)}, bf16[4,32,1664]{2,1,0:T(8,128)(2,1)S(1)}, u32[]{:S(2)}) copy-start(bf16[4,32,1664]{2,1,0:T(8,128)(2,1)S(1)} %collective-permute-done.9.refs_10_) | copy-start | bytes 1277956
  87.2 5.2 %copy-start.1 = (bf16[512,448]{1,0:T(8,128)(2,1)S(1)}, bf16[512,448]{1,0:T(8,128)(2,1)}, u32[]{:S(2)}) copy-start(bf16[512,448]{1,0:T(8,128)(2,1)} %get-tuple-element.68.wat_ref) | copy-start | bytes 1376260
  87.2 1.8 %collective-permute-start.12 = (bf16[4,32,1664]{2,1,0:T(8,128)(2,1)S(1)}, bf16[4,32,1664]{2,1,0:T(8,128)(2,1)S(1)}, u32[]{:S(2)}, u32[]{:S(2)}) collective-permute-start(bf16[4,32,1664]{2,1,0:T(8,128)(2,1)S(1)} %get-tuple-element.65), channel_id=1, source_target_pairs={{0,1},{1,0},{2,3},{3,2},{4,5},{5,4},{6,7},{7,6},{8,9},{9,8},{10,11... | collective-permute-start | bytes 1277960 | tf_op jit(solution)/shard_map/ppermute | solution.py:556
  87.4 2.2 %collective-permute-start.11 = (bf16[4,32,1664]{2,1,0:T(8,128)(2,1)S(1)}, bf16[4,32,1664]{2,1,0:T(8,128)(2,1)S(1)}, u32[]{:S(2)}, u32[]{:S(2)}) collective-permute-start(bf16[4,32,1664]{2,1,0:T(8,128)(2,1)S(1)} %get-tuple-element.63), channel_id=1, source_target_pairs={{0,1},{1,0},{2,3},{3,2},{4,5},{5,4},{6,7},{7,6},{8,9},{9,8},{10,11... | collective-permute-start | bytes 1277960 | tf_op jit(solution)/shard_map/ppermute | solution.py:556
  89.8 10.8 %collective-permute-start.13 = (bf16[512,3072]{1,0:T(8,128)(2,1)}, bf16[512,3072]{1,0:T(8,128)(2,1)S(1)}, u32[]{:S(2)}, u32[]{:S(2)}) collective-permute-start(bf16[512,3072]{1,0:T(8,128)(2,1)} %get-tuple-element.67.hg_ref), channel_id=1, source_target_pairs={{0,1},{1,0},{2,3},{3,2},{4,5},{5,4},{6,7},{7,6},{8,9},{9,8},{10,11... | collective-permute-start | bytes 9437192 | tf_op jit(solution)/shard_map/ppermute | solution.py:556
  90.0 8.9 %collective-permute-start.14 = (bf16[4,32,1664]{2,1,0:T(8,128)(2,1)S(1)}, bf16[4,32,1664]{2,1,0:T(8,128)(2,1)S(1)}, u32[]{:S(2)}, u32[]{:S(2)}) collective-permute-start(bf16[4,32,1664]{2,1,0:T(8,128)(2,1)S(1)} %get-tuple-element.70), channel_id=1, source_target_pairs={{0,1},{1,0},{2,3},{3,2},{4,5},{5,4},{6,7},{7,6},{8,9},{9,8},{10,11... | collective-permute-start | bytes 1277960 | tf_op jit(solution)/shard_map/ppermute | solution.py:556
  90.3 8.5 %collective-permute-start.15 = (bf16[4,32,1664]{2,1,0:T(8,128)(2,1)S(1)}, bf16[4,32,1664]{2,1,0:T(8,128)(2,1)S(1)}, u32[]{:S(2)}, u32[]{:S(2)}) collective-permute-start(bf16[4,32,1664]{2,1,0:T(8,128)(2,1)S(1)} %sum_fourth.1.refs_2_), channel_id=1, source_target_pairs={{0,4},{1,3},{2,6},{3,1},{4,0},{5,7},{6,2},{7,5},{8,12},{9,11},{10,... | collective-permute-start | bytes 1277960 | tf_op jit(solution)/shard_map/ppermute | solution.py:552
  90.4 14.8 %collective-permute-start.16 = (bf16[4,32,1664]{2,1,0:T(8,128)(2,1)S(1)}, bf16[4,32,1664]{2,1,0:T(8,128)(2,1)S(1)}, u32[]{:S(2)}, u32[]{:S(2)}) collective-permute-start(bf16[4,32,1664]{2,1,0:T(8,128)(2,1)S(1)} %get-tuple-element.78), channel_id=1, source_target_pairs={{0,1},{1,0},{2,3},{3,2},{4,5},{5,4},{6,7},{7,6},{8,9},{9,8},{10,11... | collective-permute-start | bytes 1277960 | tf_op jit(solution)/shard_map/ppermute | solution.py:556
  91.7 13.5 %collective-permute-start.17 = (bf16[4,32,1664]{2,1,0:T(8,128)(2,1)S(1)}, bf16[4,32,1664]{2,1,0:T(8,128)(2,1)S(1)}, u32[]{:S(2)}, u32[]{:S(2)}) collective-permute-start(bf16[4,32,1664]{2,1,0:T(8,128)(2,1)S(1)} %get-tuple-element.71.refs_0_), channel_id=1, source_target_pairs={{0,4},{1,3},{2,6},{3,1},{4,0},{5,7},{6,2},{7,5},{8,12},{9,11},{10,... | collective-permute-start | bytes 1277960 | tf_op jit(solution)/shard_map/ppermute | solution.py:552
  99.0 8.2 %collective-permute-start.18 = (bf16[4,32,1664]{2,1,0:T(8,128)(2,1)S(1)}, bf16[4,32,1664]{2,1,0:T(8,128)(2,1)S(1)}, u32[]{:S(2)}, u32[]{:S(2)}) collective-permute-start(bf16[4,32,1664]{2,1,0:T(8,128)(2,1)S(1)} %sum_second.1.refs_0_), channel_id=1, source_target_pairs={{0,2},{1,5},{2,0},{3,7},{4,6},{5,1},{6,4},{7,3},{8,10},{9,13},{10,... | collective-permute-start | bytes 1277960 | tf_op jit(solution)/shard_map/ppermute | solution.py:552
  107.5 6.8 %collective-permute-start.19 = (bf16[32,1664]{1,0:T(8,128)(2,1)S(1)}, bf16[32,1664]{1,0:T(8,128)(2,1)S(1)}, u32[]{:S(2)}, u32[]{:S(2)}) collective-permute-start(bf16[32,1664]{1,0:T(8,128)(2,1)S(1)} %get-tuple-element.81), channel_id=1, source_target_pairs={{0,8},{2,10},{4,12},{6,14},{8,0},{10,2},{12,4},{14,6},{16,24},{18,... | collective-permute-start | bytes 319496 | tf_op jit(solution)/shard_map/ppermute | solution.py:547
  107.9 11.3 %collective-permute-start.20 = (bf16[32,1664]{1,0:T(8,128)(2,1)S(1)}, bf16[32,1664]{1,0:T(8,128)(2,1)S(1)}, u32[]{:S(2)}, u32[]{:S(2)}) collective-permute-start(bf16[32,1664]{1,0:T(8,128)(2,1)S(1)} %get-tuple-element.82), channel_id=1, source_target_pairs={{0,16},{2,18},{4,20},{6,22},{8,24},{10,26},{12,28},{14,30},{16,0},... | collective-permute-start | bytes 319496 | tf_op jit(solution)/shard_map/ppermute | solution.py:547
  110.6 8.6 %collective-permute-start.21 = (bf16[32,1664]{1,0:T(8,128)(2,1)S(1)}, bf16[32,1664]{1,0:T(8,128)(2,1)S(1)}, u32[]{:S(2)}, u32[]{:S(2)}) collective-permute-start(bf16[32,1664]{1,0:T(8,128)(2,1)S(1)} %get-tuple-element.83), channel_id=1, source_target_pairs={{0,24},{2,26},{4,28},{6,30},{8,16},{10,18},{12,20},{14,22},{16,8},... | collective-permute-start | bytes 319496 | tf_op jit(solution)/shard_map/ppermute | solution.py:547
  111.9 7.8 %collective-permute-start.22 = (bf16[16,512]{1,0:T(8,128)(2,1)S(1)}, bf16[16,512]{1,0:T(8,128)(2,1)S(1)}, u32[]{:S(2)}, u32[]{:S(2)}) collective-permute-start(bf16[16,512]{1,0:T(8,128)(2,1)S(1)} %slice.20), channel_id=1, source_target_pairs={{0,1},{1,0},{2,3},{3,2},{4,5},{5,4},{6,7},{7,6},{8,9},{9,8},{10,11... | collective-permute-start | bytes 49160 | tf_op jit(solution)/shard_map/ppermute | solution.py:556
  114.3 5.4 %collective-permute-start.23 = (bf16[16,512]{1,0:T(8,128)(2,1)S(1)}, bf16[16,512]{1,0:T(8,128)(2,1)S(1)}, u32[]{:S(2)}, u32[]{:S(2)}) collective-permute-start(bf16[16,512]{1,0:T(8,128)(2,1)S(1)} %slice.24), channel_id=1, source_target_pairs={{0,1},{1,0},{2,3},{3,2},{4,5},{5,4},{6,7},{7,6},{8,9},{9,8},{10,11... | collective-permute-start | bytes 49160 | tf_op jit(solution)/shard_map/ppermute | solution.py:556
  119.2 1.2 collective-permute-start.24
  119.2 1.3 %collective-permute-start.25 = (bf16[16,512]{1,0:T(8,128)(2,1)S(1)}, bf16[16,512]{1,0:T(8,128)(2,1)S(1)}, u32[]{:S(2)}, u32[]{:S(2)}) collective-permute-start(bf16[16,512]{1,0:T(8,128)(2,1)S(1)} %slice.26), channel_id=1, source_target_pairs={{0,1},{1,0},{2,3},{3,2},{4,5},{5,4},{6,7},{7,6},{8,9},{9,8},{10,11... | collective-permute-start | bytes 49160 | tf_op jit(solution)/shard_map/ppermute | solution.py:556

commit v8 on v7

--- a/solution.py
+++ b/solution.py
@@ -590,11 +590,13 @@
         shard, line = pack_call(
             one_core, w_emb.T, w_dense, b_in[None], expert_w1, expert_w2, expert_b1, expert_b2, gate_t, tower_w1[0], *smalls, group_sizes, labels
         )
-        near = jnp.stack([shard] + [hop(shard, 4 * a, size) for a in range(1, 4)])
+        pairs = [jnp.stack([shard, hop(shard, 4, size)]), jnp.stack([hop(shard, 8, size), hop(shard, 12, size)])]
         own_line, far_line, own_dense = halves(line, dense.T, core)
-        near, own_line, far_line, own_dense = lax.optimization_barrier((near, own_line, far_line, own_dense))
-        once = cross(near, (1, 2), size)
-        own_u = [near, once, cross(near, (2, 1), size), cross(once, (2, 1), size)]
+        once, twice = cross(pairs[0], (1, 2), size), cross(pairs[0], (2, 1), size)
+        held = (pairs[1], once, twice, own_line, far_line, own_dense)
+        pairs[1], once, twice, own_line, far_line, own_dense = lax.optimization_barrier(held)
+        once, twice = [once, cross(pairs[1], (1, 2), size)], [twice, cross(pairs[1], (2, 1), size)]
+        own_u = pairs + once + twice + [cross(a, (2, 1), size) for a in once]
         steps = jnp.arange(16, dtype=jnp.int32)
         order = place ^ (steps % 4 * 4 + steps // 4)
     else:

time: 122 us -> 120 us (0.984)
  waiting for transfers between devices: 37.2 us -> 26.8 us
  starting transfers between devices: 19.1 us -> 27.4 us
    ppermute x6 -> x9, waiting for transfers between devices: 19.2 us -> 11.8 us  [cross(): return lax.ppermute(a, ('rows', 'task'), pairs)]
    ppermute x6 -> x9, starting transfers between devices: 5.48 us -> 11.8 us  [cross(): return lax.ppermute(a, ('rows', 'task'), pairs)]
    ppermute x6, waiting for transfers between devices: 13.5 us -> 10.8 us  [hop(): return lax.ppermute(a, 'rows', [(i, i ^ mask) for i in range(size)])]
    ppermute x14 -> x18, starting transfers between devices: 3.5 us -> 4.48 us  [partner(): return lax.ppermute(a, 'task', [(0, 1), (1, 0)])]
    ppermute x14 -> x18, waiting for transfers between devices: 4.41 us -> 4.19 us  [partner(): return lax.ppermute(a, 'task', [(0, 1), (1, 0)])]
  transfers between devices with their start and end apart: 26 -> 33, of which waited for: 12 -> 15; matrix products, arithmetic and copies ran while one was open for 3% -> 3% of each run, Pallas kernels for 9% -> 9%
where the time goes in v8:
time: 120 us
  Pallas kernels  60.4 us (50%)
  starting transfers between devices  27.4 us (23%)
  waiting for transfers between devices  26.8 us (22%)
  local copies, waits for them, and re-layouts  2.15 us (2%)
  between operations  1.65 us (1%)
    pallas_call x1, Pallas kernels, main_call(): pl.pallas_call(functools.partial(main_kernel, pieces, chunks, rows // siz...  46.2 us
    ppermute x9, starting transfers between devices, cross(): return lax.ppermute(a, ('rows', 'task'), pairs)  11.8 us
    ppermute x9, waiting for transfers between devices, cross(): return lax.ppermute(a, ('rows', 'task'), pairs)  11.8 us
    ppermute x6, starting transfers between devices, hop(): return lax.ppermute(a, 'rows', [(i, i ^ mask) for i in range(size)])  11.2 us
    pallas_call x2, Pallas kernels, input_call(): pl.pallas_call(input_kernel, grid_spec=spec, out_shape=[jax.ShapeDtypeStr...  11.1 us
    ppermute x6, waiting for transfers between devices, hop(): return lax.ppermute(a, 'rows', [(i, i ^ mask) for i in range(size)])  10.8 us
    ppermute x18, starting transfers between devices, partner(): return lax.ppermute(a, 'task', [(0, 1), (1, 0)])  4.48 us
    ppermute x18, waiting for transfers between devices, partner(): return lax.ppermute(a, 'task', [(0, 1), (1, 0)])  4.19 us
  transfers between devices with their start and end apart: 33, of which 15 were waited for; matrix products, arithmetic and copies ran while one was open for 3% of the time, Pallas kernels for 9%

profile of v8, /device:TPU:0, one launch (start us, length us, event | category | flops | bytes accessed | tf_op | source)
XLA Modules:
  0.0 119.6 jit_solution(5669787836287202059)
XLA Ops:
  1.4 1.7 %pack.1 = (bf16[32,1664]{1,0:T(8,128)(2,1)}, f32[1,8192]{1,0:T(1,128)}) custom-call(s32[1]{0:T(128)} %bitcast.core_ref, bf16[32,416]{1,0:T(8,128)(2,1)} %bitcast.29, bf16[13,32]{1,0:T(8,128)(2,1)} %dense_ref.1, bf16[1,32]{1,0:T(2,128)(2,1)} %bitcast.32, bf16[4,32,256]{2,1,0:T(8,128)(2,1)} %w1_ref.1, bf16[4,16,128]{2,1,0:T(8,128)(2,1)} %w2_ref.1, ...), custom_call_target="tpu_custom_call" | custom-call | tf_op jit(solution)/shard_map/pack/pallas_call | solution.py:468
  3.1 3.0 %collective-permute-start.2 = (bf16[32,1664]{1,0:T(8,128)(2,1)}, bf16[32,1664]{1,0:T(8,128)(2,1)S(1)}, u32[]{:S(2)}, u32[]{:S(2)}) collective-permute-start(bf16[32,1664]{1,0:T(8,128)(2,1)} %get-tuple-element.58), channel_id=1, source_target_pairs={{0,8},{2,10},{4,12},{6,14},{8,0},{10,2},{12,4},{14,6},{16,24},{18,... | collective-permute-start | bytes 319496 | tf_op jit(solution)/shard_map/ppermute | solution.py:547
  6.1 2.5 %collective-permute-start.1 = (bf16[32,1664]{1,0:T(8,128)(2,1)}, bf16[32,1664]{1,0:T(8,128)(2,1)S(1)}, u32[]{:S(2)}, u32[]{:S(2)}) collective-permute-start(bf16[32,1664]{1,0:T(8,128)(2,1)} %get-tuple-element.58), channel_id=1, source_target_pairs={{0,24},{2,26},{4,28},{6,30},{8,16},{10,18},{12,20},{14,22},{16,8},... | collective-permute-start | bytes 319496 | tf_op jit(solution)/shard_map/ppermute | solution.py:547
  8.7 0.7 slice.19
  9.4 0.7 constant_dynamic-slice_fusion
  10.2 0.7 slice.18
  11.0 0.9 pad_maximum_fusion.1.refs_4_
  11.9 0.6 collective-permute-start.10
  12.5 1.5 %collective-permute-start.4 = (bf16[2,32,1664]{2,1,0:T(8,128)(2,1)S(1)}, bf16[2,32,1664]{2,1,0:T(8,128)(2,1)S(1)}, u32[]{:S(2)}, u32[]{:S(2)}) collective-permute-start(bf16[2,32,1664]{2,1,0:T(8,128)(2,1)S(1)} %pad_maximum_fusion.1.refs_4_), channel_id=1, source_target_pairs={{0,4},{1,3},{2,6},{3,1},{4,0},{5,7},{6,2},{7,5},{8,12},{9,11},{10,... | collective-permute-start | bytes 638984 | tf_op jit(solution)/shard_map/ppermute | solution.py:552
  14.0 0.9 collective-permute-done.1
  14.9 1.5 %collective-permute-start.3 = (bf16[2,32,1664]{2,1,0:T(8,128)(2,1)S(1)}, bf16[2,32,1664]{2,1,0:T(8,128)(2,1)S(1)}, u32[]{:S(2)}, u32[]{:S(2)}) collective-permute-start(bf16[2,32,1664]{2,1,0:T(8,128)(2,1)S(1)} %pad_maximum_fusion.1.refs_4_), channel_id=1, source_target_pairs={{0,2},{1,5},{2,0},{3,7},{4,6},{5,1},{6,4},{7,3},{8,10},{9,13},{10,... | collective-permute-start | bytes 638984 | tf_op jit(solution)/shard_map/ppermute | solution.py:552
  16.4 2.1 %collective-permute-done = bf16[32,1664]{1,0:T(8,128)(2,1)S(1)} collective-permute-done((bf16[32,1664]{1,0:T(8,128)(2,1)}, bf16[32,1664]{1,0:T(8,128)(2,1)S(1)}, u32[]{:S(2)}, u32[]{:S(2)}) %collective-permute-start) | collective-permute-done | bytes 106528 | tf_op jit(solution)/shard_map/ppermute | solution.py:547
  18.5 1.7 %collective-permute-done.4.refs_8_ = bf16[2,32,1664]{2,1,0:T(8,128)(2,1)S(1)} collective-permute-done((bf16[2,32,1664]{2,1,0:T(8,128)(2,1)S(1)}, bf16[2,32,1664]{2,1,0:T(8,128)(2,1)S(1)}, u32[]{:S(2)}, u32[]{:S(2)}) %collective-permute-start.4) | collective-permute-done | bytes 213024 | tf_op jit(solution)/shard_map/ppermute | solution.py:552
  20.3 0.5 collective-permute-done.3.refs_6_
  20.8 1.5 %collective-permute-start.6 = (bf16[2,32,1664]{2,1,0:T(8,128)(2,1)S(1)}, bf16[2,32,1664]{2,1,0:T(8,128)(2,1)S(1)}, u32[]{:S(2)}, u32[]{:S(2)}) collective-permute-start(bf16[2,32,1664]{2,1,0:T(8,128)(2,1)S(1)} %pad_maximum_fusion.refs_5_), channel_id=1, source_target_pairs={{0,2},{1,5},{2,0},{3,7},{4,6},{5,1},{6,4},{7,3},{8,10},{9,13},{10,... | collective-permute-start | bytes 638984 | tf_op jit(solution)/shard_map/ppermute | solution.py:552
  22.2 0.5 collective-permute-start.12
  22.8 1.5 %collective-permute-start.8 = (bf16[2,32,1664]{2,1,0:T(8,128)(2,1)S(1)}, bf16[2,32,1664]{2,1,0:T(8,128)(2,1)S(1)}, u32[]{:S(2)}, u32[]{:S(2)}) collective-permute-start(bf16[2,32,1664]{2,1,0:T(8,128)(2,1)S(1)} %collective-permute-done.3.refs_6_), channel_id=1, source_target_pairs={{0,4},{1,3},{2,6},{3,1},{4,0},{5,7},{6,2},{7,5},{8,12},{9,11},{10,... | collective-permute-start | bytes 638984 | tf_op jit(solution)/shard_map/ppermute | solution.py:552
  24.3 0.5 collective-permute-start.7
  24.8 3.1 %collective-permute-done.6.refs_7_ = bf16[2,32,1664]{2,1,0:T(8,128)(2,1)S(1)} collective-permute-done((bf16[2,32,1664]{2,1,0:T(8,128)(2,1)S(1)}, bf16[2,32,1664]{2,1,0:T(8,128)(2,1)S(1)}, u32[]{:S(2)}, u32[]{:S(2)}) %collective-permute-start.6) | collective-permute-done | bytes 213024 | tf_op jit(solution)/shard_map/ppermute | solution.py:552
  27.8 1.5 %collective-permute-start.9 = (bf16[2,32,1664]{2,1,0:T(8,128)(2,1)S(1)}, bf16[2,32,1664]{2,1,0:T(8,128)(2,1)S(1)}, u32[]{:S(2)}, u32[]{:S(2)}) collective-permute-start(bf16[2,32,1664]{2,1,0:T(8,128)(2,1)S(1)} %collective-permute-done.6.refs_7_), channel_id=1, source_target_pairs={{0,4},{1,3},{2,6},{3,1},{4,0},{5,7},{6,2},{7,5},{8,12},{9,11},{10,... | collective-permute-start | bytes 638984 | tf_op jit(solution)/shard_map/ppermute | solution.py:552
  29.4 0.5 collective-permute-start.13
  30.0 0.9 collective-permute-done.7.refs_9_
  31.0 2.7 %collective-permute-done.9.refs_11_ = bf16[2,32,1664]{2,1,0:T(8,128)(2,1)S(1)} collective-permute-done((bf16[2,32,1664]{2,1,0:T(8,128)(2,1)S(1)}, bf16[2,32,1664]{2,1,0:T(8,128)(2,1)S(1)}, u32[]{:S(2)}, u32[]{:S(2)}) %collective-permute-start.9) | collective-permute-done | bytes 213024 | tf_op jit(solution)/shard_map/ppermute | solution.py:552
  33.8 1.4 %collective-permute-done.17.refs_19_ = bf16[2,32,1664]{2,1,0:T(8,128)(2,1)S(1)} collective-permute-done((bf16[2,32,1664]{2,1,0:T(8,128)(2,1)S(1)}, bf16[2,32,1664]{2,1,0:T(8,128)(2,1)S(1)}, u32[]{:S(2)}, u32[]{:S(2)}) %collective-permute-start.17) | collective-permute-done | bytes 213024 | tf_op jit(solution)/shard_map/ppermute | solution.py:556
  35.2 46.2 %experts.1 = (bf16[512,3072]{1,0:T(8,128)(2,1)}, bf16[512,448]{1,0:T(8,128)(2,1)}, bf16[4,32,1664]{2,1,0:T(8,128)(2,1)S(1)}, bf16[4,32,1664]{2,1,0:T(8,128)(2,1)...) custom-call(s32[17]{0:T(128)S(1)} %pad_add_fusion.tab_ref, ...), custom_call_target="tpu_custom_call" | custom-call | flops 49999998976 | bytes 24000000 | tf_op jit(solution)/shard_map/experts/pallas_call | solution.py:370
  81.5 0.4 collective-permute-start.18
  81.9 1.5 %collective-permute-done.19.refs_1_ = bf16[4,32,1664]{2,1,0:T(8,128)(2,1)S(1)} collective-permute-done((bf16[4,32,1664]{2,1,0:T(8,128)(2,1)}, bf16[4,32,1664]{2,1,0:T(8,128)(2,1)S(1)}, u32[]{:S(2)}, u32[]{:S(2)}) %collective-permute-start.19) | collective-permute-done | bytes 426016 | tf_op jit(solution)/shard_map/ppermute | solution.py:556
  83.5 0.5 collective-permute-done.18.refs_1_
  84.1 0.2 collective-permute-start.20
  84.3 0.4 collective-permute-start.21
  84.7 1.5 %collective-permute-start.22 = (bf16[4,32,1664]{2,1,0:T(8,128)(2,1)S(1)}, bf16[4,32,1664]{2,1,0:T(8,128)(2,1)S(1)}, u32[]{:S(2)}, u32[]{:S(2)}) collective-permute-start(bf16[4,32,1664]{2,1,0:T(8,128)(2,1)S(1)} %sum_fourth.1.refs_2_), channel_id=1, source_target_pairs={{0,4},{1,3},{2,6},{3,1},{4,0},{5,7},{6,2},{7,5},{8,12},{9,11},{10,... | collective-permute-start | bytes 1277960 | tf_op jit(solution)/shard_map/ppermute | solution.py:552
  86.2 0.8 collective-permute-start.23
  87.0 1.5 %collective-permute-start.24 = (bf16[4,32,1664]{2,1,0:T(8,128)(2,1)S(1)}, bf16[4,32,1664]{2,1,0:T(8,128)(2,1)S(1)}, u32[]{:S(2)}, u32[]{:S(2)}) collective-permute-start(bf16[4,32,1664]{2,1,0:T(8,128)(2,1)S(1)} %get-tuple-element.75.refs_0_), channel_id=1, source_target_pairs={{0,4},{1,3},{2,6},{3,1},{4,0},{5,7},{6,2},{7,5},{8,12},{9,11},{10,... | collective-permute-start | bytes 1277960 | tf_op jit(solution)/shard_map/ppermute | solution.py:552
  88.5 6.5 %input_own.1 = (f32[416,6144]{1,0:T(8,128)}, f32[13,6144]{1,0:T(8,128)}, f32[8,128]{1,0:T(8,128)S(1)}) custom-call(s32[17]{0:T(128)S(1)} %pad_add_fusion.tab_ref, bf16[512,3072]{1,0:T(8,128)(2,1)} %get-tuple-element.71.hg_ref, bf16[512,448]{1,0:T(8,128)(2,1)S(1)} %copy-done.1, bf16[4,32,1664]{2,1,0:T(8,128)(2,1)S(1)} %get-tuple-element.75.refs_0_), custom_call_target="tpu_custom_call" | custom-call | flops 4000000000 | bytes 9000000 | tf_op jit(solution)/shard_map/input_own/pallas_call | solution.py:411
  95.2 0.7 collective-permute-start.25
  95.9 4.6 %input_far.1 = (f32[416,6144]{1,0:T(8,128)}, f32[13,6144]{1,0:T(8,128)}, f32[8,128]{1,0:T(8,128)S(1)}) custom-call(s32[17]{0:T(128)S(1)} %pad_add_fusion.tab_ref, bf16[512,3072]{1,0:T(8,128)(2,1)S(1)} %collective-permute-done.20.hg_ref, bf16[512,448]{1,0:T(8,128)(2,1)S(1)} %copy-done.1, ...), custom_call_target="tpu_custom_call", output_to_operand_aliasing={{0}: (4, {}), {1}: (5, {})} | custom-call | flops 4000000000 | bytes 9000000 | tf_op jit(solution)/shard_map/input_far/pallas_call | solution.py:411
  100.5 2.9 %collective-permute-done.25.refs_3_ = bf16[4,32,1664]{2,1,0:T(8,128)(2,1)S(1)} collective-permute-done((bf16[4,32,1664]{2,1,0:T(8,128)(2,1)S(1)}, bf16[4,32,1664]{2,1,0:T(8,128)(2,1)S(1)}, u32[]{:S(2)}, u32[]{:S(2)}) %collective-permute-start.25) | collective-permute-done | bytes 426016 | tf_op jit(solution)/shard_map/ppermute | solution.py:552
  103.4 0.2 sum_first.1
  103.6 2.6 %collective-permute-start.26 = (bf16[32,1664]{1,0:T(8,128)(2,1)S(1)}, bf16[32,1664]{1,0:T(8,128)(2,1)S(1)}, u32[]{:S(2)}, u32[]{:S(2)}) collective-permute-start(bf16[32,1664]{1,0:T(8,128)(2,1)S(1)} %get-tuple-element.85), channel_id=1, source_target_pairs={{0,8},{2,10},{4,12},{6,14},{8,0},{10,2},{12,4},{14,6},{16,24},{18,... | collective-permute-start | bytes 319496 | tf_op jit(solution)/shard_map/ppermute | solution.py:547
  106.2 1.6 %collective-permute-start.27 = (bf16[32,1664]{1,0:T(8,128)(2,1)S(1)}, bf16[32,1664]{1,0:T(8,128)(2,1)S(1)}, u32[]{:S(2)}, u32[]{:S(2)}) collective-permute-start(bf16[32,1664]{1,0:T(8,128)(2,1)S(1)} %get-tuple-element.86), channel_id=1, source_target_pairs={{0,16},{2,18},{4,20},{6,22},{8,24},{10,26},{12,28},{14,30},{16,0},... | collective-permute-start | bytes 319496 | tf_op jit(solution)/shard_map/ppermute | solution.py:547
  107.7 1.4 %collective-permute-start.28 = (bf16[32,1664]{1,0:T(8,128)(2,1)S(1)}, bf16[32,1664]{1,0:T(8,128)(2,1)S(1)}, u32[]{:S(2)}, u32[]{:S(2)}) collective-permute-start(bf16[32,1664]{1,0:T(8,128)(2,1)S(1)} %get-tuple-element.87), channel_id=1, source_target_pairs={{0,24},{2,26},{4,28},{6,30},{8,16},{10,18},{12,20},{14,22},{16,8},... | collective-permute-start | bytes 319496 | tf_op jit(solution)/shard_map/ppermute | solution.py:547
  109.1 0.3 collective-permute-done.26.refs_1_
  109.4 0.2 collective-permute-start.30
  109.6 7.5 %collective-permute-done.27.refs_2_ = bf16[32,1664]{1,0:T(8,128)(2,1)S(1)} collective-permute-done((bf16[32,1664]{1,0:T(8,128)(2,1)S(1)}, bf16[32,1664]{1,0:T(8,128)(2,1)S(1)}, u32[]{:S(2)}, u32[]{:S(2)}) %collective-permute-start.27) | collective-permute-done | bytes 106528 | tf_op jit(solution)/shard_map/ppermute | solution.py:547
  117.2 0.5 collective-permute-start.32
  117.7 0.7 collective-permute-done.31.refs_6_
  118.4 0.2 collective-permute-done.32.refs_7_
  118.6 0.8 finish.1
  (45 shorter events, 1.1 us)
Async XLA Ops:
  0.7 10.3 %copy-start = (bf16[6144,13]{0,1:T(8,128)(2,1)S(1)}, bf16[6144,13]{0,1:T(8,128)(2,1)}, u32[]{:S(2)}) copy-start(bf16[6144,13]{0,1:T(8,128)(2,1)} %param.18) | copy-start | bytes 479236
  3.1 7.9 %collective-permute-start.2 = (bf16[32,1664]{1,0:T(8,128)(2,1)}, bf16[32,1664]{1,0:T(8,128)(2,1)S(1)}, u32[]{:S(2)}, u32[]{:S(2)}) collective-permute-start(bf16[32,1664]{1,0:T(8,128)(2,1)} %get-tuple-element.58), channel_id=1, source_target_pairs={{0,8},{2,10},{4,12},{6,14},{8,0},{10,2},{12,4},{14,6},{16,24},{18,... | collective-permute-start | bytes 319496 | tf_op jit(solution)/shard_map/ppermute | solution.py:547
  6.1 8.8 %collective-permute-start.1 = (bf16[32,1664]{1,0:T(8,128)(2,1)}, bf16[32,1664]{1,0:T(8,128)(2,1)S(1)}, u32[]{:S(2)}, u32[]{:S(2)}) collective-permute-start(bf16[32,1664]{1,0:T(8,128)(2,1)} %get-tuple-element.58), channel_id=1, source_target_pairs={{0,24},{2,26},{4,28},{6,30},{8,16},{10,18},{12,20},{14,22},{16,8},... | collective-permute-start | bytes 319496 | tf_op jit(solution)/shard_map/ppermute | solution.py:547
  8.6 9.9 %collective-permute-start = (bf16[32,1664]{1,0:T(8,128)(2,1)}, bf16[32,1664]{1,0:T(8,128)(2,1)S(1)}, u32[]{:S(2)}, u32[]{:S(2)}) collective-permute-start(bf16[32,1664]{1,0:T(8,128)(2,1)} %get-tuple-element.58), channel_id=1, source_target_pairs={{0,16},{2,18},{4,20},{6,22},{8,24},{10,26},{12,28},{14,30},{16,0},... | collective-permute-start | bytes 319496 | tf_op jit(solution)/shard_map/ppermute | solution.py:547
  10.1 8.4 %collective-permute-start.5 = (f32[1,3584]{1,0:T(1,128)S(1)}, f32[1,3584]{1,0:T(1,128)S(1)}, u32[]{:S(2)}, u32[]{:S(2)}) collective-permute-start(f32[1,3584]{1,0:T(1,128)S(1)} %pad_maximum_fusion.3), channel_id=1, source_target_pairs={{0,1},{1,0},{2,3},{3,2},{4,5},{5,4},{6,7},{7,6},{8,9},{9,8},{10,11... | collective-permute-start | bytes 43016 | tf_op jit(solution)/shard_map/ppermute | solution.py:556
  11.9 12.4 %collective-permute-start.10 = (bf16[2,32,1664]{2,1,0:T(8,128)(2,1)S(1)}, bf16[2,32,1664]{2,1,0:T(8,128)(2,1)S(1)}, u32[]{:S(2)}, u32[]{:S(2)}) collective-permute-start(bf16[2,32,1664]{2,1,0:T(8,128)(2,1)S(1)} %pad_maximum_fusion.1.refs_4_), channel_id=1, source_target_pairs={{0,1},{1,0},{2,3},{3,2},{4,5},{5,4},{6,7},{7,6},{8,9},{9,8},{10,11... | collective-permute-start | bytes 638984 | tf_op jit(solution)/shard_map/ppermute | solution.py:556
  12.5 7.8 %collective-permute-start.4 = (bf16[2,32,1664]{2,1,0:T(8,128)(2,1)S(1)}, bf16[2,32,1664]{2,1,0:T(8,128)(2,1)S(1)}, u32[]{:S(2)}, u32[]{:S(2)}) collective-permute-start(bf16[2,32,1664]{2,1,0:T(8,128)(2,1)S(1)} %pad_maximum_fusion.1.refs_4_), channel_id=1, source_target_pairs={{0,4},{1,3},{2,6},{3,1},{4,0},{5,7},{6,2},{7,5},{8,12},{9,11},{10,... | collective-permute-start | bytes 638984 | tf_op jit(solution)/shard_map/ppermute | solution.py:552
  14.9 5.8 %collective-permute-start.3 = (bf16[2,32,1664]{2,1,0:T(8,128)(2,1)S(1)}, bf16[2,32,1664]{2,1,0:T(8,128)(2,1)S(1)}, u32[]{:S(2)}, u32[]{:S(2)}) collective-permute-start(bf16[2,32,1664]{2,1,0:T(8,128)(2,1)S(1)} %pad_maximum_fusion.1.refs_4_), channel_id=1, source_target_pairs={{0,2},{1,5},{2,0},{3,7},{4,6},{5,1},{6,4},{7,3},{8,10},{9,13},{10,... | collective-permute-start | bytes 638984 | tf_op jit(solution)/shard_map/ppermute | solution.py:552
  20.8 7.1 %collective-permute-start.6 = (bf16[2,32,1664]{2,1,0:T(8,128)(2,1)S(1)}, bf16[2,32,1664]{2,1,0:T(8,128)(2,1)S(1)}, u32[]{:S(2)}, u32[]{:S(2)}) collective-permute-start(bf16[2,32,1664]{2,1,0:T(8,128)(2,1)S(1)} %pad_maximum_fusion.refs_5_), channel_id=1, source_target_pairs={{0,2},{1,5},{2,0},{3,7},{4,6},{5,1},{6,4},{7,3},{8,10},{9,13},{10,... | collective-permute-start | bytes 638984 | tf_op jit(solution)/shard_map/ppermute | solution.py:552
  22.2 7.1 %collective-permute-start.14 = (bf16[2,32,1664]{2,1,0:T(8,128)(2,1)S(1)}, bf16[2,32,1664]{2,1,0:T(8,128)(2,1)S(1)}, u32[]{:S(2)}, u32[]{:S(2)}) collective-permute-start(bf16[2,32,1664]{2,1,0:T(8,128)(2,1)S(1)} %collective-permute-done.4.refs_8_), channel_id=1, source_target_pairs={{0,1},{1,0},{2,3},{3,2},{4,5},{5,4},{6,7},{7,6},{8,9},{9,8},{10,11... | collective-permute-start | bytes 638984 | tf_op jit(solution)/shard_map/ppermute | solution.py:556
  22.2 7.1 %collective-permute-start.12 = (bf16[2,32,1664]{2,1,0:T(8,128)(2,1)S(1)}, bf16[2,32,1664]{2,1,0:T(8,128)(2,1)S(1)}, u32[]{:S(2)}, u32[]{:S(2)}) collective-permute-start(bf16[2,32,1664]{2,1,0:T(8,128)(2,1)S(1)} %collective-permute-done.3.refs_6_), channel_id=1, source_target_pairs={{0,1},{1,0},{2,3},{3,2},{4,5},{5,4},{6,7},{7,6},{8,9},{9,8},{10,11... | collective-permute-start | bytes 638984 | tf_op jit(solution)/shard_map/ppermute | solution.py:556
  22.8 7.1 %collective-permute-start.8 = (bf16[2,32,1664]{2,1,0:T(8,128)(2,1)S(1)}, bf16[2,32,1664]{2,1,0:T(8,128)(2,1)S(1)}, u32[]{:S(2)}, u32[]{:S(2)}) collective-permute-start(bf16[2,32,1664]{2,1,0:T(8,128)(2,1)S(1)} %collective-permute-done.3.refs_6_), channel_id=1, source_target_pairs={{0,4},{1,3},{2,6},{3,1},{4,0},{5,7},{6,2},{7,5},{8,12},{9,11},{10,... | collective-permute-start | bytes 638984 | tf_op jit(solution)/shard_map/ppermute | solution.py:552
  24.3 6.6 %collective-permute-start.7 = (bf16[2,32,1664]{2,1,0:T(8,128)(2,1)S(1)}, bf16[2,32,1664]{2,1,0:T(8,128)(2,1)S(1)}, u32[]{:S(2)}, u32[]{:S(2)}) collective-permute-start(bf16[2,32,1664]{2,1,0:T(8,128)(2,1)S(1)} %pad_maximum_fusion.refs_5_), channel_id=1, source_target_pairs={{0,4},{1,3},{2,6},{3,1},{4,0},{5,7},{6,2},{7,5},{8,12},{9,11},{10,... | collective-permute-start | bytes 638984 | tf_op jit(solution)/shard_map/ppermute | solution.py:552
  27.8 5.8 %collective-permute-start.9 = (bf16[2,32,1664]{2,1,0:T(8,128)(2,1)S(1)}, bf16[2,32,1664]{2,1,0:T(8,128)(2,1)S(1)}, u32[]{:S(2)}, u32[]{:S(2)}) collective-permute-start(bf16[2,32,1664]{2,1,0:T(8,128)(2,1)S(1)} %collective-permute-done.6.refs_7_), channel_id=1, source_target_pairs={{0,4},{1,3},{2,6},{3,1},{4,0},{5,7},{6,2},{7,5},{8,12},{9,11},{10,... | collective-permute-start | bytes 638984 | tf_op jit(solution)/shard_map/ppermute | solution.py:552
  29.4 4.4 %collective-permute-start.11 = (bf16[2,32,1664]{2,1,0:T(8,128)(2,1)S(1)}, bf16[2,32,1664]{2,1,0:T(8,128)(2,1)S(1)}, u32[]{:S(2)}, u32[]{:S(2)}) collective-permute-start(bf16[2,32,1664]{2,1,0:T(8,128)(2,1)S(1)} %pad_maximum_fusion.refs_5_), channel_id=1, source_target_pairs={{0,1},{1,0},{2,3},{3,2},{4,5},{5,4},{6,7},{7,6},{8,9},{9,8},{10,11... | collective-permute-start | bytes 638984 | tf_op jit(solution)/shard_map/ppermute | solution.py:556
  29.4 4.4 %collective-permute-start.13 = (bf16[2,32,1664]{2,1,0:T(8,128)(2,1)S(1)}, bf16[2,32,1664]{2,1,0:T(8,128)(2,1)S(1)}, u32[]{:S(2)}, u32[]{:S(2)}) collective-permute-start(bf16[2,32,1664]{2,1,0:T(8,128)(2,1)S(1)} %collective-permute-done.6.refs_7_), channel_id=1, source_target_pairs={{0,1},{1,0},{2,3},{3,2},{4,5},{5,4},{6,7},{7,6},{8,9},{9,8},{10,11... | collective-permute-start | bytes 638984 | tf_op jit(solution)/shard_map/ppermute | solution.py:556
  29.9 3.9 %collective-permute-start.16 = (bf16[2,32,1664]{2,1,0:T(8,128)(2,1)S(1)}, bf16[2,32,1664]{2,1,0:T(8,128)(2,1)S(1)}, u32[]{:S(2)}, u32[]{:S(2)}) collective-permute-start(bf16[2,32,1664]{2,1,0:T(8,128)(2,1)S(1)} %collective-permute-done.8.refs_10_), channel_id=1, source_target_pairs={{0,1},{1,0},{2,3},{3,2},{4,5},{5,4},{6,7},{7,6},{8,9},{9,8},{10,11... | collective-permute-start | bytes 638984 | tf_op jit(solution)/shard_map/ppermute | solution.py:556
  30.9 2.9 %collective-permute-start.15 = (bf16[2,32,1664]{2,1,0:T(8,128)(2,1)S(1)}, bf16[2,32,1664]{2,1,0:T(8,128)(2,1)S(1)}, u32[]{:S(2)}, u32[]{:S(2)}) collective-permute-start(bf16[2,32,1664]{2,1,0:T(8,128)(2,1)S(1)} %collective-permute-done.7.refs_9_), channel_id=1, source_target_pairs={{0,1},{1,0},{2,3},{3,2},{4,5},{5,4},{6,7},{7,6},{8,9},{9,8},{10,11... | collective-permute-start | bytes 638984 | tf_op jit(solution)/shard_map/ppermute | solution.py:556
  33.7 1.5 %collective-permute-start.17 = (bf16[2,32,1664]{2,1,0:T(8,128)(2,1)S(1)}, bf16[2,32,1664]{2,1,0:T(8,128)(2,1)S(1)}, u32[]{:S(2)}, u32[]{:S(2)}) collective-permute-start(bf16[2,32,1664]{2,1,0:T(8,128)(2,1)S(1)} %collective-permute-done.9.refs_11_), channel_id=1, source_target_pairs={{0,1},{1,0},{2,3},{3,2},{4,5},{5,4},{6,7},{7,6},{8,9},{9,8},{10,11... | collective-permute-start | bytes 638984 | tf_op jit(solution)/shard_map/ppermute | solution.py:556
  81.4 7.1 %copy-start.1 = (bf16[512,448]{1,0:T(8,128)(2,1)S(1)}, bf16[512,448]{1,0:T(8,128)(2,1)}, u32[]{:S(2)}) copy-start(bf16[512,448]{1,0:T(8,128)(2,1)} %get-tuple-element.72.wat_ref) | copy-start | bytes 1376260
  81.4 2.0 %collective-permute-start.19 = (bf16[4,32,1664]{2,1,0:T(8,128)(2,1)}, bf16[4,32,1664]{2,1,0:T(8,128)(2,1)S(1)}, u32[]{:S(2)}, u32[]{:S(2)}) collective-permute-start(bf16[4,32,1664]{2,1,0:T(8,128)(2,1)} %get-tuple-element.69), channel_id=1, source_target_pairs={{0,1},{1,0},{2,3},{3,2},{4,5},{5,4},{6,7},{7,6},{8,9},{9,8},{10,11... | collective-permute-start | bytes 1277960 | tf_op jit(solution)/shard_map/ppermute | solution.py:556
  81.5 2.5 %collective-permute-start.18 = (bf16[4,32,1664]{2,1,0:T(8,128)(2,1)}, bf16[4,32,1664]{2,1,0:T(8,128)(2,1)S(1)}, u32[]{:S(2)}, u32[]{:S(2)}) collective-permute-start(bf16[4,32,1664]{2,1,0:T(8,128)(2,1)} %get-tuple-element.67), channel_id=1, source_target_pairs={{0,1},{1,0},{2,3},{3,2},{4,5},{5,4},{6,7},{7,6},{8,9},{9,8},{10,11... | collective-permute-start | bytes 1277960 | tf_op jit(solution)/shard_map/ppermute | solution.py:556
  84.1 11.8 %collective-permute-start.20 = (bf16[512,3072]{1,0:T(8,128)(2,1)}, bf16[512,3072]{1,0:T(8,128)(2,1)S(1)}, u32[]{:S(2)}, u32[]{:S(2)}) collective-permute-start(bf16[512,3072]{1,0:T(8,128)(2,1)} %get-tuple-element.71.hg_ref), channel_id=1, source_target_pairs={{0,1},{1,0},{2,3},{3,2},{4,5},{5,4},{6,7},{7,6},{8,9},{9,8},{10,11... | collective-permute-start | bytes 9437192 | tf_op jit(solution)/shard_map/ppermute | solution.py:556
  84.3 10.7 %collective-permute-start.21 = (bf16[4,32,1664]{2,1,0:T(8,128)(2,1)S(1)}, bf16[4,32,1664]{2,1,0:T(8,128)(2,1)S(1)}, u32[]{:S(2)}, u32[]{:S(2)}) collective-permute-start(bf16[4,32,1664]{2,1,0:T(8,128)(2,1)S(1)} %get-tuple-element.74), channel_id=1, source_target_pairs={{0,1},{1,0},{2,3},{3,2},{4,5},{5,4},{6,7},{7,6},{8,9},{9,8},{10,11... | collective-permute-start | bytes 1277960 | tf_op jit(solution)/shard_map/ppermute | solution.py:556
  84.7 10.3 %collective-permute-start.22 = (bf16[4,32,1664]{2,1,0:T(8,128)(2,1)S(1)}, bf16[4,32,1664]{2,1,0:T(8,128)(2,1)S(1)}, u32[]{:S(2)}, u32[]{:S(2)}) collective-permute-start(bf16[4,32,1664]{2,1,0:T(8,128)(2,1)S(1)} %sum_fourth.1.refs_2_), channel_id=1, source_target_pairs={{0,4},{1,3},{2,6},{3,1},{4,0},{5,7},{6,2},{7,5},{8,12},{9,11},{10,... | collective-permute-start | bytes 1277960 | tf_op jit(solution)/shard_map/ppermute | solution.py:552
  86.2 14.3 %collective-permute-start.23 = (bf16[4,32,1664]{2,1,0:T(8,128)(2,1)S(1)}, bf16[4,32,1664]{2,1,0:T(8,128)(2,1)S(1)}, u32[]{:S(2)}, u32[]{:S(2)}) collective-permute-start(bf16[4,32,1664]{2,1,0:T(8,128)(2,1)S(1)} %get-tuple-element.82), channel_id=1, source_target_pairs={{0,1},{1,0},{2,3},{3,2},{4,5},{5,4},{6,7},{7,6},{8,9},{9,8},{10,11... | collective-permute-start | bytes 1277960 | tf_op jit(solution)/shard_map/ppermute | solution.py:556
  87.0 13.5 %collective-permute-start.24 = (bf16[4,32,1664]{2,1,0:T(8,128)(2,1)S(1)}, bf16[4,32,1664]{2,1,0:T(8,128)(2,1)S(1)}, u32[]{:S(2)}, u32[]{:S(2)}) collective-permute-start(bf16[4,32,1664]{2,1,0:T(8,128)(2,1)S(1)} %get-tuple-element.75.refs_0_), channel_id=1, source_target_pairs={{0,4},{1,3},{2,6},{3,1},{4,0},{5,7},{6,2},{7,5},{8,12},{9,11},{10,... | collective-permute-start | bytes 1277960 | tf_op jit(solution)/shard_map/ppermute | solution.py:552
  95.2 8.2 %collective-permute-start.25 = (bf16[4,32,1664]{2,1,0:T(8,128)(2,1)S(1)}, bf16[4,32,1664]{2,1,0:T(8,128)(2,1)S(1)}, u32[]{:S(2)}, u32[]{:S(2)}) collective-permute-start(bf16[4,32,1664]{2,1,0:T(8,128)(2,1)S(1)} %sum_second.1.refs_0_), channel_id=1, source_target_pairs={{0,2},{1,5},{2,0},{3,7},{4,6},{5,1},{6,4},{7,3},{8,10},{9,13},{10,... | collective-permute-start | bytes 1277960 | tf_op jit(solution)/shard_map/ppermute | solution.py:552
  103.6 5.8 %collective-permute-start.26 = (bf16[32,1664]{1,0:T(8,128)(2,1)S(1)}, bf16[32,1664]{1,0:T(8,128)(2,1)S(1)}, u32[]{:S(2)}, u32[]{:S(2)}) collective-permute-start(bf16[32,1664]{1,0:T(8,128)(2,1)S(1)} %get-tuple-element.85), channel_id=1, source_target_pairs={{0,8},{2,10},{4,12},{6,14},{8,0},{10,2},{12,4},{14,6},{16,24},{18,... | collective-permute-start | bytes 319496 | tf_op jit(solution)/shard_map/ppermute | solution.py:547
  106.2 11.0 %collective-permute-start.27 = (bf16[32,1664]{1,0:T(8,128)(2,1)S(1)}, bf16[32,1664]{1,0:T(8,128)(2,1)S(1)}, u32[]{:S(2)}, u32[]{:S(2)}) collective-permute-start(bf16[32,1664]{1,0:T(8,128)(2,1)S(1)} %get-tuple-element.86), channel_id=1, source_target_pairs={{0,16},{2,18},{4,20},{6,22},{8,24},{10,26},{12,28},{14,30},{16,0},... | collective-permute-start | bytes 319496 | tf_op jit(solution)/shard_map/ppermute | solution.py:547
  107.7 9.5 %collective-permute-start.28 = (bf16[32,1664]{1,0:T(8,128)(2,1)S(1)}, bf16[32,1664]{1,0:T(8,128)(2,1)S(1)}, u32[]{:S(2)}, u32[]{:S(2)}) collective-permute-start(bf16[32,1664]{1,0:T(8,128)(2,1)S(1)} %get-tuple-element.87), channel_id=1, source_target_pairs={{0,24},{2,26},{4,28},{6,30},{8,16},{10,18},{12,20},{14,22},{16,8},... | collective-permute-start | bytes 319496 | tf_op jit(solution)/shard_map/ppermute | solution.py:547
  109.1 8.6 %collective-permute-start.29 = (bf16[16,512]{1,0:T(8,128)(2,1)S(1)}, bf16[16,512]{1,0:T(8,128)(2,1)S(1)}, u32[]{:S(2)}, u32[]{:S(2)}) collective-permute-start(bf16[16,512]{1,0:T(8,128)(2,1)S(1)} %slice.20), channel_id=1, source_target_pairs={{0,1},{1,0},{2,3},{3,2},{4,5},{5,4},{6,7},{7,6},{8,9},{9,8},{10,11... | collective-permute-start | bytes 49160 | tf_op jit(solution)/shard_map/ppermute | solution.py:556
  109.4 8.3 %collective-permute-start.30 = (bf16[16,512]{1,0:T(8,128)(2,1)S(1)}, bf16[16,512]{1,0:T(8,128)(2,1)S(1)}, u32[]{:S(2)}, u32[]{:S(2)}) collective-permute-start(bf16[16,512]{1,0:T(8,128)(2,1)S(1)} %slice.24), channel_id=1, source_target_pairs={{0,1},{1,0},{2,3},{3,2},{4,5},{5,4},{6,7},{7,6},{8,9},{9,8},{10,11... | collective-permute-start | bytes 49160 | tf_op jit(solution)/shard_map/ppermute | solution.py:556
  117.2 1.2 collective-permute-start.31
  117.2 1.3 %collective-permute-start.32 = (bf16[16,512]{1,0:T(8,128)(2,1)S(1)}, bf16[16,512]{1,0:T(8,128)(2,1)S(1)}, u32[]{:S(2)}, u32[]{:S(2)}) collective-permute-start(bf16[16,512]{1,0:T(8,128)(2,1)S(1)} %slice.26), channel_id=1, source_target_pairs={{0,1},{1,0},{2,3},{3,2},{4,5},{5,4},{6,7},{7,6},{8,9},{9,8},{10,11... | collective-permute-start | bytes 49160 | tf_op jit(solution)/shard_map/ppermute | solution.py:556

commit v9 on v8

--- a/solution.py
+++ b/solution.py
@@ -634,7 +634,7 @@
         eg, dg, token = input_call(table, far_hg, wat, first, (eg, dg), "input_far")
         groups = [[(j, k) for j in range(4)] for k in range(4)]
         sums = sum_call("sum_first", [own[0], far_none, got_second, got_first], groups, [(ds, UC)] * 4, token)
-        parts = [sums[0]] + [hop(sums[a], 4 * a, size) for a in range(1, 4)]
+        parts = [sums[0]] + [hop(sums[a], 4 * a, size) for a in (3, 2, 1)]
         parts += [partner(a[fs:, QA : QA + 512]) for a in parts]
         out = finish_call(scale, one_core, sums[0], parts, ds, fs, osz)
         g_emb, g_dense, g_bias, g_w1, g_b1, g_w2, g_b2, g_gate, g_gb, g_tower, g_t1, g_t2, g_t3 = out

time: 120 us -> 119 us (level)
  transfers between devices with their start and end apart: 33 -> 33, of which waited for: 15 -> 15; matrix products, arithmetic and copies ran while one was open for 3% -> 3% of each run, Pallas kernels for 9% -> 10%
where the time goes in v9:
time: 119 us
  Pallas kernels  60.4 us (51%)
  waiting for transfers between devices  27.4 us (23%)
  starting transfers between devices  26.3 us (22%)
  local copies, waits for them, and re-layouts  2.15 us (2%)
  between operations  1.65 us (1%)
    pallas_call x1, Pallas kernels, main_call(): pl.pallas_call(functools.partial(main_kernel, pieces, chunks, rows // siz...  46.2 us
    ppermute x9, starting transfers between devices, cross(): return lax.ppermute(a, ('rows', 'task'), pairs)  11.8 us
    ppermute x9, waiting for transfers between devices, cross(): return lax.ppermute(a, ('rows', 'task'), pairs)  11.8 us
    ppermute x6, waiting for transfers between devices, hop(): return lax.ppermute(a, 'rows', [(i, i ^ mask) for i in range(size)])  11.4 us
    pallas_call x2, Pallas kernels, input_call(): pl.pallas_call(input_kernel, grid_spec=spec, out_shape=[jax.ShapeDtypeStr...  11.1 us
    ppermute x6, starting transfers between devices, hop(): return lax.ppermute(a, 'rows', [(i, i ^ mask) for i in range(size)])  10.3 us
    ppermute x18, starting transfers between devices, partner(): return lax.ppermute(a, 'task', [(0, 1), (1, 0)])  4.23 us
    ppermute x18, waiting for transfers between devices, partner(): return lax.ppermute(a, 'task', [(0, 1), (1, 0)])  4.19 us
  transfers between devices with their start and end apart: 33, of which 15 were waited for; matrix products, arithmetic and copies ran while one was open for 3% of the time, Pallas kernels for 10%

profile of v9, /device:TPU:0, one launch (start us, length us, event | category | flops | bytes accessed | tf_op | source)
XLA Modules:
  0.0 119.0 jit_solution(14198544848752299700)
XLA Ops:
  1.4 1.7 %pack.1 = (bf16[32,1664]{1,0:T(8,128)(2,1)}, f32[1,8192]{1,0:T(1,128)}) custom-call(s32[1]{0:T(128)} %bitcast.core_ref, bf16[32,416]{1,0:T(8,128)(2,1)} %bitcast.29, bf16[13,32]{1,0:T(8,128)(2,1)} %dense_ref.1, bf16[1,32]{1,0:T(2,128)(2,1)} %bitcast.32, bf16[4,32,256]{2,1,0:T(8,128)(2,1)} %w1_ref.1, bf16[4,16,128]{2,1,0:T(8,128)(2,1)} %w2_ref.1, ...), custom_call_target="tpu_custom_call" | custom-call | tf_op jit(solution)/shard_map/pack/pallas_call | solution.py:468
  3.1 3.0 %collective-permute-start.2 = (bf16[32,1664]{1,0:T(8,128)(2,1)}, bf16[32,1664]{1,0:T(8,128)(2,1)S(1)}, u32[]{:S(2)}, u32[]{:S(2)}) collective-permute-start(bf16[32,1664]{1,0:T(8,128)(2,1)} %get-tuple-element.58), channel_id=1, source_target_pairs={{0,8},{2,10},{4,12},{6,14},{8,0},{10,2},{12,4},{14,6},{16,24},{18,... | collective-permute-start | bytes 319496 | tf_op jit(solution)/shard_map/ppermute | solution.py:547
  6.1 2.5 %collective-permute-start.1 = (bf16[32,1664]{1,0:T(8,128)(2,1)}, bf16[32,1664]{1,0:T(8,128)(2,1)S(1)}, u32[]{:S(2)}, u32[]{:S(2)}) collective-permute-start(bf16[32,1664]{1,0:T(8,128)(2,1)} %get-tuple-element.58), channel_id=1, source_target_pairs={{0,24},{2,26},{4,28},{6,30},{8,16},{10,18},{12,20},{14,22},{16,8},... | collective-permute-start | bytes 319496 | tf_op jit(solution)/shard_map/ppermute | solution.py:547
  8.7 0.7 slice.19
  9.4 0.7 constant_dynamic-slice_fusion
  10.2 0.7 slice.18
  11.0 0.9 pad_maximum_fusion.1.refs_4_
  11.9 0.6 collective-permute-start.10
  12.5 1.5 %collective-permute-start.4 = (bf16[2,32,1664]{2,1,0:T(8,128)(2,1)S(1)}, bf16[2,32,1664]{2,1,0:T(8,128)(2,1)S(1)}, u32[]{:S(2)}, u32[]{:S(2)}) collective-permute-start(bf16[2,32,1664]{2,1,0:T(8,128)(2,1)S(1)} %pad_maximum_fusion.1.refs_4_), channel_id=1, source_target_pairs={{0,4},{1,3},{2,6},{3,1},{4,0},{5,7},{6,2},{7,5},{8,12},{9,11},{10,... | collective-permute-start | bytes 638984 | tf_op jit(solution)/shard_map/ppermute | solution.py:552
  14.0 0.9 collective-permute-done.1
  14.9 1.5 %collective-permute-start.3 = (bf16[2,32,1664]{2,1,0:T(8,128)(2,1)S(1)}, bf16[2,32,1664]{2,1,0:T(8,128)(2,1)S(1)}, u32[]{:S(2)}, u32[]{:S(2)}) collective-permute-start(bf16[2,32,1664]{2,1,0:T(8,128)(2,1)S(1)} %pad_maximum_fusion.1.refs_4_), channel_id=1, source_target_pairs={{0,2},{1,5},{2,0},{3,7},{4,6},{5,1},{6,4},{7,3},{8,10},{9,13},{10,... | collective-permute-start | bytes 638984 | tf_op jit(solution)/shard_map/ppermute | solution.py:552
  16.4 2.1 %collective-permute-done = bf16[32,1664]{1,0:T(8,128)(2,1)S(1)} collective-permute-done((bf16[32,1664]{1,0:T(8,128)(2,1)}, bf16[32,1664]{1,0:T(8,128)(2,1)S(1)}, u32[]{:S(2)}, u32[]{:S(2)}) %collective-permute-start) | collective-permute-done | bytes 106528 | tf_op jit(solution)/shard_map/ppermute | solution.py:547
  18.5 1.7 %collective-permute-done.4.refs_8_ = bf16[2,32,1664]{2,1,0:T(8,128)(2,1)S(1)} collective-permute-done((bf16[2,32,1664]{2,1,0:T(8,128)(2,1)S(1)}, bf16[2,32,1664]{2,1,0:T(8,128)(2,1)S(1)}, u32[]{:S(2)}, u32[]{:S(2)}) %collective-permute-start.4) | collective-permute-done | bytes 213024 | tf_op jit(solution)/shard_map/ppermute | solution.py:552
  20.3 0.5 collective-permute-done.3.refs_6_
  20.8 1.5 %collective-permute-start.6 = (bf16[2,32,1664]{2,1,0:T(8,128)(2,1)S(1)}, bf16[2,32,1664]{2,1,0:T(8,128)(2,1)S(1)}, u32[]{:S(2)}, u32[]{:S(2)}) collective-permute-start(bf16[2,32,1664]{2,1,0:T(8,128)(2,1)S(1)} %pad_maximum_fusion.refs_5_), channel_id=1, source_target_pairs={{0,2},{1,5},{2,0},{3,7},{4,6},{5,1},{6,4},{7,3},{8,10},{9,13},{10,... | collective-permute-start | bytes 638984 | tf_op jit(solution)/shard_map/ppermute | solution.py:552
  22.2 0.5 collective-permute-start.12
  22.8 1.5 %collective-permute-start.8 = (bf16[2,32,1664]{2,1,0:T(8,128)(2,1)S(1)}, bf16[2,32,1664]{2,1,0:T(8,128)(2,1)S(1)}, u32[]{:S(2)}, u32[]{:S(2)}) collective-permute-start(bf16[2,32,1664]{2,1,0:T(8,128)(2,1)S(1)} %collective-permute-done.3.refs_6_), channel_id=1, source_target_pairs={{0,4},{1,3},{2,6},{3,1},{4,0},{5,7},{6,2},{7,5},{8,12},{9,11},{10,... | collective-permute-start | bytes 638984 | tf_op jit(solution)/shard_map/ppermute | solution.py:552
  24.3 0.5 collective-permute-start.7
  24.8 3.1 %collective-permute-done.6.refs_7_ = bf16[2,32,1664]{2,1,0:T(8,128)(2,1)S(1)} collective-permute-done((bf16[2,32,1664]{2,1,0:T(8,128)(2,1)S(1)}, bf16[2,32,1664]{2,1,0:T(8,128)(2,1)S(1)}, u32[]{:S(2)}, u32[]{:S(2)}) %collective-permute-start.6) | collective-permute-done | bytes 213024 | tf_op jit(solution)/shard_map/ppermute | solution.py:552
  27.8 1.5 %collective-permute-start.9 = (bf16[2,32,1664]{2,1,0:T(8,128)(2,1)S(1)}, bf16[2,32,1664]{2,1,0:T(8,128)(2,1)S(1)}, u32[]{:S(2)}, u32[]{:S(2)}) collective-permute-start(bf16[2,32,1664]{2,1,0:T(8,128)(2,1)S(1)} %collective-permute-done.6.refs_7_), channel_id=1, source_target_pairs={{0,4},{1,3},{2,6},{3,1},{4,0},{5,7},{6,2},{7,5},{8,12},{9,11},{10,... | collective-permute-start | bytes 638984 | tf_op jit(solution)/shard_map/ppermute | solution.py:552
  29.4 0.5 collective-permute-start.13
  30.0 0.9 collective-permute-done.7.refs_9_
  31.0 2.7 %collective-permute-done.9.refs_11_ = bf16[2,32,1664]{2,1,0:T(8,128)(2,1)S(1)} collective-permute-done((bf16[2,32,1664]{2,1,0:T(8,128)(2,1)S(1)}, bf16[2,32,1664]{2,1,0:T(8,128)(2,1)S(1)}, u32[]{:S(2)}, u32[]{:S(2)}) %collective-permute-start.9) | collective-permute-done | bytes 213024 | tf_op jit(solution)/shard_map/ppermute | solution.py:552
  33.8 1.4 %collective-permute-done.17.refs_19_ = bf16[2,32,1664]{2,1,0:T(8,128)(2,1)S(1)} collective-permute-done((bf16[2,32,1664]{2,1,0:T(8,128)(2,1)S(1)}, bf16[2,32,1664]{2,1,0:T(8,128)(2,1)S(1)}, u32[]{:S(2)}, u32[]{:S(2)}) %collective-permute-start.17) | collective-permute-done | bytes 213024 | tf_op jit(solution)/shard_map/ppermute | solution.py:556
  35.2 46.2 %experts.1 = (bf16[512,3072]{1,0:T(8,128)(2,1)}, bf16[512,448]{1,0:T(8,128)(2,1)}, bf16[4,32,1664]{2,1,0:T(8,128)(2,1)S(1)}, bf16[4,32,1664]{2,1,0:T(8,128)(2,1)...) custom-call(s32[17]{0:T(128)S(1)} %pad_add_fusion.tab_ref, ...), custom_call_target="tpu_custom_call" | custom-call | flops 49999998976 | bytes 24000000 | tf_op jit(solution)/shard_map/experts/pallas_call | solution.py:370
  81.4 0.2 collective-permute-start.19
  81.5 0.4 collective-permute-start.18
  81.9 1.5 %collective-permute-done.19.refs_1_ = bf16[4,32,1664]{2,1,0:T(8,128)(2,1)S(1)} collective-permute-done((bf16[4,32,1664]{2,1,0:T(8,128)(2,1)}, bf16[4,32,1664]{2,1,0:T(8,128)(2,1)S(1)}, u32[]{:S(2)}, u32[]{:S(2)}) %collective-permute-start.19) | collective-permute-done | bytes 426016 | tf_op jit(solution)/shard_map/ppermute | solution.py:556
  83.5 0.5 collective-permute-done.18.refs_1_
  84.1 0.2 collective-permute-start.20
  84.3 0.4 collective-permute-start.21
  84.7 1.5 %collective-permute-start.22 = (bf16[4,32,1664]{2,1,0:T(8,128)(2,1)S(1)}, bf16[4,32,1664]{2,1,0:T(8,128)(2,1)S(1)}, u32[]{:S(2)}, u32[]{:S(2)}) collective-permute-start(bf16[4,32,1664]{2,1,0:T(8,128)(2,1)S(1)} %sum_fourth.1.refs_2_), channel_id=1, source_target_pairs={{0,4},{1,3},{2,6},{3,1},{4,0},{5,7},{6,2},{7,5},{8,12},{9,11},{10,... | collective-permute-start | bytes 1277960 | tf_op jit(solution)/shard_map/ppermute | solution.py:552
  86.2 0.8 collective-permute-start.23
  87.0 1.5 %collective-permute-start.24 = (bf16[4,32,1664]{2,1,0:T(8,128)(2,1)S(1)}, bf16[4,32,1664]{2,1,0:T(8,128)(2,1)S(1)}, u32[]{:S(2)}, u32[]{:S(2)}) collective-permute-start(bf16[4,32,1664]{2,1,0:T(8,128)(2,1)S(1)} %get-tuple-element.75.refs_0_), channel_id=1, source_target_pairs={{0,4},{1,3},{2,6},{3,1},{4,0},{5,7},{6,2},{7,5},{8,12},{9,11},{10,... | collective-permute-start | bytes 1277960 | tf_op jit(solution)/shard_map/ppermute | solution.py:552
  88.5 6.5 %input_own.1 = (f32[416,6144]{1,0:T(8,128)}, f32[13,6144]{1,0:T(8,128)}, f32[8,128]{1,0:T(8,128)S(1)}) custom-call(s32[17]{0:T(128)S(1)} %pad_add_fusion.tab_ref, bf16[512,3072]{1,0:T(8,128)(2,1)} %get-tuple-element.71.hg_ref, bf16[512,448]{1,0:T(8,128)(2,1)S(1)} %copy-done.1, bf16[4,32,1664]{2,1,0:T(8,128)(2,1)S(1)} %get-tuple-element.75.refs_0_), custom_call_target="tpu_custom_call" | custom-call | flops 4000000000 | bytes 9000000 | tf_op jit(solution)/shard_map/input_own/pallas_call | solution.py:411
  95.2 0.7 collective-permute-start.25
  95.9 4.6 %input_far.1 = (f32[416,6144]{1,0:T(8,128)}, f32[13,6144]{1,0:T(8,128)}, f32[8,128]{1,0:T(8,128)S(1)}) custom-call(s32[17]{0:T(128)S(1)} %pad_add_fusion.tab_ref, bf16[512,3072]{1,0:T(8,128)(2,1)S(1)} %collective-permute-done.20.hg_ref, bf16[512,448]{1,0:T(8,128)(2,1)S(1)} %copy-done.1, ...), custom_call_target="tpu_custom_call", output_to_operand_aliasing={{0}: (4, {}), {1}: (5, {})} | custom-call | flops 4000000000 | bytes 9000000 | tf_op jit(solution)/shard_map/input_far/pallas_call | solution.py:411
  100.5 2.9 %collective-permute-done.25.refs_3_ = bf16[4,32,1664]{2,1,0:T(8,128)(2,1)S(1)} collective-permute-done((bf16[4,32,1664]{2,1,0:T(8,128)(2,1)S(1)}, bf16[4,32,1664]{2,1,0:T(8,128)(2,1)S(1)}, u32[]{:S(2)}, u32[]{:S(2)}) %collective-permute-start.25) | collective-permute-done | bytes 426016 | tf_op jit(solution)/shard_map/ppermute | solution.py:552
  103.4 0.2 sum_first.1
  103.6 2.5 %collective-permute-start.26 = (bf16[32,1664]{1,0:T(8,128)(2,1)S(1)}, bf16[32,1664]{1,0:T(8,128)(2,1)S(1)}, u32[]{:S(2)}, u32[]{:S(2)}) collective-permute-start(bf16[32,1664]{1,0:T(8,128)(2,1)S(1)} %get-tuple-element.85), channel_id=1, source_target_pairs={{0,24},{2,26},{4,28},{6,30},{8,16},{10,18},{12,20},{14,22},{16,8},... | collective-permute-start | bytes 319496 | tf_op jit(solution)/shard_map/ppermute | solution.py:547
  106.1 1.6 %collective-permute-start.27 = (bf16[32,1664]{1,0:T(8,128)(2,1)S(1)}, bf16[32,1664]{1,0:T(8,128)(2,1)S(1)}, u32[]{:S(2)}, u32[]{:S(2)}) collective-permute-start(bf16[32,1664]{1,0:T(8,128)(2,1)S(1)} %get-tuple-element.86), channel_id=1, source_target_pairs={{0,16},{2,18},{4,20},{6,22},{8,24},{10,26},{12,28},{14,30},{16,0},... | collective-permute-start | bytes 319496 | tf_op jit(solution)/shard_map/ppermute | solution.py:547
  107.7 0.5 collective-permute-start.28
  108.2 2.0 %collective-permute-done.26.refs_1_ = bf16[32,1664]{1,0:T(8,128)(2,1)S(1)} collective-permute-done((bf16[32,1664]{1,0:T(8,128)(2,1)S(1)}, bf16[32,1664]{1,0:T(8,128)(2,1)S(1)}, u32[]{:S(2)}, u32[]{:S(2)}) %collective-permute-start.26) | collective-permute-done | bytes 106528 | tf_op jit(solution)/shard_map/ppermute | solution.py:547
  110.3 6.4 %collective-permute-done.27.refs_2_ = bf16[32,1664]{1,0:T(8,128)(2,1)S(1)} collective-permute-done((bf16[32,1664]{1,0:T(8,128)(2,1)S(1)}, bf16[32,1664]{1,0:T(8,128)(2,1)S(1)}, u32[]{:S(2)}, u32[]{:S(2)}) %collective-permute-start.27) | collective-permute-done | bytes 106528 | tf_op jit(solution)/shard_map/ppermute | solution.py:547
  116.7 0.5 collective-permute-start.32
  117.2 0.7 collective-permute-done.31.refs_6_
  117.9 0.2 collective-permute-done.32.refs_7_
  118.0 0.8 finish.1
  (45 shorter events, 1.0 us)
Async XLA Ops:
  0.7 10.3 %copy-start = (bf16[6144,13]{0,1:T(8,128)(2,1)S(1)}, bf16[6144,13]{0,1:T(8,128)(2,1)}, u32[]{:S(2)}) copy-start(bf16[6144,13]{0,1:T(8,128)(2,1)} %param.18) | copy-start | bytes 479236
  3.1 7.9 %collective-permute-start.2 = (bf16[32,1664]{1,0:T(8,128)(2,1)}, bf16[32,1664]{1,0:T(8,128)(2,1)S(1)}, u32[]{:S(2)}, u32[]{:S(2)}) collective-permute-start(bf16[32,1664]{1,0:T(8,128)(2,1)} %get-tuple-element.58), channel_id=1, source_target_pairs={{0,8},{2,10},{4,12},{6,14},{8,0},{10,2},{12,4},{14,6},{16,24},{18,... | collective-permute-start | bytes 319496 | tf_op jit(solution)/shard_map/ppermute | solution.py:547
  6.1 8.8 %collective-permute-start.1 = (bf16[32,1664]{1,0:T(8,128)(2,1)}, bf16[32,1664]{1,0:T(8,128)(2,1)S(1)}, u32[]{:S(2)}, u32[]{:S(2)}) collective-permute-start(bf16[32,1664]{1,0:T(8,128)(2,1)} %get-tuple-element.58), channel_id=1, source_target_pairs={{0,24},{2,26},{4,28},{6,30},{8,16},{10,18},{12,20},{14,22},{16,8},... | collective-permute-start | bytes 319496 | tf_op jit(solution)/shard_map/ppermute | solution.py:547
  8.6 9.9 %collective-permute-start = (bf16[32,1664]{1,0:T(8,128)(2,1)}, bf16[32,1664]{1,0:T(8,128)(2,1)S(1)}, u32[]{:S(2)}, u32[]{:S(2)}) collective-permute-start(bf16[32,1664]{1,0:T(8,128)(2,1)} %get-tuple-element.58), channel_id=1, source_target_pairs={{0,16},{2,18},{4,20},{6,22},{8,24},{10,26},{12,28},{14,30},{16,0},... | collective-permute-start | bytes 319496 | tf_op jit(solution)/shard_map/ppermute | solution.py:547
  10.1 8.4 %collective-permute-start.5 = (f32[1,3584]{1,0:T(1,128)S(1)}, f32[1,3584]{1,0:T(1,128)S(1)}, u32[]{:S(2)}, u32[]{:S(2)}) collective-permute-start(f32[1,3584]{1,0:T(1,128)S(1)} %pad_maximum_fusion.3), channel_id=1, source_target_pairs={{0,1},{1,0},{2,3},{3,2},{4,5},{5,4},{6,7},{7,6},{8,9},{9,8},{10,11... | collective-permute-start | bytes 43016 | tf_op jit(solution)/shard_map/ppermute | solution.py:556
  11.9 12.4 %collective-permute-start.10 = (bf16[2,32,1664]{2,1,0:T(8,128)(2,1)S(1)}, bf16[2,32,1664]{2,1,0:T(8,128)(2,1)S(1)}, u32[]{:S(2)}, u32[]{:S(2)}) collective-permute-start(bf16[2,32,1664]{2,1,0:T(8,128)(2,1)S(1)} %pad_maximum_fusion.1.refs_4_), channel_id=1, source_target_pairs={{0,1},{1,0},{2,3},{3,2},{4,5},{5,4},{6,7},{7,6},{8,9},{9,8},{10,11... | collective-permute-start | bytes 638984 | tf_op jit(solution)/shard_map/ppermute | solution.py:556
  12.5 7.8 %collective-permute-start.4 = (bf16[2,32,1664]{2,1,0:T(8,128)(2,1)S(1)}, bf16[2,32,1664]{2,1,0:T(8,128)(2,1)S(1)}, u32[]{:S(2)}, u32[]{:S(2)}) collective-permute-start(bf16[2,32,1664]{2,1,0:T(8,128)(2,1)S(1)} %pad_maximum_fusion.1.refs_4_), channel_id=1, source_target_pairs={{0,4},{1,3},{2,6},{3,1},{4,0},{5,7},{6,2},{7,5},{8,12},{9,11},{10,... | collective-permute-start | bytes 638984 | tf_op jit(solution)/shard_map/ppermute | solution.py:552
  14.9 5.8 %collective-permute-start.3 = (bf16[2,32,1664]{2,1,0:T(8,128)(2,1)S(1)}, bf16[2,32,1664]{2,1,0:T(8,128)(2,1)S(1)}, u32[]{:S(2)}, u32[]{:S(2)}) collective-permute-start(bf16[2,32,1664]{2,1,0:T(8,128)(2,1)S(1)} %pad_maximum_fusion.1.refs_4_), channel_id=1, source_target_pairs={{0,2},{1,5},{2,0},{3,7},{4,6},{5,1},{6,4},{7,3},{8,10},{9,13},{10,... | collective-permute-start | bytes 638984 | tf_op jit(solution)/shard_map/ppermute | solution.py:552
  20.8 7.1 %collective-permute-start.6 = (bf16[2,32,1664]{2,1,0:T(8,128)(2,1)S(1)}, bf16[2,32,1664]{2,1,0:T(8,128)(2,1)S(1)}, u32[]{:S(2)}, u32[]{:S(2)}) collective-permute-start(bf16[2,32,1664]{2,1,0:T(8,128)(2,1)S(1)} %pad_maximum_fusion.refs_5_), channel_id=1, source_target_pairs={{0,2},{1,5},{2,0},{3,7},{4,6},{5,1},{6,4},{7,3},{8,10},{9,13},{10,... | collective-permute-start | bytes 638984 | tf_op jit(solution)/shard_map/ppermute | solution.py:552
  22.2 7.1 %collective-permute-start.14 = (bf16[2,32,1664]{2,1,0:T(8,128)(2,1)S(1)}, bf16[2,32,1664]{2,1,0:T(8,128)(2,1)S(1)}, u32[]{:S(2)}, u32[]{:S(2)}) collective-permute-start(bf16[2,32,1664]{2,1,0:T(8,128)(2,1)S(1)} %collective-permute-done.4.refs_8_), channel_id=1, source_target_pairs={{0,1},{1,0},{2,3},{3,2},{4,5},{5,4},{6,7},{7,6},{8,9},{9,8},{10,11... | collective-permute-start | bytes 638984 | tf_op jit(solution)/shard_map/ppermute | solution.py:556
  22.2 7.1 %collective-permute-start.12 = (bf16[2,32,1664]{2,1,0:T(8,128)(2,1)S(1)}, bf16[2,32,1664]{2,1,0:T(8,128)(2,1)S(1)}, u32[]{:S(2)}, u32[]{:S(2)}) collective-permute-start(bf16[2,32,1664]{2,1,0:T(8,128)(2,1)S(1)} %collective-permute-done.3.refs_6_), channel_id=1, source_target_pairs={{0,1},{1,0},{2,3},{3,2},{4,5},{5,4},{6,7},{7,6},{8,9},{9,8},{10,11... | collective-permute-start | bytes 638984 | tf_op jit(solution)/shard_map/ppermute | solution.py:556
  22.8 7.1 %collective-permute-start.8 = (bf16[2,32,1664]{2,1,0:T(8,128)(2,1)S(1)}, bf16[2,32,1664]{2,1,0:T(8,128)(2,1)S(1)}, u32[]{:S(2)}, u32[]{:S(2)}) collective-permute-start(bf16[2,32,1664]{2,1,0:T(8,128)(2,1)S(1)} %collective-permute-done.3.refs_6_), channel_id=1, source_target_pairs={{0,4},{1,3},{2,6},{3,1},{4,0},{5,7},{6,2},{7,5},{8,12},{9,11},{10,... | collective-permute-start | bytes 638984 | tf_op jit(solution)/shard_map/ppermute | solution.py:552
  24.3 6.6 %collective-permute-start.7 = (bf16[2,32,1664]{2,1,0:T(8,128)(2,1)S(1)}, bf16[2,32,1664]{2,1,0:T(8,128)(2,1)S(1)}, u32[]{:S(2)}, u32[]{:S(2)}) collective-permute-start(bf16[2,32,1664]{2,1,0:T(8,128)(2,1)S(1)} %pad_maximum_fusion.refs_5_), channel_id=1, source_target_pairs={{0,4},{1,3},{2,6},{3,1},{4,0},{5,7},{6,2},{7,5},{8,12},{9,11},{10,... | collective-permute-start | bytes 638984 | tf_op jit(solution)/shard_map/ppermute | solution.py:552
  27.8 5.8 %collective-permute-start.9 = (bf16[2,32,1664]{2,1,0:T(8,128)(2,1)S(1)}, bf16[2,32,1664]{2,1,0:T(8,128)(2,1)S(1)}, u32[]{:S(2)}, u32[]{:S(2)}) collective-permute-start(bf16[2,32,1664]{2,1,0:T(8,128)(2,1)S(1)} %collective-permute-done.6.refs_7_), channel_id=1, source_target_pairs={{0,4},{1,3},{2,6},{3,1},{4,0},{5,7},{6,2},{7,5},{8,12},{9,11},{10,... | collective-permute-start | bytes 638984 | tf_op jit(solution)/shard_map/ppermute | solution.py:552
  29.4 4.4 %collective-permute-start.11 = (bf16[2,32,1664]{2,1,0:T(8,128)(2,1)S(1)}, bf16[2,32,1664]{2,1,0:T(8,128)(2,1)S(1)}, u32[]{:S(2)}, u32[]{:S(2)}) collective-permute-start(bf16[2,32,1664]{2,1,0:T(8,128)(2,1)S(1)} %pad_maximum_fusion.refs_5_), channel_id=1, source_target_pairs={{0,1},{1,0},{2,3},{3,2},{4,5},{5,4},{6,7},{7,6},{8,9},{9,8},{10,11... | collective-permute-start | bytes 638984 | tf_op jit(solution)/shard_map/ppermute | solution.py:556
  29.4 4.4 %collective-permute-start.13 = (bf16[2,32,1664]{2,1,0:T(8,128)(2,1)S(1)}, bf16[2,32,1664]{2,1,0:T(8,128)(2,1)S(1)}, u32[]{:S(2)}, u32[]{:S(2)}) collective-permute-start(bf16[2,32,1664]{2,1,0:T(8,128)(2,1)S(1)} %collective-permute-done.6.refs_7_), channel_id=1, source_target_pairs={{0,1},{1,0},{2,3},{3,2},{4,5},{5,4},{6,7},{7,6},{8,9},{9,8},{10,11... | collective-permute-start | bytes 638984 | tf_op jit(solution)/shard_map/ppermute | solution.py:556
  29.9 3.9 %collective-permute-start.16 = (bf16[2,32,1664]{2,1,0:T(8,128)(2,1)S(1)}, bf16[2,32,1664]{2,1,0:T(8,128)(2,1)S(1)}, u32[]{:S(2)}, u32[]{:S(2)}) collective-permute-start(bf16[2,32,1664]{2,1,0:T(8,128)(2,1)S(1)} %collective-permute-done.8.refs_10_), channel_id=1, source_target_pairs={{0,1},{1,0},{2,3},{3,2},{4,5},{5,4},{6,7},{7,6},{8,9},{9,8},{10,11... | collective-permute-start | bytes 638984 | tf_op jit(solution)/shard_map/ppermute | solution.py:556
  30.9 2.9 %collective-permute-start.15 = (bf16[2,32,1664]{2,1,0:T(8,128)(2,1)S(1)}, bf16[2,32,1664]{2,1,0:T(8,128)(2,1)S(1)}, u32[]{:S(2)}, u32[]{:S(2)}) collective-permute-start(bf16[2,32,1664]{2,1,0:T(8,128)(2,1)S(1)} %collective-permute-done.7.refs_9_), channel_id=1, source_target_pairs={{0,1},{1,0},{2,3},{3,2},{4,5},{5,4},{6,7},{7,6},{8,9},{9,8},{10,11... | collective-permute-start | bytes 638984 | tf_op jit(solution)/shard_map/ppermute | solution.py:556
  33.7 1.5 %collective-permute-start.17 = (bf16[2,32,1664]{2,1,0:T(8,128)(2,1)S(1)}, bf16[2,32,1664]{2,1,0:T(8,128)(2,1)S(1)}, u32[]{:S(2)}, u32[]{:S(2)}) collective-permute-start(bf16[2,32,1664]{2,1,0:T(8,128)(2,1)S(1)} %collective-permute-done.9.refs_11_), channel_id=1, source_target_pairs={{0,1},{1,0},{2,3},{3,2},{4,5},{5,4},{6,7},{7,6},{8,9},{9,8},{10,11... | collective-permute-start | bytes 638984 | tf_op jit(solution)/shard_map/ppermute | solution.py:556
  81.4 7.1 %copy-start.1 = (bf16[512,448]{1,0:T(8,128)(2,1)S(1)}, bf16[512,448]{1,0:T(8,128)(2,1)}, u32[]{:S(2)}) copy-start(bf16[512,448]{1,0:T(8,128)(2,1)} %get-tuple-element.72.wat_ref) | copy-start | bytes 1376260
  81.4 2.0 %collective-permute-start.19 = (bf16[4,32,1664]{2,1,0:T(8,128)(2,1)}, bf16[4,32,1664]{2,1,0:T(8,128)(2,1)S(1)}, u32[]{:S(2)}, u32[]{:S(2)}) collective-permute-start(bf16[4,32,1664]{2,1,0:T(8,128)(2,1)} %get-tuple-element.69), channel_id=1, source_target_pairs={{0,1},{1,0},{2,3},{3,2},{4,5},{5,4},{6,7},{7,6},{8,9},{9,8},{10,11... | collective-permute-start | bytes 1277960 | tf_op jit(solution)/shard_map/ppermute | solution.py:556
  81.5 2.5 %collective-permute-start.18 = (bf16[4,32,1664]{2,1,0:T(8,128)(2,1)}, bf16[4,32,1664]{2,1,0:T(8,128)(2,1)S(1)}, u32[]{:S(2)}, u32[]{:S(2)}) collective-permute-start(bf16[4,32,1664]{2,1,0:T(8,128)(2,1)} %get-tuple-element.67), channel_id=1, source_target_pairs={{0,1},{1,0},{2,3},{3,2},{4,5},{5,4},{6,7},{7,6},{8,9},{9,8},{10,11... | collective-permute-start | bytes 1277960 | tf_op jit(solution)/shard_map/ppermute | solution.py:556
  84.1 11.8 %collective-permute-start.20 = (bf16[512,3072]{1,0:T(8,128)(2,1)}, bf16[512,3072]{1,0:T(8,128)(2,1)S(1)}, u32[]{:S(2)}, u32[]{:S(2)}) collective-permute-start(bf16[512,3072]{1,0:T(8,128)(2,1)} %get-tuple-element.71.hg_ref), channel_id=1, source_target_pairs={{0,1},{1,0},{2,3},{3,2},{4,5},{5,4},{6,7},{7,6},{8,9},{9,8},{10,11... | collective-permute-start | bytes 9437192 | tf_op jit(solution)/shard_map/ppermute | solution.py:556
  84.3 10.7 %collective-permute-start.21 = (bf16[4,32,1664]{2,1,0:T(8,128)(2,1)S(1)}, bf16[4,32,1664]{2,1,0:T(8,128)(2,1)S(1)}, u32[]{:S(2)}, u32[]{:S(2)}) collective-permute-start(bf16[4,32,1664]{2,1,0:T(8,128)(2,1)S(1)} %get-tuple-element.74), channel_id=1, source_target_pairs={{0,1},{1,0},{2,3},{3,2},{4,5},{5,4},{6,7},{7,6},{8,9},{9,8},{10,11... | collective-permute-start | bytes 1277960 | tf_op jit(solution)/shard_map/ppermute | solution.py:556
  84.7 10.3 %collective-permute-start.22 = (bf16[4,32,1664]{2,1,0:T(8,128)(2,1)S(1)}, bf16[4,32,1664]{2,1,0:T(8,128)(2,1)S(1)}, u32[]{:S(2)}, u32[]{:S(2)}) collective-permute-start(bf16[4,32,1664]{2,1,0:T(8,128)(2,1)S(1)} %sum_fourth.1.refs_2_), channel_id=1, source_target_pairs={{0,4},{1,3},{2,6},{3,1},{4,0},{5,7},{6,2},{7,5},{8,12},{9,11},{10,... | collective-permute-start | bytes 1277960 | tf_op jit(solution)/shard_map/ppermute | solution.py:552
  86.2 14.3 %collective-permute-start.23 = (bf16[4,32,1664]{2,1,0:T(8,128)(2,1)S(1)}, bf16[4,32,1664]{2,1,0:T(8,128)(2,1)S(1)}, u32[]{:S(2)}, u32[]{:S(2)}) collective-permute-start(bf16[4,32,1664]{2,1,0:T(8,128)(2,1)S(1)} %get-tuple-element.82), channel_id=1, source_target_pairs={{0,1},{1,0},{2,3},{3,2},{4,5},{5,4},{6,7},{7,6},{8,9},{9,8},{10,11... | collective-permute-start | bytes 1277960 | tf_op jit(solution)/shard_map/ppermute | solution.py:556
  87.0 13.5 %collective-permute-start.24 = (bf16[4,32,1664]{2,1,0:T(8,128)(2,1)S(1)}, bf16[4,32,1664]{2,1,0:T(8,128)(2,1)S(1)}, u32[]{:S(2)}, u32[]{:S(2)}) collective-permute-start(bf16[4,32,1664]{2,1,0:T(8,128)(2,1)S(1)} %get-tuple-element.75.refs_0_), channel_id=1, source_target_pairs={{0,4},{1,3},{2,6},{3,1},{4,0},{5,7},{6,2},{7,5},{8,12},{9,11},{10,... | collective-permute-start | bytes 1277960 | tf_op jit(solution)/shard_map/ppermute | solution.py:552
  95.2 8.2 %collective-permute-start.25 = (bf16[4,32,1664]{2,1,0:T(8,128)(2,1)S(1)}, bf16[4,32,1664]{2,1,0:T(8,128)(2,1)S(1)}, u32[]{:S(2)}, u32[]{:S(2)}) collective-permute-start(bf16[4,32,1664]{2,1,0:T(8,128)(2,1)S(1)} %sum_second.1.refs_0_), channel_id=1, source_target_pairs={{0,2},{1,5},{2,0},{3,7},{4,6},{5,1},{6,4},{7,3},{8,10},{9,13},{10,... | collective-permute-start | bytes 1277960 | tf_op jit(solution)/shard_map/ppermute | solution.py:552
  103.6 6.7 %collective-permute-start.26 = (bf16[32,1664]{1,0:T(8,128)(2,1)S(1)}, bf16[32,1664]{1,0:T(8,128)(2,1)S(1)}, u32[]{:S(2)}, u32[]{:S(2)}) collective-permute-start(bf16[32,1664]{1,0:T(8,128)(2,1)S(1)} %get-tuple-element.85), channel_id=1, source_target_pairs={{0,24},{2,26},{4,28},{6,30},{8,16},{10,18},{12,20},{14,22},{16,8},... | collective-permute-start | bytes 319496 | tf_op jit(solution)/shard_map/ppermute | solution.py:547
  106.1 10.6 %collective-permute-start.27 = (bf16[32,1664]{1,0:T(8,128)(2,1)S(1)}, bf16[32,1664]{1,0:T(8,128)(2,1)S(1)}, u32[]{:S(2)}, u32[]{:S(2)}) collective-permute-start(bf16[32,1664]{1,0:T(8,128)(2,1)S(1)} %get-tuple-element.86), channel_id=1, source_target_pairs={{0,16},{2,18},{4,20},{6,22},{8,24},{10,26},{12,28},{14,30},{16,0},... | collective-permute-start | bytes 319496 | tf_op jit(solution)/shard_map/ppermute | solution.py:547
  107.7 8.9 %collective-permute-start.28 = (bf16[32,1664]{1,0:T(8,128)(2,1)S(1)}, bf16[32,1664]{1,0:T(8,128)(2,1)S(1)}, u32[]{:S(2)}, u32[]{:S(2)}) collective-permute-start(bf16[32,1664]{1,0:T(8,128)(2,1)S(1)} %get-tuple-element.87), channel_id=1, source_target_pairs={{0,8},{2,10},{4,12},{6,14},{8,0},{10,2},{12,4},{14,6},{16,24},{18,... | collective-permute-start | bytes 319496 | tf_op jit(solution)/shard_map/ppermute | solution.py:547
  108.2 9.0 %collective-permute-start.29 = (bf16[16,512]{1,0:T(8,128)(2,1)S(1)}, bf16[16,512]{1,0:T(8,128)(2,1)S(1)}, u32[]{:S(2)}, u32[]{:S(2)}) collective-permute-start(bf16[16,512]{1,0:T(8,128)(2,1)S(1)} %slice.20), channel_id=1, source_target_pairs={{0,1},{1,0},{2,3},{3,2},{4,5},{5,4},{6,7},{7,6},{8,9},{9,8},{10,11... | collective-permute-start | bytes 49160 | tf_op jit(solution)/shard_map/ppermute | solution.py:556
  110.3 6.9 %collective-permute-start.30 = (bf16[16,512]{1,0:T(8,128)(2,1)S(1)}, bf16[16,512]{1,0:T(8,128)(2,1)S(1)}, u32[]{:S(2)}, u32[]{:S(2)}) collective-permute-start(bf16[16,512]{1,0:T(8,128)(2,1)S(1)} %slice.24), channel_id=1, source_target_pairs={{0,1},{1,0},{2,3},{3,2},{4,5},{5,4},{6,7},{7,6},{8,9},{9,8},{10,11... | collective-permute-start | bytes 49160 | tf_op jit(solution)/shard_map/ppermute | solution.py:556
  116.7 1.2 collective-permute-start.31
  116.7 1.3 %collective-permute-start.32 = (bf16[16,512]{1,0:T(8,128)(2,1)S(1)}, bf16[16,512]{1,0:T(8,128)(2,1)S(1)}, u32[]{:S(2)}, u32[]{:S(2)}) collective-permute-start(bf16[16,512]{1,0:T(8,128)(2,1)S(1)} %slice.26), channel_id=1, source_target_pairs={{0,1},{1,0},{2,3},{3,2},{4,5},{5,4},{6,7},{7,6},{8,9},{9,8},{10,11... | collective-permute-start | bytes 49160 | tf_op jit(solution)/shard_map/ppermute | solution.py:556
